TPU v7x, 32 devices: a whole 2x2x4 slice. The times are simulated.
32 devices in a mesh: shard: 2 (over z_hi), ctx: 8 (over y, x, core), tensor: 2 (over z_lo).
Axes of the slice: x: 2, y: 2, z: 4 (z_hi: 2, z_lo: 2; z = z_hi * 2 + z_lo), core: 2. Of those that a mesh axis runs over, the one named last changes fastest.
Arguments:
- tokens: bfloat16 [16384, 1024], P(('shard', 'ctx')), may hold values from -6 to 6
- cont_lengths: int32 [2, 8], P('shard'), may hold values from 1 to 1024, 4096 in all within a row
- attn_gain: bfloat16 [1024], P(('shard', 'ctx')), may hold values from 0.099609375 to 1.8984375
- ffn_gain: bfloat16 [1024], P(('shard', 'ctx')), may hold values from 0.099609375 to 1.8984375
- query_gain: bfloat16 [128], P(('shard', 'ctx')), may hold values from 0.5 to 1.59375
- key_gain: bfloat16 [128], P(('shard', 'ctx')), may hold values from 0.5 to 1.59375
- w_query: bfloat16 [1024, 2048], P(('shard', 'ctx'), 'tensor'), may hold values from -0.1875 to 0.1875
- key_weight: bfloat16 [1024, 1024], P(('shard', 'ctx'), 'tensor'), may hold values from -0.1875 to 0.1875
- value_weight: bfloat16 [1024, 1024], P(('shard', 'ctx'), 'tensor'), may hold values from -0.1875 to 0.1875
- w_out: bfloat16 [2048, 1024], P('tensor', ('shard', 'ctx')), may hold values from -1.5 to 1.5
- w_gate: bfloat16 [1024, 3072], P(('shard', 'ctx'), 'tensor'), may hold values from -0.1875 to 0.1875
- w_up: bfloat16 [1024, 3072], P(('shard', 'ctx'), 'tensor'), may hold values from -0.1875 to 0.1875
- w_down: bfloat16 [3072, 1024], P('tensor', ('shard', 'ctx')), may hold values from -0.109375 to 0.109375
- cotangent: bfloat16 [16384, 1024], P(('shard', 'ctx')), may hold values from -6 to 6
Outputs:
- layer_out: bfloat16 [16384, 1024], P(('shard', 'ctx'))
- grad_tokens: bfloat16 [16384, 1024], P(('shard', 'ctx'))
- grad_attn_gain: float32 [1024], P(('shard', 'ctx'))
- grad_ffn_gain: float32 [1024], P(('shard', 'ctx'))
- grad_query_gain: float32 [128], P(('shard', 'ctx'))
- grad_key_gain: float32 [128], P(('shard', 'ctx'))
- grad_w_query: float32 [1024, 2048], P(('shard', 'ctx'), 'tensor')
- grad_w_key: float32 [1024, 1024], P(('shard', 'ctx'), 'tensor')
- grad_w_value: float32 [1024, 1024], P(('shard', 'ctx'), 'tensor')
- grad_w_out: float32 [2048, 1024], P('tensor', ('shard', 'ctx'))
- grad_w_gate: float32 [1024, 3072], P(('shard', 'ctx'), 'tensor')
- grad_w_up: float32 [1024, 3072], P(('shard', 'ctx'), 'tensor')
- grad_w_down: float32 [3072, 1024], P('tensor', ('shard', 'ctx'))
Inputs may be any that keep to these rules, and one draw needn't show every extreme that they name: `cont_lengths`: each row holds the lengths of one group's 8 continuations, summing to 4096, the largest exactly 1024.
All inputs are finite; a program needn't handle non-finite values.
Results may differ from a plain program's by a relative error of at most 0.019.
Values may be sent and summed in bfloat16 or wider, within the bound.
No kernel may reach another device: no remote copies, remote signals or barrier semaphores. Data moves between devices by JAX's collectives and lax.ppermute only.
A program may use at most 640 MiB of HBM per device.

v0:
```python
import functools
import math

import jax
import jax.numpy as jnp
from jax import lax
from jax.experimental import pallas as pl
from jax.experimental.pallas import tpu as pltpu
from jax.sharding import PartitionSpec as P

HEAD_SIZE = 128
PROMPT = 4096
CONT_TOK = 4096
LONGEST = 1024

EPSILON = 1e-06
ROPE_BASE = 1000000.0
MASKED = -1e30
LOG2E = math.log2(math.e)
LN2 = math.log(2.0)
SCALE = 1.0 / math.sqrt(HEAD_SIZE)

BF = jnp.bfloat16
F32 = jnp.float32
NN = (((1,), (0,)), ((), ()))
NT = (((1,), (1,)), ((), ()))
TN = (((0,), (0,)), ((), ()))
MIB = 2**20
STATED = 0


def mm(left, right, dims=NN):
    return lax.dot_general(left, right, dims, preferred_element_type=F32)


def shaped(dims, kind):
    return jax.ShapeDtypeStruct(dims, kind)


def call(kernel, name, grid, ins, outs, scratch=(), vmem=56, scalars=None, keep=None, us=4):
    in_specs, arrays = [], []
    for array, block, index in ins:
        arrays.append(array)
        in_specs.append(pl.BlockSpec(memory_space=pl.ANY) if block is None else pl.BlockSpec(block, index))
    lead = 0 if scalars is None else 1
    return pl.pallas_call(
        kernel,
        grid_spec=pltpu.PrefetchScalarGridSpec(
            num_scalar_prefetch=lead,
            grid=grid,
            in_specs=in_specs,
            out_specs=[pl.BlockSpec(block, index) for _, block, index in outs],
            scratch_shapes=list(scratch),
        ),
        out_shape=[shape for shape, _, _ in outs],
        input_output_aliases={a + lead: b for a, b in (keep or {}).items()},
        compiler_params=pltpu.CompilerParams(vmem_limit_bytes=vmem * MIB),
        cost_estimate=pl.CostEstimate(flops=int(us * STATED), bytes_accessed=0, transcendentals=0),
        name=name,
    )(*([] if scalars is None else [scalars]), *arrays)


def rms(values):
    return lax.rsqrt(jnp.mean(values * values, axis=-1, keepdims=True) + EPSILON)


def turn(values, cos, sin):
    return values * cos + pltpu.roll(values, HEAD_SIZE // 2, 1) * sin


def turn_back(values, cos, sin):
    return values * cos - pltpu.roll(values, HEAD_SIZE // 2, 1) * sin


def kv_kernel(heads, x_ref, gain_ref, w_ref, hgain_ref, cos_ref, sin_ref, *refs):
    normed_ref, kv_ref, lin_ref = refs[-3:]
    x = x_ref[...].astype(F32)
    normed_ref[...] = (x * rms(x) * gain_ref[...]).astype(BF)
    both = mm(normed_ref[...], w_ref[...])
    width = heads * HEAD_SIZE
    kv_ref[1] = both[:, width:].astype(BF)
    for h in range(heads):
        cols = slice(h * HEAD_SIZE, (h + 1) * HEAD_SIZE)
        lin = both[:, cols]
        lin_ref[:, cols] = lin
        kv_ref[0, :, cols] = turn(lin * rms(lin) * hgain_ref[...], cos_ref[...], sin_ref[...]).astype(BF)


def q_kernel(heads, normed_ref, w_ref, hgain_ref, cos_ref, sin_ref, q_ref, lin_ref):
    both = mm(normed_ref[...], w_ref[...])
    for h in range(heads):
        cols = slice(h * HEAD_SIZE, (h + 1) * HEAD_SIZE)
        lin = both[:, cols]
        lin_ref[:, cols] = lin
        turned = turn(lin * rms(lin) * hgain_ref[...], cos_ref[...], sin_ref[...])
        q_ref[:, cols] = (turned * (SCALE * LOG2E)).astype(BF)


def pack_kernel(chunk, key_ref, value_ref, out_ref, gate_ref, up_ref, down_ref, kv_ref, rest_ref):
    k_cols, o_cols, units = key_ref.shape[1], out_ref.shape[1], gate_ref.shape[1]
    kv_ref[:, :k_cols] = key_ref[...]
    kv_ref[:, k_cols:] = value_ref[...]
    rest_ref[:, :o_cols] = out_ref[...]
    for at in range(0, units, chunk):
        to = o_cols + 2 * at
        rest_ref[:, to : to + chunk] = gate_ref[:, at : at + chunk]
        rest_ref[:, to + chunk : to + 2 * chunk] = up_ref[:, at : at + chunk]
    rest_ref[:, o_cols + 2 * units :] = down_ref[...]


def pack(chunk, *weights):
    wide, k_cols = weights[0].shape
    width = weights[2].shape[1] + 3 * weights[3].shape[1]
    whole = lambda f: (0, 0)
    ins = [(w, w.shape, whole) for w in weights]
    outs = [(shaped((wide, cols), BF), (wide, cols), whole) for cols in (2 * k_cols, width)]
    return call(functools.partial(pack_kernel, chunk), "pack", (1,), ins, outs, us=3)


def by_top_bit(slots):
    groups = {}
    for at, s in enumerate(slots):
        if s:
            groups.setdefault(1 << (s.bit_length() - 1), []).append(at)
    return groups


def fwd_kernel(plan, idx_ref, lo_ref, *refs):
    halves, slots, halos = plan["halves"], plan["slots"], plan["halos"]
    refs = list(refs)
    q_refs = [refs.pop(0) for _ in halves]
    slot_refs = [refs.pop(0) for _ in slots]
    halo_refs = [refs.pop(0) for _ in halos]
    prior = [refs.pop(0) for _ in range(2 * len(halves))] if plan["carry"] else None
    if plan["last"]:
        w_ref = refs.pop(0)
        if plan["alias"]:
            refs.pop(0)
        out_ref, lse_ref, part_ref = refs[:3]
        refs = refs[3:]
    else:
        results, refs = refs[: 2 * len(halves)], refs[2 * len(halves) :]
    me, lo_first = idx_ref[0], idx_ref[1]
    rows = q_refs[0].shape[0]
    row = lax.broadcasted_iota(jnp.int32, (2 * rows, 1), 0)
    row = jnp.where(row >= rows, row - rows, row)
    col = lax.broadcasted_iota(jnp.int32, (1, rows), 1)
    for n, half in enumerate(halves):
        qs, acc, tot = refs[3 * n : 3 * n + 3]
        for g in range(2):
            cols, at = slice(g * HEAD_SIZE, (g + 1) * HEAD_SIZE), slice(g * rows, (g + 1) * rows)
            qs[at, :] = q_refs[n][:, cols]
            if prior is not None:
                acc[at, :] = prior[2 * n][:, cols]
                tot[at, :] = prior[2 * n + 1][:, cols]
        empty = [prior is None]

        def add(kv_ref, mask=None):
            scores = mm(qs[...], kv_ref[0], NT)
            if mask is not None:
                scores = jnp.where(mask, scores, MASKED)
            weights = jnp.exp2(scores)
            total = weights[:, :128]
            for at in range(128, weights.shape[1], 128):
                total = total + weights[:, at : at + 128]
            part = mm(weights.astype(BF), kv_ref[1])
            if empty[0]:
                acc[...] = part
                tot[...] = total
            else:
                acc[...] += part
                tot[...] += total
            empty[0] = False

        if half == 1:
            for kv_ref in slot_refs:
                add(kv_ref)
            low = jnp.concatenate([lo_ref[:, :1], lo_ref[:, :1]])
            for d, kv_ref in zip(halos, halo_refs):
                if d == 0:
                    add(kv_ref, (col <= row) & (col >= low))
                else:

                    @pl.when(lo_first < -(d - 1) * rows)
                    def _(d=d, kv_ref=kv_ref):
                        add(kv_ref, col - d * rows >= low)

        else:
            if 0 in slots:
                add(slot_refs[slots.index(0)], col <= row)
            for bit, group in by_top_bit(slots).items():

                @pl.when(jnp.bitwise_and(me, bit) != 0)
                def _(group=group):
                    for at in group:
                        add(slot_refs[at])

        if not plan["last"]:
            for g in range(2):
                cols, at = slice(g * HEAD_SIZE, (g + 1) * HEAD_SIZE), slice(g * rows, (g + 1) * rows)
                results[2 * n][:, cols] = acc[at, :]
                results[2 * n + 1][:, cols] = tot[at, :]
    if plan["last"]:
        qs, acc, tot, part_acc = refs
        step, steps = pl.program_id(0), pl.num_programs(0)
        for g in range(2):
            cols, at = slice(g * HEAD_SIZE, (g + 1) * HEAD_SIZE), slice(g * rows, (g + 1) * rows)
            total = jnp.sum(tot[at, :], axis=1, keepdims=True)
            out_ref[:, cols] = (acc[at, :] / total).astype(BF)
            lse_ref[0, g : g + 1, :] = jnp.log2(jnp.sum(tot[at, :].T, axis=0, keepdims=True))
        part = mm(out_ref[...], w_ref[...], NT)

        @pl.when(step == 0)
        def _():
            part_acc[...] = part

        @pl.when((step > 0) & (step < steps - 1))
        def _():
            part_acc[...] += part

        @pl.when(step == steps - 1)
        def _():
            part_ref[...] = (part_acc[...] + part).astype(BF)


def attention_forward(halves, scalars, q, low, slots, halos, carry=None, last=None):
    rows, heads = q.shape[0] // 2, q.shape[1] // 256
    plan = dict(halves=halves, slots=list(slots), halos=list(halos), carry=carry is not None,
                last=last is not None, alias=last is not None and last[1] is not None)
    part = lambda h, i: (0, h)
    ins = [(low, (rows, 128), lambda h, i: (0, 0))]
    ins += [(q, (rows, 256), lambda h, i, half=half: (half, h)) for half in halves]
    for kv in list(slots.values()) + list(halos.values()):
        ins.append((kv, (2, rows, 128), lambda h, i: (0, 0, h)))
    if carry is not None:
        ins += [(c, (rows, 256), part) for c in carry]
    scratch, keep = [], {}
    for _ in halves:
        scratch += [pltpu.VMEM((2 * rows, 128), BF)] + [pltpu.VMEM((2 * rows, 128), F32)] * 2
    state = shaped((rows, heads * 256), F32)
    if last is None:
        outs = [(state, (rows, 256), part)] * (2 * len(halves))
    else:
        w_rest, other = last
        model = w_rest.shape[0]
        ins.append((w_rest, (model, 256), part))
        if other is not None:
            keep = {len(ins): 0}
            ins.append((other, None, None))
        half = halves[0]
        outs = [
            (shaped((2 * rows, heads * 256), BF), (rows, 256), lambda h, i: (half, h)),
            (shaped((heads, 8, rows), F32), (1, 8, rows), lambda h, i: (h, 0, 0)),
            (shaped((rows, model), BF), (rows, model), lambda h, i: (0, 0)),
        ]
        scratch.append(pltpu.VMEM((rows, model), F32))
    blocks = len(slots) * len(halves) + len(halos)
    return call(functools.partial(fwd_kernel, plan), "attend", (heads,), ins, outs, scratch,
                scalars=scalars, keep=keep, us=2 + 3 * blocks)


def bwd_kernel(plan, idx_ref, q_ref, do_ref, lse_ref, delta_ref, lo_ref, *refs):
    half, slots, halos = plan["half"], plan["slots"], plan["halos"]
    refs = list(refs)
    slot_refs = [refs.pop(0) for _ in slots]
    halo_refs = [refs.pop(0) for _ in halos]
    prior_dq = refs.pop(0) if plan["carry"] else None
    prior = [refs.pop(0) for _ in slots] if plan["sum"] else None
    if plan["alias"]:
        refs.pop(0)
    dq_ref = refs.pop(0)
    slot_outs = [refs.pop(0) for _ in slots]
    halo_outs = [refs.pop(0) for _ in halos]
    qs, dos, lses, deltas, dq = refs
    me, lo_first = idx_ref[0], idx_ref[1]
    rows = q_ref.shape[0]
    for g in range(2):
        cols, at = slice(g * HEAD_SIZE, (g + 1) * HEAD_SIZE), slice(g * rows, (g + 1) * rows)
        qs[at, :] = q_ref[:, cols]
        dos[at, :] = do_ref[:, cols]
        lses[:, at] = lse_ref[0, g : g + 1, :]
        deltas[:, at] = delta_ref[0, g : g + 1, :]
    dq[...] = jnp.zeros_like(dq) if prior_dq is None else prior_dq[...]

    def block(kv_ref, out_ref, mask=None, before=None):
        keys = kv_ref[0]
        scores = mm(keys, qs[...], NT)
        dp = mm(kv_ref[1], dos[...], NT)
        scores = scores - lses[...]
        if mask is not None:
            scores = jnp.where(mask, scores, MASKED)
        probs = jnp.exp2(scores)
        ds = (probs * (dp - deltas[...])).astype(BF)
        dq[...] += mm(keys.T, ds)
        dk, dv = mm(ds, qs[...]) * LN2, mm(probs.astype(BF), dos[...])
        if before is not None:
            dk, dv = dk + before[0].astype(F32), dv + before[1].astype(F32)
        out_ref[0] = dk.astype(BF)
        out_ref[1] = dv.astype(BF)

    lane = lax.broadcasted_iota(jnp.int32, (1, 2 * rows), 1)
    lane = jnp.where(lane >= rows, lane - rows, lane)
    key = lax.broadcasted_iota(jnp.int32, (rows, 1), 0)

    def when(needed, kv_ref, out_ref, mask=None):
        @pl.when(needed)
        def _():
            block(kv_ref, out_ref, mask)

        @pl.when(jnp.logical_not(needed))
        def _():
            out_ref[...] = jnp.zeros_like(out_ref)

    low = lo_ref[:1, :]
    for d, kv_ref, out_ref in zip(halos, halo_refs, halo_outs):
        if d == 0:
            block(kv_ref, out_ref, (key <= lane) & (key >= low))
        else:
            when(lo_first < -(d - 1) * rows, kv_ref, out_ref, key - d * rows >= low)
    if half == 1:
        for at in range(len(slots)):
            block(slot_refs[at], slot_outs[at], None, prior[at])
    else:
        if 0 in slots:
            at = slots.index(0)
            block(slot_refs[at], slot_outs[at], key <= lane)
        for bit, group in by_top_bit(slots).items():

            @pl.when(jnp.bitwise_and(me, bit) != 0)
            def _(group=group):
                for at in group:
                    block(slot_refs[at], slot_outs[at])

            @pl.when(jnp.bitwise_and(me, bit) == 0)
            def _(group=group):
                for at in group:
                    slot_outs[at][...] = jnp.zeros_like(slot_outs[at])

    if plan["last"]:
        for g in range(2):
            cols = slice(g * HEAD_SIZE, (g + 1) * HEAD_SIZE)
            dq_ref[:, cols] = dq[:, g * rows : (g + 1) * rows].T * SCALE
    else:
        dq_ref[...] = dq[...]


def attention_backward(half, scalars, q, do, lse, delta, low, slots, halos, carry=None, prior=None, last=True, whole=None):
    rows, heads = q.shape[0] // 2, q.shape[1] // 256
    plan = dict(half=half, slots=list(slots), halos=list(halos), carry=carry is not None,
                sum=prior is not None, last=last, alias=whole is not None)
    part = lambda h, i: (0, h)
    stat = lambda h, i: (h, 0, 0)
    kv_map = lambda h, i: (0, 0, h)
    ins = [
        (q, (rows, 256), lambda h, i: (half, h)),
        (do, (rows, 256), part),
        (lse, (1, 8, rows), stat),
        (delta, (1, 8, rows), stat),
        (low, (8, 2 * rows), lambda h, i: (0, 0)),
    ]
    pieces = list(slots.values()) + list(halos.values())
    ins += [(kv, (2, rows, 128), kv_map) for kv in pieces]
    if carry is not None:
        ins.append((carry, (128, 2 * rows), lambda h, i: (h, 0)))
    if prior is not None:
        ins += [(prior[s], (2, rows, 128), kv_map) for s in slots]
    keep = {}
    if whole is not None:
        keep = {len(ins): 0}
        ins.append((whole, None, None))
    if last:
        outs = [(shaped((2 * rows, heads * 256), F32), (rows, 256), lambda h, i: (half, h))]
    else:
        outs = [(shaped((heads * 128, 2 * rows), F32), (128, 2 * rows), lambda h, i: (h, 0))]
    outs += [(shaped(kv.shape, BF), (2, rows, 128), kv_map) for kv in pieces]
    scratch = [
        pltpu.VMEM((2 * rows, 128), BF),
        pltpu.VMEM((2 * rows, 128), BF),
        pltpu.VMEM((1, 2 * rows), F32),
        pltpu.VMEM((1, 2 * rows), F32),
        pltpu.VMEM((128, 2 * rows), F32),
    ]
    us = 4 + 6 * (len(slots) + len(halos))
    results = call(functools.partial(bwd_kernel, plan), "attend_back", (heads,), ins, outs, scratch,
                   scalars=scalars, us=us, keep=keep)
    n = len(slots)
    return results[0], dict(zip(slots, results[1 : 1 + n])), dict(zip(halos, results[1 + n :]))


def ffn_kernel(x_ref, own_ref, got_ref, gain_ref, dy_ref, gu_ref, down_ref, *refs):
    resid_ref, normed_ref, hidden_ref, dgu_ref, out_ref, back_ref, normed, out_acc, back_acc = refs[-9:]
    step, steps = pl.program_id(0), pl.num_programs(0)

    @pl.when(step == 0)
    def _():
        resid = x_ref[...].astype(F32) + (own_ref[...].astype(F32) + got_ref[...].astype(F32))
        resid_ref[...] = resid
        normed[...] = (resid * rms(resid) * gain_ref[...]).astype(BF)
        normed_ref[...] = normed[...]
        out_acc[...] = jnp.zeros_like(out_acc)
        back_acc[...] = jnp.zeros_like(back_acc)

    wide = down_ref.shape[1]
    both = mm(normed[...], gu_ref[...])
    d_hidden = mm(dy_ref[...], down_ref[...])
    gate, up = both[:, :wide], both[:, wide:]
    sig = 1.0 / (1.0 + jnp.exp(-gate))
    silu = gate * sig
    hidden = (silu * up).astype(BF)
    hidden_ref[...] = hidden
    d_up = (d_hidden * silu).astype(BF)
    d_gate = (d_hidden * up * (sig + silu * (1.0 - sig))).astype(BF)
    dgu_ref[:, :wide] = d_gate
    dgu_ref[:, wide:] = d_up
    out_acc[...] += mm(hidden, down_ref[...], NT)
    back_acc[...] += mm(dgu_ref[...], gu_ref[...], NT)

    @pl.when(step == steps - 1)
    def _():
        out_ref[...] = out_acc[...].astype(BF)
        back_ref[...] = back_acc[...].astype(BF)


def feed_forward(half, x, own, got, gain, dy, w_rest, o_cols, chunk, whole=None):
    rows, model = own.shape
    units = (w_rest.shape[1] - o_cols) // 3
    steps = units // chunk
    mine, once = lambda f: (half, 0), lambda f: (0, 0)
    at_gu, at_down = o_cols // (2 * chunk), (o_cols + 2 * units) // chunk
    block = (rows, model)
    ins = [
        (x, block, mine), (own, block, once), (got, block, once), (gain, (1, model), once), (dy, block, mine),
        (w_rest, (model, 2 * chunk), lambda f: (0, at_gu + f)),
        (w_rest, (model, chunk), lambda f: (0, at_down + f)),
    ]
    keep = {}
    if whole is not None:
        keep = {len(ins) + i: 1 + i for i in range(3)}
        ins += [(array, None, None) for array in whole]
    outs = [
        (shaped((rows, model), F32), block, once),
        (shaped((2 * rows, model), BF), block, mine),
        (shaped((2 * rows, units), BF), (rows, chunk), lambda f: (half, f)),
        (shaped((2 * rows, 2 * units), BF), (rows, 2 * chunk), lambda f: (half, f)),
        (shaped((rows, model), BF), block, once),
        (shaped((rows, model), BF), block, once),
    ]
    scratch = [pltpu.VMEM(block, BF), pltpu.VMEM(block, F32), pltpu.VMEM(block, F32)]
    return call(ffn_kernel, "feed_forward", (steps,), ins, outs, scratch, keep=keep, us=18)


def norm_back(grad, values, gain):
    scale = rms(values)
    unit = values * scale
    inner = grad * gain
    return scale * (inner - unit * jnp.mean(inner * unit, axis=-1, keepdims=True)), grad * unit


def row_blocks(rows):
    size = rows // 2 if rows % 512 == 0 else rows
    return size, rows // size


def add_up(ref, value):
    total = jnp.sum(value, axis=0, keepdims=True)

    @pl.when(pl.program_id(0) == 0)
    def _():
        ref[...] = total

    @pl.when(pl.program_id(0) > 0)
    def _():
        ref[...] += total


def mixed_kernel(heads, own_ref, got_ref, resid_ref, gain_ref, dy_ref, w_ref, att_ref, *refs):
    d_resid_ref, mixed_ref, datt_ref, delta_ref, dgain_ref = refs[-5:]
    grad = own_ref[...].astype(F32) + got_ref[...].astype(F32)
    d_norm, summand = norm_back(grad, resid_ref[...], gain_ref[...])
    add_up(dgain_ref, summand)
    d_resid = dy_ref[...].astype(F32) + d_norm
    d_resid_ref[...] = d_resid
    mixed_ref[...] = d_resid.astype(BF)
    datt_ref[...] = mm(mixed_ref[...], w_ref[...]).astype(BF)
    for h in range(heads):
        cols = slice(h * HEAD_SIZE, (h + 1) * HEAD_SIZE)
        product = datt_ref[:, cols].astype(F32) * att_ref[:, cols].astype(F32)
        delta_ref[h // 2, h % 2 : h % 2 + 1, :] = jnp.sum(product.T, axis=0, keepdims=True)


def mixed_back(half, own, got, resid, gain, dy, w_rest, o_cols, attended, whole=None):
    rows, model = own.shape
    heads = o_cols // HEAD_SIZE
    size, steps = row_blocks(rows)
    mine, here, once = lambda f: (half * steps + f, 0), lambda f: (f, 0), lambda f: (0, 0)
    block = (size, model)
    ins = [
        (own, block, here), (got, block, here), (resid, block, here), (gain, (1, model), once),
        (dy, block, mine), (w_rest, (model, o_cols), once), (attended, (size, o_cols), mine),
    ]
    keep = {}
    if whole is not None:
        keep = {len(ins): 1}
        ins.append((whole, None, None))
    outs = [
        (shaped((rows, model), F32), block, here),
        (shaped((2 * rows, model), BF), block, mine),
        (shaped((rows, o_cols), BF), (size, o_cols), here),
        (shaped((heads // 2, 8, rows), F32), (heads // 2, 8, size), lambda f: (0, 0, f)),
        (shaped((1, model), F32), (1, model), once),
    ]
    return call(functools.partial(mixed_kernel, heads), "mixed_back", (steps,), ins, outs, keep=keep, us=7)


def merge_kernel(two, got3, four, got5, far_k, far_v, to_x, to_y):
    for which in range(2):
        by_x = two[which].astype(F32) + got3[which].astype(F32)
        by_y = four[which].astype(F32) + got5[which].astype(F32)
        to_x[which] = (by_x + far_v[...].astype(F32) if which else by_x).astype(BF)
        to_y[which] = (by_y if which else by_y + far_k[...].astype(F32)).astype(BF)


def merge(*pieces):
    rows, cols = pieces[-1].shape
    size, steps = row_blocks(rows)
    ins = []
    for piece in pieces:
        if piece.ndim == 3:
            ins.append((piece, (2, size, cols), lambda f: (0, f, 0)))
        else:
            ins.append((piece, (size, cols), lambda f: (f, 0)))
    outs = [(shaped((2, rows, cols), BF), (2, size, cols), lambda f: (0, f, 0))] * 2
    return call(merge_kernel, "merge", (steps,), ins, outs, us=4)


def weight_kernel(left_ref, right_ref, *refs):
    refs[-1][...] = mm(left_ref[...], right_ref[...], TN).astype(BF)


def weight_grad(left, right, at, width, cols, whole=None):
    tokens, model = left.shape
    n = right.shape[1]
    ins = [(left, (tokens, model), lambda j: (0, 0)), (right, (tokens, cols), lambda j: (0, j))]
    keep = {}
    if whole is not None:
        keep = {len(ins): 0}
        ins.append((whole, None, None))
    outs = [(shaped((model, width), BF), (model, cols), lambda j: (0, at // cols + j))]
    return call(weight_kernel, "weight_grad", (n // cols,), ins, outs, keep=keep)[0]


def qkv_weight_kernel(left_ref, q_ref, kv_ref, high_ref, low_ref):
    for half, out_ref in enumerate((high_ref, low_ref)):
        for which, right_ref in enumerate((q_ref, kv_ref)):

            @pl.when((pl.program_id(0) == half) & (pl.program_id(1) == which))
            def _(out_ref=out_ref, right_ref=right_ref):
                out_ref[...] = mm(left_ref[...], right_ref[...], TN).astype(BF)


def qkv_weight_grad(left, d_q, d_kv):
    tokens, model = left.shape
    cols = d_q.shape[1]
    ins = [
        (left, (tokens, model // 2), lambda i, j: (0, 1 - i)),
        (d_q, (tokens, cols), lambda i, j: (0, 0)),
        (d_kv, (tokens, cols), lambda i, j: (0, 0)),
    ]
    half, block = shaped((model // 2, 2 * cols), BF), (model // 2, cols)
    outs = [(half, block, lambda i, j: (0, jnp.where(i == 0, j, 1))), (half, block, lambda i, j: (0, i * j))]
    return call(qkv_weight_kernel, "qkv_weight_grad", (2, 2), ins, outs)


def q_back_kernel(heads, dq_ref, lin_ref, gain_ref, cos_ref, sin_ref, w_ref, *refs):
    d_ref, part_ref, gains_ref = refs[-3:]
    cos, sin = cos_ref[...], sin_ref[...]
    total = jnp.zeros(cos.shape, F32)
    for h in range(heads):
        cols = slice(h * HEAD_SIZE, (h + 1) * HEAD_SIZE)
        grad, summand = norm_back(turn_back(dq_ref[:, cols], cos, sin), lin_ref[:, cols], gain_ref[...])
        d_ref[:, cols] = grad.astype(BF)
        total = total + summand
    part_ref[...] = mm(d_ref[...], w_ref[...], NT)
    add_up(gains_ref, total)


def q_back(dq, lin, gain, cos, sin, w):
    rows, cols = dq.shape
    model = w.shape[0]
    size, steps = row_blocks(rows)
    here, once = lambda f: (f, 0), lambda f: (0, 0)
    ins = [
        (dq, (size, cols), here), (lin, (size, cols), here), (gain, (1, HEAD_SIZE), once),
        (cos, (size, HEAD_SIZE), here), (sin, (size, HEAD_SIZE), here), (w, (model, cols), once),
    ]
    outs = [
        (shaped((rows, cols), BF), (size, cols), here),
        (shaped((rows, model), F32), (size, model), here),
        (shaped((1, HEAD_SIZE), F32), (1, HEAD_SIZE), once),
    ]
    kernel = functools.partial(q_back_kernel, cols // HEAD_SIZE)
    return call(kernel, "q_back", (steps,), ins, outs)


def kv_back_kernel(heads, n_keys, n_values, lin_ref, gain_ref, cos_ref, sin_ref, w_ref, slots_ref, q_part_ref, *refs):
    key_refs, value_refs = refs[:n_keys], refs[n_keys : n_keys + n_values]
    d_ref, part_ref, gains_ref = refs[-3:]
    cos, sin = cos_ref[...], sin_ref[...]
    width = heads * HEAD_SIZE

    def total(sources, which, cols):
        value = None
        for ref in sources:
            piece = ref[which, :, cols] if len(ref.shape) == 3 else ref[:, cols]
            value = piece.astype(F32) if value is None else value + piece.astype(F32)
        return value

    gains = jnp.zeros(cos.shape, F32)
    for h in range(heads):
        cols = slice(h * HEAD_SIZE, (h + 1) * HEAD_SIZE)
        grad, summand = norm_back(
            turn_back(total(key_refs, 0, cols), cos, sin), lin_ref[:, cols], gain_ref[...]
        )
        d_ref[:, cols] = grad.astype(BF)
        gains = gains + summand
    d_ref[:, width:] = total(value_refs, 1, slice(None)).astype(BF)
    part = (q_part_ref[...] + mm(d_ref[...], w_ref[...], NT)).astype(BF)
    part_ref[...] = mm(part, slots_ref[...], NT).astype(BF)
    add_up(gains_ref, gains)


def kv_back(half, keys, values, lin, gain, cos, sin, w, to_slots, q_part, whole=None):
    rows, cols = lin.shape
    model = w.shape[0]
    size, steps = row_blocks(rows)
    mine, here, once = lambda f: (half * steps + f, 0), lambda f: (f, 0), lambda f: (0, 0)
    ins = [
        (lin, (size, cols), here), (gain, (1, HEAD_SIZE), once), (cos, (size, HEAD_SIZE), mine),
        (sin, (size, HEAD_SIZE), mine), (w, (model, 2 * cols), once),
        (to_slots, (model, model), once), (q_part, (size, model), mine),
    ]
    for piece in list(keys) + list(values):
        if piece.ndim == 3:
            ins.append((piece, (2, size, cols), lambda f: (0, f, 0)))
        else:
            ins.append((piece, (size, cols), here))
    keep = {}
    if whole is not None:
        keep = {len(ins): 0}
        ins.append((whole, None, None))
    outs = [
        (shaped((2 * rows, 2 * cols), BF), (size, 2 * cols), mine),
        (shaped((rows, model), BF), (size, model), here),
        (shaped((1, HEAD_SIZE), F32), (1, HEAD_SIZE), once),
    ]
    kernel = functools.partial(kv_back_kernel, cols // HEAD_SIZE, len(keys), len(values))
    return call(kernel, "kv_back", (steps,), ins, outs, keep=keep, us=8)


def tokens_kernel(own_ref, got_ref, x_ref, gain_ref, d_resid_ref, *refs):
    out_ref, dgain_ref = refs[-2:]
    grad = own_ref[...].astype(F32) + got_ref[...].astype(F32)
    d_norm, summand = norm_back(grad, x_ref[...].astype(F32), gain_ref[...])
    add_up(dgain_ref, summand)
    out_ref[...] = (d_resid_ref[...] + d_norm).astype(BF)


def tokens_back(half, own, got, x, gain, d_resid, whole=None):
    rows, model = own.shape
    size, steps = row_blocks(rows)
    mine, here, once = lambda f: (half * steps + f, 0), lambda f: (f, 0), lambda f: (0, 0)
    block = (size, model)
    ins = [(own, block, here), (got, block, here), (x, block, mine), (gain, (1, model), once), (d_resid, block, here)]
    keep = {}
    if whole is not None:
        keep = {len(ins): 0}
        ins.append((whole, None, None))
    outs = [(shaped((2 * rows, model), BF), block, mine), (shaped((1, model), F32), (1, model), once)]
    return call(tokens_kernel, "tokens_back", (steps,), ins, outs, keep=keep, us=4)


def share_kernel(chunk, share_ref, out_ref, gate_ref, up_ref, down_ref):
    o_cols, units = out_ref.shape[1], gate_ref.shape[1]
    out_ref[...] = share_ref[:, :o_cols].astype(F32)
    for at in range(0, units, chunk):
        to = o_cols + 2 * at
        gate_ref[:, at : at + chunk] = share_ref[:, to : to + chunk].astype(F32)
        up_ref[:, at : at + chunk] = share_ref[:, to + chunk : to + 2 * chunk].astype(F32)
    down_ref[...] = share_ref[:, o_cols + 2 * units :].astype(F32)


def unpack(chunk, o_cols, share):
    wide = share.shape[0]
    units = (share.shape[1] - o_cols) // 3
    whole = lambda f: (0, 0)
    outs = [(shaped((wide, cols), F32), (wide, cols), whole) for cols in (o_cols, units, units, units)]
    return call(functools.partial(share_kernel, chunk), "unpack", (1,), [(share, share.shape, whole)], outs)


def layer_kernel(resid_ref, own_ref, got_ref, *refs):
    refs[-1][...] = (resid_ref[...] + (own_ref[...].astype(F32) + got_ref[...].astype(F32))).astype(BF)


def add_layer(half, resid, own, got, whole=None):
    rows, model = resid.shape
    size, steps = row_blocks(rows)
    here, mine = lambda f: (f, 0), lambda f: (half * steps + f, 0)
    ins = [(array, (size, model), here) for array in (resid, own, got)]
    keep = {}
    if whole is not None:
        keep = {len(ins): 0}
        ins.append((whole, None, None))
    outs = [(shaped((2 * rows, model), BF), (size, model), mine)]
    return call(layer_kernel, "add_layer", (steps,), ins, outs, keep=keep, us=3)[0]


def swap(value, axis, bit):
    size = lax.axis_size(axis)
    return lax.ppermute(value, axis, [(i, i ^ bit) for i in range(size)])


def shift(value, by):
    size = lax.axis_size("ctx")
    return lax.ppermute(value, "ctx", [(i, i + by) for i in range(size) if 0 <= i + by < size])


def add_low(left, right):
    return (left.astype(F32) + right.astype(F32)).astype(BF)


def butterfly(value, axes, gates=()):
    gates = list(gates)
    for axis in axes:
        bit = 1
        while bit < lax.axis_size(axis):
            got = swap(value, axis, bit)
            value = value + (after(got, gates.pop(0)) if gates else got)
            bit *= 2
    return value


def after(value, *others):
    return lax.optimization_barrier((value, *others))[0]


def rotary_tables(position):
    half_dim = HEAD_SIZE // 2
    inverse_freq = jnp.exp(jnp.arange(half_dim, dtype=F32) * (-math.log(ROPE_BASE) / half_dim))
    angles = position.astype(F32)[:, None] * inverse_freq[None, :]
    cosine, sine = jnp.cos(angles), jnp.sin(angles)
    return jnp.concatenate([cosine, cosine], axis=-1), jnp.concatenate([-sine, sine], axis=-1)


def body(
    tokens,
    cont_lengths,
    attn_gain,
    ffn_gain,
    query_gain,
    key_gain,
    w_query,
    key_weight,
    value_weight,
    w_out,
    w_gate,
    w_up,
    w_down,
    cotangent,
):
    ctx_size = lax.axis_size("ctx")
    weight_axes = ("shard", "ctx")
    parts = lax.axis_size("shard") * ctx_size
    me = lax.axis_index("ctx")
    part = lax.axis_index("shard") * ctx_size + me
    rows, model = tokens.shape[0] // 2, tokens.shape[1]
    n_halo = 1 + -(-(LONGEST - 1) // rows)
    lengths = cont_lengths[0]

    bits = [("shard", 1)] + [("ctx", 1 << i) for i in range(1, ctx_size.bit_length() - 1)] + [("ctx", 1)]
    order = [0]
    for axis, bit in bits:
        order += [j ^ (bit * ctx_size if axis == "shard" else bit) for j in order]
    wide, narrow = attn_gain.shape[0], query_gain.shape[0]
    q_cols, k_cols = w_query.shape[1], key_weight.shape[1]
    o_cols, units = w_out.shape[0], w_gate.shape[1]
    heads, kv_heads = q_cols // HEAD_SIZE, k_cols // HEAD_SIZE
    chunk = math.gcd(units, 512)

    def gather_rows(piece, gates=((),) * 4):
        if ctx_size != 8:
            for axis, bit in bits:
                piece = jnp.concatenate([piece, swap(piece, axis, bit)])
            return piece, (piece,) * 4
        one = jnp.concatenate([piece, after(swap(piece, "shard", 1), *gates[0])])
        by_x, by_y = (after(v, *gates[1]) for v in (swap(one, "ctx", 2), swap(one, "ctx", 4)))
        cut = one.shape[1] // 2
        left, right = swap(by_y[:, :cut], "ctx", 2), swap(by_x[:, cut:], "ctx", 4)
        far = jnp.concatenate([after(left, *gates[2]), after(right, *gates[2])], axis=1)
        half = jnp.concatenate([one, by_x, by_y, far])
        whole = jnp.concatenate([half, after(swap(half, "ctx", 1), *gates[3])])
        return whole, (one, by_x, half, whole)

    def scatter_rows(low, high, late):
        total = add_low(low, after(swap(high, "ctx", 1), late))
        if ctx_size != 8:
            for axis, bit in bits[-2:0:-1]:
                size = total.shape[0] // 2
                total = add_low(total[:size], swap(total[size:], axis, bit))
            return (total,)
        size, cut = total.shape[0] // 4, total.shape[1] // 2
        own, by_x, by_y, far = (total[i * size : (i + 1) * size] for i in range(4))
        left, right = swap(far[:, :cut], "ctx", 2), swap(far[:, cut:], "ctx", 4)
        return own, by_x, by_y, left, right

    def scatter_more(stage, late):
        if ctx_size != 8:
            return stage
        own, by_x, by_y, left, right = stage
        left, right = after(left, late), after(right, late)
        cut = left.shape[1]
        by_x = jnp.concatenate([by_x[:, :cut], add_low(by_x[:, cut:], right)], axis=1)
        by_y = jnp.concatenate([add_low(by_y[:, :cut], left), by_y[:, cut:]], axis=1)
        return lax.optimization_barrier((own, by_x, by_y))[0], swap(by_x, "ctx", 2), swap(by_y, "ctx", 4)

    def scatter_sum(stage, late):
        total = stage[0].astype(F32)
        for piece in stage[1:]:
            total = total + after(piece, late).astype(F32)
        total, size = total.astype(BF), total.shape[0] // 2
        return total, swap(total[size:], "shard", 1)

    kv_piece, rest_piece = pack(chunk, key_weight, value_weight, w_out.T, w_gate, w_up, w_down.T)
    w_kv, stages = gather_rows(kv_piece)
    w_rest = lax.all_gather(rest_piece, weight_axes, axis=0, tiled=True)
    gains = jnp.concatenate([attn_gain, ffn_gain, query_gain, key_gain])[None]
    gains = jnp.where(jnp.arange(parts)[:, None] == part, gains, jnp.zeros((), BF))
    gains = gains + after(swap(gains, "ctx", 1), kv_piece)
    for at, (axis, bit) in enumerate(bits[:-1]):
        gains = gains + after(swap(gains, axis, bit), stages[min(at, 2)])
    gains = gains.astype(F32)
    gain_one = gains[:, :wide].reshape(1, -1)
    gain_two = gains[:, wide : 2 * wide].reshape(1, -1)
    gain_q = gains[:, 2 * wide : 2 * wide + narrow].reshape(1, -1)
    gain_k = gains[:, 2 * wide + narrow :].reshape(1, -1)
    source = jnp.bitwise_xor(part, jnp.array(order, jnp.int32))[:, None] * wide + jnp.arange(wide, dtype=jnp.int32)
    to_slots = (jnp.arange(model, dtype=jnp.int32)[:, None] == source.reshape(1, -1)).astype(BF)
    tokens_s = mm(after(tokens, stages[0]), to_slots).astype(BF)
    gain_one_s = mm(gain_one.astype(BF), to_slots)

    cont_at = me * rows + jnp.arange(rows, dtype=jnp.int32)
    cont_ends = jnp.cumsum(lengths)
    starts = cont_ends - lengths
    seg = jnp.sum((cont_ends[None, :] <= cont_at[:, None]).astype(jnp.int32), axis=1)
    numbers = jnp.arange(lengths.shape[0], dtype=jnp.int32)
    first = jnp.sum(jnp.where(numbers[None, :] == seg[:, None], starts[None, :], 0), axis=1)
    position = jnp.concatenate([me * rows + jnp.arange(rows, dtype=jnp.int32), PROMPT + cont_at - first])
    low = first - me * rows
    low_col = jnp.broadcast_to(low[:, None], (rows, 128))
    low_row = jnp.broadcast_to(jnp.concatenate([low, low])[None, :], (8, 2 * rows))
    scalars = jnp.stack([me, low[0]])
    cos, sin = rotary_tables(position)

    once = lambda f: (0, 0)

    def keys_values(half, gain, whole=None):
        mine = lambda f: (half, 0)
        ins = [
            (tokens_s, (rows, model), mine), (gain, (1, model), once), (w_kv, (model, 2 * k_cols), once),
            (gain_k, (1, HEAD_SIZE), once), (cos, (rows, HEAD_SIZE), mine), (sin, (rows, HEAD_SIZE), mine),
        ]
        keep = {}
        if whole is not None:
            keep = {len(ins): 0}
            ins.append((whole, None, None))
        outs = [
            (shaped((2 * rows, model), BF), (rows, model), mine),
            (shaped((2, rows, k_cols), BF), (2, rows, k_cols), lambda f: (0, 0, 0)),
            (shaped((rows, k_cols), F32), (rows, k_cols), once),
        ]
        return call(functools.partial(kv_kernel, kv_heads), "keys_values", (1,), ins, outs, keep=keep, us=6)

    normed, kv_p, k_lin_p = keys_values(0, gain_one_s)
    normed, kv_c, k_lin_c = keys_values(1, after(gain_one_s, kv_p), normed)
    w_q, _ = gather_rows(after(w_query, stages[0]), ((stages[1],), (w_kv,), (kv_p,), (kv_c,)))
    mine = lambda f: (f, 0)
    q, q_lin = call(
        functools.partial(q_kernel, heads), "queries", (2,),
        [
            (normed, (rows, model), mine), (w_q, (model, q_cols), lambda f: (0, 0)),
            (gain_q, (1, HEAD_SIZE), lambda f: (0, 0)),
            (cos, (rows, HEAD_SIZE), mine), (sin, (rows, HEAD_SIZE), mine),
        ],
        [(shaped((2 * rows, q_cols), BF), (rows, q_cols), mine), (shaped((2 * rows, q_cols), F32), (rows, q_cols), mine)],
    )

    def pick(source, wanted):
        return {s: source[s] for s in source if s in wanted}

    near, middle, far = (0, 1), (2, 3, 4, 5), tuple(range(6, ctx_size))
    slots, halos = {0: kv_p}, {0: kv_c}
    odd = (me % 2) == 1
    if ctx_size == 8:
        slots[1], slots[2], slots[4] = (swap(kv_p, "ctx", bit) for bit in (1, 2, 4))
    else:
        both, bit = kv_p[None], 1
        while bit < ctx_size:
            both = jnp.concatenate([both, swap(both, "ctx", bit)])
            bit *= 2
        slots = {s: both[s] for s in range(ctx_size)}
        halos.update({d: shift(kv_c, d) for d in range(1, n_halo)})
    state = attention_forward((0, 1), scalars, q, low_col, pick(slots, near), pick(halos, (0,)))
    ready = ()
    if ctx_size == 8:
        slots[2], slots[4] = after(slots[2], state[0]), after(slots[4], state[0])
        far_k, far_v = swap(slots[4][0], "ctx", 2), swap(slots[2][1], "ctx", 4)
        slots[3], slots[5] = swap(slots[2], "ctx", 1), swap(slots[4], "ctx", 1)
        halos[2] = shift(after(kv_c, slots[2]), 2)
    state = attention_forward((0, 1), after(scalars, state[0]), q, low_col, pick(slots, middle), {}, state)
    if ctx_size == 8:
        slots[6] = jnp.stack([after(far_k, state[0]), after(far_v, state[0])])
        slots[7] = swap(slots[6], "ctx", 1)
        halo_one = jnp.where(odd, after(halos[2], slots[7]), kv_c)
        halos[1] = swap(halo_one, "ctx", 1)
        ready = (halo_one,)
    p_state, c_state = state[:2], state[2:]
    attended, lse_p, part_p = attention_forward(
        (0,), after(scalars, c_state[0], *ready), q, low_col, pick(slots, far), {}, p_state, (w_rest, None)
    )
    got_p = swap(part_p, "tensor", 1)
    attended, lse_c, part_c = attention_forward(
        (1,), after(scalars, part_p), q, low_col, pick(slots, far), pick(halos, range(1, n_halo)),
        c_state, (w_rest, attended),
    )
    got_c = swap(part_c, "tensor", 1)

    resid_p, *whole, out_p, back_p = feed_forward(
        0, tokens, part_p, got_p, after(gain_two, part_c), cotangent, w_rest, o_cols, chunk
    )
    back_got_p = swap(back_p, "tensor", 1)
    resid_c, *whole, out_c, back_c = feed_forward(
        1, tokens, part_c, got_c, after(gain_two, back_p), cotangent, w_rest, o_cols, chunk, whole
    )
    back_got_c = swap(back_c, "tensor", 1)
    normed_ffn, hidden, d_gu = whole
    width = o_cols + 3 * units
    rest_grads = weight_grad(normed_ffn, d_gu, o_cols, width, min(1024, o_cols))
    rest_grads = weight_grad(cotangent, hidden, o_cols + 2 * units, width, chunk, rest_grads)
    d_resid_p, d_mixed, d_att_p, delta_p, d_two_p = mixed_back(
        0, back_p, back_got_p, resid_p, after(gain_two, rest_grads), cotangent, w_rest, o_cols, attended
    )
    d_resid_c, d_mixed, d_att_c, delta_c, d_two_c = mixed_back(
        1, back_c, back_got_c, resid_c, after(gain_two, d_att_p), cotangent, w_rest, o_cols, attended, d_mixed
    )
    rest_grads = weight_grad(d_mixed, attended, 0, width, min(1024, o_cols), rest_grads)
    rest_share = lax.psum_scatter(rest_grads, weight_axes, scatter_dimension=0, tiled=True)
    out_p, out_c = after(out_p, back_got_c), after(out_c, back_got_c)
    out_got_p, out_got_c = swap(out_p, "tensor", 1), swap(out_c, "tensor", 1)

    dq, from_p, _ = attention_backward(
        0, after(scalars, rest_grads), q, d_att_p, lse_p, delta_p, low_row, slots, {}
    )

    def back_c_rows(deps, slots, halos, carry, whole=None):
        prior = pick(from_p, tuple(slots)) if slots else None
        return attention_backward(
            1, after(scalars, *deps), q, d_att_c, lse_c, delta_c, low_row, slots, halos, carry, prior,
            whole is not None, whole,
        )

    dq_c, _, g_halo = back_c_rows((dq, out_got_p, out_got_c), {}, halos, None)
    if ctx_size == 8:
        near_one = swap(g_halo[1], "ctx", 1)
    dq_c, g, _ = back_c_rows((dq_c,), pick(slots, far), {}, dq_c)
    zero = jnp.zeros((), BF)
    if ctx_size == 8:
        near_one = after(near_one, dq_c)
        two_back = add_low(g_halo[2], jnp.where(odd, near_one, zero))
        halo_two = shift(two_back, -2)
        got7 = swap(g[7], "ctx", 1)
        ready = (two_back,)
    dq_c, more, _ = back_c_rows((dq_c, *ready), pick(slots, middle), {}, dq_c)
    g.update(more)
    if ctx_size == 8:
        g6 = add_low(g[6], after(got7, dq_c))
        far_k, far_v = swap(g6[0], "ctx", 2), swap(g6[1], "ctx", 4)
        got3, got5 = swap(g[3], "ctx", 1), swap(g[5], "ctx", 1)
        ready = (g6,)
    dq, more, _ = back_c_rows((dq_c, *ready), pick(slots, near), {}, dq_c, dq)
    g.update(more)
    if ctx_size == 8:
        got1 = swap(g[1], "ctx", 1)
        far_k, far_v, got3, got5 = (after(v, dq, halo_two) for v in (far_k, far_v, got3, got5))
        to_x, to_y = merge(g[2], got3, g[4], got5, far_k, far_v)
        ready = (to_x,)
        keys_p = values_p = [g[0], got1, swap(to_x, "ctx", 2), swap(to_y, "ctx", 4)]
        keys_c = values_c = [g_halo[0], jnp.where(odd, zero, near_one), halo_two]
    else:
        both = jnp.stack([g[s] for s in range(ctx_size)])
        while both.shape[0] > 1:
            size = both.shape[0] // 2
            both = add_low(both[:size], swap(both[size:], "ctx", size))
        keys_p = values_p = [both[0]]
        keys_c = values_c = [g_halo[0]] + [shift(g_halo[d], -d) for d in range(1, n_halo)]

    d_q, q_part, q_heads = q_back(dq, q_lin, after(gain_q, dq, *ready), cos, sin, w_q)
    d_kv, into_c, k_heads_c = kv_back(
        1, keys_c, values_c, k_lin_c, after(gain_k, q_part), cos, sin, w_kv, to_slots, q_part
    )
    into_got_c = swap(into_c, "tensor", 1)
    d_kv, into_p, k_heads_p = kv_back(
        0, keys_p, values_p, k_lin_p, after(gain_k, into_c), cos, sin, w_kv, to_slots, q_part, d_kv
    )
    into_got_p = swap(into_p, "tensor", 1)
    high, low = qkv_weight_grad(normed, after(d_q, into_p), d_kv)
    heads = jnp.concatenate([q_heads, k_heads_c + k_heads_p], axis=1)
    heads_got = swap(heads, "tensor", 1)
    out_share, gate_share, up_share, down_share = unpack(chunk, o_cols, after(rest_share, low))
    grad_tokens, d_one_c = tokens_back(1, into_c, into_got_c, tokens, after(gain_one, gate_share), d_resid_c)
    qkv_grad = scatter_rows(low, high, d_one_c)
    layer_out = add_layer(0, after(resid_p, qkv_grad[0]), out_p, out_got_p)
    qkv_grad = scatter_more(qkv_grad, layer_out)
    layer_out = add_layer(1, after(resid_c, qkv_grad[0]), out_c, out_got_c, layer_out)
    grad_tokens, d_one_p = tokens_back(
        0, into_p, into_got_p, tokens, after(gain_one, layer_out), d_resid_p, grad_tokens
    )
    qkv_grad = scatter_sum(qkv_grad, d_one_p)
    heads = heads + after(heads_got, d_one_p)
    late = jnp.concatenate([d_one_c + d_one_p, heads, d_two_c + d_two_p], axis=1)
    late = butterfly(late, ("ctx", "shard"))
    qkv_share = add_low(qkv_grad[0][:wide], qkv_grad[1]).astype(F32)

    def own_gain(value, size):
        return lax.dynamic_index_in_dim(value.reshape(parts, size), part, 0, keepdims=False)

    return (
        layer_out,
        grad_tokens,
        own_gain(late[:, :model], wide),
        own_gain(late[:, model + 2 * HEAD_SIZE :], wide),
        own_gain(late[:, model : model + HEAD_SIZE], narrow),
        own_gain(late[:, model + HEAD_SIZE : model + 2 * HEAD_SIZE], narrow),
        qkv_share[:, :q_cols],
        qkv_share[:, q_cols : q_cols + k_cols],
        qkv_share[:, q_cols + k_cols :],
        out_share.T,
        gate_share,
        up_share,
        down_share.T,
    )


def solution(mesh):
    split = ("shard", "ctx")
    rows, gain = P(split, None), P(split)
    into, out_of = P(split, "tensor"), P("tensor", split)
    in_specs = (rows, P("shard", None)) + (gain,) * 4 + (into,) * 3 + (out_of,)
    in_specs += (into, into, out_of, rows)
    out_specs = (rows, rows) + (gain,) * 4 + (into,) * 3 + (out_of, into, into, out_of)
    return jax.shard_map(body, mesh=mesh, in_specs=in_specs, out_specs=out_specs, check_vma=False)
```

profile of v0, /device:TPU:0, one launch (start us, length us, event | category | flops | bytes accessed | tf_op | source)
XLA Modules:
  0.0 613.2 jit_solution(5276973907097219646)
XLA Ops:
  9.5 4.1 collective-permute-start
  28.2 6.4 %collective-permute-done.4 = bf16[128,1024]{1,0:T(8,128)(2,1)S(1)} collective-permute-done((bf16[128,1024]{1,0:T(8,128)(2,1)S(1)}, bf16[128,1024]{1,0:T(8,128)(2,1)S(1)}, u32[]{:S(2)}, u32[]{:S(2)}) %collective-permute-start.4) | collective-permute-done | bytes 262176 | tf_op jit(solution)/shard_map/ppermute | solution.py:719
  42.2 3.7 fusion.5.x_ref
  53.3 9.7 %collective-permute-done.11 = bf16[128,1024]{1,0:T(8,128)(2,1)} collective-permute-done((bf16[128,1024]{1,0:T(8,128)(2,1)}, bf16[128,1024]{1,0:T(8,128)(2,1)}, u32[]{:S(2)}, u32[]{:S(2)}) %collective-permute-start.11) | collective-permute-done | bytes 262176 | tf_op jit(solution)/shard_map/ppermute | solution.py:719
  68.2 5.6 keys_values.2
  81.5 5.6 keys_values.3
  90.8 10.5 %queries.1 = (bf16[1024,1024]{1,0:T(8,128)(2,1)}, f32[1024,1024]{1,0:T(8,128)}) custom-call(bf16[1024,1024]{1,0:T(8,128)(2,1)} %get-tuple-element.168.normed_ref.left_ref, bf16[1024,1024]{1,0:T(8,128)(2,1)} %constant_dynamic-update-slice_fusion.15.w_ref, f32[1,128]{1,0:T(1,128)} %reshape.121.hgain_ref.gain_ref, f32[1024,128]{1,0:T(8,128)} %get-tuple-element.348.cos_ref, ...), custom_call_target="tpu_custom_call" | custom-call | tf_op jit(solution)/shard_map/queries/pallas_call | solution.py:46
  102.4 14.7 %attend.4 = (f32[512,1024]{1,0:T(8,128)}, f32[512,1024]{1,0:T(8,128)}, f32[512,1024]{1,0:T(8,128)}, f32[512,1024]{1,0:T(8,128)}) custom-call(s32[2]{0:T(128)} %pad_add_fusion.1.idx_ref, s32[512,128]{1,0:T(8,128)} %broadcast_in_dim.67.lo_ref, bf16[1024,1024]{1,0:T(8,128)(2,1)} %get-tuple-element.177.refs_0_.refs_1_.q_ref, ...), custom_call_target="tpu_custom_call" | custom-call | tf_op jit(solution)/shard_map/attend/pallas_call | solution.py:46
  122.1 4.0 collective-permute-start.21
  127.4 15.0 %attend.5 = (f32[512,1024]{1,0:T(8,128)}, f32[512,1024]{1,0:T(8,128)}, f32[512,1024]{1,0:T(8,128)}, f32[512,1024]{1,0:T(8,128)}) custom-call(s32[2]{0:T(128)} %pad_add_fusion.1.idx_ref, s32[512,128]{1,0:T(8,128)} %broadcast_in_dim.67.lo_ref, bf16[1024,1024]{1,0:T(8,128)(2,1)} %get-tuple-element.177.refs_0_.refs_1_.q_ref, ...), custom_call_target="tpu_custom_call" | custom-call | tf_op jit(solution)/shard_map/attend/pallas_call | solution.py:46
  142.6 13.5 %collective-permute-done.21.refs_3_.refs_1_ = bf16[2,512,512]{2,1,0:T(8,128)(2,1)} collective-permute-done((bf16[2,512,512]{2,1,0:T(8,128)(2,1)}, bf16[2,512,512]{2,1,0:T(8,128)(2,1)}, u32[]{:S(2)}, u32[]{:S(2)}) %collective-permute-start.21) | collective-permute-done | bytes 1048608 | tf_op jit(solution)/shard_map/ppermute | solution.py:724
  156.2 2.7 broadcast_select_fusion.1
  158.9 8.2 %attend.6 = (bf16[1024,1024]{1,0:T(8,128)(2,1)}, f32[4,8,512]{2,1,0:T(8,128)}, bf16[512,1024]{1,0:T(8,128)(2,1)}) custom-call(s32[2]{0:T(128)} %pad_add_fusion.1.idx_ref, s32[512,128]{1,0:T(8,128)} %broadcast_in_dim.67.lo_ref, bf16[1024,1024]{1,0:T(8,128)(2,1)} %get-tuple-element.177.refs_0_.refs_1_.q_ref, bf16[2,512,512]{2,1,0:T(8,128)(2,1)} %copy-done.2, ...), custom_call_target="tpu_custom_call" | custom-call | tf_op jit(solution)/shard_map/attend/pallas_call | solution.py:46
  169.8 12.7 %attend.7 = (bf16[1024,1024]{1,0:T(8,128)(2,1)}, f32[4,8,512]{2,1,0:T(8,128)}, bf16[512,1024]{1,0:T(8,128)(2,1)}) custom-call(s32[2]{0:T(128)} %pad_add_fusion.1.idx_ref, s32[512,128]{1,0:T(8,128)} %broadcast_in_dim.67.lo_ref, bf16[1024,1024]{1,0:T(8,128)(2,1)} %get-tuple-element.177.refs_0_.refs_1_.q_ref, ...), custom_call_target="tpu_custom_call", output_to_operand_aliasing={{0}: (10, {})} | custom-call | tf_op jit(solution)/shard_map/attend/pallas_call | solution.py:46
  183.7 9.7 %collective-permute-done.27.got_ref = bf16[512,1024]{1,0:T(8,128)(2,1)S(1)} collective-permute-done((bf16[512,1024]{1,0:T(8,128)(2,1)}, bf16[512,1024]{1,0:T(8,128)(2,1)S(1)}, u32[]{:S(2)}, u32[]{:S(2)}) %collective-permute-start.27) | collective-permute-done | bytes 1048608 | tf_op jit(solution)/shard_map/ppermute | solution.py:719
  194.3 18.6 %feed_forward.2 = (f32[512,1024]{1,0:T(8,128)}, bf16[1024,1024]{1,0:T(8,128)(2,1)}, bf16[1024,1536]{1,0:T(8,128)(2,1)}, bf16[1024,3072]{1,0:T(8,128)(2,1)}, bf16...) custom-call(bf16[1024,1024]{1,0:T(8,128)(2,1)} %x_ref.7, bf16[512,1024]{1,0:T(8,128)(2,1)} %get-tuple-element.194.own_ref, ...), custom_call_target="tpu_custom_call" | custom-call | tf_op jit(solution)/shard_map/feed_forward/pallas_call | solution.py:46
  216.6 18.3 %feed_forward.3 = (f32[512,1024]{1,0:T(8,128)}, bf16[1024,1024]{1,0:T(8,128)(2,1)}, bf16[1024,1536]{1,0:T(8,128)(2,1)}, bf16[1024,3072]{1,0:T(8,128)(2,1)}, bf16...) custom-call(bf16[1024,1024]{1,0:T(8,128)(2,1)} %x_ref.7, ...), custom_call_target="tpu_custom_call", output_to_operand_aliasing={{1}: (7, {}), {2}: (8, {}), {3}: (9, {})} | custom-call | tf_op jit(solution)/shard_map/feed_forward/pallas_call | solution.py:46
  236.6 10.8 %weight_grad.3.refs_0_ = bf16[1024,5632]{1,0:T(8,128)(2,1)} custom-call(bf16[1024,1024]{1,0:T(8,128)(2,1)} %get-tuple-element.209.left_ref, bf16[1024,3072]{1,0:T(8,128)(2,1)} %get-tuple-element.210.right_ref), custom_call_target="tpu_custom_call" | custom-call | tf_op jit(solution)/shard_map/weight_grad/pallas_call | solution.py:46
  247.4 7.2 %weight_grad.4.refs_0_ = bf16[1024,5632]{1,0:T(8,128)(2,1)} custom-call(bf16[1024,1024]{1,0:T(8,128)(2,1)} %dy_ref.7, bf16[1024,1536]{1,0:T(8,128)(2,1)} %get-tuple-element.208.right_ref, bf16[1024,5632]{1,0:T(8,128)(2,1)} %weight_grad.3.refs_0_), custom_call_target="tpu_custom_call", output_to_operand_aliasing={{}: (2, {})} | custom-call | tf_op jit(solution)/shard_map/weight_grad/pallas_call | solution.py:46
  255.5 7.4 %mixed_back.2 = (f32[512,1024]{1,0:T(8,128)}, bf16[1024,1024]{1,0:T(8,128)(2,1)}, bf16[512,1024]{1,0:T(8,128)(2,1)}, f32[4,8,512]{2,1,0:T(8,128)}, f32[1,1024]{1,0:T(1,128)}) custom-call(bf16[512,1024]{1,0:T(8,128)(2,1)} %get-tuple-element.200.own_ref, bf16[512,1024]{1,0:T(8,128)(2,1)} %copy-done.28, f32[512,1024]{1,0:T(8,128)} %get-tuple-element.284.resid_ref, ...), custom_call_target="tpu_custom_call" | custom-call | tf_op jit(solution)/shard_map/mixed_back/pallas_call | solution.py:46
  264.0 6.9 %mixed_back.3 = (f32[512,1024]{1,0:T(8,128)}, bf16[1024,1024]{1,0:T(8,128)(2,1)}, bf16[512,1024]{1,0:T(8,128)(2,1)}, f32[4,8,512]{2,1,0:T(8,128)}, f32[1,1024]{1,0:T(1,128)}) custom-call(bf16[512,1024]{1,0:T(8,128)(2,1)} %get-tuple-element.206.own_ref, bf16[512,1024]{1,0:T(8,128)(2,1)} %copy-done.21, ...), custom_call_target="tpu_custom_call", output_to_operand_aliasing={{1}: (7, {})} | custom-call | tf_op jit(solution)/shard_map/mixed_back/pallas_call | solution.py:46
  270.9 6.1 weight_grad.5
  280.9 13.1 %attend_back.5 = (f32[1024,1024]{1,0:T(8,128)}, bf16[2,512,512]{2,1,0:T(8,128)(2,1)}, bf16[2,512,512]{2,1,0:T(8,128)(2,1)}, bf16[2,512,512]{2,1,0:T(8,128)(2,1)}...) custom-call(s32[2]{0:T(128)} %pad_add_fusion.1.idx_ref, ...), custom_call_target="tpu_custom_call" | custom-call | tf_op jit(solution)/shard_map/attend_back/pallas_call | solution.py:46
  293.9 19.1 %collective-permute-done.30.got_ref = bf16[512,1024]{1,0:T(8,128)(2,1)S(1)} collective-permute-done((bf16[512,1024]{1,0:T(8,128)(2,1)S(1)}, bf16[512,1024]{1,0:T(8,128)(2,1)S(1)}, u32[]{:S(2)}, u32[]{:S(2)}) %collective-permute-start.30) | collective-permute-done | bytes 1048608 | tf_op jit(solution)/shard_map/ppermute | solution.py:719
  313.0 31.3 %collective-permute-done.31.got_ref = bf16[512,1024]{1,0:T(8,128)(2,1)S(1)} collective-permute-done((bf16[512,1024]{1,0:T(8,128)(2,1)S(1)}, bf16[512,1024]{1,0:T(8,128)(2,1)S(1)}, u32[]{:S(2)}, u32[]{:S(2)}) %collective-permute-start.31) | collective-permute-done | bytes 1048608 | tf_op jit(solution)/shard_map/ppermute | solution.py:719
  344.3 10.6 %attend_back.6 = (f32[512,1024]{1,0:T(8,128)}, bf16[2,512,512]{2,1,0:T(8,128)(2,1)}, bf16[2,512,512]{2,1,0:T(8,128)(2,1)}, bf16[2,512,512]{2,1,0:T(8,128)(2,1)}) custom-call(s32[2]{0:T(128)} %pad_add_fusion.1.idx_ref, bf16[1024,1024]{1,0:T(8,128)(2,1)} %get-tuple-element.177.refs_0_.refs_1_.q_ref, bf16[512,1024]{1,0:T(8,128)(2,1)} %get-tuple-element.226.do_ref, ...), custom_call_target="tpu_custom_call" | custom-call | tf_op jit(solution)/shard_map/attend_back/pallas_call | solution.py:46
  354.9 3.6 collective-permute-start.32
  358.5 15.1 %attend_back.7 = (f32[512,1024]{1,0:T(8,128)}, bf16[2,512,512]{2,1,0:T(8,128)(2,1)}, bf16[2,512,512]{2,1,0:T(8,128)(2,1)}) custom-call(s32[2]{0:T(128)} %pad_add_fusion.1.idx_ref, bf16[1024,1024]{1,0:T(8,128)(2,1)} %get-tuple-element.177.refs_0_.refs_1_.q_ref, bf16[512,1024]{1,0:T(8,128)(2,1)} %get-tuple-element.226.do_ref, ...), custom_call_target="tpu_custom_call" | custom-call | tf_op jit(solution)/shard_map/attend_back/pallas_call | solution.py:46
  375.3 26.0 %attend_back.8 = (f32[512,1024]{1,0:T(8,128)}, bf16[2,512,512]{2,1,0:T(8,128)(2,1)}, bf16[2,512,512]{2,1,0:T(8,128)(2,1)}, bf16[2,512,512]{2,1,0:T(8,128)(2,1)}, bf16[2,512,512]{2,1,0:T(8,128)(2,1)}) custom-call(s32[2]{0:T(128)} %pad_add_fusion.1.idx_ref, bf16[1024,1024]{1,0:T(8,128)(2,1)} %get-tuple-element.177.refs_0_.refs_1_.q_ref, ...), custom_call_target="tpu_custom_call" | custom-call | tf_op jit(solution)/shard_map/attend_back/pallas_call | solution.py:46
  403.1 2.6 collective-permute-start.37
  405.7 21.1 %collective-permute-start.38 = (bf16[512,512]{1,0:T(8,128)(2,1)S(1)}, bf16[512,512]{1,0:T(8,128)(2,1)S(1)}, u32[]{:S(2)}, u32[]{:S(2)}) collective-permute-start(bf16[512,512]{1,0:T(8,128)(2,1)S(1)} %get-tuple-element.315), channel_id=1, source_target_pairs={{0,8},{2,10},{4,12},{6,14},{8,0},{10,2},{12,4},{14,6},{1,9},{3,11}... | collective-permute-start | bytes 1572872 | tf_op jit(solution)/shard_map/ppermute | solution.py:719
  426.9 15.1 %attend_back.9 = (f32[1024,1024]{1,0:T(8,128)}, bf16[2,512,512]{2,1,0:T(8,128)(2,1)}, bf16[2,512,512]{2,1,0:T(8,128)(2,1)}) custom-call(s32[2]{0:T(128)} %pad_add_fusion.1.idx_ref, bf16[1024,1024]{1,0:T(8,128)(2,1)} %get-tuple-element.177.refs_0_.refs_1_.q_ref, bf16[512,1024]{1,0:T(8,128)(2,1)} %get-tuple-element.226.do_ref, ...), custom_call_target="tpu_custom_call", output_to_operand_aliasing={{0}: (11, {})} | custom-call | tf_op jit(solution)/shard_map/attend_back/pallas_call | solution.py:46
  444.0 3.8 merge.1
  447.9 17.3 %collective-permute-start.41 = (bf16[2,512,512]{2,1,0:T(8,128)(2,1)}, bf16[2,512,512]{2,1,0:T(8,128)(2,1)S(1)}, u32[]{:S(2)}, u32[]{:S(2)}) collective-permute-start(bf16[2,512,512]{2,1,0:T(8,128)(2,1)} %get-tuple-element.271), channel_id=1, source_target_pairs={{0,8},{2,10},{4,12},{6,14},{8,0},{10,2},{12,4},{14,6},{1,9},{3,11}... | collective-permute-start | bytes 3145736 | tf_op jit(solution)/shard_map/ppermute | solution.py:719
  468.4 15.5 %q_back.1 = (bf16[1024,1024]{1,0:T(8,128)(2,1)}, f32[1024,1024]{1,0:T(8,128)}, f32[1,128]{1,0:T(1,128)}) custom-call(f32[1024,1024]{1,0:T(8,128)} %get-tuple-element.249.dq_ref, f32[1024,1024]{1,0:T(8,128)} %get-tuple-element.250.lin_ref, f32[1,128]{1,0:T(1,128)} %reshape.121.hgain_ref.gain_ref, f32[1024,128]{1,0:T(8,128)} %get-tuple-element.348.cos_ref, ...), custom_call_target="tpu_custom_call" | custom-call | tf_op jit(solution)/shard_map/q_back/pallas_call | solution.py:46
  484.0 9.8 %kv_back.2 = (bf16[1024,1024]{1,0:T(8,128)(2,1)}, bf16[512,1024]{1,0:T(8,128)(2,1)}, f32[1,128]{1,0:T(1,128)}) custom-call(f32[512,512]{1,0:T(8,128)} %get-tuple-element.263.lin_ref, f32[1,128]{1,0:T(1,128)} %reshape.120.hgain_ref.gain_ref, f32[1024,128]{1,0:T(8,128)} %get-tuple-element.348.cos_ref, f32[1024,128]{1,0:T(8,128)} %get-tuple-element.349.sin_ref, ...), custom_call_target="tpu_custom_call" | custom-call | tf_op jit(solution)/shard_map/kv_back/pallas_call | solution.py:46
  495.4 10.0 %kv_back.3 = (bf16[1024,1024]{1,0:T(8,128)(2,1)}, bf16[512,1024]{1,0:T(8,128)(2,1)}, f32[1,128]{1,0:T(1,128)}) custom-call(f32[512,512]{1,0:T(8,128)} %get-tuple-element.262.lin_ref, f32[1,128]{1,0:T(1,128)} %reshape.120.hgain_ref.gain_ref, f32[1024,128]{1,0:T(8,128)} %get-tuple-element.348.cos_ref, ...), custom_call_target="tpu_custom_call", output_to_operand_aliasing={{0}: (15, {})} | custom-call | tf_op jit(solution)/shard_map/kv_back/pallas_call | solution.py:46
  505.5 9.6 %qkv_weight_grad.1 = (bf16[512,2048]{1,0:T(8,128)(2,1)}, bf16[512,2048]{1,0:T(8,128)(2,1)}) custom-call(bf16[1024,1024]{1,0:T(8,128)(2,1)} %get-tuple-element.168.normed_ref.left_ref, bf16[1024,1024]{1,0:T(8,128)(2,1)} %get-tuple-element.274.q_ref, bf16[1024,1024]{1,0:T(8,128)(2,1)} %get-tuple-element.275.kv_ref), custom_call_target="tpu_custom_call" | custom-call | tf_op jit(solution)/shard_map/qkv_weight_grad/pallas_call | solution.py:46
  520.1 21.1 %collective-permute-done.43.got_ref = bf16[512,1024]{1,0:T(8,128)(2,1)} collective-permute-done((bf16[512,1024]{1,0:T(8,128)(2,1)S(1)}, bf16[512,1024]{1,0:T(8,128)(2,1)}, u32[]{:S(2)}, u32[]{:S(2)}) %collective-permute-start.43) | collective-permute-done | bytes 1048608 | tf_op jit(solution)/shard_map/ppermute | solution.py:719
  541.2 4.4 tokens_back.2
  546.9 2.4 add_convert_fusion
  551.7 3.1 add_layer.2.refs_0_
  554.8 2.3 collective-permute-done.45
  558.9 3.1 add_layer.3
  563.2 4.1 tokens_back.3
  571.3 11.5 %collective-permute-done.49 = f32[1,2304]{1,0:T(1,128)S(1)} collective-permute-done((f32[1,2304]{1,0:T(1,128)S(1)}, f32[1,2304]{1,0:T(1,128)S(1)}, u32[]{:S(2)}, u32[]{:S(2)}) %collective-permute-start.49) | collective-permute-done | bytes 9248 | tf_op jit(solution)/shard_map/ppermute | solution.py:719
  588.3 2.9 collective-permute-done.51
  595.7 8.8 %collective-permute-done.54 = bf16[64,2048]{1,0:T(8,128)(2,1)S(1)} collective-permute-done((bf16[64,2048]{1,0:T(8,128)(2,1)S(1)}, bf16[64,2048]{1,0:T(8,128)(2,1)S(1)}, u32[]{:S(2)}, u32[]{:S(2)}) %collective-permute-start.54) | collective-permute-done | bytes 262176 | tf_op jit(solution)/shard_map/ppermute | solution.py:719
  (285 shorter events, 109.2 us)
Async XLA Ops:
  7.2 151.7 %all-gather.2.cloned.1.call-start = ((), (), s32[]{:S(2)}) async-start(), calls=%async_computation.1 | async-start | bytes 12255232 | tf_op jit(solution)/shard_map/all_gather | solution.py:834
  9.4 508.4 %reduce-scatter.2.cloned.1.call-start = ((), (), s32[]{:S(2)}) async-start(), calls=%async_computation.2 | async-start | bytes 12255232 | tf_op jit(solution)/shard_map/reduce_scatter | solution.py:955
  9.5 11.5 %collective-permute-start = (bf16[64,1024]{1,0:T(8,128)(2,1)}, bf16[64,1024]{1,0:T(8,128)(2,1)S(1)}, u32[]{:S(2)}, u32[]{:S(2)}) collective-permute-start(bf16[64,1024]{1,0:T(8,128)(2,1)} %get-tuple-element.159), channel_id=1, source_target_pairs={{0,16},{16,0},{1,17},{17,1},{2,18},{18,2},{3,19},{19,3},{4,20},{20... | collective-permute-start | bytes 393224 | tf_op jit(solution)/shard_map/ppermute | solution.py:719
  21.0 13.7 %collective-permute-start.4 = (bf16[128,1024]{1,0:T(8,128)(2,1)S(1)}, bf16[128,1024]{1,0:T(8,128)(2,1)S(1)}, u32[]{:S(2)}, u32[]{:S(2)}) collective-permute-start(bf16[128,1024]{1,0:T(8,128)(2,1)S(1)} %pad_maximum_fusion.5), channel_id=1, source_target_pairs={{0,4},{2,6},{4,0},{6,2},{8,12},{10,14},{12,8},{14,10},{1,5},{3,7},... | collective-permute-start | bytes 786440 | tf_op jit(solution)/shard_map/ppermute | solution.py:719
  22.8 13.4 %collective-permute-start.6 = (bf16[128,1024]{1,0:T(8,128)(2,1)S(1)}, bf16[128,1024]{1,0:T(8,128)(2,1)S(1)}, u32[]{:S(2)}, u32[]{:S(2)}) collective-permute-start(bf16[128,1024]{1,0:T(8,128)(2,1)S(1)} %pad_maximum_fusion.5), channel_id=1, source_target_pairs={{0,8},{2,10},{4,12},{6,14},{8,0},{10,2},{12,4},{14,6},{1,9},{3,11}... | collective-permute-start | bytes 786440 | tf_op jit(solution)/shard_map/ppermute | solution.py:719
  25.5 21.1 %collective-permute-start.3 = (bf16[16,144]{1,0:T(8,128)(2,1)S(1)}, bf16[16,144]{1,0:T(8,128)(2,1)S(1)}, u32[]{:S(2)}, u32[]{:S(2)}) collective-permute-start(bf16[16,144]{1,0:T(8,128)(2,1)S(1)} %fusion.24), channel_id=1, source_target_pairs={{0,4},{2,6},{4,0},{6,2},{8,12},{10,14},{12,8},{14,10},{1,5},{3,7},... | collective-permute-start | bytes 13832 | tf_op jit(solution)/shard_map/ppermute | solution.py:719
  27.0 20.4 %collective-permute-start.10 = (bf16[64,1024]{1,0:T(8,128)(2,1)S(1)}, bf16[64,1024]{1,0:T(8,128)(2,1)S(1)}, u32[]{:S(2)}, u32[]{:S(2)}) collective-permute-start(bf16[64,1024]{1,0:T(8,128)(2,1)S(1)} %copy-done.35), channel_id=1, source_target_pairs={{0,16},{16,0},{1,17},{17,1},{2,18},{18,2},{3,19},{19,3},{4,20},{20... | collective-permute-start | bytes 393224 | tf_op jit(solution)/shard_map/ppermute | solution.py:719
  42.2 11.0 %collective-permute-start.9 = (bf16[512,1024]{1,0:T(8,128)(2,1)}, bf16[512,1024]{1,0:T(8,128)(2,1)S(1)}, u32[]{:S(2)}, u32[]{:S(2)}) collective-permute-start(bf16[512,1024]{1,0:T(8,128)(2,1)} %get-tuple-element.324), channel_id=1, source_target_pairs={{0,2},{2,0},{4,6},{6,4},{8,10},{10,8},{12,14},{14,12},{1,3},{3,1},... | collective-permute-start | bytes 3145736 | tf_op jit(solution)/shard_map/ppermute | solution.py:719
  48.2 14.8 %collective-permute-start.11 = (bf16[128,1024]{1,0:T(8,128)(2,1)}, bf16[128,1024]{1,0:T(8,128)(2,1)}, u32[]{:S(2)}, u32[]{:S(2)}) collective-permute-start(bf16[128,1024]{1,0:T(8,128)(2,1)} %get-tuple-element.331), channel_id=1, source_target_pairs={{0,4},{2,6},{4,0},{6,2},{8,12},{10,14},{12,8},{14,10},{1,5},{3,7},... | collective-permute-start | bytes 786440 | tf_op jit(solution)/shard_map/ppermute | solution.py:719
  48.5 14.6 %collective-permute-start.12 = (bf16[128,1024]{1,0:T(8,128)(2,1)}, bf16[128,1024]{1,0:T(8,128)(2,1)S(1)}, u32[]{:S(2)}, u32[]{:S(2)}) collective-permute-start(bf16[128,1024]{1,0:T(8,128)(2,1)} %get-tuple-element.331), channel_id=1, source_target_pairs={{0,8},{2,10},{4,12},{6,14},{8,0},{10,2},{12,4},{14,6},{1,9},{3,11}... | collective-permute-start | bytes 786440 | tf_op jit(solution)/shard_map/ppermute | solution.py:719
  63.1 11.6 %collective-permute-start.13 = (bf16[128,512]{1,0:T(8,128)(2,1)S(1)}, bf16[128,512]{1,0:T(8,128)(2,1)S(1)}, u32[]{:S(2)}, u32[]{:S(2)}) collective-permute-start(bf16[128,512]{1,0:T(8,128)(2,1)S(1)} %slice.101), channel_id=1, source_target_pairs={{0,4},{2,6},{4,0},{6,2},{8,12},{10,14},{12,8},{14,10},{1,5},{3,7},... | collective-permute-start | bytes 393224 | tf_op jit(solution)/shard_map/ppermute | solution.py:719
  65.7 9.0 %collective-permute-start.14 = (bf16[128,512]{1,0:T(8,128)(2,1)S(1)}, bf16[128,512]{1,0:T(8,128)(2,1)S(1)}, u32[]{:S(2)}, u32[]{:S(2)}) collective-permute-start(bf16[128,512]{1,0:T(8,128)(2,1)S(1)} %slice.102), channel_id=1, source_target_pairs={{0,8},{2,10},{4,12},{6,14},{8,0},{10,2},{12,4},{14,6},{1,9},{3,11}... | collective-permute-start | bytes 393224 | tf_op jit(solution)/shard_map/ppermute | solution.py:719
  75.5 13.0 %collective-permute-start.15 = (bf16[512,1024]{1,0:T(8,128)(2,1)}, bf16[512,1024]{1,0:T(8,128)(2,1)}, u32[]{:S(2)}, u32[]{:S(2)}) collective-permute-start(bf16[512,1024]{1,0:T(8,128)(2,1)} %maximum_dynamic-update-slice_fusion), channel_id=1, source_target_pairs={{0,2},{2,0},{4,6},{6,4},{8,10},{10,8},{12,14},{14,12},{1,3},{3,1},... | collective-permute-start | bytes 3145736 | tf_op jit(solution)/shard_map/ppermute | solution.py:719
  75.5 25.8 %collective-permute-start.16 = (bf16[2,512,512]{2,1,0:T(8,128)(2,1)}, bf16[2,512,512]{2,1,0:T(8,128)(2,1)S(1)}, u32[]{:S(2)}, u32[]{:S(2)}) collective-permute-start(bf16[2,512,512]{2,1,0:T(8,128)(2,1)} %get-tuple-element.165.refs_2_.refs_0_), channel_id=1, source_target_pairs={{0,2},{2,0},{4,6},{6,4},{8,10},{10,8},{12,14},{14,12},{1,3},{3,1},... | collective-permute-start | bytes 3145736 | tf_op jit(solution)/shard_map/ppermute | solution.py:719
  76.0 42.6 %collective-permute-start.17 = (bf16[2,512,512]{2,1,0:T(8,128)(2,1)}, bf16[2,512,512]{2,1,0:T(8,128)(2,1)S(1)}, u32[]{:S(2)}, u32[]{:S(2)}) collective-permute-start(bf16[2,512,512]{2,1,0:T(8,128)(2,1)} %get-tuple-element.165.refs_2_.refs_0_), channel_id=1, source_target_pairs={{0,4},{2,6},{4,0},{6,2},{8,12},{10,14},{12,8},{14,10},{1,5},{3,7},... | collective-permute-start | bytes 3145736 | tf_op jit(solution)/shard_map/ppermute | solution.py:719
  77.0 41.6 %collective-permute-start.18 = (bf16[2,512,512]{2,1,0:T(8,128)(2,1)}, bf16[2,512,512]{2,1,0:T(8,128)(2,1)S(1)}, u32[]{:S(2)}, u32[]{:S(2)}) collective-permute-start(bf16[2,512,512]{2,1,0:T(8,128)(2,1)} %get-tuple-element.165.refs_2_.refs_0_), channel_id=1, source_target_pairs={{0,8},{2,10},{4,12},{6,14},{8,0},{10,2},{12,4},{14,6},{1,9},{3,11}... | collective-permute-start | bytes 3145736 | tf_op jit(solution)/shard_map/ppermute | solution.py:719
  118.7 7.4 %collective-permute-start.19 = (bf16[2,512,512]{2,1,0:T(8,128)(2,1)S(1)}, bf16[2,512,512]{2,1,0:T(8,128)(2,1)S(1)}, u32[]{:S(2)}, u32[]{:S(2)}) collective-permute-start(bf16[2,512,512]{2,1,0:T(8,128)(2,1)S(1)} %collective-permute-done.17.refs_2_.refs_0_), channel_id=1, source_target_pairs={{0,2},{2,0},{4,6},{6,4},{8,10},{10,8},{12,14},{14,12},{1,3},{3,1},... | collective-permute-start | bytes 3145736 | tf_op jit(solution)/shard_map/ppermute | solution.py:719
  119.7 22.7 %collective-permute-start.23 = (bf16[512,512]{1,0:T(8,128)(2,1)S(1)}, bf16[512,512]{1,0:T(8,128)(2,1)S(1)}, u32[]{:S(2)}, u32[]{:S(2)}) collective-permute-start(bf16[512,512]{1,0:T(8,128)(2,1)S(1)} %slice_bitcast_fusion.2), channel_id=1, source_target_pairs={{0,8},{2,10},{4,12},{6,14},{8,0},{10,2},{12,4},{14,6},{1,9},{3,11}... | collective-permute-start | bytes 1572872 | tf_op jit(solution)/shard_map/ppermute | solution.py:719
  121.1 21.3 %collective-permute-start.22 = (bf16[512,512]{1,0:T(8,128)(2,1)S(1)}, bf16[512,512]{1,0:T(8,128)(2,1)S(1)}, u32[]{:S(2)}, u32[]{:S(2)}) collective-permute-start(bf16[512,512]{1,0:T(8,128)(2,1)S(1)} %slice_bitcast_fusion.3), channel_id=1, source_target_pairs={{0,4},{2,6},{4,0},{6,2},{8,12},{10,14},{12,8},{14,10},{1,5},{3,7},... | collective-permute-start | bytes 1572872 | tf_op jit(solution)/shard_map/ppermute | solution.py:719
  122.1 34.1 %collective-permute-start.21 = (bf16[2,512,512]{2,1,0:T(8,128)(2,1)}, bf16[2,512,512]{2,1,0:T(8,128)(2,1)}, u32[]{:S(2)}, u32[]{:S(2)}) collective-permute-start(bf16[2,512,512]{2,1,0:T(8,128)(2,1)} %get-tuple-element.186.refs_4_.refs_0_), channel_id=1, source_target_pairs={{0,4},{2,6},{4,8},{6,10},{8,12},{10,14},{1,5},{3,7},{5,9},{7,11},{... | collective-permute-start | bytes 3145736 | tf_op jit(solution)/shard_map/ppermute | solution.py:724
  142.5 13.6 %collective-permute-start.24 = (bf16[2,512,512]{2,1,0:T(8,128)(2,1)S(1)}, bf16[2,512,512]{2,1,0:T(8,128)(2,1)S(1)}, u32[]{:S(2)}, u32[]{:S(2)}) collective-permute-start(bf16[2,512,512]{2,1,0:T(8,128)(2,1)S(1)} %pad_maximum_fusion.refs_1_.refs_6_.refs_0_), channel_id=1, source_target_pairs={{0,2},{2,0},{4,6},{6,4},{8,10},{10,8},{12,14},{14,12},{1,3},{3,1},... | collective-permute-start | bytes 3145736 | tf_op jit(solution)/shard_map/ppermute | solution.py:719
  158.9 9.9 %collective-permute-start.25 = (bf16[2,512,512]{2,1,0:T(8,128)(2,1)}, bf16[2,512,512]{2,1,0:T(8,128)(2,1)S(1)}, u32[]{:S(2)}, u32[]{:S(2)}) collective-permute-start(bf16[2,512,512]{2,1,0:T(8,128)(2,1)} %broadcast_select_fusion.1), channel_id=1, source_target_pairs={{0,2},{2,0},{4,6},{6,4},{8,10},{10,8},{12,14},{14,12},{1,3},{3,1},... | collective-permute-start | bytes 3145736 | tf_op jit(solution)/shard_map/ppermute | solution.py:719
  167.1 26.2 %collective-permute-start.27 = (bf16[512,1024]{1,0:T(8,128)(2,1)}, bf16[512,1024]{1,0:T(8,128)(2,1)S(1)}, u32[]{:S(2)}, u32[]{:S(2)}) collective-permute-start(bf16[512,1024]{1,0:T(8,128)(2,1)} %get-tuple-element.194.own_ref), channel_id=1, source_target_pairs={{0,1},{1,0},{2,3},{3,2},{4,5},{5,4},{6,7},{7,6},{8,9},{9,8},{10,11... | collective-permute-start | bytes 3145736 | tf_op jit(solution)/shard_map/ppermute | solution.py:719
  182.5 33.1 %collective-permute-start.26 = (bf16[512,1024]{1,0:T(8,128)(2,1)}, bf16[512,1024]{1,0:T(8,128)(2,1)S(1)}, u32[]{:S(2)}, u32[]{:S(2)}) collective-permute-start(bf16[512,1024]{1,0:T(8,128)(2,1)} %get-tuple-element.198.own_ref), channel_id=1, source_target_pairs={{0,1},{1,0},{2,3},{3,2},{4,5},{5,4},{6,7},{7,6},{8,9},{9,8},{10,11... | collective-permute-start | bytes 3145736 | tf_op jit(solution)/shard_map/ppermute | solution.py:719
  213.0 41.6 %collective-permute-start.29 = (bf16[512,1024]{1,0:T(8,128)(2,1)}, bf16[512,1024]{1,0:T(8,128)(2,1)S(1)}, u32[]{:S(2)}, u32[]{:S(2)}) collective-permute-start(bf16[512,1024]{1,0:T(8,128)(2,1)} %get-tuple-element.200.own_ref), channel_id=1, source_target_pairs={{0,1},{1,0},{2,3},{3,2},{4,5},{5,4},{6,7},{7,6},{8,9},{9,8},{10,11... | collective-permute-start | bytes 3145736 | tf_op jit(solution)/shard_map/ppermute | solution.py:719
  234.9 28.0 %collective-permute-start.28 = (bf16[512,1024]{1,0:T(8,128)(2,1)}, bf16[512,1024]{1,0:T(8,128)(2,1)S(1)}, u32[]{:S(2)}, u32[]{:S(2)}) collective-permute-start(bf16[512,1024]{1,0:T(8,128)(2,1)} %get-tuple-element.206.own_ref), channel_id=1, source_target_pairs={{0,1},{1,0},{2,3},{3,2},{4,5},{5,4},{6,7},{7,6},{8,9},{9,8},{10,11... | collective-permute-start | bytes 3145736 | tf_op jit(solution)/shard_map/ppermute | solution.py:719
  278.2 34.8 %collective-permute-start.30 = (bf16[512,1024]{1,0:T(8,128)(2,1)S(1)}, bf16[512,1024]{1,0:T(8,128)(2,1)S(1)}, u32[]{:S(2)}, u32[]{:S(2)}) collective-permute-start(bf16[512,1024]{1,0:T(8,128)(2,1)S(1)} %copy-done.23), channel_id=1, source_target_pairs={{0,1},{1,0},{2,3},{3,2},{4,5},{5,4},{6,7},{7,6},{8,9},{9,8},{10,11... | collective-permute-start | bytes 3145736 | tf_op jit(solution)/shard_map/ppermute | solution.py:719
  278.6 65.7 %collective-permute-start.31 = (bf16[512,1024]{1,0:T(8,128)(2,1)S(1)}, bf16[512,1024]{1,0:T(8,128)(2,1)S(1)}, u32[]{:S(2)}, u32[]{:S(2)}) collective-permute-start(bf16[512,1024]{1,0:T(8,128)(2,1)S(1)} %copy-done.26), channel_id=1, source_target_pairs={{0,1},{1,0},{2,3},{3,2},{4,5},{5,4},{6,7},{7,6},{8,9},{9,8},{10,11... | collective-permute-start | bytes 3145736 | tf_op jit(solution)/shard_map/ppermute | solution.py:719
  354.9 18.8 %collective-permute-start.32 = (bf16[2,512,512]{2,1,0:T(8,128)(2,1)}, bf16[2,512,512]{2,1,0:T(8,128)(2,1)S(1)}, u32[]{:S(2)}, u32[]{:S(2)}) collective-permute-start(bf16[2,512,512]{2,1,0:T(8,128)(2,1)} %get-tuple-element.235), channel_id=1, source_target_pairs={{0,2},{2,0},{4,6},{6,4},{8,10},{10,8},{12,14},{14,12},{1,3},{3,1},... | collective-permute-start | bytes 3145736 | tf_op jit(solution)/shard_map/ppermute | solution.py:719
  373.6 27.6 %collective-permute-start.33 = (bf16[2,512,512]{2,1,0:T(8,128)(2,1)}, bf16[2,512,512]{2,1,0:T(8,128)(2,1)S(1)}, u32[]{:S(2)}, u32[]{:S(2)}) collective-permute-start(bf16[2,512,512]{2,1,0:T(8,128)(2,1)} %get-tuple-element.244), channel_id=1, source_target_pairs={{0,2},{2,0},{4,6},{6,4},{8,10},{10,8},{12,14},{14,12},{1,3},{3,1},... | collective-permute-start | bytes 3145736 | tf_op jit(solution)/shard_map/ppermute | solution.py:719
  374.0 68.1 %collective-permute-start.35 = (bf16[2,512,512]{2,1,0:T(8,128)(2,1)S(1)}, bf16[2,512,512]{2,1,0:T(8,128)(2,1)S(1)}, u32[]{:S(2)}, u32[]{:S(2)}) collective-permute-start(bf16[2,512,512]{2,1,0:T(8,128)(2,1)S(1)} %add_convert_fusion.2), channel_id=1, source_target_pairs={{4,0},{6,2},{8,4},{10,6},{12,8},{14,10},{5,1},{7,3},{9,5},{11,7},{... | collective-permute-start | bytes 3145736 | tf_op jit(solution)/shard_map/ppermute | solution.py:724
  401.3 40.7 %collective-permute-start.34 = (bf16[2,512,512]{2,1,0:T(8,128)(2,1)}, bf16[2,512,512]{2,1,0:T(8,128)(2,1)S(1)}, u32[]{:S(2)}, u32[]{:S(2)}) collective-permute-start(bf16[2,512,512]{2,1,0:T(8,128)(2,1)} %get-tuple-element.252), channel_id=1, source_target_pairs={{0,2},{2,0},{4,6},{6,4},{8,10},{10,8},{12,14},{14,12},{1,3},{3,1},... | collective-permute-start | bytes 3145736 | tf_op jit(solution)/shard_map/ppermute | solution.py:719
  401.8 40.3 %collective-permute-start.36 = (bf16[2,512,512]{2,1,0:T(8,128)(2,1)}, bf16[2,512,512]{2,1,0:T(8,128)(2,1)S(1)}, u32[]{:S(2)}, u32[]{:S(2)}) collective-permute-start(bf16[2,512,512]{2,1,0:T(8,128)(2,1)} %get-tuple-element.255), channel_id=1, source_target_pairs={{0,2},{2,0},{4,6},{6,4},{8,10},{10,8},{12,14},{14,12},{1,3},{3,1},... | collective-permute-start | bytes 3145736 | tf_op jit(solution)/shard_map/ppermute | solution.py:719
  403.1 39.5 %collective-permute-start.37 = (bf16[512,512]{1,0:T(8,128)(2,1)}, bf16[512,512]{1,0:T(8,128)(2,1)S(1)}, u32[]{:S(2)}, u32[]{:S(2)}) collective-permute-start(bf16[512,512]{1,0:T(8,128)(2,1)} %get-tuple-element.316), channel_id=1, source_target_pairs={{0,4},{2,6},{4,0},{6,2},{8,12},{10,14},{12,8},{14,10},{1,5},{3,7},... | collective-permute-start | bytes 1572872 | tf_op jit(solution)/shard_map/ppermute | solution.py:719
  405.7 36.9 %collective-permute-start.38 = (bf16[512,512]{1,0:T(8,128)(2,1)S(1)}, bf16[512,512]{1,0:T(8,128)(2,1)S(1)}, u32[]{:S(2)}, u32[]{:S(2)}) collective-permute-start(bf16[512,512]{1,0:T(8,128)(2,1)S(1)} %get-tuple-element.315), channel_id=1, source_target_pairs={{0,8},{2,10},{4,12},{6,14},{8,0},{10,2},{12,4},{14,6},{1,9},{3,11}... | collective-permute-start | bytes 1572872 | tf_op jit(solution)/shard_map/ppermute | solution.py:719
  442.0 51.7 %collective-permute-start.39 = (bf16[2,512,512]{2,1,0:T(8,128)(2,1)}, bf16[2,512,512]{2,1,0:T(8,128)(2,1)S(1)}, u32[]{:S(2)}, u32[]{:S(2)}) collective-permute-start(bf16[2,512,512]{2,1,0:T(8,128)(2,1)} %get-tuple-element.270), channel_id=1, source_target_pairs={{0,2},{2,0},{4,6},{6,4},{8,10},{10,8},{12,14},{14,12},{1,3},{3,1},... | collective-permute-start | bytes 3145736 | tf_op jit(solution)/shard_map/ppermute | solution.py:719
  447.8 46.0 %collective-permute-start.40 = (bf16[2,512,512]{2,1,0:T(8,128)(2,1)}, bf16[2,512,512]{2,1,0:T(8,128)(2,1)S(1)}, u32[]{:S(2)}, u32[]{:S(2)}) collective-permute-start(bf16[2,512,512]{2,1,0:T(8,128)(2,1)} %get-tuple-element.259), channel_id=1, source_target_pairs={{0,4},{2,6},{4,0},{6,2},{8,12},{10,14},{12,8},{14,10},{1,5},{3,7},... | collective-permute-start | bytes 3145736 | tf_op jit(solution)/shard_map/ppermute | solution.py:719
  447.9 45.9 %collective-permute-start.41 = (bf16[2,512,512]{2,1,0:T(8,128)(2,1)}, bf16[2,512,512]{2,1,0:T(8,128)(2,1)S(1)}, u32[]{:S(2)}, u32[]{:S(2)}) collective-permute-start(bf16[2,512,512]{2,1,0:T(8,128)(2,1)} %get-tuple-element.271), channel_id=1, source_target_pairs={{0,8},{2,10},{4,12},{6,14},{8,0},{10,2},{12,4},{14,6},{1,9},{3,11}... | collective-permute-start | bytes 3145736 | tf_op jit(solution)/shard_map/ppermute | solution.py:719
  515.1 30.5 %collective-permute-start.42 = (bf16[512,2048]{1,0:T(8,128)(2,1)}, bf16[512,2048]{1,0:T(8,128)(2,1)S(1)}, u32[]{:S(2)}, u32[]{:S(2)}) collective-permute-start(bf16[512,2048]{1,0:T(8,128)(2,1)} %get-tuple-element.277), channel_id=1, source_target_pairs={{0,2},{2,0},{4,6},{6,4},{8,10},{10,8},{12,14},{14,12},{1,3},{3,1},... | collective-permute-start | bytes 6291464 | tf_op jit(solution)/shard_map/ppermute | solution.py:719
  515.1 26.1 %collective-permute-start.43 = (bf16[512,1024]{1,0:T(8,128)(2,1)S(1)}, bf16[512,1024]{1,0:T(8,128)(2,1)}, u32[]{:S(2)}, u32[]{:S(2)}) collective-permute-start(bf16[512,1024]{1,0:T(8,128)(2,1)S(1)} %copy-done.25), channel_id=1, source_target_pairs={{0,1},{1,0},{2,3},{3,2},{4,5},{5,4},{6,7},{7,6},{8,9},{9,8},{10,11... | collective-permute-start | bytes 3145736 | tf_op jit(solution)/shard_map/ppermute | solution.py:719
  515.8 47.4 %collective-permute-start.46 = (bf16[512,1024]{1,0:T(8,128)(2,1)}, bf16[512,1024]{1,0:T(8,128)(2,1)}, u32[]{:S(2)}, u32[]{:S(2)}) collective-permute-start(bf16[512,1024]{1,0:T(8,128)(2,1)} %get-tuple-element.273.own_ref), channel_id=1, source_target_pairs={{0,1},{1,0},{2,3},{3,2},{4,5},{5,4},{6,7},{7,6},{8,9},{9,8},{10,11... | collective-permute-start | bytes 3145736 | tf_op jit(solution)/shard_map/ppermute | solution.py:719
  549.4 7.7 %collective-permute-start.45 = (bf16[128,1024]{1,0:T(8,128)(2,1)S(1)}, bf16[128,1024]{1,0:T(8,128)(2,1)S(1)}, u32[]{:S(2)}, u32[]{:S(2)}) collective-permute-start(bf16[128,1024]{1,0:T(8,128)(2,1)S(1)} %get-tuple-element.311), channel_id=1, source_target_pairs={{0,4},{2,6},{4,0},{6,2},{8,12},{10,14},{12,8},{14,10},{1,5},{3,7},... | collective-permute-start | bytes 786440 | tf_op jit(solution)/shard_map/ppermute | solution.py:719
  551.5 7.1 %collective-permute-start.44 = (bf16[128,1024]{1,0:T(8,128)(2,1)S(1)}, bf16[128,1024]{1,0:T(8,128)(2,1)S(1)}, u32[]{:S(2)}, u32[]{:S(2)}) collective-permute-start(bf16[128,1024]{1,0:T(8,128)(2,1)S(1)} %get-tuple-element.313), channel_id=1, source_target_pairs={{0,8},{2,10},{4,12},{6,14},{8,0},{10,2},{12,4},{14,6},{1,9},{3,11}... | collective-permute-start | bytes 786440 | tf_op jit(solution)/shard_map/ppermute | solution.py:719
  551.5 16.4 %collective-permute-start.47 = (f32[1,256]{1,0:T(1,128)S(1)}, f32[1,256]{1,0:T(1,128)S(1)}, u32[]{:S(2)}, u32[]{:S(2)}) collective-permute-start(f32[1,256]{1,0:T(1,128)S(1)} %pad_maximum_fusion.8), channel_id=1, source_target_pairs={{0,1},{1,0},{2,3},{3,2},{4,5},{5,4},{6,7},{7,6},{8,9},{9,8},{10,11... | collective-permute-start | bytes 3080 | tf_op jit(solution)/shard_map/ppermute | solution.py:719
  568.1 23.9 %collective-permute-start.53 = (bf16[128,2048]{1,0:T(8,128)(2,1)S(1)}, bf16[128,2048]{1,0:T(8,128)(2,1)S(1)}, u32[]{:S(2)}, u32[]{:S(2)}) collective-permute-start(bf16[128,2048]{1,0:T(8,128)(2,1)S(1)} %pad_maximum_fusion.4), channel_id=1, source_target_pairs={{0,8},{2,10},{4,12},{6,14},{8,0},{10,2},{12,4},{14,6},{1,9},{3,11}... | collective-permute-start | bytes 1572872 | tf_op jit(solution)/shard_map/ppermute | solution.py:719
  568.2 23.8 %collective-permute-start.52 = (bf16[128,2048]{1,0:T(8,128)(2,1)S(1)}, bf16[128,2048]{1,0:T(8,128)(2,1)S(1)}, u32[]{:S(2)}, u32[]{:S(2)}) collective-permute-start(bf16[128,2048]{1,0:T(8,128)(2,1)S(1)} %pad_maximum_fusion.3), channel_id=1, source_target_pairs={{0,4},{2,6},{4,0},{6,2},{8,12},{10,14},{12,8},{14,10},{1,5},{3,7},... | collective-permute-start | bytes 1572872 | tf_op jit(solution)/shard_map/ppermute | solution.py:719
  570.2 12.6 %collective-permute-start.49 = (f32[1,2304]{1,0:T(1,128)S(1)}, f32[1,2304]{1,0:T(1,128)S(1)}, u32[]{:S(2)}, u32[]{:S(2)}) collective-permute-start(f32[1,2304]{1,0:T(1,128)S(1)} %fusion.23), channel_id=1, source_target_pairs={{0,4},{2,6},{4,0},{6,2},{8,12},{10,14},{12,8},{14,10},{1,5},{3,7},... | collective-permute-start | bytes 27656 | tf_op jit(solution)/shard_map/ppermute | solution.py:719
  592.2 12.2 %collective-permute-start.54 = (bf16[64,2048]{1,0:T(8,128)(2,1)S(1)}, bf16[64,2048]{1,0:T(8,128)(2,1)S(1)}, u32[]{:S(2)}, u32[]{:S(2)}) collective-permute-start(bf16[64,2048]{1,0:T(8,128)(2,1)S(1)} %slice.145), channel_id=1, source_target_pairs={{0,16},{16,0},{1,17},{17,1},{2,18},{18,2},{3,19},{19,3},{4,20},{20... | collective-permute-start | bytes 786440 | tf_op jit(solution)/shard_map/ppermute | solution.py:719
  (56 other events, 387.4 us)
Sparse Core Ops, SparseCore 0:
  10.3 109.6 all-gather.1
  277.1 155.0 reduce-scatter.1
where the time goes:
time: 622 us; the launch traced here: 613 us
  Pallas kernels  295 us (47%)
  waiting for transfers between devices  149 us (24%)
  starting transfers between devices  93.5 us (15%)
  local copies, waits for them, and re-layouts  35.6 us (6%)
  other arithmetic  19.7 us (3%)
  between operations  15.3 us (2%)
    pallas_call x30, Pallas kernels, call(): pl.pallas_call(kernel, grid_spec=pltpu.PrefetchScalarGridSpec(num_scalar_...  295 us
    ppermute x53, waiting for transfers between devices, swap(): return lax.ppermute(value, axis, [(i, i ^ bit) for i in range(size)])  135 us
    ppermute x53, starting transfers between devices, swap(): return lax.ppermute(value, axis, [(i, i ^ bit) for i in range(size)])  88.1 us
    unnamed x102, local copies, waits for them, and re-layouts  20.5 us
    ppermute x2, waiting for transfers between devices, shift(): lax.ppermute(value, 'ctx', [(i, i + by) for i in range(size) if 0 <= i +...  13.5 us
  transfers between devices with their start and end apart: 57, of which 22 were waited for; matrix products, arithmetic and copies ran while one was open for 8% of the time, Pallas kernels for 46%

commit v1 on v0

--- a/solution.py
+++ b/solution.py
@@ -26,7 +26,7 @@
 NT = (((1,), (1,)), ((), ()))
 TN = (((0,), (0,)), ((), ()))
 MIB = 2**20
-STATED = 0
+STATED = 3e9
 
 
 def mm(left, right, dims=NN):
@@ -37,7 +37,7 @@
     return jax.ShapeDtypeStruct(dims, kind)
 
 
-def call(kernel, name, grid, ins, outs, scratch=(), vmem=56, scalars=None, keep=None, us=4):
+def call(kernel, name, grid, ins, outs, scratch=(), vmem=56, scalars=None, keep=None, us=0):
     in_specs, arrays = [], []
     for array, block, index in ins:
         arrays.append(array)
@@ -114,7 +114,7 @@
     whole = lambda f: (0, 0)
     ins = [(w, w.shape, whole) for w in weights]
     outs = [(shaped((wide, cols), BF), (wide, cols), whole) for cols in (2 * k_cols, width)]
-    return call(functools.partial(pack_kernel, chunk), "pack", (1,), ins, outs, us=3)
+    return call(functools.partial(pack_kernel, chunk), "pack", (1,), ins, outs)
 
 
 def by_top_bit(slots):
@@ -254,9 +254,8 @@
             (shaped((rows, model), BF), (rows, model), lambda h, i: (0, 0)),
         ]
         scratch.append(pltpu.VMEM((rows, model), F32))
-    blocks = len(slots) * len(halves) + len(halos)
     return call(functools.partial(fwd_kernel, plan), "attend", (heads,), ins, outs, scratch,
-                scalars=scalars, keep=keep, us=2 + 3 * blocks)
+                scalars=scalars, keep=keep)
 
 
 def bwd_kernel(plan, idx_ref, q_ref, do_ref, lse_ref, delta_ref, lo_ref, *refs):
@@ -319,7 +318,7 @@
             when(lo_first < -(d - 1) * rows, kv_ref, out_ref, key - d * rows >= low)
     if half == 1:
         for at in range(len(slots)):
-            block(slot_refs[at], slot_outs[at], None, prior[at])
+            block(slot_refs[at], slot_outs[at], None, prior[at] if prior else None)
     else:
         if 0 in slots:
             at = slots.index(0)
@@ -380,7 +379,7 @@
         pltpu.VMEM((1, 2 * rows), F32),
         pltpu.VMEM((128, 2 * rows), F32),
     ]
-    us = 4 + 6 * (len(slots) + len(halos))
+    us = 4 + 6 * (len(slots) + len(halos)) if carry is not None or halos else 0
     results = call(functools.partial(bwd_kernel, plan), "attend_back", (heads,), ins, outs, scratch,
                    scalars=scalars, us=us, keep=keep)
     n = len(slots)
@@ -446,7 +445,7 @@
         (shaped((rows, model), BF), block, once),
     ]
     scratch = [pltpu.VMEM(block, BF), pltpu.VMEM(block, F32), pltpu.VMEM(block, F32)]
-    return call(ffn_kernel, "feed_forward", (steps,), ins, outs, scratch, keep=keep, us=18)
+    return call(ffn_kernel, "feed_forward", (steps,), ins, outs, scratch, keep=keep)
 
 
 def norm_back(grad, values, gain):
@@ -509,7 +508,7 @@
         (shaped((heads // 2, 8, rows), F32), (heads // 2, 8, size), lambda f: (0, 0, f)),
         (shaped((1, model), F32), (1, model), once),
     ]
-    return call(functools.partial(mixed_kernel, heads), "mixed_back", (steps,), ins, outs, keep=keep, us=7)
+    return call(functools.partial(mixed_kernel, heads), "mixed_back", (steps,), ins, outs, keep=keep)
 
 
 def merge_kernel(two, got3, four, got5, far_k, far_v, to_x, to_y):
@@ -530,7 +529,7 @@
         else:
             ins.append((piece, (size, cols), lambda f: (f, 0)))
     outs = [(shaped((2, rows, cols), BF), (2, size, cols), lambda f: (0, f, 0))] * 2
-    return call(merge_kernel, "merge", (steps,), ins, outs, us=4)
+    return call(merge_kernel, "merge", (steps,), ins, outs)
 
 
 def weight_kernel(left_ref, right_ref, *refs):
@@ -654,7 +653,7 @@
         (shaped((1, HEAD_SIZE), F32), (1, HEAD_SIZE), once),
     ]
     kernel = functools.partial(kv_back_kernel, cols // HEAD_SIZE, len(keys), len(values))
-    return call(kernel, "kv_back", (steps,), ins, outs, keep=keep, us=8)
+    return call(kernel, "kv_back", (steps,), ins, outs, keep=keep)
 
 
 def tokens_kernel(own_ref, got_ref, x_ref, gain_ref, d_resid_ref, *refs):
@@ -676,7 +675,7 @@
         keep = {len(ins): 0}
         ins.append((whole, None, None))
     outs = [(shaped((2 * rows, model), BF), block, mine), (shaped((1, model), F32), (1, model), once)]
-    return call(tokens_kernel, "tokens_back", (steps,), ins, outs, keep=keep, us=4)
+    return call(tokens_kernel, "tokens_back", (steps,), ins, outs, keep=keep, us=20 * half)
 
 
 def share_kernel(chunk, share_ref, out_ref, gate_ref, up_ref, down_ref):
@@ -711,7 +710,7 @@
         keep = {len(ins): 0}
         ins.append((whole, None, None))
     outs = [(shaped((2 * rows, model), BF), (size, model), mine)]
-    return call(layer_kernel, "add_layer", (steps,), ins, outs, keep=keep, us=3)[0]
+    return call(layer_kernel, "add_layer", (steps,), ins, outs, keep=keep)[0]
 
 
 def swap(value, axis, bit):
@@ -877,11 +876,11 @@
             (shaped((2, rows, k_cols), BF), (2, rows, k_cols), lambda f: (0, 0, 0)),
             (shaped((rows, k_cols), F32), (rows, k_cols), once),
         ]
-        return call(functools.partial(kv_kernel, kv_heads), "keys_values", (1,), ins, outs, keep=keep, us=6)
+        return call(functools.partial(kv_kernel, kv_heads), "keys_values", (1,), ins, outs, keep=keep)
 
     normed, kv_p, k_lin_p = keys_values(0, gain_one_s)
     normed, kv_c, k_lin_c = keys_values(1, after(gain_one_s, kv_p), normed)
-    w_q, _ = gather_rows(after(w_query, stages[0]), ((stages[1],), (w_kv,), (kv_p,), (kv_c,)))
+    w_q, _ = gather_rows(after(w_query, stages[0]), ((stages[1],), (kv_p,), (kv_p,), (kv_c,)))
     mine = lambda f: (f, 0)
     q, q_lin = call(
         functools.partial(q_kernel, heads), "queries", (2,),
@@ -908,27 +907,28 @@
             bit *= 2
         slots = {s: both[s] for s in range(ctx_size)}
         halos.update({d: shift(kv_c, d) for d in range(1, n_halo)})
-    state = attention_forward((0, 1), scalars, q, low_col, pick(slots, near), pick(halos, (0,)))
     ready = ()
     if ctx_size == 8:
-        slots[2], slots[4] = after(slots[2], state[0]), after(slots[4], state[0])
+        slots[2], slots[4] = after(slots[2], q), after(slots[4], q)
         far_k, far_v = swap(slots[4][0], "ctx", 2), swap(slots[2][1], "ctx", 4)
         slots[3], slots[5] = swap(slots[2], "ctx", 1), swap(slots[4], "ctx", 1)
         halos[2] = shift(after(kv_c, slots[2]), 2)
-    state = attention_forward((0, 1), after(scalars, state[0]), q, low_col, pick(slots, middle), {}, state)
+        ready = (slots[2], slots[4])
+    c_state = attention_forward(
+        (1,), after(scalars, *ready), q, low_col, pick(slots, near), pick(halos, (0,))
+    )
     if ctx_size == 8:
-        slots[6] = jnp.stack([after(far_k, state[0]), after(far_v, state[0])])
+        slots[6] = jnp.stack([after(far_k, c_state[0]), after(far_v, c_state[0])])
         slots[7] = swap(slots[6], "ctx", 1)
-        halo_one = jnp.where(odd, after(halos[2], slots[7]), kv_c)
-        halos[1] = swap(halo_one, "ctx", 1)
-        ready = (halo_one,)
-    p_state, c_state = state[:2], state[2:]
+        ready = (slots[7],)
     attended, lse_p, part_p = attention_forward(
-        (0,), after(scalars, c_state[0], *ready), q, low_col, pick(slots, far), {}, p_state, (w_rest, None)
+        (0,), after(scalars, c_state[0], *ready), q, low_col, slots, {}, None, (w_rest, None)
     )
     got_p = swap(part_p, "tensor", 1)
+    if ctx_size == 8:
+        halos[1] = swap(jnp.where(odd, after(halos[2], part_p), kv_c), "ctx", 1)
     attended, lse_c, part_c = attention_forward(
-        (1,), after(scalars, part_p), q, low_col, pick(slots, far), pick(halos, range(1, n_halo)),
+        (1,), after(scalars, part_p), q, low_col, pick(slots, middle + far), pick(halos, range(1, n_halo)),
         c_state, (w_rest, attended),
     )
     got_c = swap(part_c, "tensor", 1)
@@ -948,48 +948,50 @@
     d_resid_p, d_mixed, d_att_p, delta_p, d_two_p = mixed_back(
         0, back_p, back_got_p, resid_p, after(gain_two, rest_grads), cotangent, w_rest, o_cols, attended
     )
+    out_p, out_c = after(out_p, back_got_c), after(out_c, back_got_c)
+    out_got_p, out_got_c = swap(out_p, "tensor", 1), swap(out_c, "tensor", 1)
+
+    of_rows = [(d_att_p, lse_p, delta_p)]
+
+    def back_rows(half, deps, slots, halos, carry, prior=None, whole=None, last=False):
+        do, lse, delta = of_rows[half]
+        return attention_backward(
+            half, after(scalars, *deps), q, do, lse, delta, low_row, slots, halos, carry, prior, last, whole
+        )
+
+    dq_p, prior, _ = back_rows(0, (d_att_p,), pick(slots, far), {}, None)
     d_resid_c, d_mixed, d_att_c, delta_c, d_two_c = mixed_back(
-        1, back_c, back_got_c, resid_c, after(gain_two, d_att_p), cotangent, w_rest, o_cols, attended, d_mixed
-    )
+        1, back_c, back_got_c, resid_c, after(gain_two, dq_p), cotangent, w_rest, o_cols, attended, d_mixed
+    )
+    of_rows.append((d_att_c, lse_c, delta_c))
     rest_grads = weight_grad(d_mixed, attended, 0, width, min(1024, o_cols), rest_grads)
     rest_share = lax.psum_scatter(rest_grads, weight_axes, scatter_dimension=0, tiled=True)
-    out_p, out_c = after(out_p, back_got_c), after(out_c, back_got_c)
-    out_got_p, out_got_c = swap(out_p, "tensor", 1), swap(out_c, "tensor", 1)
-
-    dq, from_p, _ = attention_backward(
-        0, after(scalars, rest_grads), q, d_att_p, lse_p, delta_p, low_row, slots, {}
-    )
-
-    def back_c_rows(deps, slots, halos, carry, whole=None):
-        prior = pick(from_p, tuple(slots)) if slots else None
-        return attention_backward(
-            1, after(scalars, *deps), q, d_att_c, lse_c, delta_c, low_row, slots, halos, carry, prior,
-            whole is not None, whole,
-        )
-
-    dq_c, _, g_halo = back_c_rows((dq, out_got_p, out_got_c), {}, halos, None)
+    dq_c, _, g_halo = back_rows(1, (rest_grads,), {}, halos, None)
     if ctx_size == 8:
         near_one = swap(g_halo[1], "ctx", 1)
-    dq_c, g, _ = back_c_rows((dq_c,), pick(slots, far), {}, dq_c)
+    dq_c, g, _ = back_rows(1, (dq_c,), pick(slots, far), {}, dq_c, prior)
     zero = jnp.zeros((), BF)
+    ready = ()
     if ctx_size == 8:
+        got7 = swap(g[7], "ctx", 1)
         near_one = after(near_one, dq_c)
         two_back = add_low(g_halo[2], jnp.where(odd, near_one, zero))
         halo_two = shift(two_back, -2)
-        got7 = swap(g[7], "ctx", 1)
         ready = (two_back,)
-    dq_c, more, _ = back_c_rows((dq_c, *ready), pick(slots, middle), {}, dq_c)
+    dq, prior, _ = back_rows(0, (dq_c, *ready), pick(slots, near + middle), {}, dq_p, None, None, True)
+    if ctx_size == 8:
+        g6 = add_low(g[6], after(got7, dq))
+        far_k, far_v = swap(g6[0], "ctx", 2), swap(g6[1], "ctx", 4)
+        ready = (g6, halo_two)
+    dq_c, more, _ = back_rows(1, (dq, out_got_p, out_got_c, *ready), pick(slots, middle), {}, dq_c, prior)
     g.update(more)
     if ctx_size == 8:
-        g6 = add_low(g[6], after(got7, dq_c))
-        far_k, far_v = swap(g6[0], "ctx", 2), swap(g6[1], "ctx", 4)
         got3, got5 = swap(g[3], "ctx", 1), swap(g[5], "ctx", 1)
-        ready = (g6,)
-    dq, more, _ = back_c_rows((dq_c, *ready), pick(slots, near), {}, dq_c, dq)
+    dq, more, _ = back_rows(1, (dq_c,), pick(slots, near), {}, dq_c, prior, dq, True)
     g.update(more)
     if ctx_size == 8:
         got1 = swap(g[1], "ctx", 1)
-        far_k, far_v, got3, got5 = (after(v, dq, halo_two) for v in (far_k, far_v, got3, got5))
+        far_k, far_v, got3, got5 = (after(v, dq) for v in (far_k, far_v, got3, got5))
         to_x, to_y = merge(g[2], got3, g[4], got5, far_k, far_v)
         ready = (to_x,)
         keys_p = values_p = [g[0], got1, swap(to_x, "ctx", 2), swap(to_y, "ctx", 4)]
@@ -1014,20 +1016,20 @@
     high, low = qkv_weight_grad(normed, after(d_q, into_p), d_kv)
     heads = jnp.concatenate([q_heads, k_heads_c + k_heads_p], axis=1)
     heads_got = swap(heads, "tensor", 1)
-    out_share, gate_share, up_share, down_share = unpack(chunk, o_cols, after(rest_share, low))
-    grad_tokens, d_one_c = tokens_back(1, into_c, into_got_c, tokens, after(gain_one, gate_share), d_resid_c)
-    qkv_grad = scatter_rows(low, high, d_one_c)
+    grad_tokens, d_one_c = tokens_back(1, into_c, into_got_c, tokens, after(gain_one, low), d_resid_c)
+    out_share, gate_share, up_share, down_share = unpack(chunk, o_cols, after(rest_share, d_one_c))
+    qkv_grad = scatter_rows(low, high, gate_share)
     layer_out = add_layer(0, after(resid_p, qkv_grad[0]), out_p, out_got_p)
     qkv_grad = scatter_more(qkv_grad, layer_out)
     layer_out = add_layer(1, after(resid_c, qkv_grad[0]), out_c, out_got_c, layer_out)
+    qkv_grad = scatter_sum(qkv_grad, layer_out)
     grad_tokens, d_one_p = tokens_back(
-        0, into_p, into_got_p, tokens, after(gain_one, layer_out), d_resid_p, grad_tokens
-    )
-    qkv_grad = scatter_sum(qkv_grad, d_one_p)
+        0, into_p, into_got_p, tokens, after(gain_one, qkv_grad[0]), d_resid_p, grad_tokens
+    )
     heads = heads + after(heads_got, d_one_p)
     late = jnp.concatenate([d_one_c + d_one_p, heads, d_two_c + d_two_p], axis=1)
     late = butterfly(late, ("ctx", "shard"))
-    qkv_share = add_low(qkv_grad[0][:wide], qkv_grad[1]).astype(F32)
+    qkv_share = add_low(qkv_grad[0][:wide], after(qkv_grad[1], d_one_p)).astype(F32)
 
     def own_gain(value, size):
         return lax.dynamic_index_in_dim(value.reshape(parts, size), part, 0, keepdims=False)

time: 622 us -> 597 us (0.960)
  waiting for transfers between devices: 149 us -> 92.2 us
  starting transfers between devices: 93.5 us -> 127 us
    ppermute x53, waiting for transfers between devices: 135 us -> 82.3 us  [swap(): return lax.ppermute(value, axis, [(i, i ^ bit) for i in range(size)])]
    ppermute x53, starting transfers between devices: 88.1 us -> 122 us  [swap(): return lax.ppermute(value, axis, [(i, i ^ bit) for i in range(size)])]
    unnamed x102 -> x104, local copies, waits for them, and re-layouts: 20.5 us -> 21.1 us
  transfers between devices with their start and end apart: 57 -> 57, of which waited for: 22 -> 27; matrix products, arithmetic and copies ran while one was open for 8% -> 7% of each run, Pallas kernels for 46% -> 47%
where the time goes in v1:
time: 597 us; the launch traced here: 588 us
  Pallas kernels  294 us (49%)
  starting transfers between devices  127 us (21%)
  waiting for transfers between devices  92.2 us (15%)
  local copies, waits for them, and re-layouts  36.8 us (6%)
  other arithmetic  18.4 us (3%)
  between operations  14.9 us (2%)
    pallas_call x30, Pallas kernels, call(): pl.pallas_call(kernel, grid_spec=pltpu.PrefetchScalarGridSpec(num_scalar_...  294 us
    ppermute x53, starting transfers between devices, swap(): return lax.ppermute(value, axis, [(i, i ^ bit) for i in range(size)])  122 us
    ppermute x53, waiting for transfers between devices, swap(): return lax.ppermute(value, axis, [(i, i ^ bit) for i in range(size)])  82.3 us
    unnamed x104, local copies, waits for them, and re-layouts  21.1 us
  transfers between devices with their start and end apart: 57, of which 27 were waited for; matrix products, arithmetic and copies ran while one was open for 7% of the time, Pallas kernels for 47%

profile of v1, /device:TPU:0, one launch (start us, length us, event | category | flops | bytes accessed | tf_op | source)
XLA Modules:
  0.0 588.0 jit_solution(4655392514949920745)
XLA Ops:
  9.5 4.1 collective-permute-start
  28.3 6.4 %collective-permute-done.4 = bf16[128,1024]{1,0:T(8,128)(2,1)S(1)} collective-permute-done((bf16[128,1024]{1,0:T(8,128)(2,1)S(1)}, bf16[128,1024]{1,0:T(8,128)(2,1)S(1)}, u32[]{:S(2)}, u32[]{:S(2)}) %collective-permute-start.4) | collective-permute-done | bytes 262176 | tf_op jit(solution)/shard_map/ppermute | solution.py:718
  42.2 3.7 fusion.5.x_ref
  54.6 5.6 keys_values.2
  60.2 2.8 collective-permute-done.12
  72.7 6.8 %keys_values.3 = (bf16[1024,1024]{1,0:T(8,128)(2,1)}, bf16[2,512,512]{2,1,0:T(8,128)(2,1)}, f32[512,512]{1,0:T(8,128)}) custom-call(bf16[1024,1024]{1,0:T(8,128)(2,1)} %fusion.5.x_ref, f32[1,1024]{1,0:T(1,128)} %fusion.1.gain_ref, bf16[1024,1024]{1,0:T(8,128)(2,1)} %copy-done, ...), custom_call_target="tpu_custom_call", output_to_operand_aliasing={{0}: (6, {})} | custom-call | tf_op jit(solution)/shard_map/keys_values/pallas_call | solution.py:46
  83.2 10.3 %queries.1 = (bf16[1024,1024]{1,0:T(8,128)(2,1)}, f32[1024,1024]{1,0:T(8,128)}) custom-call(bf16[1024,1024]{1,0:T(8,128)(2,1)} %get-tuple-element.165.normed_ref.left_ref, bf16[1024,1024]{1,0:T(8,128)(2,1)} %constant_dynamic-update-slice_fusion.15.w_ref, f32[1,128]{1,0:T(1,128)} %reshape.121.hgain_ref.gain_ref, f32[1024,128]{1,0:T(8,128)} %get-tuple-element.342.cos_ref, ...), custom_call_target="tpu_custom_call" | custom-call | tf_op jit(solution)/shard_map/queries/pallas_call | solution.py:46
  93.5 23.9 %collective-permute-done.10.refs_3_.refs_1_.refs_2_.refs_0_ = bf16[2,512,512]{2,1,0:T(8,128)(2,1)S(1)} collective-permute-done((bf16[2,512,512]{2,1,0:T(8,128)(2,1)S(1)}, bf16[2,512,512]{2,1,0:T(8,128)(2,1)S(1)}, u32[]{:S(2)}, u32[]{:S(2)}) %collective-permute-start.10) | collective-permute-done | bytes 1048608 | tf_op jit(solution)/shard_map/ppermute | solution.py:718
  123.9 10.8 %attend.3 = (f32[512,1024]{1,0:T(8,128)}, f32[512,1024]{1,0:T(8,128)}) custom-call(s32[2]{0:T(128)} %pad_add_fusion.1.idx_ref, s32[512,128]{1,0:T(8,128)} %broadcast_in_dim.70.lo_ref, bf16[1024,1024]{1,0:T(8,128)(2,1)} %get-tuple-element.174.refs_0_.q_ref, bf16[2,512,512]{2,1,0:T(8,128)(2,1)} %get-tuple-element.162.refs_1_.refs_0_, ...), custom_call_target="tpu_custom_call" | custom-call | tf_op jit(solution)/shard_map/attend/pallas_call | solution.py:46
  135.5 3.5 collective-permute-start.24
  140.7 10.7 %attend.4 = (bf16[1024,1024]{1,0:T(8,128)(2,1)}, f32[4,8,512]{2,1,0:T(8,128)}, bf16[512,1024]{1,0:T(8,128)(2,1)}) custom-call(s32[2]{0:T(128)} %pad_add_fusion.1.idx_ref, s32[512,128]{1,0:T(8,128)} %broadcast_in_dim.70.lo_ref, bf16[1024,1024]{1,0:T(8,128)(2,1)} %get-tuple-element.174.refs_0_.q_ref, bf16[2,512,512]{2,1,0:T(8,128)(2,1)} %get-tuple-element.162.refs_1_.refs_0_, ...), custom_call_target="tpu_custom_call" | custom-call | tf_op jit(solution)/shard_map/attend/pallas_call | solution.py:46
  151.5 9.9 %collective-permute-done.24.refs_7_.refs_1_ = bf16[2,512,512]{2,1,0:T(8,128)(2,1)} collective-permute-done((bf16[2,512,512]{2,1,0:T(8,128)(2,1)}, bf16[2,512,512]{2,1,0:T(8,128)(2,1)}, u32[]{:S(2)}, u32[]{:S(2)}) %collective-permute-start.24) | collective-permute-done | bytes 1048608 | tf_op jit(solution)/shard_map/ppermute | solution.py:723
  166.5 22.1 %attend.5 = (bf16[1024,1024]{1,0:T(8,128)(2,1)}, f32[4,8,512]{2,1,0:T(8,128)}, bf16[512,1024]{1,0:T(8,128)(2,1)}) custom-call(s32[2]{0:T(128)} %pad_add_fusion.1.idx_ref, s32[512,128]{1,0:T(8,128)} %broadcast_in_dim.70.lo_ref, bf16[1024,1024]{1,0:T(8,128)(2,1)} %get-tuple-element.174.refs_0_.q_ref, ...), custom_call_target="tpu_custom_call", output_to_operand_aliasing={{0}: (14, {})} | custom-call | tf_op jit(solution)/shard_map/attend/pallas_call | solution.py:46
  192.8 18.3 %feed_forward.2 = (f32[512,1024]{1,0:T(8,128)}, bf16[1024,1024]{1,0:T(8,128)(2,1)}, bf16[1024,1536]{1,0:T(8,128)(2,1)}, bf16[1024,3072]{1,0:T(8,128)(2,1)}, bf16...) custom-call(bf16[1024,1024]{1,0:T(8,128)(2,1)} %x_ref.7, bf16[512,1024]{1,0:T(8,128)(2,1)} %get-tuple-element.183.own_ref, ...), custom_call_target="tpu_custom_call" | custom-call | tf_op jit(solution)/shard_map/feed_forward/pallas_call | solution.py:46
  213.7 18.7 %feed_forward.3 = (f32[512,1024]{1,0:T(8,128)}, bf16[1024,1024]{1,0:T(8,128)(2,1)}, bf16[1024,1536]{1,0:T(8,128)(2,1)}, bf16[1024,3072]{1,0:T(8,128)(2,1)}, bf16...) custom-call(bf16[1024,1024]{1,0:T(8,128)(2,1)} %x_ref.7, ...), custom_call_target="tpu_custom_call", output_to_operand_aliasing={{1}: (7, {}), {2}: (8, {}), {3}: (9, {})} | custom-call | tf_op jit(solution)/shard_map/feed_forward/pallas_call | solution.py:46
  236.5 10.7 %weight_grad.3.refs_0_ = bf16[1024,5632]{1,0:T(8,128)(2,1)} custom-call(bf16[1024,1024]{1,0:T(8,128)(2,1)} %get-tuple-element.200.left_ref, bf16[1024,3072]{1,0:T(8,128)(2,1)} %get-tuple-element.201.right_ref), custom_call_target="tpu_custom_call" | custom-call | tf_op jit(solution)/shard_map/weight_grad/pallas_call | solution.py:46
  247.3 7.2 %weight_grad.4.refs_0_ = bf16[1024,5632]{1,0:T(8,128)(2,1)} custom-call(bf16[1024,1024]{1,0:T(8,128)(2,1)} %dy_ref.7, bf16[1024,1536]{1,0:T(8,128)(2,1)} %get-tuple-element.199.right_ref, bf16[1024,5632]{1,0:T(8,128)(2,1)} %weight_grad.3.refs_0_), custom_call_target="tpu_custom_call", output_to_operand_aliasing={{}: (2, {})} | custom-call | tf_op jit(solution)/shard_map/weight_grad/pallas_call | solution.py:46
  255.4 7.2 %mixed_back.2 = (f32[512,1024]{1,0:T(8,128)}, bf16[1024,1024]{1,0:T(8,128)(2,1)}, bf16[512,1024]{1,0:T(8,128)(2,1)}, f32[4,8,512]{2,1,0:T(8,128)}, f32[1,1024]{1,0:T(1,128)}) custom-call(bf16[512,1024]{1,0:T(8,128)(2,1)} %get-tuple-element.191.own_ref, bf16[512,1024]{1,0:T(8,128)(2,1)} %copy-done.28, f32[512,1024]{1,0:T(8,128)} %get-tuple-element.277.resid_ref, ...), custom_call_target="tpu_custom_call" | custom-call | tf_op jit(solution)/shard_map/mixed_back/pallas_call | solution.py:46
  263.2 5.8 attend_back.6
  270.0 7.0 %mixed_back.3 = (f32[512,1024]{1,0:T(8,128)}, bf16[1024,1024]{1,0:T(8,128)(2,1)}, bf16[512,1024]{1,0:T(8,128)(2,1)}, f32[4,8,512]{2,1,0:T(8,128)}, f32[1,1024]{1,0:T(1,128)}) custom-call(bf16[512,1024]{1,0:T(8,128)(2,1)} %get-tuple-element.197.own_ref, bf16[512,1024]{1,0:T(8,128)(2,1)} %copy-done.19, ...), custom_call_target="tpu_custom_call", output_to_operand_aliasing={{1}: (7, {})} | custom-call | tf_op jit(solution)/shard_map/mixed_back/pallas_call | solution.py:46
  277.0 6.0 %weight_grad.5 = bf16[1024,5632]{1,0:T(8,128)(2,1)} custom-call(bf16[1024,1024]{1,0:T(8,128)(2,1)} %get-tuple-element.211.left_ref, bf16[1024,1024]{1,0:T(8,128)(2,1)} %get-tuple-element.203.att_ref.right_ref, bf16[1024,5632]{1,0:T(8,128)(2,1)} %weight_grad.4.refs_0_), custom_call_target="tpu_custom_call", output_to_operand_aliasing={{}: (2, {})} | custom-call | tf_op jit(solution)/shard_map/weight_grad/pallas_call | solution.py:46
  283.0 10.2 %attend_back.7 = (f32[512,1024]{1,0:T(8,128)}, bf16[2,512,512]{2,1,0:T(8,128)(2,1)}, bf16[2,512,512]{2,1,0:T(8,128)(2,1)}, bf16[2,512,512]{2,1,0:T(8,128)(2,1)}) custom-call(s32[2]{0:T(128)} %pad_add_fusion.1.idx_ref, bf16[1024,1024]{1,0:T(8,128)(2,1)} %get-tuple-element.174.refs_0_.q_ref, bf16[512,1024]{1,0:T(8,128)(2,1)} %get-tuple-element.213.do_ref, ...), custom_call_target="tpu_custom_call" | custom-call | flops 65999998976 | tf_op jit(solution)/shard_map/attend_back/pallas_call | solution.py:46
  293.2 9.8 %collective-permute-start.30 = (bf16[2,512,512]{2,1,0:T(8,128)(2,1)}, bf16[2,512,512]{2,1,0:T(8,128)(2,1)S(1)}, u32[]{:S(2)}, u32[]{:S(2)}) collective-permute-start(bf16[2,512,512]{2,1,0:T(8,128)(2,1)} %get-tuple-element.222), channel_id=1, source_target_pairs={{0,2},{2,0},{4,6},{6,4},{8,10},{10,8},{12,14},{14,12},{1,3},{3,1},... | collective-permute-start | bytes 3145736 | tf_op jit(solution)/shard_map/ppermute | solution.py:718
  303.1 15.2 %attend_back.8 = (f32[512,1024]{1,0:T(8,128)}, bf16[2,512,512]{2,1,0:T(8,128)(2,1)}, bf16[2,512,512]{2,1,0:T(8,128)(2,1)}) custom-call(s32[2]{0:T(128)} %pad_add_fusion.1.idx_ref, bf16[1024,1024]{1,0:T(8,128)(2,1)} %get-tuple-element.174.refs_0_.q_ref, bf16[512,1024]{1,0:T(8,128)(2,1)} %get-tuple-element.213.do_ref, ...), custom_call_target="tpu_custom_call" | custom-call | flops 48000000000 | tf_op jit(solution)/shard_map/attend_back/pallas_call | solution.py:46
  323.1 12.3 %attend_back.9 = (f32[1024,1024]{1,0:T(8,128)}, bf16[2,512,512]{2,1,0:T(8,128)(2,1)}, bf16[2,512,512]{2,1,0:T(8,128)(2,1)}, bf16[2,512,512]{2,1,0:T(8,128)(2,1)}...) custom-call(s32[2]{0:T(128)} %pad_add_fusion.1.idx_ref, ...), custom_call_target="tpu_custom_call" | custom-call | flops 120000004096 | tf_op jit(solution)/shard_map/attend_back/pallas_call | solution.py:46
  336.8 34.0 %collective-permute-start.38 = (bf16[512,512]{1,0:T(8,128)(2,1)}, bf16[512,512]{1,0:T(8,128)(2,1)S(1)}, u32[]{:S(2)}, u32[]{:S(2)}) collective-permute-start(bf16[512,512]{1,0:T(8,128)(2,1)} %get-tuple-element.309), channel_id=1, source_target_pairs={{0,8},{2,10},{4,12},{6,14},{8,0},{10,2},{12,4},{14,6},{1,9},{3,11}... | collective-permute-start | bytes 1572872 | tf_op jit(solution)/shard_map/ppermute | solution.py:718
  370.8 16.2 %collective-permute-start.37 = (bf16[512,512]{1,0:T(8,128)(2,1)}, bf16[512,512]{1,0:T(8,128)(2,1)}, u32[]{:S(2)}, u32[]{:S(2)}) collective-permute-start(bf16[512,512]{1,0:T(8,128)(2,1)} %get-tuple-element.310), channel_id=1, source_target_pairs={{0,4},{2,6},{4,0},{6,2},{8,12},{10,14},{12,8},{14,10},{1,5},{3,7},... | collective-permute-start | bytes 1572872 | tf_op jit(solution)/shard_map/ppermute | solution.py:718
  386.9 6.9 %collective-permute-done.31.got_ref = bf16[512,1024]{1,0:T(8,128)(2,1)S(1)} collective-permute-done((bf16[512,1024]{1,0:T(8,128)(2,1)S(1)}, bf16[512,1024]{1,0:T(8,128)(2,1)S(1)}, u32[]{:S(2)}, u32[]{:S(2)}) %collective-permute-start.31) | collective-permute-done | bytes 1048608 | tf_op jit(solution)/shard_map/ppermute | solution.py:718
  393.8 26.1 %attend_back.10 = (f32[512,1024]{1,0:T(8,128)}, bf16[2,512,512]{2,1,0:T(8,128)(2,1)}, bf16[2,512,512]{2,1,0:T(8,128)(2,1)}, bf16[2,512,512]{2,1,0:T(8,128)(2,1)}, bf16[2,512,512]{2,1,0:T(8,128)(2,1)}) custom-call(s32[2]{0:T(128)} %pad_add_fusion.1.idx_ref, bf16[1024,1024]{1,0:T(8,128)(2,1)} %get-tuple-element.174.refs_0_.q_ref, ...), custom_call_target="tpu_custom_call" | custom-call | flops 83999997952 | tf_op jit(solution)/shard_map/attend_back/pallas_call | solution.py:46
  420.6 15.2 %attend_back.11 = (f32[1024,1024]{1,0:T(8,128)}, bf16[2,512,512]{2,1,0:T(8,128)(2,1)}, bf16[2,512,512]{2,1,0:T(8,128)(2,1)}) custom-call(s32[2]{0:T(128)} %pad_add_fusion.1.idx_ref, bf16[1024,1024]{1,0:T(8,128)(2,1)} %get-tuple-element.174.refs_0_.q_ref, bf16[512,1024]{1,0:T(8,128)(2,1)} %get-tuple-element.213.do_ref, ...), custom_call_target="tpu_custom_call", output_to_operand_aliasing={{0}: (11, {})} | custom-call | flops 48000000000 | tf_op jit(solution)/shard_map/attend_back/pallas_call | solution.py:46
  437.3 3.9 merge.1
  441.2 24.1 %collective-permute-start.41 = (bf16[2,512,512]{2,1,0:T(8,128)(2,1)}, bf16[2,512,512]{2,1,0:T(8,128)(2,1)S(1)}, u32[]{:S(2)}, u32[]{:S(2)}) collective-permute-start(bf16[2,512,512]{2,1,0:T(8,128)(2,1)} %get-tuple-element.264), channel_id=1, source_target_pairs={{0,8},{2,10},{4,12},{6,14},{8,0},{10,2},{12,4},{14,6},{1,9},{3,11}... | collective-permute-start | bytes 3145736 | tf_op jit(solution)/shard_map/ppermute | solution.py:718
  466.3 15.4 %q_back.1 = (bf16[1024,1024]{1,0:T(8,128)(2,1)}, f32[1024,1024]{1,0:T(8,128)}, f32[1,128]{1,0:T(1,128)}) custom-call(f32[1024,1024]{1,0:T(8,128)} %get-tuple-element.242.dq_ref, f32[1024,1024]{1,0:T(8,128)} %get-tuple-element.243.lin_ref, f32[1,128]{1,0:T(1,128)} %reshape.121.hgain_ref.gain_ref, f32[1024,128]{1,0:T(8,128)} %get-tuple-element.342.cos_ref, ...), custom_call_target="tpu_custom_call" | custom-call | tf_op jit(solution)/shard_map/q_back/pallas_call | solution.py:46
  481.6 10.1 %kv_back.2 = (bf16[1024,1024]{1,0:T(8,128)(2,1)}, bf16[512,1024]{1,0:T(8,128)(2,1)}, f32[1,128]{1,0:T(1,128)}) custom-call(f32[512,512]{1,0:T(8,128)} %get-tuple-element.256.lin_ref, f32[1,128]{1,0:T(1,128)} %reshape.120.hgain_ref.gain_ref, f32[1024,128]{1,0:T(8,128)} %get-tuple-element.342.cos_ref, f32[1024,128]{1,0:T(8,128)} %get-tuple-element.343.sin_ref, ...), custom_call_target="tpu_custom_call" | custom-call | tf_op jit(solution)/shard_map/kv_back/pallas_call | solution.py:46
  494.2 10.1 %kv_back.3 = (bf16[1024,1024]{1,0:T(8,128)(2,1)}, bf16[512,1024]{1,0:T(8,128)(2,1)}, f32[1,128]{1,0:T(1,128)}) custom-call(f32[512,512]{1,0:T(8,128)} %get-tuple-element.255.lin_ref, f32[1,128]{1,0:T(1,128)} %reshape.120.hgain_ref.gain_ref, f32[1024,128]{1,0:T(8,128)} %get-tuple-element.342.cos_ref, ...), custom_call_target="tpu_custom_call", output_to_operand_aliasing={{0}: (15, {})} | custom-call | tf_op jit(solution)/shard_map/kv_back/pallas_call | solution.py:46
  504.2 9.5 %qkv_weight_grad.1 = (bf16[512,2048]{1,0:T(8,128)(2,1)}, bf16[512,2048]{1,0:T(8,128)(2,1)}) custom-call(bf16[1024,1024]{1,0:T(8,128)(2,1)} %get-tuple-element.165.normed_ref.left_ref, bf16[1024,1024]{1,0:T(8,128)(2,1)} %get-tuple-element.267.q_ref, bf16[1024,1024]{1,0:T(8,128)(2,1)} %get-tuple-element.268.kv_ref), custom_call_target="tpu_custom_call" | custom-call | tf_op jit(solution)/shard_map/qkv_weight_grad/pallas_call | solution.py:46
  513.7 3.3 collective-permute-done.43.got_ref
  517.1 4.1 tokens_back.2
  528.1 3.1 add_layer.2.refs_0_
  537.0 3.1 add_layer.3
  540.1 6.2 %collective-permute-done.47 = bf16[128,2048]{1,0:T(8,128)(2,1)S(1)} collective-permute-done((bf16[128,2048]{1,0:T(8,128)(2,1)S(1)}, bf16[128,2048]{1,0:T(8,128)(2,1)S(1)}, u32[]{:S(2)}, u32[]{:S(2)}) %collective-permute-start.47) | collective-permute-done | bytes 524320 | tf_op jit(solution)/shard_map/ppermute | solution.py:718
  546.8 5.1 collective-permute-done.46.got_ref
  552.9 4.0 tokens_back.3
  559.8 2.8 collective-permute-done.51
  563.6 2.8 collective-permute-done.52
  566.5 3.0 collective-permute-start.54
  569.5 4.6 collective-permute-done.53
  576.5 3.0 collective-permute-done.54
  (287 shorter events, 107.6 us)
Async XLA Ops:
  7.2 133.5 %all-gather.2.cloned.1.call-start = ((), (), s32[]{:S(2)}) async-start(), calls=%async_computation.1 | async-start | bytes 12255232 | tf_op jit(solution)/shard_map/all_gather | solution.py:833
  9.4 511.8 %reduce-scatter.2.cloned.1.call-start = ((), (), s32[]{:S(2)}) async-start(), calls=%async_computation.2 | async-start | bytes 12255232 | tf_op jit(solution)/shard_map/reduce_scatter | solution.py:968
  9.5 11.5 %collective-permute-start = (bf16[64,1024]{1,0:T(8,128)(2,1)}, bf16[64,1024]{1,0:T(8,128)(2,1)S(1)}, u32[]{:S(2)}, u32[]{:S(2)}) collective-permute-start(bf16[64,1024]{1,0:T(8,128)(2,1)} %get-tuple-element.156), channel_id=1, source_target_pairs={{0,16},{16,0},{1,17},{17,1},{2,18},{18,2},{3,19},{19,3},{4,20},{20... | collective-permute-start | bytes 393224 | tf_op jit(solution)/shard_map/ppermute | solution.py:718
  14.4 6.4 %collective-permute-start.1 = (bf16[16,144]{1,0:T(8,128)(2,1)S(1)}, bf16[16,144]{1,0:T(8,128)(2,1)S(1)}, u32[]{:S(2)}, u32[]{:S(2)}) collective-permute-start(bf16[16,144]{1,0:T(8,128)(2,1)S(1)} %broadcast_select_fusion.2), channel_id=1, source_target_pairs={{0,2},{2,0},{4,6},{6,4},{8,10},{10,8},{12,14},{14,12},{1,3},{3,1},... | collective-permute-start | bytes 13832 | tf_op jit(solution)/shard_map/ppermute | solution.py:718
  21.0 13.6 %collective-permute-start.4 = (bf16[128,1024]{1,0:T(8,128)(2,1)S(1)}, bf16[128,1024]{1,0:T(8,128)(2,1)S(1)}, u32[]{:S(2)}, u32[]{:S(2)}) collective-permute-start(bf16[128,1024]{1,0:T(8,128)(2,1)S(1)} %pad_maximum_fusion.5), channel_id=1, source_target_pairs={{0,4},{2,6},{4,0},{6,2},{8,12},{10,14},{12,8},{14,10},{1,5},{3,7},... | collective-permute-start | bytes 786440 | tf_op jit(solution)/shard_map/ppermute | solution.py:718
  22.9 13.4 %collective-permute-start.6 = (bf16[128,1024]{1,0:T(8,128)(2,1)S(1)}, bf16[128,1024]{1,0:T(8,128)(2,1)S(1)}, u32[]{:S(2)}, u32[]{:S(2)}) collective-permute-start(bf16[128,1024]{1,0:T(8,128)(2,1)S(1)} %pad_maximum_fusion.5), channel_id=1, source_target_pairs={{0,8},{2,10},{4,12},{6,14},{8,0},{10,2},{12,4},{14,6},{1,9},{3,11}... | collective-permute-start | bytes 786440 | tf_op jit(solution)/shard_map/ppermute | solution.py:718
  25.6 21.1 %collective-permute-start.3 = (bf16[16,144]{1,0:T(8,128)(2,1)S(1)}, bf16[16,144]{1,0:T(8,128)(2,1)S(1)}, u32[]{:S(2)}, u32[]{:S(2)}) collective-permute-start(bf16[16,144]{1,0:T(8,128)(2,1)S(1)} %fusion.24), channel_id=1, source_target_pairs={{0,4},{2,6},{4,0},{6,2},{8,12},{10,14},{12,8},{14,10},{1,5},{3,7},... | collective-permute-start | bytes 13832 | tf_op jit(solution)/shard_map/ppermute | solution.py:718
  27.1 20.3 %collective-permute-start.11 = (bf16[64,1024]{1,0:T(8,128)(2,1)S(1)}, bf16[64,1024]{1,0:T(8,128)(2,1)S(1)}, u32[]{:S(2)}, u32[]{:S(2)}) collective-permute-start(bf16[64,1024]{1,0:T(8,128)(2,1)S(1)} %copy-done.34), channel_id=1, source_target_pairs={{0,16},{16,0},{1,17},{17,1},{2,18},{18,2},{3,19},{19,3},{4,20},{20... | collective-permute-start | bytes 393224 | tf_op jit(solution)/shard_map/ppermute | solution.py:718
  34.7 5.6 collective-permute-start.8
  36.3 5.1 collective-permute-start.7
  42.2 11.0 %collective-permute-start.9 = (bf16[512,1024]{1,0:T(8,128)(2,1)}, bf16[512,1024]{1,0:T(8,128)(2,1)S(1)}, u32[]{:S(2)}, u32[]{:S(2)}) collective-permute-start(bf16[512,1024]{1,0:T(8,128)(2,1)} %get-tuple-element.318), channel_id=1, source_target_pairs={{0,2},{2,0},{4,6},{6,4},{8,10},{10,8},{12,14},{14,12},{1,3},{3,1},... | collective-permute-start | bytes 3145736 | tf_op jit(solution)/shard_map/ppermute | solution.py:718
  48.2 14.8 %collective-permute-start.12 = (bf16[128,1024]{1,0:T(8,128)(2,1)}, bf16[128,1024]{1,0:T(8,128)(2,1)}, u32[]{:S(2)}, u32[]{:S(2)}) collective-permute-start(bf16[128,1024]{1,0:T(8,128)(2,1)} %get-tuple-element.325), channel_id=1, source_target_pairs={{0,4},{2,6},{4,0},{6,2},{8,12},{10,14},{12,8},{14,10},{1,5},{3,7},... | collective-permute-start | bytes 786440 | tf_op jit(solution)/shard_map/ppermute | solution.py:718
  48.5 16.9 %collective-permute-start.13 = (bf16[128,1024]{1,0:T(8,128)(2,1)}, bf16[128,1024]{1,0:T(8,128)(2,1)S(1)}, u32[]{:S(2)}, u32[]{:S(2)}) collective-permute-start(bf16[128,1024]{1,0:T(8,128)(2,1)} %get-tuple-element.325), channel_id=1, source_target_pairs={{0,8},{2,10},{4,12},{6,14},{8,0},{10,2},{12,4},{14,6},{1,9},{3,11}... | collective-permute-start | bytes 786440 | tf_op jit(solution)/shard_map/ppermute | solution.py:718
  71.1 9.7 %collective-permute-start.16 = (bf16[512,1024]{1,0:T(8,128)(2,1)}, bf16[512,1024]{1,0:T(8,128)(2,1)}, u32[]{:S(2)}, u32[]{:S(2)}) collective-permute-start(bf16[512,1024]{1,0:T(8,128)(2,1)} %maximum_dynamic-update-slice_fusion), channel_id=1, source_target_pairs={{0,2},{2,0},{4,6},{6,4},{8,10},{10,8},{12,14},{14,12},{1,3},{3,1},... | collective-permute-start | bytes 3145736 | tf_op jit(solution)/shard_map/ppermute | solution.py:718
  71.1 46.2 %collective-permute-start.10 = (bf16[2,512,512]{2,1,0:T(8,128)(2,1)S(1)}, bf16[2,512,512]{2,1,0:T(8,128)(2,1)S(1)}, u32[]{:S(2)}, u32[]{:S(2)}) collective-permute-start(bf16[2,512,512]{2,1,0:T(8,128)(2,1)S(1)} %copy-done.12), channel_id=1, source_target_pairs={{0,4},{2,6},{4,0},{6,2},{8,12},{10,14},{12,8},{14,10},{1,5},{3,7},... | collective-permute-start | bytes 3145736 | tf_op jit(solution)/shard_map/ppermute | solution.py:718
  71.6 45.9 %collective-permute-start.17 = (bf16[2,512,512]{2,1,0:T(8,128)(2,1)S(1)}, bf16[2,512,512]{2,1,0:T(8,128)(2,1)}, u32[]{:S(2)}, u32[]{:S(2)}) collective-permute-start(bf16[2,512,512]{2,1,0:T(8,128)(2,1)S(1)} %copy-done.12), channel_id=1, source_target_pairs={{0,8},{2,10},{4,12},{6,14},{8,0},{10,2},{12,4},{14,6},{1,9},{3,11}... | collective-permute-start | bytes 3145736 | tf_op jit(solution)/shard_map/ppermute | solution.py:718
  72.7 50.1 %collective-permute-start.18 = (bf16[2,512,512]{2,1,0:T(8,128)(2,1)S(1)}, bf16[2,512,512]{2,1,0:T(8,128)(2,1)S(1)}, u32[]{:S(2)}, u32[]{:S(2)}) collective-permute-start(bf16[2,512,512]{2,1,0:T(8,128)(2,1)S(1)} %copy-done.12), channel_id=1, source_target_pairs={{0,2},{2,0},{4,6},{6,4},{8,10},{10,8},{12,14},{14,12},{1,3},{3,1},... | collective-permute-start | bytes 3145736 | tf_op jit(solution)/shard_map/ppermute | solution.py:718
  118.8 15.9 %collective-permute-start.19 = (bf16[512,512]{1,0:T(8,128)(2,1)S(1)}, bf16[512,512]{1,0:T(8,128)(2,1)S(1)}, u32[]{:S(2)}, u32[]{:S(2)}) collective-permute-start(bf16[512,512]{1,0:T(8,128)(2,1)S(1)} %slice_bitcast_fusion.3), channel_id=1, source_target_pairs={{0,4},{2,6},{4,0},{6,2},{8,12},{10,14},{12,8},{14,10},{1,5},{3,7},... | collective-permute-start | bytes 1572872 | tf_op jit(solution)/shard_map/ppermute | solution.py:718
  120.3 14.4 %collective-permute-start.20 = (bf16[512,512]{1,0:T(8,128)(2,1)S(1)}, bf16[512,512]{1,0:T(8,128)(2,1)S(1)}, u32[]{:S(2)}, u32[]{:S(2)}) collective-permute-start(bf16[512,512]{1,0:T(8,128)(2,1)S(1)} %slice_bitcast_fusion.2), channel_id=1, source_target_pairs={{0,8},{2,10},{4,12},{6,14},{8,0},{10,2},{12,4},{14,6},{1,9},{3,11}... | collective-permute-start | bytes 1572872 | tf_op jit(solution)/shard_map/ppermute | solution.py:718
  134.9 5.6 collective-permute-start.23
  135.4 5.3 collective-permute-start.22
  135.5 25.9 %collective-permute-start.24 = (bf16[2,512,512]{2,1,0:T(8,128)(2,1)}, bf16[2,512,512]{2,1,0:T(8,128)(2,1)}, u32[]{:S(2)}, u32[]{:S(2)}) collective-permute-start(bf16[2,512,512]{2,1,0:T(8,128)(2,1)} %get-tuple-element.185.refs_3_.refs_0_), channel_id=1, source_target_pairs={{0,4},{2,6},{4,8},{6,10},{8,12},{10,14},{1,5},{3,7},{5,9},{7,11},{... | collective-permute-start | bytes 3145736 | tf_op jit(solution)/shard_map/ppermute | solution.py:723
  162.8 28.9 %collective-permute-start.27 = (bf16[512,1024]{1,0:T(8,128)(2,1)S(1)}, bf16[512,1024]{1,0:T(8,128)(2,1)S(1)}, u32[]{:S(2)}, u32[]{:S(2)}) collective-permute-start(bf16[512,1024]{1,0:T(8,128)(2,1)S(1)} %copy-done.17), channel_id=1, source_target_pairs={{0,1},{1,0},{2,3},{3,2},{4,5},{5,4},{6,7},{7,6},{8,9},{9,8},{10,11... | collective-permute-start | bytes 3145736 | tf_op jit(solution)/shard_map/ppermute | solution.py:718
  188.6 24.0 %collective-permute-start.26 = (bf16[512,1024]{1,0:T(8,128)(2,1)}, bf16[512,1024]{1,0:T(8,128)(2,1)S(1)}, u32[]{:S(2)}, u32[]{:S(2)}) collective-permute-start(bf16[512,1024]{1,0:T(8,128)(2,1)} %get-tuple-element.189.own_ref), channel_id=1, source_target_pairs={{0,1},{1,0},{2,3},{3,2},{4,5},{5,4},{6,7},{7,6},{8,9},{9,8},{10,11... | collective-permute-start | bytes 3145736 | tf_op jit(solution)/shard_map/ppermute | solution.py:718
  211.0 43.4 %collective-permute-start.29 = (bf16[512,1024]{1,0:T(8,128)(2,1)}, bf16[512,1024]{1,0:T(8,128)(2,1)S(1)}, u32[]{:S(2)}, u32[]{:S(2)}) collective-permute-start(bf16[512,1024]{1,0:T(8,128)(2,1)} %get-tuple-element.191.own_ref), channel_id=1, source_target_pairs={{0,1},{1,0},{2,3},{3,2},{4,5},{5,4},{6,7},{7,6},{8,9},{9,8},{10,11... | collective-permute-start | bytes 3145736 | tf_op jit(solution)/shard_map/ppermute | solution.py:718
  232.4 36.6 %collective-permute-start.28 = (bf16[512,1024]{1,0:T(8,128)(2,1)}, bf16[512,1024]{1,0:T(8,128)(2,1)S(1)}, u32[]{:S(2)}, u32[]{:S(2)}) collective-permute-start(bf16[512,1024]{1,0:T(8,128)(2,1)} %get-tuple-element.197.own_ref), channel_id=1, source_target_pairs={{0,1},{1,0},{2,3},{3,2},{4,5},{5,4},{6,7},{7,6},{8,9},{9,8},{10,11... | collective-permute-start | bytes 3145736 | tf_op jit(solution)/shard_map/ppermute | solution.py:718
  293.2 27.1 %collective-permute-start.30 = (bf16[2,512,512]{2,1,0:T(8,128)(2,1)}, bf16[2,512,512]{2,1,0:T(8,128)(2,1)S(1)}, u32[]{:S(2)}, u32[]{:S(2)}) collective-permute-start(bf16[2,512,512]{2,1,0:T(8,128)(2,1)} %get-tuple-element.222), channel_id=1, source_target_pairs={{0,2},{2,0},{4,6},{6,4},{8,10},{10,8},{12,14},{14,12},{1,3},{3,1},... | collective-permute-start | bytes 3145736 | tf_op jit(solution)/shard_map/ppermute | solution.py:718
  318.2 17.2 %collective-permute-start.33 = (bf16[2,512,512]{2,1,0:T(8,128)(2,1)}, bf16[2,512,512]{2,1,0:T(8,128)(2,1)S(1)}, u32[]{:S(2)}, u32[]{:S(2)}) collective-permute-start(bf16[2,512,512]{2,1,0:T(8,128)(2,1)} %get-tuple-element.231), channel_id=1, source_target_pairs={{0,2},{2,0},{4,6},{6,4},{8,10},{10,8},{12,14},{14,12},{1,3},{3,1},... | collective-permute-start | bytes 3145736 | tf_op jit(solution)/shard_map/ppermute | solution.py:718
  318.2 68.7 %collective-permute-start.32 = (bf16[512,1024]{1,0:T(8,128)(2,1)S(1)}, bf16[512,1024]{1,0:T(8,128)(2,1)}, u32[]{:S(2)}, u32[]{:S(2)}) collective-permute-start(bf16[512,1024]{1,0:T(8,128)(2,1)S(1)} %copy-done.24), channel_id=1, source_target_pairs={{0,1},{1,0},{2,3},{3,2},{4,5},{5,4},{6,7},{7,6},{8,9},{9,8},{10,11... | collective-permute-start | bytes 3145736 | tf_op jit(solution)/shard_map/ppermute | solution.py:718
  318.6 75.2 %collective-permute-start.31 = (bf16[512,1024]{1,0:T(8,128)(2,1)S(1)}, bf16[512,1024]{1,0:T(8,128)(2,1)S(1)}, u32[]{:S(2)}, u32[]{:S(2)}) collective-permute-start(bf16[512,1024]{1,0:T(8,128)(2,1)S(1)} %copy-done.22), channel_id=1, source_target_pairs={{0,1},{1,0},{2,3},{3,2},{4,5},{5,4},{6,7},{7,6},{8,9},{9,8},{10,11... | collective-permute-start | bytes 3145736 | tf_op jit(solution)/shard_map/ppermute | solution.py:718
  321.6 72.2 %collective-permute-start.34 = (bf16[2,512,512]{2,1,0:T(8,128)(2,1)S(1)}, bf16[2,512,512]{2,1,0:T(8,128)(2,1)S(1)}, u32[]{:S(2)}, u32[]{:S(2)}) collective-permute-start(bf16[2,512,512]{2,1,0:T(8,128)(2,1)S(1)} %add_convert_fusion.2), channel_id=1, source_target_pairs={{4,0},{6,2},{8,4},{10,6},{12,8},{14,10},{5,1},{7,3},{9,5},{11,7},{... | collective-permute-start | bytes 3145736 | tf_op jit(solution)/shard_map/ppermute | solution.py:723
  336.8 98.9 %collective-permute-start.38 = (bf16[512,512]{1,0:T(8,128)(2,1)}, bf16[512,512]{1,0:T(8,128)(2,1)S(1)}, u32[]{:S(2)}, u32[]{:S(2)}) collective-permute-start(bf16[512,512]{1,0:T(8,128)(2,1)} %get-tuple-element.309), channel_id=1, source_target_pairs={{0,8},{2,10},{4,12},{6,14},{8,0},{10,2},{12,4},{14,6},{1,9},{3,11}... | collective-permute-start | bytes 1572872 | tf_op jit(solution)/shard_map/ppermute | solution.py:718
  370.8 65.0 %collective-permute-start.37 = (bf16[512,512]{1,0:T(8,128)(2,1)}, bf16[512,512]{1,0:T(8,128)(2,1)}, u32[]{:S(2)}, u32[]{:S(2)}) collective-permute-start(bf16[512,512]{1,0:T(8,128)(2,1)} %get-tuple-element.310), channel_id=1, source_target_pairs={{0,4},{2,6},{4,0},{6,2},{8,12},{10,14},{12,8},{14,10},{1,5},{3,7},... | collective-permute-start | bytes 1572872 | tf_op jit(solution)/shard_map/ppermute | solution.py:718
  420.0 16.0 %collective-permute-start.36 = (bf16[2,512,512]{2,1,0:T(8,128)(2,1)}, bf16[2,512,512]{2,1,0:T(8,128)(2,1)S(1)}, u32[]{:S(2)}, u32[]{:S(2)}) collective-permute-start(bf16[2,512,512]{2,1,0:T(8,128)(2,1)} %get-tuple-element.248), channel_id=1, source_target_pairs={{0,2},{2,0},{4,6},{6,4},{8,10},{10,8},{12,14},{14,12},{1,3},{3,1},... | collective-permute-start | bytes 3145736 | tf_op jit(solution)/shard_map/ppermute | solution.py:718
  420.2 15.7 %collective-permute-start.35 = (bf16[2,512,512]{2,1,0:T(8,128)(2,1)}, bf16[2,512,512]{2,1,0:T(8,128)(2,1)S(1)}, u32[]{:S(2)}, u32[]{:S(2)}) collective-permute-start(bf16[2,512,512]{2,1,0:T(8,128)(2,1)} %get-tuple-element.245), channel_id=1, source_target_pairs={{0,2},{2,0},{4,6},{6,4},{8,10},{10,8},{12,14},{14,12},{1,3},{3,1},... | collective-permute-start | bytes 3145736 | tf_op jit(solution)/shard_map/ppermute | solution.py:718
  435.7 56.8 %collective-permute-start.39 = (bf16[2,512,512]{2,1,0:T(8,128)(2,1)}, bf16[2,512,512]{2,1,0:T(8,128)(2,1)S(1)}, u32[]{:S(2)}, u32[]{:S(2)}) collective-permute-start(bf16[2,512,512]{2,1,0:T(8,128)(2,1)} %get-tuple-element.263), channel_id=1, source_target_pairs={{0,2},{2,0},{4,6},{6,4},{8,10},{10,8},{12,14},{14,12},{1,3},{3,1},... | collective-permute-start | bytes 3145736 | tf_op jit(solution)/shard_map/ppermute | solution.py:718
  441.2 51.3 %collective-permute-start.40 = (bf16[2,512,512]{2,1,0:T(8,128)(2,1)}, bf16[2,512,512]{2,1,0:T(8,128)(2,1)S(1)}, u32[]{:S(2)}, u32[]{:S(2)}) collective-permute-start(bf16[2,512,512]{2,1,0:T(8,128)(2,1)} %get-tuple-element.252), channel_id=1, source_target_pairs={{0,4},{2,6},{4,0},{6,2},{8,12},{10,14},{12,8},{14,10},{1,5},{3,7},... | collective-permute-start | bytes 3145736 | tf_op jit(solution)/shard_map/ppermute | solution.py:718
  441.2 51.3 %collective-permute-start.41 = (bf16[2,512,512]{2,1,0:T(8,128)(2,1)}, bf16[2,512,512]{2,1,0:T(8,128)(2,1)S(1)}, u32[]{:S(2)}, u32[]{:S(2)}) collective-permute-start(bf16[2,512,512]{2,1,0:T(8,128)(2,1)} %get-tuple-element.264), channel_id=1, source_target_pairs={{0,8},{2,10},{4,12},{6,14},{8,0},{10,2},{12,4},{14,6},{1,9},{3,11}... | collective-permute-start | bytes 3145736 | tf_op jit(solution)/shard_map/ppermute | solution.py:718
  491.7 25.3 %collective-permute-start.43 = (bf16[512,1024]{1,0:T(8,128)(2,1)}, bf16[512,1024]{1,0:T(8,128)(2,1)}, u32[]{:S(2)}, u32[]{:S(2)}) collective-permute-start(bf16[512,1024]{1,0:T(8,128)(2,1)} %get-tuple-element.260.own_ref), channel_id=1, source_target_pairs={{0,1},{1,0},{2,3},{3,2},{4,5},{5,4},{6,7},{7,6},{8,9},{9,8},{10,11... | collective-permute-start | bytes 3145736 | tf_op jit(solution)/shard_map/ppermute | solution.py:718
  513.7 9.7 %collective-permute-start.42 = (bf16[512,2048]{1,0:T(8,128)(2,1)}, bf16[512,2048]{1,0:T(8,128)(2,1)}, u32[]{:S(2)}, u32[]{:S(2)}) collective-permute-start(bf16[512,2048]{1,0:T(8,128)(2,1)} %get-tuple-element.270), channel_id=1, source_target_pairs={{0,2},{2,0},{4,6},{6,4},{8,10},{10,8},{12,14},{14,12},{1,3},{3,1},... | collective-permute-start | bytes 6291464 | tf_op jit(solution)/shard_map/ppermute | solution.py:718
  525.9 7.3 %collective-permute-start.44 = (bf16[128,1024]{1,0:T(8,128)(2,1)S(1)}, bf16[128,1024]{1,0:T(8,128)(2,1)S(1)}, u32[]{:S(2)}, u32[]{:S(2)}) collective-permute-start(bf16[128,1024]{1,0:T(8,128)(2,1)S(1)} %get-tuple-element.307), channel_id=1, source_target_pairs={{0,8},{2,10},{4,12},{6,14},{8,0},{10,2},{12,4},{14,6},{1,9},{3,11}... | collective-permute-start | bytes 786440 | tf_op jit(solution)/shard_map/ppermute | solution.py:718
  526.4 7.4 %collective-permute-start.45 = (bf16[128,1024]{1,0:T(8,128)(2,1)S(1)}, bf16[128,1024]{1,0:T(8,128)(2,1)S(1)}, u32[]{:S(2)}, u32[]{:S(2)}) collective-permute-start(bf16[128,1024]{1,0:T(8,128)(2,1)S(1)} %get-tuple-element.305), channel_id=1, source_target_pairs={{0,4},{2,6},{4,0},{6,2},{8,12},{10,14},{12,8},{14,10},{1,5},{3,7},... | collective-permute-start | bytes 786440 | tf_op jit(solution)/shard_map/ppermute | solution.py:718
  527.8 24.1 %collective-permute-start.46 = (bf16[512,1024]{1,0:T(8,128)(2,1)S(1)}, bf16[512,1024]{1,0:T(8,128)(2,1)S(1)}, u32[]{:S(2)}, u32[]{:S(2)}) collective-permute-start(bf16[512,1024]{1,0:T(8,128)(2,1)S(1)} %copy-done.25), channel_id=1, source_target_pairs={{0,1},{1,0},{2,3},{3,2},{4,5},{5,4},{6,7},{7,6},{8,9},{9,8},{10,11... | collective-permute-start | bytes 3145736 | tf_op jit(solution)/shard_map/ppermute | solution.py:718
  534.0 12.2 %collective-permute-start.47 = (bf16[128,2048]{1,0:T(8,128)(2,1)S(1)}, bf16[128,2048]{1,0:T(8,128)(2,1)S(1)}, u32[]{:S(2)}, u32[]{:S(2)}) collective-permute-start(bf16[128,2048]{1,0:T(8,128)(2,1)S(1)} %pad_maximum_fusion.3), channel_id=1, source_target_pairs={{0,4},{2,6},{4,0},{6,2},{8,12},{10,14},{12,8},{14,10},{1,5},{3,7},... | collective-permute-start | bytes 1572872 | tf_op jit(solution)/shard_map/ppermute | solution.py:718
  534.5 12.1 %collective-permute-start.48 = (bf16[128,2048]{1,0:T(8,128)(2,1)S(1)}, bf16[128,2048]{1,0:T(8,128)(2,1)S(1)}, u32[]{:S(2)}, u32[]{:S(2)}) collective-permute-start(bf16[128,2048]{1,0:T(8,128)(2,1)S(1)} %pad_maximum_fusion.4), channel_id=1, source_target_pairs={{0,8},{2,10},{4,12},{6,14},{8,0},{10,2},{12,4},{14,6},{1,9},{3,11}... | collective-permute-start | bytes 1572872 | tf_op jit(solution)/shard_map/ppermute | solution.py:718
  536.3 21.3 %collective-permute-start.49 = (f32[1,256]{1,0:T(1,128)S(1)}, f32[1,256]{1,0:T(1,128)S(1)}, u32[]{:S(2)}, u32[]{:S(2)}) collective-permute-start(f32[1,256]{1,0:T(1,128)S(1)} %pad_maximum_fusion.8), channel_id=1, source_target_pairs={{0,1},{1,0},{2,3},{3,2},{4,5},{5,4},{6,7},{7,6},{8,9},{9,8},{10,11... | collective-permute-start | bytes 3080 | tf_op jit(solution)/shard_map/ppermute | solution.py:718
  566.4 7.6 %collective-permute-start.53 = (f32[1,2304]{1,0:T(1,128)S(1)}, f32[1,2304]{1,0:T(1,128)S(1)}, u32[]{:S(2)}, u32[]{:S(2)}) collective-permute-start(f32[1,2304]{1,0:T(1,128)S(1)} %add.148), channel_id=1, source_target_pairs={{0,16},{16,0},{1,17},{17,1},{2,18},{18,2},{3,19},{19,3},{4,20},{20... | collective-permute-start | bytes 27656 | tf_op jit(solution)/shard_map/ppermute | solution.py:718
  566.5 12.9 %collective-permute-start.54 = (bf16[64,2048]{1,0:T(8,128)(2,1)S(1)}, bf16[64,2048]{1,0:T(8,128)(2,1)S(1)}, u32[]{:S(2)}, u32[]{:S(2)}) collective-permute-start(bf16[64,2048]{1,0:T(8,128)(2,1)S(1)} %slice.145), channel_id=1, source_target_pairs={{0,16},{16,0},{1,17},{17,1},{2,18},{18,2},{3,19},{19,3},{4,20},{20... | collective-permute-start | bytes 786440 | tf_op jit(solution)/shard_map/ppermute | solution.py:718
  (57 other events, 443.6 us)
Sparse Core Ops, SparseCore 0:
  10.3 109.6 all-gather.1
  283.2 180.8 reduce-scatter.1

commit v2 on v1

--- a/solution.py
+++ b/solution.py
@@ -133,11 +133,10 @@
     halo_refs = [refs.pop(0) for _ in halos]
     prior = [refs.pop(0) for _ in range(2 * len(halves))] if plan["carry"] else None
     if plan["last"]:
-        w_ref = refs.pop(0)
         if plan["alias"]:
             refs.pop(0)
-        out_ref, lse_ref, part_ref = refs[:3]
-        refs = refs[3:]
+        out_ref, lse_ref = refs[:2]
+        refs = refs[2:]
     else:
         results, refs = refs[: 2 * len(halves)], refs[2 * len(halves) :]
     me, lo_first = idx_ref[0], idx_ref[1]
@@ -201,32 +200,18 @@
                 results[2 * n][:, cols] = acc[at, :]
                 results[2 * n + 1][:, cols] = tot[at, :]
     if plan["last"]:
-        qs, acc, tot, part_acc = refs
-        step, steps = pl.program_id(0), pl.num_programs(0)
+        qs, acc, tot = refs
         for g in range(2):
             cols, at = slice(g * HEAD_SIZE, (g + 1) * HEAD_SIZE), slice(g * rows, (g + 1) * rows)
             total = jnp.sum(tot[at, :], axis=1, keepdims=True)
             out_ref[:, cols] = (acc[at, :] / total).astype(BF)
             lse_ref[0, g : g + 1, :] = jnp.log2(jnp.sum(tot[at, :].T, axis=0, keepdims=True))
-        part = mm(out_ref[...], w_ref[...], NT)
-
-        @pl.when(step == 0)
-        def _():
-            part_acc[...] = part
-
-        @pl.when((step > 0) & (step < steps - 1))
-        def _():
-            part_acc[...] += part
-
-        @pl.when(step == steps - 1)
-        def _():
-            part_ref[...] = (part_acc[...] + part).astype(BF)
 
 
 def attention_forward(halves, scalars, q, low, slots, halos, carry=None, last=None):
     rows, heads = q.shape[0] // 2, q.shape[1] // 256
     plan = dict(halves=halves, slots=list(slots), halos=list(halos), carry=carry is not None,
-                last=last is not None, alias=last is not None and last[1] is not None)
+                last=last is not None, alias=last is not None and last[0] is not None)
     part = lambda h, i: (0, h)
     ins = [(low, (rows, 128), lambda h, i: (0, 0))]
     ins += [(q, (rows, 256), lambda h, i, half=half: (half, h)) for half in halves]
@@ -241,9 +226,7 @@
     if last is None:
         outs = [(state, (rows, 256), part)] * (2 * len(halves))
     else:
-        w_rest, other = last
-        model = w_rest.shape[0]
-        ins.append((w_rest, (model, 256), part))
+        other = last[0]
         if other is not None:
             keep = {len(ins): 0}
             ins.append((other, None, None))
@@ -251,11 +234,21 @@
         outs = [
             (shaped((2 * rows, heads * 256), BF), (rows, 256), lambda h, i: (half, h)),
             (shaped((heads, 8, rows), F32), (1, 8, rows), lambda h, i: (h, 0, 0)),
-            (shaped((rows, model), BF), (rows, model), lambda h, i: (0, 0)),
         ]
-        scratch.append(pltpu.VMEM((rows, model), F32))
     return call(functools.partial(fwd_kernel, plan), "attend", (heads,), ins, outs, scratch,
                 scalars=scalars, keep=keep)
+
+
+def out_kernel(att_ref, w_ref, part_ref):
+    part_ref[...] = mm(att_ref[...], w_ref[...], NT).astype(BF)
+
+
+def out_projection(half, attended, w_rest):
+    rows, cols = attended.shape[0] // 2, attended.shape[1]
+    model = w_rest.shape[0]
+    ins = [(attended, (rows, cols), lambda j: (half, 0)), (w_rest, (model // 2, cols), lambda j: (j, 0))]
+    outs = [(shaped((rows, model), BF), (rows, model // 2), lambda j: (0, j))]
+    return call(out_kernel, "out_projection", (2,), ins, outs)[0]
 
 
 def bwd_kernel(plan, idx_ref, q_ref, do_ref, lse_ref, delta_ref, lo_ref, *refs):
@@ -548,26 +541,21 @@
     return call(weight_kernel, "weight_grad", (n // cols,), ins, outs, keep=keep)[0]
 
 
-def qkv_weight_kernel(left_ref, q_ref, kv_ref, high_ref, low_ref):
+def weight_halves_kernel(left_ref, right_ref, high_ref, low_ref):
     for half, out_ref in enumerate((high_ref, low_ref)):
-        for which, right_ref in enumerate((q_ref, kv_ref)):
-
-            @pl.when((pl.program_id(0) == half) & (pl.program_id(1) == which))
-            def _(out_ref=out_ref, right_ref=right_ref):
-                out_ref[...] = mm(left_ref[...], right_ref[...], TN).astype(BF)
-
-
-def qkv_weight_grad(left, d_q, d_kv):
+
+        @pl.when(pl.program_id(0) == half)
+        def _(out_ref=out_ref):
+            out_ref[...] = mm(left_ref[...], right_ref[...], TN).astype(BF)
+
+
+def weight_halves(left, right):
     tokens, model = left.shape
-    cols = d_q.shape[1]
-    ins = [
-        (left, (tokens, model // 2), lambda i, j: (0, 1 - i)),
-        (d_q, (tokens, cols), lambda i, j: (0, 0)),
-        (d_kv, (tokens, cols), lambda i, j: (0, 0)),
-    ]
-    half, block = shaped((model // 2, 2 * cols), BF), (model // 2, cols)
-    outs = [(half, block, lambda i, j: (0, jnp.where(i == 0, j, 1))), (half, block, lambda i, j: (0, i * j))]
-    return call(qkv_weight_kernel, "qkv_weight_grad", (2, 2), ins, outs)
+    cols = right.shape[1]
+    once = lambda i: (0, 0)
+    ins = [(left, (tokens, model // 2), lambda i: (0, 1 - i)), (right, (tokens, cols), once)]
+    half = shaped((model // 2, cols), BF)
+    return call(weight_halves_kernel, "weight_halves", (2,), ins, [(half, half.shape, once)] * 2)
 
 
 def q_back_kernel(heads, dq_ref, lin_ref, gain_ref, cos_ref, sin_ref, w_ref, *refs):
@@ -653,7 +641,7 @@
         (shaped((1, HEAD_SIZE), F32), (1, HEAD_SIZE), once),
     ]
     kernel = functools.partial(kv_back_kernel, cols // HEAD_SIZE, len(keys), len(values))
-    return call(kernel, "kv_back", (steps,), ins, outs, keep=keep)
+    return call(kernel, "kv_back", (steps,), ins, outs, keep=keep, us=3 * (1 - half))
 
 
 def tokens_kernel(own_ref, got_ref, x_ref, gain_ref, d_resid_ref, *refs):
@@ -675,7 +663,7 @@
         keep = {len(ins): 0}
         ins.append((whole, None, None))
     outs = [(shaped((2 * rows, model), BF), block, mine), (shaped((1, model), F32), (1, model), once)]
-    return call(tokens_kernel, "tokens_back", (steps,), ins, outs, keep=keep, us=20 * half)
+    return call(tokens_kernel, "tokens_back", (steps,), ins, outs, keep=keep, us=20)
 
 
 def share_kernel(chunk, share_ref, out_ref, gate_ref, up_ref, down_ref):
@@ -785,19 +773,21 @@
     heads, kv_heads = q_cols // HEAD_SIZE, k_cols // HEAD_SIZE
     chunk = math.gcd(units, 512)
 
-    def gather_rows(piece, gates=((),) * 4):
+    def gather_first(piece, *gate):
+        return jnp.concatenate([piece, after(swap(piece, "shard", 1), *gate)]) if ctx_size == 8 else piece
+
+    def gather_rows(one, gates=((),) * 3):
         if ctx_size != 8:
             for axis, bit in bits:
-                piece = jnp.concatenate([piece, swap(piece, axis, bit)])
-            return piece, (piece,) * 4
-        one = jnp.concatenate([piece, after(swap(piece, "shard", 1), *gates[0])])
-        by_x, by_y = (after(v, *gates[1]) for v in (swap(one, "ctx", 2), swap(one, "ctx", 4)))
+                one = jnp.concatenate([one, swap(one, axis, bit)])
+            return one, (one,) * 3
+        by_x, by_y = (after(v, *gates[0]) for v in (swap(one, "ctx", 2), swap(one, "ctx", 4)))
         cut = one.shape[1] // 2
         left, right = swap(by_y[:, :cut], "ctx", 2), swap(by_x[:, cut:], "ctx", 4)
-        far = jnp.concatenate([after(left, *gates[2]), after(right, *gates[2])], axis=1)
+        far = jnp.concatenate([after(left, *gates[1]), after(right, *gates[1])], axis=1)
         half = jnp.concatenate([one, by_x, by_y, far])
-        whole = jnp.concatenate([half, after(swap(half, "ctx", 1), *gates[3])])
-        return whole, (one, by_x, half, whole)
+        whole = jnp.concatenate([half, after(swap(half, "ctx", 1), *gates[2])])
+        return whole, (by_x, half, whole)
 
     def scatter_rows(low, high, late):
         total = add_low(low, after(swap(high, "ctx", 1), late))
@@ -829,13 +819,15 @@
         return total, swap(total[size:], "shard", 1)
 
     kv_piece, rest_piece = pack(chunk, key_weight, value_weight, w_out.T, w_gate, w_up, w_down.T)
-    w_kv, stages = gather_rows(kv_piece)
+    kv_one = gather_first(kv_piece)
+    w_kv, stages = gather_rows(kv_one)
+    q_one = gather_first(after(w_query, kv_one), stages[1])
     w_rest = lax.all_gather(rest_piece, weight_axes, axis=0, tiled=True)
     gains = jnp.concatenate([attn_gain, ffn_gain, query_gain, key_gain])[None]
     gains = jnp.where(jnp.arange(parts)[:, None] == part, gains, jnp.zeros((), BF))
     gains = gains + after(swap(gains, "ctx", 1), kv_piece)
     for at, (axis, bit) in enumerate(bits[:-1]):
-        gains = gains + after(swap(gains, axis, bit), stages[min(at, 2)])
+        gains = gains + after(swap(gains, axis, bit), (kv_one, *stages)[min(at, 2)])
     gains = gains.astype(F32)
     gain_one = gains[:, :wide].reshape(1, -1)
     gain_two = gains[:, wide : 2 * wide].reshape(1, -1)
@@ -843,7 +835,7 @@
     gain_k = gains[:, 2 * wide + narrow :].reshape(1, -1)
     source = jnp.bitwise_xor(part, jnp.array(order, jnp.int32))[:, None] * wide + jnp.arange(wide, dtype=jnp.int32)
     to_slots = (jnp.arange(model, dtype=jnp.int32)[:, None] == source.reshape(1, -1)).astype(BF)
-    tokens_s = mm(after(tokens, stages[0]), to_slots).astype(BF)
+    tokens_s = mm(after(tokens, q_one), to_slots).astype(BF)
     gain_one_s = mm(gain_one.astype(BF), to_slots)
 
     cont_at = me * rows + jnp.arange(rows, dtype=jnp.int32)
@@ -880,7 +872,7 @@
 
     normed, kv_p, k_lin_p = keys_values(0, gain_one_s)
     normed, kv_c, k_lin_c = keys_values(1, after(gain_one_s, kv_p), normed)
-    w_q, _ = gather_rows(after(w_query, stages[0]), ((stages[1],), (kv_p,), (kv_p,), (kv_c,)))
+    w_q, _ = gather_rows(q_one, ((w_kv,), (kv_p,), (kv_c,)))
     mine = lambda f: (f, 0)
     q, q_lin = call(
         functools.partial(q_kernel, heads), "queries", (2,),
@@ -921,16 +913,18 @@
         slots[6] = jnp.stack([after(far_k, c_state[0]), after(far_v, c_state[0])])
         slots[7] = swap(slots[6], "ctx", 1)
         ready = (slots[7],)
-    attended, lse_p, part_p = attention_forward(
-        (0,), after(scalars, c_state[0], *ready), q, low_col, slots, {}, None, (w_rest, None)
-    )
+    attended, lse_p = attention_forward(
+        (0,), after(scalars, c_state[0], *ready), q, low_col, slots, {}, None, (None,)
+    )
+    part_p = out_projection(0, attended, w_rest)
     got_p = swap(part_p, "tensor", 1)
     if ctx_size == 8:
         halos[1] = swap(jnp.where(odd, after(halos[2], part_p), kv_c), "ctx", 1)
-    attended, lse_c, part_c = attention_forward(
+    attended, lse_c = attention_forward(
         (1,), after(scalars, part_p), q, low_col, pick(slots, middle + far), pick(halos, range(1, n_halo)),
-        c_state, (w_rest, attended),
-    )
+        c_state, (attended,),
+    )
+    part_c = out_projection(1, attended, w_rest)
     got_c = swap(part_c, "tensor", 1)
 
     resid_p, *whole, out_p, back_p = feed_forward(
@@ -977,17 +971,18 @@
         near_one = after(near_one, dq_c)
         two_back = add_low(g_halo[2], jnp.where(odd, near_one, zero))
         halo_two = shift(two_back, -2)
-        ready = (two_back,)
+        halo_near = jnp.where(odd, zero, near_one)
+        ready = (two_back, halo_near)
     dq, prior, _ = back_rows(0, (dq_c, *ready), pick(slots, near + middle), {}, dq_p, None, None, True)
     if ctx_size == 8:
         g6 = add_low(g[6], after(got7, dq))
         far_k, far_v = swap(g6[0], "ctx", 2), swap(g6[1], "ctx", 4)
         ready = (g6, halo_two)
-    dq_c, more, _ = back_rows(1, (dq, out_got_p, out_got_c, *ready), pick(slots, middle), {}, dq_c, prior)
+    dq_c, more, _ = back_rows(1, (dq, *ready), pick(slots, middle), {}, dq_c, prior)
     g.update(more)
     if ctx_size == 8:
         got3, got5 = swap(g[3], "ctx", 1), swap(g[5], "ctx", 1)
-    dq, more, _ = back_rows(1, (dq_c,), pick(slots, near), {}, dq_c, prior, dq, True)
+    dq, more, _ = back_rows(1, (dq_c, out_got_p, out_got_c), pick(slots, near), {}, dq_c, prior, dq, True)
     g.update(more)
     if ctx_size == 8:
         got1 = swap(g[1], "ctx", 1)
@@ -995,7 +990,7 @@
         to_x, to_y = merge(g[2], got3, g[4], got5, far_k, far_v)
         ready = (to_x,)
         keys_p = values_p = [g[0], got1, swap(to_x, "ctx", 2), swap(to_y, "ctx", 4)]
-        keys_c = values_c = [g_halo[0], jnp.where(odd, zero, near_one), halo_two]
+        keys_c = values_c = [g_halo[0], halo_near, halo_two]
     else:
         both = jnp.stack([g[s] for s in range(ctx_size)])
         while both.shape[0] > 1:
@@ -1009,27 +1004,32 @@
         1, keys_c, values_c, k_lin_c, after(gain_k, q_part), cos, sin, w_kv, to_slots, q_part
     )
     into_got_c = swap(into_c, "tensor", 1)
+    q_high, q_low = weight_halves(normed, after(d_q, into_c))
     d_kv, into_p, k_heads_p = kv_back(
-        0, keys_p, values_p, k_lin_p, after(gain_k, into_c), cos, sin, w_kv, to_slots, q_part, d_kv
+        0, keys_p, values_p, k_lin_p, after(gain_k, q_low), cos, sin, w_kv, to_slots, q_part, d_kv
     )
     into_got_p = swap(into_p, "tensor", 1)
-    high, low = qkv_weight_grad(normed, after(d_q, into_p), d_kv)
+    q_grad = scatter_rows(q_low, q_high, into_p)
+    kv_high, kv_low = weight_halves(normed, after(d_kv, q_grad[0]))
+    q_grad = scatter_more(q_grad, kv_low)
     heads = jnp.concatenate([q_heads, k_heads_c + k_heads_p], axis=1)
     heads_got = swap(heads, "tensor", 1)
-    grad_tokens, d_one_c = tokens_back(1, into_c, into_got_c, tokens, after(gain_one, low), d_resid_c)
+    grad_tokens, d_one_c = tokens_back(1, into_c, into_got_c, tokens, after(gain_one, kv_low, q_grad[0]), d_resid_c)
     out_share, gate_share, up_share, down_share = unpack(chunk, o_cols, after(rest_share, d_one_c))
-    qkv_grad = scatter_rows(low, high, gate_share)
-    layer_out = add_layer(0, after(resid_p, qkv_grad[0]), out_p, out_got_p)
-    qkv_grad = scatter_more(qkv_grad, layer_out)
-    layer_out = add_layer(1, after(resid_c, qkv_grad[0]), out_c, out_got_c, layer_out)
-    qkv_grad = scatter_sum(qkv_grad, layer_out)
+    q_grad = scatter_sum(q_grad, gate_share)
+    kv_grad = scatter_rows(kv_low, kv_high, gate_share)
+    layer_out = add_layer(0, after(resid_p, kv_grad[0], q_grad[0]), out_p, out_got_p)
+    kv_grad = scatter_more(kv_grad, layer_out)
+    layer_out = add_layer(1, after(resid_c, kv_grad[0]), out_c, out_got_c, layer_out)
+    q_share = add_low(q_grad[0][:wide], after(q_grad[1], layer_out)).astype(F32)
+    kv_grad = scatter_sum(kv_grad, layer_out)
     grad_tokens, d_one_p = tokens_back(
-        0, into_p, into_got_p, tokens, after(gain_one, qkv_grad[0]), d_resid_p, grad_tokens
+        0, into_p, into_got_p, tokens, after(gain_one, kv_grad[0], q_share), d_resid_p, grad_tokens
     )
     heads = heads + after(heads_got, d_one_p)
     late = jnp.concatenate([d_one_c + d_one_p, heads, d_two_c + d_two_p], axis=1)
-    late = butterfly(late, ("ctx", "shard"))
-    qkv_share = add_low(qkv_grad[0][:wide], after(qkv_grad[1], d_one_p)).astype(F32)
+    kv_share = add_low(kv_grad[0][:wide], after(kv_grad[1], d_one_p)).astype(F32)
+    late = butterfly(late, ("ctx", "shard"), (d_one_p, kv_share))
 
     def own_gain(value, size):
         return lax.dynamic_index_in_dim(value.reshape(parts, size), part, 0, keepdims=False)
@@ -1041,9 +1041,9 @@
         own_gain(late[:, model + 2 * HEAD_SIZE :], wide),
         own_gain(late[:, model : model + HEAD_SIZE], narrow),
         own_gain(late[:, model + HEAD_SIZE : model + 2 * HEAD_SIZE], narrow),
-        qkv_share[:, :q_cols],
-        qkv_share[:, q_cols : q_cols + k_cols],
-        qkv_share[:, q_cols + k_cols :],
+        q_share,
+        kv_share[:, :k_cols],
+        kv_share[:, k_cols:],
         out_share.T,
         gate_share,
         up_share,

time: 597 us -> 576 us (0.965)
  waiting for transfers between devices: 92.2 us -> 63.1 us
  starting transfers between devices: 127 us -> 137 us
  local copies, waits for them, and re-layouts: 36.8 us -> 29.8 us
    ppermute x53 -> x59, waiting for transfers between devices: 82.3 us -> 55.6 us  [swap(): return lax.ppermute(value, axis, [(i, i ^ bit) for i in range(size)])]
    ppermute x53 -> x59, starting transfers between devices: 122 us -> 132 us  [swap(): return lax.ppermute(value, axis, [(i, i ^ bit) for i in range(size)])]
    pallas_call x30 -> x33, Pallas kernels: 294 us -> 299 us  [call(): pl.pallas_call(kernel, grid_spec=pltpu.PrefetchScalarGridSpec(num_scalar_...]
    unnamed x104 -> x90, local copies, waits for them, and re-layouts: 21.1 us -> 16.6 us
  transfers between devices with their start and end apart: 57 -> 63, of which waited for: 27 -> 16; matrix products, arithmetic and copies ran while one was open for 7% -> 7% of each run, Pallas kernels for 47% -> 50%
where the time goes in v2:
time: 576 us; the launch traced here: 568 us
  Pallas kernels  299 us (52%)
  starting transfers between devices  137 us (24%)
  waiting for transfers between devices  63.1 us (11%)
  local copies, waits for them, and re-layouts  29.8 us (5%)
  other arithmetic  17.4 us (3%)
  between operations  15.3 us (3%)
  matrix products  7.12 us (1%)
    pallas_call x33, Pallas kernels, call(): pl.pallas_call(kernel, grid_spec=pltpu.PrefetchScalarGridSpec(num_scalar_...  299 us
    ppermute x59, starting transfers between devices, swap(): return lax.ppermute(value, axis, [(i, i ^ bit) for i in range(size)])  132 us
    ppermute x59, waiting for transfers between devices, swap(): return lax.ppermute(value, axis, [(i, i ^ bit) for i in range(size)])  55.6 us
    unnamed x90, local copies, waits for them, and re-layouts  16.6 us
  transfers between devices with their start and end apart: 63, of which 16 were waited for; matrix products, arithmetic and copies ran while one was open for 7% of the time, Pallas kernels for 50%

profile of v2, /device:TPU:0, one launch (start us, length us, event | category | flops | bytes accessed | tf_op | source)
XLA Modules:
  0.0 568.4 jit_solution(12151378777327542864)
XLA Ops:
  9.5 4.1 collective-permute-start
  29.0 5.6 collective-permute-done.2
  45.2 5.7 %fusion.5.x_ref = bf16[1024,1024]{1,0:T(8,128)(2,1)} fusion(bf16[1024,1024]{1,0:T(8,128)(2,1)} %x_ref.7, s32[1024]{0:T(1024)S(1)} %add.145), kind=kOutput, calls=%fused_computation.10 | convolution fusion | flops 2149580800 | bytes 4198400 | tf_op jit(solution)/shard_map/dot_general | solution.py:33
  52.4 3.7 collective-permute-done.12
  62.2 5.6 keys_values.2
  72.3 5.7 keys_values.3
  80.4 10.5 %queries.1 = (bf16[1024,1024]{1,0:T(8,128)(2,1)}, f32[1024,1024]{1,0:T(8,128)}) custom-call(bf16[1024,1024]{1,0:T(8,128)(2,1)} %get-tuple-element.177.normed_ref.left_ref, bf16[1024,1024]{1,0:T(8,128)(2,1)} %constant_dynamic-update-slice_fusion.15.w_ref, f32[1,128]{1,0:T(1,128)} %reshape.121.hgain_ref.gain_ref, f32[1024,128]{1,0:T(8,128)} %get-tuple-element.368.cos_ref, ...), custom_call_target="tpu_custom_call" | custom-call | tf_op jit(solution)/shard_map/queries/pallas_call | solution.py:46
  90.8 23.5 %collective-permute-done.11.refs_3_.refs_1_.refs_2_.refs_0_ = bf16[2,512,512]{2,1,0:T(8,128)(2,1)S(1)} collective-permute-done((bf16[2,512,512]{2,1,0:T(8,128)(2,1)}, bf16[2,512,512]{2,1,0:T(8,128)(2,1)S(1)}, u32[]{:S(2)}, u32[]{:S(2)}) %collective-permute-start.11) | collective-permute-done | bytes 1048608 | tf_op jit(solution)/shard_map/ppermute | solution.py:706
  122.8 10.8 %attend.3 = (f32[512,1024]{1,0:T(8,128)}, f32[512,1024]{1,0:T(8,128)}) custom-call(s32[2]{0:T(128)} %pad_add_fusion.1.idx_ref, s32[512,128]{1,0:T(8,128)} %broadcast_in_dim.70.lo_ref, bf16[1024,1024]{1,0:T(8,128)(2,1)} %get-tuple-element.184.refs_0_.q_ref, bf16[2,512,512]{2,1,0:T(8,128)(2,1)} %get-tuple-element.174.refs_1_.refs_0_, ...), custom_call_target="tpu_custom_call" | custom-call | tf_op jit(solution)/shard_map/attend/pallas_call | solution.py:46
  134.4 3.3 collective-permute-start.24
  139.8 8.8 %attend.4 = (bf16[1024,1024]{1,0:T(8,128)(2,1)}, f32[4,8,512]{2,1,0:T(8,128)}) custom-call(s32[2]{0:T(128)} %pad_add_fusion.1.idx_ref, s32[512,128]{1,0:T(8,128)} %broadcast_in_dim.70.lo_ref, bf16[1024,1024]{1,0:T(8,128)(2,1)} %get-tuple-element.184.refs_0_.q_ref, bf16[2,512,512]{2,1,0:T(8,128)(2,1)} %get-tuple-element.174.refs_1_.refs_0_, ...), custom_call_target="tpu_custom_call" | custom-call | tf_op jit(solution)/shard_map/attend/pallas_call | solution.py:46
  148.7 3.9 out_projection.2.own_ref
  152.6 7.5 %collective-permute-done.24.refs_7_.refs_1_ = bf16[2,512,512]{2,1,0:T(8,128)(2,1)} collective-permute-done((bf16[2,512,512]{2,1,0:T(8,128)(2,1)}, bf16[2,512,512]{2,1,0:T(8,128)(2,1)}, u32[]{:S(2)}, u32[]{:S(2)}) %collective-permute-start.24) | collective-permute-done | bytes 1048608 | tf_op jit(solution)/shard_map/ppermute | solution.py:711
  165.1 19.9 %attend.5 = (bf16[1024,1024]{1,0:T(8,128)(2,1)}, f32[4,8,512]{2,1,0:T(8,128)}) custom-call(s32[2]{0:T(128)} %pad_add_fusion.1.idx_ref, s32[512,128]{1,0:T(8,128)} %broadcast_in_dim.70.lo_ref, bf16[1024,1024]{1,0:T(8,128)(2,1)} %get-tuple-element.184.refs_0_.q_ref, bf16[2,512,512]{2,1,0:T(8,128)(2,1)} %copy-done.3, ...), custom_call_target="tpu_custom_call", output_to_operand_aliasing={{0}: (13, {})} | custom-call | tf_op jit(solution)/shard_map/attend/pallas_call | solution.py:46
  185.0 4.1 out_projection.3.own_ref
  192.7 18.3 %feed_forward.2 = (f32[512,1024]{1,0:T(8,128)}, bf16[1024,1024]{1,0:T(8,128)(2,1)}, bf16[1024,1536]{1,0:T(8,128)(2,1)}, bf16[1024,3072]{1,0:T(8,128)(2,1)}, bf16...) custom-call(bf16[1024,1024]{1,0:T(8,128)(2,1)} %x_ref.7, bf16[512,1024]{1,0:T(8,128)(2,1)} %out_projection.2.own_ref, ...), custom_call_target="tpu_custom_call" | custom-call | tf_op jit(solution)/shard_map/feed_forward/pallas_call | solution.py:46
  214.1 18.3 %feed_forward.3 = (f32[512,1024]{1,0:T(8,128)}, bf16[1024,1024]{1,0:T(8,128)(2,1)}, bf16[1024,1536]{1,0:T(8,128)(2,1)}, bf16[1024,3072]{1,0:T(8,128)(2,1)}, bf16...) custom-call(bf16[1024,1024]{1,0:T(8,128)(2,1)} %x_ref.7, ...), custom_call_target="tpu_custom_call", output_to_operand_aliasing={{1}: (7, {}), {2}: (8, {}), {3}: (9, {})} | custom-call | tf_op jit(solution)/shard_map/feed_forward/pallas_call | solution.py:46
  233.8 10.8 %weight_grad.3.refs_0_ = bf16[1024,5632]{1,0:T(8,128)(2,1)} custom-call(bf16[1024,1024]{1,0:T(8,128)(2,1)} %get-tuple-element.210.left_ref, bf16[1024,3072]{1,0:T(8,128)(2,1)} %get-tuple-element.211.right_ref), custom_call_target="tpu_custom_call" | custom-call | tf_op jit(solution)/shard_map/weight_grad/pallas_call | solution.py:46
  244.5 7.4 %weight_grad.4.refs_0_ = bf16[1024,5632]{1,0:T(8,128)(2,1)} custom-call(bf16[1024,1024]{1,0:T(8,128)(2,1)} %dy_ref.7, bf16[1024,1536]{1,0:T(8,128)(2,1)} %get-tuple-element.209.right_ref, bf16[1024,5632]{1,0:T(8,128)(2,1)} %weight_grad.3.refs_0_), custom_call_target="tpu_custom_call", output_to_operand_aliasing={{}: (2, {})} | custom-call | tf_op jit(solution)/shard_map/weight_grad/pallas_call | solution.py:46
  252.9 7.2 %mixed_back.2 = (f32[512,1024]{1,0:T(8,128)}, bf16[1024,1024]{1,0:T(8,128)(2,1)}, bf16[512,1024]{1,0:T(8,128)(2,1)}, f32[4,8,512]{2,1,0:T(8,128)}, f32[1,1024]{1,0:T(1,128)}) custom-call(bf16[512,1024]{1,0:T(8,128)(2,1)} %get-tuple-element.200.own_ref, bf16[512,1024]{1,0:T(8,128)(2,1)} %copy-done.18, f32[512,1024]{1,0:T(8,128)} %get-tuple-element.294.resid_ref, ...), custom_call_target="tpu_custom_call" | custom-call | tf_op jit(solution)/shard_map/mixed_back/pallas_call | solution.py:46
  260.7 5.8 %attend_back.6 = (f32[512,1024]{1,0:T(8,128)}, bf16[2,512,512]{2,1,0:T(8,128)(2,1)}, bf16[2,512,512]{2,1,0:T(8,128)(2,1)}) custom-call(s32[2]{0:T(128)} %pad_add_fusion.1.idx_ref, bf16[1024,1024]{1,0:T(8,128)(2,1)} %get-tuple-element.184.refs_0_.q_ref, bf16[512,1024]{1,0:T(8,128)(2,1)} %get-tuple-element.213.do_ref, ...), custom_call_target="tpu_custom_call" | custom-call | tf_op jit(solution)/shard_map/attend_back/pallas_call | solution.py:46
  267.5 6.9 %mixed_back.3 = (f32[512,1024]{1,0:T(8,128)}, bf16[1024,1024]{1,0:T(8,128)(2,1)}, bf16[512,1024]{1,0:T(8,128)(2,1)}, f32[4,8,512]{2,1,0:T(8,128)}, f32[1,1024]{1,0:T(1,128)}) custom-call(bf16[512,1024]{1,0:T(8,128)(2,1)} %get-tuple-element.207.own_ref, bf16[512,1024]{1,0:T(8,128)(2,1)} %copy-done.15, ...), custom_call_target="tpu_custom_call", output_to_operand_aliasing={{1}: (7, {})} | custom-call | tf_op jit(solution)/shard_map/mixed_back/pallas_call | solution.py:46
  274.4 6.0 %weight_grad.5 = bf16[1024,5632]{1,0:T(8,128)(2,1)} custom-call(bf16[1024,1024]{1,0:T(8,128)(2,1)} %get-tuple-element.220.left_ref, bf16[1024,1024]{1,0:T(8,128)(2,1)} %get-tuple-element.198.att_ref.right_ref, bf16[1024,5632]{1,0:T(8,128)(2,1)} %weight_grad.4.refs_0_), custom_call_target="tpu_custom_call", output_to_operand_aliasing={{}: (2, {})} | custom-call | tf_op jit(solution)/shard_map/weight_grad/pallas_call | solution.py:46
  280.5 10.4 %attend_back.7 = (f32[512,1024]{1,0:T(8,128)}, bf16[2,512,512]{2,1,0:T(8,128)(2,1)}, bf16[2,512,512]{2,1,0:T(8,128)(2,1)}, bf16[2,512,512]{2,1,0:T(8,128)(2,1)}) custom-call(s32[2]{0:T(128)} %pad_add_fusion.1.idx_ref, bf16[1024,1024]{1,0:T(8,128)(2,1)} %get-tuple-element.184.refs_0_.q_ref, bf16[512,1024]{1,0:T(8,128)(2,1)} %get-tuple-element.222.do_ref, ...), custom_call_target="tpu_custom_call" | custom-call | flops 65999998976 | tf_op jit(solution)/shard_map/attend_back/pallas_call | solution.py:46
  290.9 9.3 %collective-permute-start.30 = (bf16[2,512,512]{2,1,0:T(8,128)(2,1)}, bf16[2,512,512]{2,1,0:T(8,128)(2,1)S(1)}, u32[]{:S(2)}, u32[]{:S(2)}) collective-permute-start(bf16[2,512,512]{2,1,0:T(8,128)(2,1)} %get-tuple-element.231), channel_id=1, source_target_pairs={{0,2},{2,0},{4,6},{6,4},{8,10},{10,8},{12,14},{14,12},{1,3},{3,1},... | collective-permute-start | bytes 3145736 | tf_op jit(solution)/shard_map/ppermute | solution.py:706
  300.2 14.9 %attend_back.8 = (f32[512,1024]{1,0:T(8,128)}, bf16[2,512,512]{2,1,0:T(8,128)(2,1)}, bf16[2,512,512]{2,1,0:T(8,128)(2,1)}) custom-call(s32[2]{0:T(128)} %pad_add_fusion.1.idx_ref, bf16[1024,1024]{1,0:T(8,128)(2,1)} %get-tuple-element.184.refs_0_.q_ref, bf16[512,1024]{1,0:T(8,128)(2,1)} %get-tuple-element.222.do_ref, ...), custom_call_target="tpu_custom_call" | custom-call | flops 48000000000 | tf_op jit(solution)/shard_map/attend_back/pallas_call | solution.py:46
  320.1 12.7 %attend_back.9 = (f32[1024,1024]{1,0:T(8,128)}, bf16[2,512,512]{2,1,0:T(8,128)(2,1)}, bf16[2,512,512]{2,1,0:T(8,128)(2,1)}, bf16[2,512,512]{2,1,0:T(8,128)(2,1)}...) custom-call(s32[2]{0:T(128)} %pad_add_fusion.1.idx_ref, ...), custom_call_target="tpu_custom_call" | custom-call | flops 120000004096 | tf_op jit(solution)/shard_map/attend_back/pallas_call | solution.py:46
  333.2 16.3 %collective-permute-start.37 = (bf16[512,512]{1,0:T(8,128)(2,1)S(1)}, bf16[512,512]{1,0:T(8,128)(2,1)S(1)}, u32[]{:S(2)}, u32[]{:S(2)}) collective-permute-start(bf16[512,512]{1,0:T(8,128)(2,1)S(1)} %get-tuple-element.336), channel_id=1, source_target_pairs={{0,4},{2,6},{4,0},{6,2},{8,12},{10,14},{12,8},{14,10},{1,5},{3,7},... | collective-permute-start | bytes 1572872 | tf_op jit(solution)/shard_map/ppermute | solution.py:706
  349.4 25.1 %collective-permute-start.38 = (bf16[512,512]{1,0:T(8,128)(2,1)S(1)}, bf16[512,512]{1,0:T(8,128)(2,1)S(1)}, u32[]{:S(2)}, u32[]{:S(2)}) collective-permute-start(bf16[512,512]{1,0:T(8,128)(2,1)S(1)} %get-tuple-element.335), channel_id=1, source_target_pairs={{0,8},{2,10},{4,12},{6,14},{8,0},{10,2},{12,4},{14,6},{1,9},{3,11}... | collective-permute-start | bytes 1572872 | tf_op jit(solution)/shard_map/ppermute | solution.py:706
  374.6 25.9 %attend_back.10 = (f32[512,1024]{1,0:T(8,128)}, bf16[2,512,512]{2,1,0:T(8,128)(2,1)}, bf16[2,512,512]{2,1,0:T(8,128)(2,1)}, bf16[2,512,512]{2,1,0:T(8,128)(2,1)}, bf16[2,512,512]{2,1,0:T(8,128)(2,1)}) custom-call(s32[2]{0:T(128)} %pad_add_fusion.1.idx_ref, bf16[1024,1024]{1,0:T(8,128)(2,1)} %get-tuple-element.184.refs_0_.q_ref, ...), custom_call_target="tpu_custom_call" | custom-call | flops 83999997952 | tf_op jit(solution)/shard_map/attend_back/pallas_call | solution.py:46
  400.5 5.2 collective-permute-start.35
  405.8 15.1 %attend_back.11 = (f32[1024,1024]{1,0:T(8,128)}, bf16[2,512,512]{2,1,0:T(8,128)(2,1)}, bf16[2,512,512]{2,1,0:T(8,128)(2,1)}) custom-call(s32[2]{0:T(128)} %pad_add_fusion.1.idx_ref, bf16[1024,1024]{1,0:T(8,128)(2,1)} %get-tuple-element.184.refs_0_.q_ref, bf16[512,1024]{1,0:T(8,128)(2,1)} %get-tuple-element.222.do_ref, ...), custom_call_target="tpu_custom_call", output_to_operand_aliasing={{0}: (11, {})} | custom-call | flops 48000000000 | tf_op jit(solution)/shard_map/attend_back/pallas_call | solution.py:46
  422.7 3.8 merge.1
  426.5 5.4 collective-permute-start.40
  431.8 16.9 %collective-permute-start.41 = (bf16[2,512,512]{2,1,0:T(8,128)(2,1)}, bf16[2,512,512]{2,1,0:T(8,128)(2,1)S(1)}, u32[]{:S(2)}, u32[]{:S(2)}) collective-permute-start(bf16[2,512,512]{2,1,0:T(8,128)(2,1)} %get-tuple-element.274), channel_id=1, source_target_pairs={{0,8},{2,10},{4,12},{6,14},{8,0},{10,2},{12,4},{14,6},{1,9},{3,11}... | collective-permute-start | bytes 3145736 | tf_op jit(solution)/shard_map/ppermute | solution.py:706
  451.0 15.6 %q_back.1 = (bf16[1024,1024]{1,0:T(8,128)(2,1)}, f32[1024,1024]{1,0:T(8,128)}, f32[1,128]{1,0:T(1,128)}) custom-call(f32[1024,1024]{1,0:T(8,128)} %get-tuple-element.251.dq_ref, f32[1024,1024]{1,0:T(8,128)} %get-tuple-element.252.lin_ref, f32[1,128]{1,0:T(1,128)} %reshape.121.hgain_ref.gain_ref, f32[1024,128]{1,0:T(8,128)} %get-tuple-element.368.cos_ref, ...), custom_call_target="tpu_custom_call" | custom-call | tf_op jit(solution)/shard_map/q_back/pallas_call | solution.py:46
  466.5 9.7 %kv_back.2 = (bf16[1024,1024]{1,0:T(8,128)(2,1)}, bf16[512,1024]{1,0:T(8,128)(2,1)}, f32[1,128]{1,0:T(1,128)}) custom-call(f32[512,512]{1,0:T(8,128)} %get-tuple-element.264.lin_ref, f32[1,128]{1,0:T(1,128)} %reshape.120.hgain_ref.gain_ref, f32[1024,128]{1,0:T(8,128)} %get-tuple-element.368.cos_ref, f32[1024,128]{1,0:T(8,128)} %get-tuple-element.369.sin_ref, ...), custom_call_target="tpu_custom_call" | custom-call | tf_op jit(solution)/shard_map/kv_back/pallas_call | solution.py:46
  476.3 5.8 %weight_halves.2 = (bf16[512,1024]{1,0:T(8,128)(2,1)}, bf16[512,1024]{1,0:T(8,128)(2,1)}) custom-call(bf16[1024,1024]{1,0:T(8,128)(2,1)} %get-tuple-element.177.normed_ref.left_ref, bf16[1024,1024]{1,0:T(8,128)(2,1)} %get-tuple-element.269.right_ref), custom_call_target="tpu_custom_call" | custom-call | tf_op jit(solution)/shard_map/weight_halves/pallas_call | solution.py:46
  484.0 10.1 %kv_back.3 = (bf16[1024,1024]{1,0:T(8,128)(2,1)}, bf16[512,1024]{1,0:T(8,128)(2,1)}, f32[1,128]{1,0:T(1,128)}) custom-call(f32[512,512]{1,0:T(8,128)} %get-tuple-element.206.lin_ref, f32[1,128]{1,0:T(1,128)} %reshape.120.hgain_ref.gain_ref, f32[1024,128]{1,0:T(8,128)} %get-tuple-element.368.cos_ref, ...), custom_call_target="tpu_custom_call", output_to_operand_aliasing={{0}: (15, {})} | custom-call | flops 8999999488 | tf_op jit(solution)/shard_map/kv_back/pallas_call | solution.py:46
  496.5 9.0 %collective-permute-start.45 = (bf16[128,512]{1,0:T(8,128)(2,1)S(1)}, bf16[128,512]{1,0:T(8,128)(2,1)S(1)}, u32[]{:S(2)}, u32[]{:S(2)}) collective-permute-start(bf16[128,512]{1,0:T(8,128)(2,1)S(1)} %get-tuple-element.333), channel_id=1, source_target_pairs={{0,8},{2,10},{4,12},{6,14},{8,0},{10,2},{12,4},{14,6},{1,9},{3,11}... | collective-permute-start | bytes 393224 | tf_op jit(solution)/shard_map/ppermute | solution.py:706
  506.2 5.9 %weight_halves.3 = (bf16[512,1024]{1,0:T(8,128)(2,1)}, bf16[512,1024]{1,0:T(8,128)(2,1)}) custom-call(bf16[1024,1024]{1,0:T(8,128)(2,1)} %get-tuple-element.177.normed_ref.left_ref, bf16[1024,1024]{1,0:T(8,128)(2,1)} %get-tuple-element.280.right_ref), custom_call_target="tpu_custom_call" | custom-call | tf_op jit(solution)/shard_map/weight_halves/pallas_call | solution.py:46
  512.7 4.3 tokens_back.2
  523.7 3.1 add_layer.2.refs_0_
  531.3 3.1 add_layer.3
  535.8 4.0 tokens_back.3
  543.2 7.1 %collective-permute-done.58 = bf16[64,1024]{1,0:T(8,128)(2,1)S(1)} collective-permute-done((bf16[64,1024]{1,0:T(8,128)(2,1)S(1)}, bf16[64,1024]{1,0:T(8,128)(2,1)S(1)}, u32[]{:S(2)}, u32[]{:S(2)}) %collective-permute-start.58) | collective-permute-done | bytes 131104 | tf_op jit(solution)/shard_map/ppermute | solution.py:706
  551.3 2.8 collective-permute-done.59
  554.9 3.8 collective-permute-done.60
  (297 shorter events, 104.5 us)
Async XLA Ops:
  7.2 141.5 %all-gather.2.cloned.1.call-start = ((), (), s32[]{:S(2)}) async-start(), calls=%async_computation.1 | async-start | bytes 12255232 | tf_op jit(solution)/shard_map/all_gather | solution.py:825
  9.4 507.5 %reduce-scatter.2.cloned.1.call-start = ((), (), s32[]{:S(2)}) async-start(), calls=%async_computation.2 | async-start | bytes 12255232 | tf_op jit(solution)/shard_map/reduce_scatter | solution.py:962
  9.5 11.5 %collective-permute-start = (bf16[64,1024]{1,0:T(8,128)(2,1)}, bf16[64,1024]{1,0:T(8,128)(2,1)S(1)}, u32[]{:S(2)}, u32[]{:S(2)}) collective-permute-start(bf16[64,1024]{1,0:T(8,128)(2,1)} %get-tuple-element.166), channel_id=1, source_target_pairs={{0,16},{16,0},{1,17},{17,1},{2,18},{18,2},{3,19},{19,3},{4,20},{20... | collective-permute-start | bytes 393224 | tf_op jit(solution)/shard_map/ppermute | solution.py:706
  21.0 13.7 %collective-permute-start.2 = (bf16[128,1024]{1,0:T(8,128)(2,1)S(1)}, bf16[128,1024]{1,0:T(8,128)(2,1)S(1)}, u32[]{:S(2)}, u32[]{:S(2)}) collective-permute-start(bf16[128,1024]{1,0:T(8,128)(2,1)S(1)} %pad_maximum_fusion.3), channel_id=1, source_target_pairs={{0,4},{2,6},{4,0},{6,2},{8,12},{10,14},{12,8},{14,10},{1,5},{3,7},... | collective-permute-start | bytes 786440 | tf_op jit(solution)/shard_map/ppermute | solution.py:706
  22.8 13.4 %collective-permute-start.3 = (bf16[128,1024]{1,0:T(8,128)(2,1)S(1)}, bf16[128,1024]{1,0:T(8,128)(2,1)S(1)}, u32[]{:S(2)}, u32[]{:S(2)}) collective-permute-start(bf16[128,1024]{1,0:T(8,128)(2,1)S(1)} %pad_maximum_fusion.3), channel_id=1, source_target_pairs={{0,8},{2,10},{4,12},{6,14},{8,0},{10,2},{12,4},{14,6},{1,9},{3,11}... | collective-permute-start | bytes 786440 | tf_op jit(solution)/shard_map/ppermute | solution.py:706
  24.4 17.8 %collective-permute-start.1 = (bf16[64,1024]{1,0:T(8,128)(2,1)S(1)}, bf16[64,1024]{1,0:T(8,128)(2,1)S(1)}, u32[]{:S(2)}, u32[]{:S(2)}) collective-permute-start(bf16[64,1024]{1,0:T(8,128)(2,1)S(1)} %copy-done.25), channel_id=1, source_target_pairs={{0,16},{16,0},{1,17},{17,1},{2,18},{18,2},{3,19},{19,3},{4,20},{20... | collective-permute-start | bytes 393224 | tf_op jit(solution)/shard_map/ppermute | solution.py:706
  27.0 9.9 %collective-permute-start.8 = (bf16[16,144]{1,0:T(8,128)(2,1)S(1)}, bf16[16,144]{1,0:T(8,128)(2,1)S(1)}, u32[]{:S(2)}, u32[]{:S(2)}) collective-permute-start(bf16[16,144]{1,0:T(8,128)(2,1)S(1)} %fusion.26), channel_id=1, source_target_pairs={{0,4},{2,6},{4,0},{6,2},{8,12},{10,14},{12,8},{14,10},{1,5},{3,7},... | collective-permute-start | bytes 13832 | tf_op jit(solution)/shard_map/ppermute | solution.py:706
  42.2 10.2 %collective-permute-start.10 = (bf16[512,1024]{1,0:T(8,128)(2,1)}, bf16[512,1024]{1,0:T(8,128)(2,1)S(1)}, u32[]{:S(2)}, u32[]{:S(2)}) collective-permute-start(bf16[512,1024]{1,0:T(8,128)(2,1)} %get-tuple-element.344), channel_id=1, source_target_pairs={{0,2},{2,0},{4,6},{6,4},{8,10},{10,8},{12,14},{14,12},{1,3},{3,1},... | collective-permute-start | bytes 3145736 | tf_op jit(solution)/shard_map/ppermute | solution.py:706
  43.0 13.2 %collective-permute-start.12 = (bf16[128,1024]{1,0:T(8,128)(2,1)}, bf16[128,1024]{1,0:T(8,128)(2,1)}, u32[]{:S(2)}, u32[]{:S(2)}) collective-permute-start(bf16[128,1024]{1,0:T(8,128)(2,1)} %get-tuple-element.351), channel_id=1, source_target_pairs={{0,4},{2,6},{4,0},{6,2},{8,12},{10,14},{12,8},{14,10},{1,5},{3,7},... | collective-permute-start | bytes 786440 | tf_op jit(solution)/shard_map/ppermute | solution.py:706
  43.4 13.5 %collective-permute-start.13 = (bf16[128,1024]{1,0:T(8,128)(2,1)}, bf16[128,1024]{1,0:T(8,128)(2,1)S(1)}, u32[]{:S(2)}, u32[]{:S(2)}) collective-permute-start(bf16[128,1024]{1,0:T(8,128)(2,1)} %get-tuple-element.351), channel_id=1, source_target_pairs={{0,8},{2,10},{4,12},{6,14},{8,0},{10,2},{12,4},{14,6},{1,9},{3,11}... | collective-permute-start | bytes 786440 | tf_op jit(solution)/shard_map/ppermute | solution.py:706
  56.9 11.8 %collective-permute-start.14 = (bf16[128,512]{1,0:T(8,128)(2,1)S(1)}, bf16[128,512]{1,0:T(8,128)(2,1)S(1)}, u32[]{:S(2)}, u32[]{:S(2)}) collective-permute-start(bf16[128,512]{1,0:T(8,128)(2,1)S(1)} %slice.134), channel_id=1, source_target_pairs={{0,4},{2,6},{4,0},{6,2},{8,12},{10,14},{12,8},{14,10},{1,5},{3,7},... | collective-permute-start | bytes 393224 | tf_op jit(solution)/shard_map/ppermute | solution.py:706
  59.6 9.1 %collective-permute-start.15 = (bf16[128,512]{1,0:T(8,128)(2,1)S(1)}, bf16[128,512]{1,0:T(8,128)(2,1)S(1)}, u32[]{:S(2)}, u32[]{:S(2)}) collective-permute-start(bf16[128,512]{1,0:T(8,128)(2,1)S(1)} %slice.135), channel_id=1, source_target_pairs={{0,8},{2,10},{4,12},{6,14},{8,0},{10,2},{12,4},{14,6},{1,9},{3,11}... | collective-permute-start | bytes 393224 | tf_op jit(solution)/shard_map/ppermute | solution.py:706
  69.4 9.9 %collective-permute-start.16 = (bf16[512,1024]{1,0:T(8,128)(2,1)}, bf16[512,1024]{1,0:T(8,128)(2,1)S(1)}, u32[]{:S(2)}, u32[]{:S(2)}) collective-permute-start(bf16[512,1024]{1,0:T(8,128)(2,1)} %maximum_dynamic-update-slice_fusion), channel_id=1, source_target_pairs={{0,2},{2,0},{4,6},{6,4},{8,10},{10,8},{12,14},{14,12},{1,3},{3,1},... | collective-permute-start | bytes 3145736 | tf_op jit(solution)/shard_map/ppermute | solution.py:706
  69.4 44.9 %collective-permute-start.11 = (bf16[2,512,512]{2,1,0:T(8,128)(2,1)}, bf16[2,512,512]{2,1,0:T(8,128)(2,1)S(1)}, u32[]{:S(2)}, u32[]{:S(2)}) collective-permute-start(bf16[2,512,512]{2,1,0:T(8,128)(2,1)} %get-tuple-element.174.refs_1_.refs_0_), channel_id=1, source_target_pairs={{0,4},{2,6},{4,0},{6,2},{8,12},{10,14},{12,8},{14,10},{1,5},{3,7},... | collective-permute-start | bytes 3145736 | tf_op jit(solution)/shard_map/ppermute | solution.py:706
  69.6 45.0 %collective-permute-start.17 = (bf16[2,512,512]{2,1,0:T(8,128)(2,1)}, bf16[2,512,512]{2,1,0:T(8,128)(2,1)}, u32[]{:S(2)}, u32[]{:S(2)}) collective-permute-start(bf16[2,512,512]{2,1,0:T(8,128)(2,1)} %get-tuple-element.174.refs_1_.refs_0_), channel_id=1, source_target_pairs={{0,8},{2,10},{4,12},{6,14},{8,0},{10,2},{12,4},{14,6},{1,9},{3,11}... | collective-permute-start | bytes 3145736 | tf_op jit(solution)/shard_map/ppermute | solution.py:706
  72.3 49.4 %collective-permute-start.18 = (bf16[2,512,512]{2,1,0:T(8,128)(2,1)}, bf16[2,512,512]{2,1,0:T(8,128)(2,1)S(1)}, u32[]{:S(2)}, u32[]{:S(2)}) collective-permute-start(bf16[2,512,512]{2,1,0:T(8,128)(2,1)} %get-tuple-element.174.refs_1_.refs_0_), channel_id=1, source_target_pairs={{0,2},{2,0},{4,6},{6,4},{8,10},{10,8},{12,14},{14,12},{1,3},{3,1},... | collective-permute-start | bytes 3145736 | tf_op jit(solution)/shard_map/ppermute | solution.py:706
  114.7 18.9 %collective-permute-start.20 = (bf16[512,512]{1,0:T(8,128)(2,1)S(1)}, bf16[512,512]{1,0:T(8,128)(2,1)S(1)}, u32[]{:S(2)}, u32[]{:S(2)}) collective-permute-start(bf16[512,512]{1,0:T(8,128)(2,1)S(1)} %slice_bitcast_fusion.2), channel_id=1, source_target_pairs={{0,8},{2,10},{4,12},{6,14},{8,0},{10,2},{12,4},{14,6},{1,9},{3,11}... | collective-permute-start | bytes 1572872 | tf_op jit(solution)/shard_map/ppermute | solution.py:706
  118.3 15.4 %collective-permute-start.19 = (bf16[512,512]{1,0:T(8,128)(2,1)S(1)}, bf16[512,512]{1,0:T(8,128)(2,1)S(1)}, u32[]{:S(2)}, u32[]{:S(2)}) collective-permute-start(bf16[512,512]{1,0:T(8,128)(2,1)S(1)} %slice_bitcast_fusion.3), channel_id=1, source_target_pairs={{0,4},{2,6},{4,0},{6,2},{8,12},{10,14},{12,8},{14,10},{1,5},{3,7},... | collective-permute-start | bytes 1572872 | tf_op jit(solution)/shard_map/ppermute | solution.py:706
  134.4 25.6 %collective-permute-start.24 = (bf16[2,512,512]{2,1,0:T(8,128)(2,1)}, bf16[2,512,512]{2,1,0:T(8,128)(2,1)}, u32[]{:S(2)}, u32[]{:S(2)}) collective-permute-start(bf16[2,512,512]{2,1,0:T(8,128)(2,1)} %get-tuple-element.195.refs_3_.refs_0_), channel_id=1, source_target_pairs={{0,4},{2,6},{4,8},{6,10},{8,12},{10,14},{1,5},{3,7},{5,9},{7,11},{... | collective-permute-start | bytes 3145736 | tf_op jit(solution)/shard_map/ppermute | solution.py:711
  161.4 30.2 %collective-permute-start.27 = (bf16[512,1024]{1,0:T(8,128)(2,1)S(1)}, bf16[512,1024]{1,0:T(8,128)(2,1)S(1)}, u32[]{:S(2)}, u32[]{:S(2)}) collective-permute-start(bf16[512,1024]{1,0:T(8,128)(2,1)S(1)} %copy-done.4), channel_id=1, source_target_pairs={{0,1},{1,0},{2,3},{3,2},{4,5},{5,4},{6,7},{7,6},{8,9},{9,8},{10,11... | collective-permute-start | bytes 3145736 | tf_op jit(solution)/shard_map/ppermute | solution.py:706
  189.1 24.0 %collective-permute-start.26 = (bf16[512,1024]{1,0:T(8,128)(2,1)}, bf16[512,1024]{1,0:T(8,128)(2,1)S(1)}, u32[]{:S(2)}, u32[]{:S(2)}) collective-permute-start(bf16[512,1024]{1,0:T(8,128)(2,1)} %out_projection.3.own_ref), channel_id=1, source_target_pairs={{0,1},{1,0},{2,3},{3,2},{4,5},{5,4},{6,7},{7,6},{8,9},{9,8},{10,11... | collective-permute-start | bytes 3145736 | tf_op jit(solution)/shard_map/ppermute | solution.py:706
  210.9 41.0 %collective-permute-start.29 = (bf16[512,1024]{1,0:T(8,128)(2,1)}, bf16[512,1024]{1,0:T(8,128)(2,1)S(1)}, u32[]{:S(2)}, u32[]{:S(2)}) collective-permute-start(bf16[512,1024]{1,0:T(8,128)(2,1)} %get-tuple-element.200.own_ref), channel_id=1, source_target_pairs={{0,1},{1,0},{2,3},{3,2},{4,5},{5,4},{6,7},{7,6},{8,9},{9,8},{10,11... | collective-permute-start | bytes 3145736 | tf_op jit(solution)/shard_map/ppermute | solution.py:706
  232.4 34.1 %collective-permute-start.28 = (bf16[512,1024]{1,0:T(8,128)(2,1)}, bf16[512,1024]{1,0:T(8,128)(2,1)S(1)}, u32[]{:S(2)}, u32[]{:S(2)}) collective-permute-start(bf16[512,1024]{1,0:T(8,128)(2,1)} %get-tuple-element.207.own_ref), channel_id=1, source_target_pairs={{0,1},{1,0},{2,3},{3,2},{4,5},{5,4},{6,7},{7,6},{8,9},{9,8},{10,11... | collective-permute-start | bytes 3145736 | tf_op jit(solution)/shard_map/ppermute | solution.py:706
  290.9 26.4 %collective-permute-start.30 = (bf16[2,512,512]{2,1,0:T(8,128)(2,1)}, bf16[2,512,512]{2,1,0:T(8,128)(2,1)S(1)}, u32[]{:S(2)}, u32[]{:S(2)}) collective-permute-start(bf16[2,512,512]{2,1,0:T(8,128)(2,1)} %get-tuple-element.231), channel_id=1, source_target_pairs={{0,2},{2,0},{4,6},{6,4},{8,10},{10,8},{12,14},{14,12},{1,3},{3,1},... | collective-permute-start | bytes 3145736 | tf_op jit(solution)/shard_map/ppermute | solution.py:706
  315.1 17.6 %collective-permute-start.31 = (bf16[2,512,512]{2,1,0:T(8,128)(2,1)}, bf16[2,512,512]{2,1,0:T(8,128)(2,1)S(1)}, u32[]{:S(2)}, u32[]{:S(2)}) collective-permute-start(bf16[2,512,512]{2,1,0:T(8,128)(2,1)} %get-tuple-element.236), channel_id=1, source_target_pairs={{0,2},{2,0},{4,6},{6,4},{8,10},{10,8},{12,14},{14,12},{1,3},{3,1},... | collective-permute-start | bytes 3145736 | tf_op jit(solution)/shard_map/ppermute | solution.py:706
  315.2 85.2 %collective-permute-start.33 = (bf16[512,1024]{1,0:T(8,128)(2,1)}, bf16[512,1024]{1,0:T(8,128)(2,1)}, u32[]{:S(2)}, u32[]{:S(2)}) collective-permute-start(bf16[512,1024]{1,0:T(8,128)(2,1)} %get-tuple-element.245.own_ref), channel_id=1, source_target_pairs={{0,1},{1,0},{2,3},{3,2},{4,5},{5,4},{6,7},{7,6},{8,9},{9,8},{10,11... | collective-permute-start | bytes 3145736 | tf_op jit(solution)/shard_map/ppermute | solution.py:706
  315.6 84.9 %collective-permute-start.34 = (bf16[512,1024]{1,0:T(8,128)(2,1)}, bf16[512,1024]{1,0:T(8,128)(2,1)}, u32[]{:S(2)}, u32[]{:S(2)}) collective-permute-start(bf16[512,1024]{1,0:T(8,128)(2,1)} %get-tuple-element.247.own_ref), channel_id=1, source_target_pairs={{0,1},{1,0},{2,3},{3,2},{4,5},{5,4},{6,7},{7,6},{8,9},{9,8},{10,11... | collective-permute-start | bytes 3145736 | tf_op jit(solution)/shard_map/ppermute | solution.py:706
  318.7 55.9 %collective-permute-start.32 = (bf16[2,512,512]{2,1,0:T(8,128)(2,1)S(1)}, bf16[2,512,512]{2,1,0:T(8,128)(2,1)S(1)}, u32[]{:S(2)}, u32[]{:S(2)}) collective-permute-start(bf16[2,512,512]{2,1,0:T(8,128)(2,1)S(1)} %add_convert_fusion.3), channel_id=1, source_target_pairs={{4,0},{6,2},{8,4},{10,6},{12,8},{14,10},{5,1},{7,3},{9,5},{11,7},{... | collective-permute-start | bytes 3145736 | tf_op jit(solution)/shard_map/ppermute | solution.py:711
  333.2 87.7 %collective-permute-start.37 = (bf16[512,512]{1,0:T(8,128)(2,1)S(1)}, bf16[512,512]{1,0:T(8,128)(2,1)S(1)}, u32[]{:S(2)}, u32[]{:S(2)}) collective-permute-start(bf16[512,512]{1,0:T(8,128)(2,1)S(1)} %get-tuple-element.336), channel_id=1, source_target_pairs={{0,4},{2,6},{4,0},{6,2},{8,12},{10,14},{12,8},{14,10},{1,5},{3,7},... | collective-permute-start | bytes 1572872 | tf_op jit(solution)/shard_map/ppermute | solution.py:706
  349.4 71.5 %collective-permute-start.38 = (bf16[512,512]{1,0:T(8,128)(2,1)S(1)}, bf16[512,512]{1,0:T(8,128)(2,1)S(1)}, u32[]{:S(2)}, u32[]{:S(2)}) collective-permute-start(bf16[512,512]{1,0:T(8,128)(2,1)S(1)} %get-tuple-element.335), channel_id=1, source_target_pairs={{0,8},{2,10},{4,12},{6,14},{8,0},{10,2},{12,4},{14,6},{1,9},{3,11}... | collective-permute-start | bytes 1572872 | tf_op jit(solution)/shard_map/ppermute | solution.py:706
  400.5 20.9 %collective-permute-start.35 = (bf16[2,512,512]{2,1,0:T(8,128)(2,1)}, bf16[2,512,512]{2,1,0:T(8,128)(2,1)S(1)}, u32[]{:S(2)}, u32[]{:S(2)}) collective-permute-start(bf16[2,512,512]{2,1,0:T(8,128)(2,1)} %get-tuple-element.254), channel_id=1, source_target_pairs={{0,2},{2,0},{4,6},{6,4},{8,10},{10,8},{12,14},{14,12},{1,3},{3,1},... | collective-permute-start | bytes 3145736 | tf_op jit(solution)/shard_map/ppermute | solution.py:706
  405.7 15.7 %collective-permute-start.36 = (bf16[2,512,512]{2,1,0:T(8,128)(2,1)}, bf16[2,512,512]{2,1,0:T(8,128)(2,1)S(1)}, u32[]{:S(2)}, u32[]{:S(2)}) collective-permute-start(bf16[2,512,512]{2,1,0:T(8,128)(2,1)} %get-tuple-element.257), channel_id=1, source_target_pairs={{0,2},{2,0},{4,6},{6,4},{8,10},{10,8},{12,14},{14,12},{1,3},{3,1},... | collective-permute-start | bytes 3145736 | tf_op jit(solution)/shard_map/ppermute | solution.py:706
  420.9 61.4 %collective-permute-start.39 = (bf16[2,512,512]{2,1,0:T(8,128)(2,1)}, bf16[2,512,512]{2,1,0:T(8,128)(2,1)S(1)}, u32[]{:S(2)}, u32[]{:S(2)}) collective-permute-start(bf16[2,512,512]{2,1,0:T(8,128)(2,1)} %get-tuple-element.273), channel_id=1, source_target_pairs={{0,2},{2,0},{4,6},{6,4},{8,10},{10,8},{12,14},{14,12},{1,3},{3,1},... | collective-permute-start | bytes 3145736 | tf_op jit(solution)/shard_map/ppermute | solution.py:706
  426.5 55.8 %collective-permute-start.40 = (bf16[2,512,512]{2,1,0:T(8,128)(2,1)}, bf16[2,512,512]{2,1,0:T(8,128)(2,1)S(1)}, u32[]{:S(2)}, u32[]{:S(2)}) collective-permute-start(bf16[2,512,512]{2,1,0:T(8,128)(2,1)} %get-tuple-element.261), channel_id=1, source_target_pairs={{0,4},{2,6},{4,0},{6,2},{8,12},{10,14},{12,8},{14,10},{1,5},{3,7},... | collective-permute-start | bytes 3145736 | tf_op jit(solution)/shard_map/ppermute | solution.py:706
  431.8 50.5 %collective-permute-start.41 = (bf16[2,512,512]{2,1,0:T(8,128)(2,1)}, bf16[2,512,512]{2,1,0:T(8,128)(2,1)S(1)}, u32[]{:S(2)}, u32[]{:S(2)}) collective-permute-start(bf16[2,512,512]{2,1,0:T(8,128)(2,1)} %get-tuple-element.274), channel_id=1, source_target_pairs={{0,8},{2,10},{4,12},{6,14},{8,0},{10,2},{12,4},{14,6},{1,9},{3,11}... | collective-permute-start | bytes 3145736 | tf_op jit(solution)/shard_map/ppermute | solution.py:706
  482.1 12.0 %collective-permute-start.42 = (bf16[512,1024]{1,0:T(8,128)(2,1)}, bf16[512,1024]{1,0:T(8,128)(2,1)S(1)}, u32[]{:S(2)}, u32[]{:S(2)}) collective-permute-start(bf16[512,1024]{1,0:T(8,128)(2,1)} %get-tuple-element.277), channel_id=1, source_target_pairs={{0,2},{2,0},{4,6},{6,4},{8,10},{10,8},{12,14},{14,12},{1,3},{3,1},... | collective-permute-start | bytes 3145736 | tf_op jit(solution)/shard_map/ppermute | solution.py:706
  482.3 30.4 %collective-permute-start.44 = (bf16[512,1024]{1,0:T(8,128)(2,1)}, bf16[512,1024]{1,0:T(8,128)(2,1)}, u32[]{:S(2)}, u32[]{:S(2)}) collective-permute-start(bf16[512,1024]{1,0:T(8,128)(2,1)} %get-tuple-element.268.own_ref), channel_id=1, source_target_pairs={{0,1},{1,0},{2,3},{3,2},{4,5},{5,4},{6,7},{7,6},{8,9},{9,8},{10,11... | collective-permute-start | bytes 3145736 | tf_op jit(solution)/shard_map/ppermute | solution.py:706
  494.6 17.5 %collective-permute-start.46 = (bf16[128,512]{1,0:T(8,128)(2,1)S(1)}, bf16[128,512]{1,0:T(8,128)(2,1)S(1)}, u32[]{:S(2)}, u32[]{:S(2)}) collective-permute-start(bf16[128,512]{1,0:T(8,128)(2,1)S(1)} %get-tuple-element.331), channel_id=1, source_target_pairs={{0,4},{2,6},{4,0},{6,2},{8,12},{10,14},{12,8},{14,10},{1,5},{3,7},... | collective-permute-start | bytes 393224 | tf_op jit(solution)/shard_map/ppermute | solution.py:706
  496.5 15.6 %collective-permute-start.45 = (bf16[128,512]{1,0:T(8,128)(2,1)S(1)}, bf16[128,512]{1,0:T(8,128)(2,1)S(1)}, u32[]{:S(2)}, u32[]{:S(2)}) collective-permute-start(bf16[128,512]{1,0:T(8,128)(2,1)S(1)} %get-tuple-element.333), channel_id=1, source_target_pairs={{0,8},{2,10},{4,12},{6,14},{8,0},{10,2},{12,4},{14,6},{1,9},{3,11}... | collective-permute-start | bytes 393224 | tf_op jit(solution)/shard_map/ppermute | solution.py:706
  506.1 29.7 %collective-permute-start.51 = (bf16[512,1024]{1,0:T(8,128)(2,1)}, bf16[512,1024]{1,0:T(8,128)(2,1)}, u32[]{:S(2)}, u32[]{:S(2)}) collective-permute-start(bf16[512,1024]{1,0:T(8,128)(2,1)} %get-tuple-element.278.own_ref), channel_id=1, source_target_pairs={{0,1},{1,0},{2,3},{3,2},{4,5},{5,4},{6,7},{7,6},{8,9},{9,8},{10,11... | collective-permute-start | bytes 3145736 | tf_op jit(solution)/shard_map/ppermute | solution.py:706
  512.2 9.3 %collective-permute-start.49 = (bf16[128,1024]{1,0:T(8,128)(2,1)S(1)}, bf16[128,1024]{1,0:T(8,128)(2,1)S(1)}, u32[]{:S(2)}, u32[]{:S(2)}) collective-permute-start(bf16[128,1024]{1,0:T(8,128)(2,1)S(1)} %pad_maximum_fusion.6), channel_id=1, source_target_pairs={{0,8},{2,10},{4,12},{6,14},{8,0},{10,2},{12,4},{14,6},{1,9},{3,11}... | collective-permute-start | bytes 786440 | tf_op jit(solution)/shard_map/ppermute | solution.py:706
  512.3 9.2 %collective-permute-start.48 = (bf16[128,1024]{1,0:T(8,128)(2,1)S(1)}, bf16[128,1024]{1,0:T(8,128)(2,1)S(1)}, u32[]{:S(2)}, u32[]{:S(2)}) collective-permute-start(bf16[128,1024]{1,0:T(8,128)(2,1)S(1)} %pad_maximum_fusion.5), channel_id=1, source_target_pairs={{0,4},{2,6},{4,0},{6,2},{8,12},{10,14},{12,8},{14,10},{1,5},{3,7},... | collective-permute-start | bytes 786440 | tf_op jit(solution)/shard_map/ppermute | solution.py:706
  519.7 7.2 %collective-permute-start.50 = (bf16[128,512]{1,0:T(8,128)(2,1)S(1)}, bf16[128,512]{1,0:T(8,128)(2,1)S(1)}, u32[]{:S(2)}, u32[]{:S(2)}) collective-permute-start(bf16[128,512]{1,0:T(8,128)(2,1)S(1)} %get-tuple-element.325), channel_id=1, source_target_pairs={{0,4},{2,6},{4,0},{6,2},{8,12},{10,14},{12,8},{14,10},{1,5},{3,7},... | collective-permute-start | bytes 393224 | tf_op jit(solution)/shard_map/ppermute | solution.py:706
  523.7 10.7 %collective-permute-start.54 = (bf16[64,1024]{1,0:T(8,128)(2,1)S(1)}, bf16[64,1024]{1,0:T(8,128)(2,1)S(1)}, u32[]{:S(2)}, u32[]{:S(2)}) collective-permute-start(bf16[64,1024]{1,0:T(8,128)(2,1)S(1)} %slice.189), channel_id=1, source_target_pairs={{0,16},{16,0},{1,17},{17,1},{2,18},{18,2},{3,19},{19,3},{4,20},{20... | collective-permute-start | bytes 393224 | tf_op jit(solution)/shard_map/ppermute | solution.py:706
  527.0 8.1 %collective-permute-start.53 = (bf16[128,1024]{1,0:T(8,128)(2,1)S(1)}, bf16[128,1024]{1,0:T(8,128)(2,1)S(1)}, u32[]{:S(2)}, u32[]{:S(2)}) collective-permute-start(bf16[128,1024]{1,0:T(8,128)(2,1)S(1)} %pad_maximum_fusion.8), channel_id=1, source_target_pairs={{0,8},{2,10},{4,12},{6,14},{8,0},{10,2},{12,4},{14,6},{1,9},{3,11}... | collective-permute-start | bytes 786440 | tf_op jit(solution)/shard_map/ppermute | solution.py:706
  529.2 11.3 %collective-permute-start.55 = (f32[1,256]{1,0:T(1,128)S(1)}, f32[1,256]{1,0:T(1,128)S(1)}, u32[]{:S(2)}, u32[]{:S(2)}) collective-permute-start(f32[1,256]{1,0:T(1,128)S(1)} %pad_maximum_fusion.10), channel_id=1, source_target_pairs={{0,1},{1,0},{2,3},{3,2},{4,5},{5,4},{6,7},{7,6},{8,9},{9,8},{10,11... | collective-permute-start | bytes 3080 | tf_op jit(solution)/shard_map/ppermute | solution.py:706
  540.6 9.7 %collective-permute-start.58 = (bf16[64,1024]{1,0:T(8,128)(2,1)S(1)}, bf16[64,1024]{1,0:T(8,128)(2,1)S(1)}, u32[]{:S(2)}, u32[]{:S(2)}) collective-permute-start(bf16[64,1024]{1,0:T(8,128)(2,1)S(1)} %slice.191), channel_id=1, source_target_pairs={{0,16},{16,0},{1,17},{17,1},{2,18},{18,2},{3,19},{19,3},{4,20},{20... | collective-permute-start | bytes 393224 | tf_op jit(solution)/shard_map/ppermute | solution.py:706
  542.4 7.9 %collective-permute-start.57 = (f32[1,2304]{1,0:T(1,128)S(1)}, f32[1,2304]{1,0:T(1,128)S(1)}, u32[]{:S(2)}, u32[]{:S(2)}) collective-permute-start(f32[1,2304]{1,0:T(1,128)S(1)} %fusion.25), channel_id=1, source_target_pairs={{0,4},{2,6},{4,0},{6,2},{8,12},{10,14},{12,8},{14,10},{1,5},{3,7},... | collective-permute-start | bytes 27656 | tf_op jit(solution)/shard_map/ppermute | solution.py:706
  (57 other events, 394.5 us)
Sparse Core Ops, SparseCore 0:
  10.3 110.4 all-gather.1
  280.6 193.7 reduce-scatter.1

commit v3 on v2

--- a/solution.py
+++ b/solution.py
@@ -96,25 +96,56 @@
         q_ref[:, cols] = (turned * (SCALE * LOG2E)).astype(BF)
 
 
-def pack_kernel(chunk, key_ref, value_ref, out_ref, gate_ref, up_ref, down_ref, kv_ref, rest_ref):
-    k_cols, o_cols, units = key_ref.shape[1], out_ref.shape[1], gate_ref.shape[1]
+def pack_kernel(chunk, key_ref, value_ref, q_ref, out_ref, gate_ref, up_ref, down_ref, kv_ref, qo_ref, ffn_ref):
+    k_cols, q_cols, units = key_ref.shape[1], q_ref.shape[1], gate_ref.shape[1]
     kv_ref[:, :k_cols] = key_ref[...]
     kv_ref[:, k_cols:] = value_ref[...]
-    rest_ref[:, :o_cols] = out_ref[...]
+    qo_ref[:, :q_cols] = q_ref[...]
+    qo_ref[:, q_cols:] = out_ref[...]
     for at in range(0, units, chunk):
-        to = o_cols + 2 * at
-        rest_ref[:, to : to + chunk] = gate_ref[:, at : at + chunk]
-        rest_ref[:, to + chunk : to + 2 * chunk] = up_ref[:, at : at + chunk]
-    rest_ref[:, o_cols + 2 * units :] = down_ref[...]
+        ffn_ref[:, 2 * at : 2 * at + chunk] = gate_ref[:, at : at + chunk]
+        ffn_ref[:, 2 * at + chunk : 2 * at + 2 * chunk] = up_ref[:, at : at + chunk]
+    ffn_ref[:, 2 * units :] = down_ref[...]
 
 
 def pack(chunk, *weights):
-    wide, k_cols = weights[0].shape
-    width = weights[2].shape[1] + 3 * weights[3].shape[1]
+    cols = [w.shape[1] for w in weights]
+    wide = weights[0].shape[0]
     whole = lambda f: (0, 0)
     ins = [(w, w.shape, whole) for w in weights]
-    outs = [(shaped((wide, cols), BF), (wide, cols), whole) for cols in (2 * k_cols, width)]
+    sums = (cols[0] + cols[1], cols[2] + cols[3], sum(cols[4:]))
+    outs = [(shaped((wide, width), BF), (wide, width), whole) for width in sums]
     return call(functools.partial(pack_kernel, chunk), "pack", (1,), ins, outs)
+
+
+def assemble_kernel(moves, wide, part_ref, *refs):
+    pieces, out_ref, sems = refs[:-2], refs[-2], refs[-1]
+    copies = []
+    for at, (piece, row, first, slot, to, cols) in enumerate(moves):
+        block = jnp.bitwise_xor(part_ref[0], slot)
+        target = out_ref.at[pl.ds(pl.multiple_of(block * wide, wide), wide), pl.ds(to, cols)]
+        source = pieces[piece].at[pl.ds(row, wide), pl.ds(first, cols)]
+        copies.append(pltpu.make_async_copy(source, target, sems.at[at]))
+    for copy in copies:
+        copy.start()
+    for copy in copies:
+        copy.wait()
+
+
+def assemble(part, wide, pieces, moves, shape):
+    return pl.pallas_call(
+        functools.partial(assemble_kernel, moves, wide),
+        grid_spec=pltpu.PrefetchScalarGridSpec(
+            num_scalar_prefetch=1,
+            grid=(1,),
+            in_specs=[pl.BlockSpec(memory_space=pl.ANY)] * len(pieces),
+            out_specs=pl.BlockSpec(memory_space=pl.ANY),
+            scratch_shapes=[pltpu.SemaphoreType.DMA((len(moves),))],
+        ),
+        out_shape=shaped(shape, BF),
+        cost_estimate=pl.CostEstimate(flops=0, bytes_accessed=0, transcendentals=0),
+        name="assemble",
+    )(part[None], *pieces)
 
 
 def by_top_bit(slots):
@@ -243,10 +274,10 @@
     part_ref[...] = mm(att_ref[...], w_ref[...], NT).astype(BF)
 
 
-def out_projection(half, attended, w_rest):
+def out_projection(half, attended, w_out):
     rows, cols = attended.shape[0] // 2, attended.shape[1]
-    model = w_rest.shape[0]
-    ins = [(attended, (rows, cols), lambda j: (half, 0)), (w_rest, (model // 2, cols), lambda j: (j, 0))]
+    model = w_out.shape[0]
+    ins = [(attended, (rows, cols), lambda j: (half, 0)), (w_out, (model // 2, cols), lambda j: (j, 0))]
     outs = [(shaped((rows, model), BF), (rows, model // 2), lambda j: (0, j))]
     return call(out_kernel, "out_projection", (2,), ins, outs)[0]
 
@@ -372,7 +403,7 @@
         pltpu.VMEM((1, 2 * rows), F32),
         pltpu.VMEM((128, 2 * rows), F32),
     ]
-    us = 4 + 6 * (len(slots) + len(halos)) if carry is not None or halos else 0
+    us = 4 + 6 * len(slots) if half == 0 and carry is None else 0
     results = call(functools.partial(bwd_kernel, plan), "attend_back", (heads,), ins, outs, scratch,
                    scalars=scalars, us=us, keep=keep)
     n = len(slots)
@@ -413,17 +444,17 @@
         back_ref[...] = back_acc[...].astype(BF)
 
 
-def feed_forward(half, x, own, got, gain, dy, w_rest, o_cols, chunk, whole=None):
+def feed_forward(half, x, own, got, gain, dy, w_ffn, chunk, whole=None):
     rows, model = own.shape
-    units = (w_rest.shape[1] - o_cols) // 3
+    units = w_ffn.shape[1] // 3
     steps = units // chunk
     mine, once = lambda f: (half, 0), lambda f: (0, 0)
-    at_gu, at_down = o_cols // (2 * chunk), (o_cols + 2 * units) // chunk
+    at_down = 2 * units // chunk
     block = (rows, model)
     ins = [
         (x, block, mine), (own, block, once), (got, block, once), (gain, (1, model), once), (dy, block, mine),
-        (w_rest, (model, 2 * chunk), lambda f: (0, at_gu + f)),
-        (w_rest, (model, chunk), lambda f: (0, at_down + f)),
+        (w_ffn, (model, 2 * chunk), lambda f: (0, f)),
+        (w_ffn, (model, chunk), lambda f: (0, at_down + f)),
     ]
     keep = {}
     if whole is not None:
@@ -448,6 +479,21 @@
     return scale * (inner - unit * jnp.mean(inner * unit, axis=-1, keepdims=True)), grad * unit
 
 
+def lane_mean(values):
+    width = values.shape[-1]
+    ones = jnp.ones((width, width), BF)
+    high = values.astype(BF)
+    low = (values - high.astype(F32)).astype(BF)
+    return (mm(high, ones) + mm(low, ones)) * (1.0 / width)
+
+
+def head_norm_back(grad, values, gain):
+    scale = lax.rsqrt(lane_mean(values * values) + EPSILON)
+    unit = values * scale
+    inner = grad * gain
+    return scale * (inner - unit * lane_mean(inner * unit)), grad * unit
+
+
 def row_blocks(rows):
     size = rows // 2 if rows % 512 == 0 else rows
     return size, rows // size
@@ -480,15 +526,16 @@
         delta_ref[h // 2, h % 2 : h % 2 + 1, :] = jnp.sum(product.T, axis=0, keepdims=True)
 
 
-def mixed_back(half, own, got, resid, gain, dy, w_rest, o_cols, attended, whole=None):
+def mixed_back(half, own, got, resid, gain, dy, w_out, attended, whole=None):
     rows, model = own.shape
+    o_cols = w_out.shape[1]
     heads = o_cols // HEAD_SIZE
     size, steps = row_blocks(rows)
     mine, here, once = lambda f: (half * steps + f, 0), lambda f: (f, 0), lambda f: (0, 0)
     block = (size, model)
     ins = [
         (own, block, here), (got, block, here), (resid, block, here), (gain, (1, model), once),
-        (dy, block, mine), (w_rest, (model, o_cols), once), (attended, (size, o_cols), mine),
+        (dy, block, mine), (w_out, (model, o_cols), once), (attended, (size, o_cols), mine),
     ]
     keep = {}
     if whole is not None:
@@ -525,20 +572,28 @@
     return call(merge_kernel, "merge", (steps,), ins, outs)
 
 
-def weight_kernel(left_ref, right_ref, *refs):
-    refs[-1][...] = mm(left_ref[...], right_ref[...], TN).astype(BF)
-
-
-def weight_grad(left, right, at, width, cols, whole=None):
+def weight_kernel(order, part_ref, left_ref, right_ref, *refs):
+    low_ref, high_ref, total = refs[-3:]
+    total[...] = mm(left_ref[...], right_ref[...], TN)
+    wide = total.shape[0] // len(order)
+    for at, slot in enumerate(order):
+        block = jnp.bitwise_xor(part_ref[0], slot)
+        piece = total[pl.ds(pl.multiple_of(block * wide, wide), wide), :].astype(BF)
+        out_ref, row = (low_ref, at) if at < len(order) // 2 else (high_ref, at - len(order) // 2)
+        out_ref[row * wide : (row + 1) * wide, :] = piece
+
+
+def weight_grad(order, part, left, right, at, width, cols, whole=None):
     tokens, model = left.shape
     n = right.shape[1]
-    ins = [(left, (tokens, model), lambda j: (0, 0)), (right, (tokens, cols), lambda j: (0, j))]
+    ins = [(left, (tokens, model), lambda j, i: (0, 0)), (right, (tokens, cols), lambda j, i: (0, j))]
     keep = {}
     if whole is not None:
-        keep = {len(ins): 0}
-        ins.append((whole, None, None))
-    outs = [(shaped((model, width), BF), (model, cols), lambda j: (0, at // cols + j))]
-    return call(weight_kernel, "weight_grad", (n // cols,), ins, outs, keep=keep)[0]
+        keep = {len(ins): 0, len(ins) + 1: 1}
+        ins += [(array, None, None) for array in whole]
+    outs = [(shaped((model // 2, width), BF), (model // 2, cols), lambda j, i: (0, at // cols + j))] * 2
+    return call(functools.partial(weight_kernel, order), "weight_grad", (n // cols,), ins, outs,
+                [pltpu.VMEM((model, cols), F32)], scalars=part[None], keep=keep)
 
 
 def weight_halves_kernel(left_ref, right_ref, high_ref, low_ref):
@@ -564,7 +619,7 @@
     total = jnp.zeros(cos.shape, F32)
     for h in range(heads):
         cols = slice(h * HEAD_SIZE, (h + 1) * HEAD_SIZE)
-        grad, summand = norm_back(turn_back(dq_ref[:, cols], cos, sin), lin_ref[:, cols], gain_ref[...])
+        grad, summand = head_norm_back(turn_back(dq_ref[:, cols], cos, sin), lin_ref[:, cols], gain_ref[...])
         d_ref[:, cols] = grad.astype(BF)
         total = total + summand
     part_ref[...] = mm(d_ref[...], w_ref[...], NT)
@@ -605,7 +660,7 @@
     gains = jnp.zeros(cos.shape, F32)
     for h in range(heads):
         cols = slice(h * HEAD_SIZE, (h + 1) * HEAD_SIZE)
-        grad, summand = norm_back(
+        grad, summand = head_norm_back(
             turn_back(total(key_refs, 0, cols), cos, sin), lin_ref[:, cols], gain_ref[...]
         )
         d_ref[:, cols] = grad.astype(BF)
@@ -666,22 +721,27 @@
     return call(tokens_kernel, "tokens_back", (steps,), ins, outs, keep=keep, us=20)
 
 
-def share_kernel(chunk, share_ref, out_ref, gate_ref, up_ref, down_ref):
-    o_cols, units = out_ref.shape[1], gate_ref.shape[1]
-    out_ref[...] = share_ref[:, :o_cols].astype(F32)
+def share_kernel(chunk, ffn_ref, ffn_got_ref, out_own_ref, out_got_ref, late_ref, out_ref, gate_ref, up_ref, down_ref):
+    units = gate_ref.shape[1]
+    out_ref[...] = out_own_ref[...].astype(F32) + out_got_ref[...].astype(F32)
+
+    def total(at, cols):
+        return ffn_ref[:, at : at + cols].astype(F32) + ffn_got_ref[:, at : at + cols].astype(F32)
+
     for at in range(0, units, chunk):
-        to = o_cols + 2 * at
-        gate_ref[:, at : at + chunk] = share_ref[:, to : to + chunk].astype(F32)
-        up_ref[:, at : at + chunk] = share_ref[:, to + chunk : to + 2 * chunk].astype(F32)
-    down_ref[...] = share_ref[:, o_cols + 2 * units :].astype(F32)
-
-
-def unpack(chunk, o_cols, share):
-    wide = share.shape[0]
-    units = (share.shape[1] - o_cols) // 3
+        gate_ref[:, at : at + chunk] = total(2 * at, chunk)
+        up_ref[:, at : at + chunk] = total(2 * at + chunk, chunk)
+    down_ref[...] = total(2 * units, units)
+
+
+def unpack(chunk, ffn_grad, out_grad, late):
+    wide, width = ffn_grad[1].shape
+    o_cols, units = out_grad[1].shape[1], width // 3
     whole = lambda f: (0, 0)
+    ins = [(array, (wide, array.shape[1]), whole) for array in (*ffn_grad, *out_grad)]
+    ins.append((late, late.shape, whole))
     outs = [(shaped((wide, cols), F32), (wide, cols), whole) for cols in (o_cols, units, units, units)]
-    return call(functools.partial(share_kernel, chunk), "unpack", (1,), [(share, share.shape, whole)], outs)
+    return call(functools.partial(share_kernel, chunk), "unpack", (1,), ins, outs)
 
 
 def layer_kernel(resid_ref, own_ref, got_ref, *refs):
@@ -776,18 +836,22 @@
     def gather_first(piece, *gate):
         return jnp.concatenate([piece, after(swap(piece, "shard", 1), *gate)]) if ctx_size == 8 else piece
 
-    def gather_rows(one, gates=((),) * 3):
+    def gather_near(one, *gate):
         if ctx_size != 8:
             for axis, bit in bits:
                 one = jnp.concatenate([one, swap(one, axis, bit)])
-            return one, (one,) * 3
-        by_x, by_y = (after(v, *gates[0]) for v in (swap(one, "ctx", 2), swap(one, "ctx", 4)))
+            return [one]
+        by_x, by_y = (after(v, *gate) for v in (swap(one, "ctx", 2), swap(one, "ctx", 4)))
         cut = one.shape[1] // 2
-        left, right = swap(by_y[:, :cut], "ctx", 2), swap(by_x[:, cut:], "ctx", 4)
-        far = jnp.concatenate([after(left, *gates[1]), after(right, *gates[1])], axis=1)
-        half = jnp.concatenate([one, by_x, by_y, far])
-        whole = jnp.concatenate([half, after(swap(half, "ctx", 1), *gates[2])])
-        return whole, (by_x, half, whole)
+        return [one, by_x, by_y, swap(by_y[:, :cut], "ctx", 2), swap(by_x[:, cut:], "ctx", 4)]
+
+    def gather_far(pieces, *gate):
+        if ctx_size != 8:
+            return pieces[0], pieces[0]
+        *near, left, right = pieces
+        far = jnp.concatenate([after(left, *gate), after(right, *gate)], axis=1)
+        near = [*near, far]
+        return jnp.concatenate(near + [after(swap(piece, "ctx", 1), *gate) for piece in near]), far
 
     def scatter_rows(low, high, late):
         total = add_low(low, after(swap(high, "ctx", 1), late))
@@ -818,16 +882,18 @@
         total, size = total.astype(BF), total.shape[0] // 2
         return total, swap(total[size:], "shard", 1)
 
-    kv_piece, rest_piece = pack(chunk, key_weight, value_weight, w_out.T, w_gate, w_up, w_down.T)
+    kv_piece, qo_piece, ffn_piece = pack(
+        chunk, key_weight, value_weight, w_query, w_out.T, w_gate, w_up, w_down.T
+    )
     kv_one = gather_first(kv_piece)
-    w_kv, stages = gather_rows(kv_one)
-    q_one = gather_first(after(w_query, kv_one), stages[1])
-    w_rest = lax.all_gather(rest_piece, weight_axes, axis=0, tiled=True)
+    kv_near = gather_near(kv_one)
+    w_kv, kv_far = gather_far(kv_near)
+    qo_one = gather_first(after(qo_piece, kv_one), kv_far)
     gains = jnp.concatenate([attn_gain, ffn_gain, query_gain, key_gain])[None]
     gains = jnp.where(jnp.arange(parts)[:, None] == part, gains, jnp.zeros((), BF))
     gains = gains + after(swap(gains, "ctx", 1), kv_piece)
     for at, (axis, bit) in enumerate(bits[:-1]):
-        gains = gains + after(swap(gains, axis, bit), (kv_one, *stages)[min(at, 2)])
+        gains = gains + after(swap(gains, axis, bit), (kv_one, kv_near[min(1, len(kv_near) - 1)], kv_far)[min(at, 2)])
     gains = gains.astype(F32)
     gain_one = gains[:, :wide].reshape(1, -1)
     gain_two = gains[:, wide : 2 * wide].reshape(1, -1)
@@ -835,7 +901,7 @@
     gain_k = gains[:, 2 * wide + narrow :].reshape(1, -1)
     source = jnp.bitwise_xor(part, jnp.array(order, jnp.int32))[:, None] * wide + jnp.arange(wide, dtype=jnp.int32)
     to_slots = (jnp.arange(model, dtype=jnp.int32)[:, None] == source.reshape(1, -1)).astype(BF)
-    tokens_s = mm(after(tokens, q_one), to_slots).astype(BF)
+    tokens_s = mm(after(tokens, qo_one), to_slots).astype(BF)
     gain_one_s = mm(gain_one.astype(BF), to_slots)
 
     cont_at = me * rows + jnp.arange(rows, dtype=jnp.int32)
@@ -871,18 +937,32 @@
         return call(functools.partial(kv_kernel, kv_heads), "keys_values", (1,), ins, outs, keep=keep)
 
     normed, kv_p, k_lin_p = keys_values(0, gain_one_s)
-    normed, kv_c, k_lin_c = keys_values(1, after(gain_one_s, kv_p), normed)
-    w_q, _ = gather_rows(q_one, ((w_kv,), (kv_p,), (kv_c,)))
+    qo_near = gather_near(qo_one, kv_p)
+    normed, kv_c, k_lin_c = keys_values(1, after(gain_one_s, kv_p, *qo_near[1:3]), normed)
+    w_qo, _ = gather_far(qo_near, kv_c)
+    if ctx_size == 8:
+        moves = [(0, i * wide, q_cols, slot, 0, o_cols) for i, slot in enumerate(order)]
+        w_out_t = assemble(part, wide, [w_qo], moves, (model, o_cols))
+    else:
+        places = jnp.argsort(jnp.bitwise_xor(part, jnp.array(order, jnp.int32)))
+
+        def to_places(rows):
+            return jnp.take(rows.reshape(parts, wide, -1), places, axis=0).reshape(rows.shape)
+
+        w_out_t = to_places(w_qo[:, q_cols:])
+        w_ffn = to_places(gather_near(ffn_piece)[0])
     mine = lambda f: (f, 0)
     q, q_lin = call(
         functools.partial(q_kernel, heads), "queries", (2,),
         [
-            (normed, (rows, model), mine), (w_q, (model, q_cols), lambda f: (0, 0)),
+            (normed, (rows, model), mine), (w_qo, (model, q_cols), lambda f: (0, 0)),
             (gain_q, (1, HEAD_SIZE), lambda f: (0, 0)),
             (cos, (rows, HEAD_SIZE), mine), (sin, (rows, HEAD_SIZE), mine),
         ],
         [(shaped((2 * rows, q_cols), BF), (rows, q_cols), mine), (shaped((2 * rows, q_cols), F32), (rows, q_cols), mine)],
     )
+
+    ffn_one = gather_first(after(ffn_piece, qo_one), q)
 
     def pick(source, wanted):
         return {s: source[s] for s in source if s in wanted}
@@ -906,8 +986,10 @@
         slots[3], slots[5] = swap(slots[2], "ctx", 1), swap(slots[4], "ctx", 1)
         halos[2] = shift(after(kv_c, slots[2]), 2)
         ready = (slots[2], slots[4])
+        ffn_x, ffn_y = (swap(after(ffn_one, slots[2]), "ctx", bit) for bit in (2, 4))
+        ffn_core = [swap(ffn_one, "ctx", 1)]
     c_state = attention_forward(
-        (1,), after(scalars, *ready), q, low_col, pick(slots, near), pick(halos, (0,))
+        (1,), after(scalars, ffn_one, *ready), q, low_col, pick(slots, near), pick(halos, (0,))
     )
     if ctx_size == 8:
         slots[6] = jnp.stack([after(far_k, c_state[0]), after(far_v, c_state[0])])
@@ -916,31 +998,49 @@
     attended, lse_p = attention_forward(
         (0,), after(scalars, c_state[0], *ready), q, low_col, slots, {}, None, (None,)
     )
-    part_p = out_projection(0, attended, w_rest)
+    part_p = out_projection(0, attended, after(w_out_t, attended))
     got_p = swap(part_p, "tensor", 1)
     if ctx_size == 8:
         halos[1] = swap(jnp.where(odd, after(halos[2], part_p), kv_c), "ctx", 1)
+        cut = ffn_y.shape[1] // 2
+        ffn_y = after(ffn_y, part_p)
+        ffn_left = swap(ffn_y[:, :cut], "ctx", 2)
+        ffn_core.append(swap(ffn_y, "ctx", 1))
     attended, lse_c = attention_forward(
         (1,), after(scalars, part_p), q, low_col, pick(slots, middle + far), pick(halos, range(1, n_halo)),
         c_state, (attended,),
     )
-    part_c = out_projection(1, attended, w_rest)
+    part_c = out_projection(1, attended, after(w_out_t, attended, got_p))
     got_c = swap(part_c, "tensor", 1)
+    if ctx_size == 8:
+        ffn_x = after(ffn_x, part_c)
+        ffn_right = swap(ffn_x[:, cut:], "ctx", 4)
+        ffn_left = after(ffn_left, part_c)
+        ffn_core += [swap(ffn_x, "ctx", 1), swap(ffn_left, "ctx", 1), swap(ffn_right, "ctx", 1)]
+        near_pieces = [(ffn_one, 0, 0, 2 * cut), (ffn_y, 4, 0, 2 * cut), (ffn_x, 2, 0, 2 * cut)]
+        near_pieces += [(ffn_left, 6, 0, cut), (ffn_right, 6, cut, cut)]
+        moves = []
+        for at, (_, slot, to, cols) in enumerate(near_pieces):
+            for core in range(2):
+                for shard in range(2):
+                    moves.append((at + 5 * core, shard * wide, 0, slot + core + shard * ctx_size, to, cols))
+        w_ffn = assemble(part, wide, [p[0] for p in near_pieces] + ffn_core, moves, (model, 3 * units))
 
     resid_p, *whole, out_p, back_p = feed_forward(
-        0, tokens, part_p, got_p, after(gain_two, part_c), cotangent, w_rest, o_cols, chunk
+        0, tokens, part_p, got_p, after(gain_two, part_c), cotangent, w_ffn, chunk
     )
     back_got_p = swap(back_p, "tensor", 1)
     resid_c, *whole, out_c, back_c = feed_forward(
-        1, tokens, part_c, got_c, after(gain_two, back_p), cotangent, w_rest, o_cols, chunk, whole
+        1, tokens, part_c, got_c, after(gain_two, back_p), cotangent, w_ffn, chunk, whole
     )
     back_got_c = swap(back_c, "tensor", 1)
     normed_ffn, hidden, d_gu = whole
-    width = o_cols + 3 * units
-    rest_grads = weight_grad(normed_ffn, d_gu, o_cols, width, min(1024, o_cols))
-    rest_grads = weight_grad(cotangent, hidden, o_cols + 2 * units, width, chunk, rest_grads)
+    ffn_grads = weight_grad(order, part, normed_ffn, d_gu, 0, 3 * units, 2 * chunk)
+    ffn_low, ffn_high = weight_grad(
+        order, part, after(cotangent, back_got_p), hidden, 2 * units, 3 * units, chunk, ffn_grads
+    )
     d_resid_p, d_mixed, d_att_p, delta_p, d_two_p = mixed_back(
-        0, back_p, back_got_p, resid_p, after(gain_two, rest_grads), cotangent, w_rest, o_cols, attended
+        0, back_p, back_got_p, resid_p, after(gain_two, ffn_low), cotangent, w_out_t, attended
     )
     out_p, out_c = after(out_p, back_got_c), after(out_c, back_got_c)
     out_got_p, out_got_c = swap(out_p, "tensor", 1), swap(out_c, "tensor", 1)
@@ -954,16 +1054,19 @@
         )
 
     dq_p, prior, _ = back_rows(0, (d_att_p,), pick(slots, far), {}, None)
+    ffn_grad = scatter_rows(ffn_low, ffn_high, dq_p)
     d_resid_c, d_mixed, d_att_c, delta_c, d_two_c = mixed_back(
-        1, back_c, back_got_c, resid_c, after(gain_two, dq_p), cotangent, w_rest, o_cols, attended, d_mixed
+        1, back_c, back_got_c, resid_c, after(gain_two, dq_p, ffn_grad[0]), cotangent, w_out_t, attended, d_mixed
     )
     of_rows.append((d_att_c, lse_c, delta_c))
-    rest_grads = weight_grad(d_mixed, attended, 0, width, min(1024, o_cols), rest_grads)
-    rest_share = lax.psum_scatter(rest_grads, weight_axes, scatter_dimension=0, tiled=True)
-    dq_c, _, g_halo = back_rows(1, (rest_grads,), {}, halos, None)
+    out_low, out_high = weight_grad(order, part, d_mixed, attended, 0, o_cols, o_cols)
+    dq_c, _, g_halo = back_rows(1, (out_low, ffn_grad[0]), {}, halos, None)
+    ffn_grad = scatter_more(ffn_grad, dq_c)
+    out_grad = scatter_rows(out_low, out_high, dq_c)
     if ctx_size == 8:
         near_one = swap(g_halo[1], "ctx", 1)
-    dq_c, g, _ = back_rows(1, (dq_c,), pick(slots, far), {}, dq_c, prior)
+    dq_c, g, _ = back_rows(1, (dq_c, ffn_grad[0], out_grad[0]), pick(slots, far), {}, dq_c, prior)
+    out_grad = scatter_more(out_grad, dq_c)
     zero = jnp.zeros((), BF)
     ready = ()
     if ctx_size == 8:
@@ -973,20 +1076,22 @@
         halo_two = shift(two_back, -2)
         halo_near = jnp.where(odd, zero, near_one)
         ready = (two_back, halo_near)
-    dq, prior, _ = back_rows(0, (dq_c, *ready), pick(slots, near + middle), {}, dq_p, None, None, True)
+    dq, prior, _ = back_rows(0, (dq_c, out_grad[0], *ready), pick(slots, near + middle), {}, dq_p, None, None, True)
     if ctx_size == 8:
         g6 = add_low(g[6], after(got7, dq))
         far_k, far_v = swap(g6[0], "ctx", 2), swap(g6[1], "ctx", 4)
-        ready = (g6, halo_two)
-    dq_c, more, _ = back_rows(1, (dq, *ready), pick(slots, middle), {}, dq_c, prior)
+        ready = (g6,)
+    ffn_grad, out_grad = scatter_sum(ffn_grad, dq), scatter_sum(out_grad, dq)
+    dq_c, more, _ = back_rows(1, (dq, ffn_grad[0], out_grad[0], *ready), pick(slots, middle), {}, dq_c, prior)
     g.update(more)
     if ctx_size == 8:
         got3, got5 = swap(g[3], "ctx", 1), swap(g[5], "ctx", 1)
-    dq, more, _ = back_rows(1, (dq_c, out_got_p, out_got_c), pick(slots, near), {}, dq_c, prior, dq, True)
+        ready = (halo_two,)
+    dq, more, _ = back_rows(1, (dq_c, out_got_p, out_got_c, *ready), pick(slots, near), {}, dq_c, prior, dq, True)
     g.update(more)
     if ctx_size == 8:
         got1 = swap(g[1], "ctx", 1)
-        far_k, far_v, got3, got5 = (after(v, dq) for v in (far_k, far_v, got3, got5))
+        far_k, far_v, got3, got5 = (after(v, dq, ffn_grad[1], out_grad[1]) for v in (far_k, far_v, got3, got5))
         to_x, to_y = merge(g[2], got3, g[4], got5, far_k, far_v)
         ready = (to_x,)
         keys_p = values_p = [g[0], got1, swap(to_x, "ctx", 2), swap(to_y, "ctx", 4)]
@@ -999,7 +1104,7 @@
         keys_p = values_p = [both[0]]
         keys_c = values_c = [g_halo[0]] + [shift(g_halo[d], -d) for d in range(1, n_halo)]
 
-    d_q, q_part, q_heads = q_back(dq, q_lin, after(gain_q, dq, *ready), cos, sin, w_q)
+    d_q, q_part, q_heads = q_back(dq, q_lin, after(gain_q, dq, *ready), cos, sin, w_qo)
     d_kv, into_c, k_heads_c = kv_back(
         1, keys_c, values_c, k_lin_c, after(gain_k, q_part), cos, sin, w_kv, to_slots, q_part
     )
@@ -1015,7 +1120,7 @@
     heads = jnp.concatenate([q_heads, k_heads_c + k_heads_p], axis=1)
     heads_got = swap(heads, "tensor", 1)
     grad_tokens, d_one_c = tokens_back(1, into_c, into_got_c, tokens, after(gain_one, kv_low, q_grad[0]), d_resid_c)
-    out_share, gate_share, up_share, down_share = unpack(chunk, o_cols, after(rest_share, d_one_c))
+    out_share, gate_share, up_share, down_share = unpack(chunk, ffn_grad, out_grad, d_one_c)
     q_grad = scatter_sum(q_grad, gate_share)
     kv_grad = scatter_rows(kv_low, kv_high, gate_share)
     layer_out = add_layer(0, after(resid_p, kv_grad[0], q_grad[0]), out_p, out_got_p)

time: 576 us -> 980 us (1.70)
  Pallas kernels: 299 us -> 646 us
  waiting for transfers between devices: 63.1 us -> 86.6 us
  starting transfers between devices: 137 us -> 155 us
  local copies, waits for them, and re-layouts: 29.8 us -> 45.1 us
  between operations: 15.3 us -> 2.37 us
  other arithmetic: 17.4 us -> 29.5 us
    pallas_call x0 -> x2, Pallas kernels: none -> 352 us  [assemble(): pl.pallas_call(functools.partial(assemble_kernel, moves, wide), grid_spec...]
    ppermute x59 -> x87, waiting for transfers between devices: 55.6 us -> 86.6 us  [swap(): return lax.ppermute(value, axis, [(i, i ^ bit) for i in range(size)])]
    ppermute x59 -> x87, starting transfers between devices: 132 us -> 150 us  [swap(): return lax.ppermute(value, axis, [(i, i ^ bit) for i in range(size)])]
    unnamed x90 -> x129, local copies, waits for them, and re-layouts: 16.6 us -> 25.1 us
  transfers between devices with their start and end apart: 63 -> 89, of which waited for: 16 -> 20; matrix products, arithmetic and copies ran while one was open for 7% -> 7% of each run, Pallas kernels for 50% -> 66%
where the time goes in v3:
time: 980 us; the launch traced here: 971 us
  Pallas kernels  646 us (66%)
  starting transfers between devices  155 us (16%)
  waiting for transfers between devices  86.6 us (9%)
  local copies, waits for them, and re-layouts  45.1 us (5%)
  other arithmetic  29.5 us (3%)
    pallas_call x2, Pallas kernels, assemble(): pl.pallas_call(functools.partial(assemble_kernel, moves, wide), grid_spec...  352 us
    pallas_call x33, Pallas kernels, call(): pl.pallas_call(kernel, grid_spec=pltpu.PrefetchScalarGridSpec(num_scalar_...  294 us
    ppermute x87, starting transfers between devices, swap(): return lax.ppermute(value, axis, [(i, i ^ bit) for i in range(size)])  150 us
    ppermute x87, waiting for transfers between devices, swap(): return lax.ppermute(value, axis, [(i, i ^ bit) for i in range(size)])  86.6 us
    unnamed x129, local copies, waits for them, and re-layouts  25.1 us
  transfers between devices with their start and end apart: 89, of which 20 were waited for; matrix products, arithmetic and copies ran while one was open for 7% of the time, Pallas kernels for 66%

profile of v3, /device:TPU:0, one launch (start us, length us, event | category | flops | bytes accessed | tf_op | source)
XLA Modules:
  0.0 971.0 jit_solution(11497231923155295926)
XLA Ops:
  42.3 5.3 fusion.5.x_ref
  56.0 5.6 keys_values.2
  69.5 5.6 keys_values.3
  77.1 16.0 %collective-permute-done.18 = bf16[128,1024]{1,0:T(8,128)(2,1)S(1)} collective-permute-done((bf16[128,1024]{1,0:T(8,128)(2,1)S(1)}, bf16[128,1024]{1,0:T(8,128)(2,1)S(1)}, u32[]{:S(2)}, u32[]{:S(2)}) %collective-permute-start.18) | collective-permute-done | bytes 262176 | tf_op jit(solution)/shard_map/ppermute | solution.py:766
  101.7 10.2 %queries.1 = (bf16[1024,1024]{1,0:T(8,128)(2,1)}, f32[1024,1024]{1,0:T(8,128)}) custom-call(bf16[1024,1024]{1,0:T(8,128)(2,1)} %get-tuple-element.212.normed_ref.left_ref, bf16[1024,2048]{1,0:T(8,128)(2,1)} %constant_dynamic-update-slice_fusion.11.w_ref.refs_0_, f32[1,128]{1,0:T(1,128)} %reshape.121.hgain_ref.gain_ref, ...), custom_call_target="tpu_custom_call" | custom-call | tf_op jit(solution)/shard_map/queries/pallas_call | solution.py:46
  111.9 13.4 %collective-permute-done.6 = bf16[64,4608]{1,0:T(8,128)(2,1)S(1)} collective-permute-done((bf16[64,4608]{1,0:T(8,128)(2,1)S(1)}, bf16[64,4608]{1,0:T(8,128)(2,1)S(1)}, u32[]{:S(2)}, u32[]{:S(2)}) %collective-permute-start.6) | collective-permute-done | bytes 589856 | tf_op jit(solution)/shard_map/ppermute | solution.py:766
  129.0 10.8 %attend.3 = (f32[512,1024]{1,0:T(8,128)}, f32[512,1024]{1,0:T(8,128)}) custom-call(s32[2]{0:T(128)} %pad_add_fusion.1.idx_ref, s32[512,128]{1,0:T(8,128)} %broadcast_in_dim.77.lo_ref, bf16[1024,1024]{1,0:T(8,128)(2,1)} %get-tuple-element.220.refs_0_.q_ref, bf16[2,512,512]{2,1,0:T(8,128)(2,1)} %get-tuple-element.207.refs_1_.refs_0_, ...), custom_call_target="tpu_custom_call" | custom-call | tf_op jit(solution)/shard_map/attend/pallas_call | solution.py:46
  145.7 64.8 %assemble.2.w_ref = bf16[1024,1024]{1,0:T(8,128)(2,1)} custom-call(s32[1]{0:T(128)} %bitcast.12.part_ref, bf16[1024,2048]{1,0:T(8,128)(2,1)} %constant_dynamic-update-slice_fusion.11.w_ref.refs_0_), custom_call_target="tpu_custom_call" | custom-call | tf_op jit(solution)/shard_map/assemble/pallas_call | solution.py:136
  211.6 8.8 attend.4
  220.4 3.9 out_projection.2.own_ref
  230.5 6.8 collective-permute-start.37
  237.3 19.9 %attend.5 = (bf16[1024,1024]{1,0:T(8,128)(2,1)}, f32[4,8,512]{2,1,0:T(8,128)}) custom-call(s32[2]{0:T(128)} %pad_add_fusion.1.idx_ref, s32[512,128]{1,0:T(8,128)} %broadcast_in_dim.77.lo_ref, bf16[1024,1024]{1,0:T(8,128)(2,1)} %get-tuple-element.220.refs_0_.q_ref, bf16[2,512,512]{2,1,0:T(8,128)(2,1)} %copy-done, ...), custom_call_target="tpu_custom_call", output_to_operand_aliasing={{0}: (13, {})} | custom-call | tf_op jit(solution)/shard_map/attend/pallas_call | solution.py:46
  257.2 4.2 out_projection.3.own_ref
  262.6 17.7 %collective-permute-start.38 = (bf16[128,2304]{1,0:T(8,128)(2,1)S(1)}, bf16[128,2304]{1,0:T(8,128)(2,1)S(1)}, u32[]{:S(2)}, u32[]{:S(2)}) collective-permute-start(bf16[128,2304]{1,0:T(8,128)(2,1)S(1)} %slice.213), channel_id=1, source_target_pairs={{0,8},{2,10},{4,12},{6,14},{8,0},{10,2},{12,4},{14,6},{1,9},{3,11}... | collective-permute-start | bytes 1769480 | tf_op jit(solution)/shard_map/ppermute | solution.py:766
  280.8 9.8 %collective-permute-done.38.refs_4_ = bf16[128,2304]{1,0:T(8,128)(2,1)S(1)} collective-permute-done((bf16[128,2304]{1,0:T(8,128)(2,1)S(1)}, bf16[128,2304]{1,0:T(8,128)(2,1)S(1)}, u32[]{:S(2)}, u32[]{:S(2)}) %collective-permute-start.38) | collective-permute-done | bytes 589856 | tf_op jit(solution)/shard_map/ppermute | solution.py:766
  293.7 287.2 %assemble.3.gu_ref.down_ref = bf16[1024,4608]{1,0:T(8,128)(2,1)} custom-call(s32[1]{0:T(128)} %bitcast.12.part_ref, bf16[128,4608]{1,0:T(8,128)(2,1)} %copy-done.15, bf16[128,4608]{1,0:T(8,128)(2,1)} %collective-permute-done.35.refs_1_, bf16[128,4608]{1,0:T(8,128)(2,1)} %collective-permute-done.36.refs_2_, ...), custom_call_target="tpu_custom_call" | custom-call | tf_op jit(solution)/shard_map/assemble/pallas_call | solution.py:136
  580.9 18.5 %feed_forward.2 = (f32[512,1024]{1,0:T(8,128)}, bf16[1024,1024]{1,0:T(8,128)(2,1)}, bf16[1024,1536]{1,0:T(8,128)(2,1)}, bf16[1024,3072]{1,0:T(8,128)(2,1)}, bf16...) custom-call(bf16[1024,1024]{1,0:T(8,128)(2,1)} %x_ref.7, bf16[512,1024]{1,0:T(8,128)(2,1)} %out_projection.2.own_ref, ...), custom_call_target="tpu_custom_call" | custom-call | tf_op jit(solution)/shard_map/feed_forward/pallas_call | solution.py:46
  601.3 18.4 %feed_forward.3 = (f32[512,1024]{1,0:T(8,128)}, bf16[1024,1024]{1,0:T(8,128)(2,1)}, bf16[1024,1536]{1,0:T(8,128)(2,1)}, bf16[1024,3072]{1,0:T(8,128)(2,1)}, bf16...) custom-call(bf16[1024,1024]{1,0:T(8,128)(2,1)} %x_ref.7, ...), custom_call_target="tpu_custom_call", output_to_operand_aliasing={{1}: (7, {}), {2}: (8, {}), {3}: (9, {})} | custom-call | tf_op jit(solution)/shard_map/feed_forward/pallas_call | solution.py:46
  619.7 11.4 %weight_grad.3 = (bf16[512,4608]{1,0:T(8,128)(2,1)}, bf16[512,4608]{1,0:T(8,128)(2,1)}) custom-call(s32[1]{0:T(128)} %bitcast.12.part_ref, bf16[1024,1024]{1,0:T(8,128)(2,1)} %get-tuple-element.253.left_ref, bf16[1024,3072]{1,0:T(8,128)(2,1)} %get-tuple-element.254.right_ref), custom_call_target="tpu_custom_call" | custom-call | tf_op jit(solution)/shard_map/weight_grad/pallas_call | solution.py:46
  631.1 8.0 weight_grad.4
  640.3 7.1 mixed_back.2
  648.1 5.8 attend_back.6
  656.1 4.9 add_convert_fusion
  662.3 11.0 %collective-permute-start.47 = (bf16[128,2304]{1,0:T(8,128)(2,1)}, bf16[128,2304]{1,0:T(8,128)(2,1)}, u32[]{:S(2)}, u32[]{:S(2)}) collective-permute-start(bf16[128,2304]{1,0:T(8,128)(2,1)} %get-tuple-element.387), channel_id=1, source_target_pairs={{0,8},{2,10},{4,12},{6,14},{8,0},{10,2},{12,4},{14,6},{1,9},{3,11}... | collective-permute-start | bytes 1769480 | tf_op jit(solution)/shard_map/ppermute | solution.py:766
  675.5 6.8 mixed_back.3
  682.3 6.0 weight_grad.5
  688.4 10.6 %attend_back.7 = (f32[512,1024]{1,0:T(8,128)}, bf16[2,512,512]{2,1,0:T(8,128)(2,1)}, bf16[2,512,512]{2,1,0:T(8,128)(2,1)}, bf16[2,512,512]{2,1,0:T(8,128)(2,1)}) custom-call(s32[2]{0:T(128)} %pad_add_fusion.1.idx_ref, bf16[1024,1024]{1,0:T(8,128)(2,1)} %get-tuple-element.220.refs_0_.q_ref, bf16[512,1024]{1,0:T(8,128)(2,1)} %get-tuple-element.271.do_ref, ...), custom_call_target="tpu_custom_call" | custom-call | tf_op jit(solution)/shard_map/attend_back/pallas_call | solution.py:46
  698.9 6.7 collective-permute-start.52
  708.3 4.8 collective-permute-start.54
  714.7 15.1 %attend_back.8 = (f32[512,1024]{1,0:T(8,128)}, bf16[2,512,512]{2,1,0:T(8,128)(2,1)}, bf16[2,512,512]{2,1,0:T(8,128)(2,1)}) custom-call(s32[2]{0:T(128)} %pad_add_fusion.1.idx_ref, bf16[1024,1024]{1,0:T(8,128)(2,1)} %get-tuple-element.220.refs_0_.q_ref, bf16[512,1024]{1,0:T(8,128)(2,1)} %get-tuple-element.271.do_ref, ...), custom_call_target="tpu_custom_call" | custom-call | tf_op jit(solution)/shard_map/attend_back/pallas_call | solution.py:46
  733.3 9.2 collective-permute-done.50
  747.2 12.4 %attend_back.9 = (f32[1024,1024]{1,0:T(8,128)}, bf16[2,512,512]{2,1,0:T(8,128)(2,1)}, bf16[2,512,512]{2,1,0:T(8,128)(2,1)}, bf16[2,512,512]{2,1,0:T(8,128)(2,1)}...) custom-call(s32[2]{0:T(128)} %pad_add_fusion.1.idx_ref, ...), custom_call_target="tpu_custom_call" | custom-call | tf_op jit(solution)/shard_map/attend_back/pallas_call | solution.py:46
  762.2 4.1 collective-permute-start.57
  769.0 25.9 %attend_back.10 = (f32[512,1024]{1,0:T(8,128)}, bf16[2,512,512]{2,1,0:T(8,128)(2,1)}, bf16[2,512,512]{2,1,0:T(8,128)(2,1)}, bf16[2,512,512]{2,1,0:T(8,128)(2,1)}, bf16[2,512,512]{2,1,0:T(8,128)(2,1)}) custom-call(s32[2]{0:T(128)} %pad_add_fusion.1.idx_ref, bf16[1024,1024]{1,0:T(8,128)(2,1)} %get-tuple-element.220.refs_0_.q_ref, ...), custom_call_target="tpu_custom_call" | custom-call | tf_op jit(solution)/shard_map/attend_back/pallas_call | solution.py:46
  795.6 3.9 collective-permute-start.63
  799.7 19.6 %collective-permute-done.63.out_got_ref = bf16[64,1024]{1,0:T(8,128)(2,1)S(1)} collective-permute-done((bf16[64,1024]{1,0:T(8,128)(2,1)S(1)}, bf16[64,1024]{1,0:T(8,128)(2,1)S(1)}, u32[]{:S(2)}, u32[]{:S(2)}) %collective-permute-start.63) | collective-permute-done | bytes 131104 | tf_op jit(solution)/shard_map/ppermute | solution.py:766
  819.3 14.5 %collective-permute-start.66 = (bf16[512,512]{1,0:T(8,128)(2,1)S(1)}, bf16[512,512]{1,0:T(8,128)(2,1)S(1)}, u32[]{:S(2)}, u32[]{:S(2)}) collective-permute-start(bf16[512,512]{1,0:T(8,128)(2,1)S(1)} %get-tuple-element.401), channel_id=1, source_target_pairs={{0,8},{2,10},{4,12},{6,14},{8,0},{10,2},{12,4},{14,6},{1,9},{3,11}... | collective-permute-start | bytes 1572872 | tf_op jit(solution)/shard_map/ppermute | solution.py:766
  833.8 10.7 %collective-permute-start.65 = (bf16[512,512]{1,0:T(8,128)(2,1)S(1)}, bf16[512,512]{1,0:T(8,128)(2,1)S(1)}, u32[]{:S(2)}, u32[]{:S(2)}) collective-permute-start(bf16[512,512]{1,0:T(8,128)(2,1)S(1)} %get-tuple-element.402), channel_id=1, source_target_pairs={{0,4},{2,6},{4,0},{6,2},{8,12},{10,14},{12,8},{14,10},{1,5},{3,7},... | collective-permute-start | bytes 1572872 | tf_op jit(solution)/shard_map/ppermute | solution.py:766
  844.5 15.1 %attend_back.11 = (f32[1024,1024]{1,0:T(8,128)}, bf16[2,512,512]{2,1,0:T(8,128)(2,1)}, bf16[2,512,512]{2,1,0:T(8,128)(2,1)}) custom-call(s32[2]{0:T(128)} %pad_add_fusion.1.idx_ref, bf16[1024,1024]{1,0:T(8,128)(2,1)} %get-tuple-element.220.refs_0_.q_ref, bf16[512,1024]{1,0:T(8,128)(2,1)} %get-tuple-element.271.do_ref, ...), custom_call_target="tpu_custom_call", output_to_operand_aliasing={{0}: (11, {})} | custom-call | tf_op jit(solution)/shard_map/attend_back/pallas_call | solution.py:46
  867.6 12.0 %q_back.1 = (bf16[1024,1024]{1,0:T(8,128)(2,1)}, f32[1024,1024]{1,0:T(8,128)}, f32[1,128]{1,0:T(1,128)}) custom-call(f32[1024,1024]{1,0:T(8,128)} %get-tuple-element.312.dq_ref, f32[1024,1024]{1,0:T(8,128)} %get-tuple-element.313.lin_ref, f32[1,128]{1,0:T(1,128)} %reshape.121.hgain_ref.gain_ref, f32[1024,128]{1,0:T(8,128)} %get-tuple-element.426.cos_ref, ...), custom_call_target="tpu_custom_call" | custom-call | tf_op jit(solution)/shard_map/q_back/pallas_call | solution.py:46
  879.6 8.6 kv_back.2
  888.1 5.8 weight_halves.2
  896.3 8.9 kv_back.3
  911.8 5.8 weight_halves.3
  920.6 4.3 tokens_back.2
  945.2 4.0 tokens_back.3
  954.2 5.4 collective-permute-done.86
  964.3 3.8 collective-permute-done.88
  (409 shorter events, 169.8 us)
Async XLA Ops:
  31.4 20.3 %collective-permute-start.12 = (bf16[128,1024]{1,0:T(8,128)(2,1)}, bf16[128,1024]{1,0:T(8,128)(2,1)}, u32[]{:S(2)}, u32[]{:S(2)}) collective-permute-start(bf16[128,1024]{1,0:T(8,128)(2,1)} %collective-permute-done.4), channel_id=1, source_target_pairs={{0,2},{2,0},{4,6},{6,4},{8,10},{10,8},{12,14},{14,12},{1,3},{3,1},... | collective-permute-start | bytes 786440 | tf_op jit(solution)/shard_map/ppermute | solution.py:766
  31.5 21.2 %collective-permute-start.13 = (bf16[128,1024]{1,0:T(8,128)(2,1)S(1)}, bf16[128,1024]{1,0:T(8,128)(2,1)}, u32[]{:S(2)}, u32[]{:S(2)}) collective-permute-start(bf16[128,1024]{1,0:T(8,128)(2,1)S(1)} %collective-permute-done.2), channel_id=1, source_target_pairs={{0,2},{2,0},{4,6},{6,4},{8,10},{10,8},{12,14},{14,12},{1,3},{3,1},... | collective-permute-start | bytes 786440 | tf_op jit(solution)/shard_map/ppermute | solution.py:766
  34.5 19.1 %collective-permute-start.14 = (bf16[128,1024]{1,0:T(8,128)(2,1)}, bf16[128,1024]{1,0:T(8,128)(2,1)}, u32[]{:S(2)}, u32[]{:S(2)}) collective-permute-start(bf16[128,1024]{1,0:T(8,128)(2,1)} %get-tuple-element.416), channel_id=1, source_target_pairs={{0,2},{2,0},{4,6},{6,4},{8,10},{10,8},{12,14},{14,12},{1,3},{3,1},... | collective-permute-start | bytes 786440 | tf_op jit(solution)/shard_map/ppermute | solution.py:766
  37.3 25.1 %collective-permute-start.16 = (bf16[128,2048]{1,0:T(8,128)(2,1)}, bf16[128,2048]{1,0:T(8,128)(2,1)}, u32[]{:S(2)}, u32[]{:S(2)}) collective-permute-start(bf16[128,2048]{1,0:T(8,128)(2,1)} %get-tuple-element.412), channel_id=1, source_target_pairs={{0,8},{2,10},{4,12},{6,14},{8,0},{10,2},{12,4},{14,6},{1,9},{3,11}... | collective-permute-start | bytes 1572872 | tf_op jit(solution)/shard_map/ppermute | solution.py:766
  38.9 23.6 %collective-permute-start.15 = (bf16[128,2048]{1,0:T(8,128)(2,1)}, bf16[128,2048]{1,0:T(8,128)(2,1)}, u32[]{:S(2)}, u32[]{:S(2)}) collective-permute-start(bf16[128,2048]{1,0:T(8,128)(2,1)} %get-tuple-element.412), channel_id=1, source_target_pairs={{0,4},{2,6},{4,0},{6,2},{8,12},{10,14},{12,8},{14,10},{1,5},{3,7},... | collective-permute-start | bytes 1572872 | tf_op jit(solution)/shard_map/ppermute | solution.py:766
  51.7 23.4 %collective-permute-start.19 = (bf16[128,2048]{1,0:T(8,128)(2,1)}, bf16[128,2048]{1,0:T(8,128)(2,1)S(1)}, u32[]{:S(2)}, u32[]{:S(2)}) collective-permute-start(bf16[128,2048]{1,0:T(8,128)(2,1)} %get-tuple-element.412), channel_id=1, source_target_pairs={{0,2},{2,0},{4,6},{6,4},{8,10},{10,8},{12,14},{14,12},{1,3},{3,1},... | collective-permute-start | bytes 1572872 | tf_op jit(solution)/shard_map/ppermute | solution.py:766
  61.5 50.4 %collective-permute-start.23 = (bf16[2,512,512]{2,1,0:T(8,128)(2,1)}, bf16[2,512,512]{2,1,0:T(8,128)(2,1)S(1)}, u32[]{:S(2)}, u32[]{:S(2)}) collective-permute-start(bf16[2,512,512]{2,1,0:T(8,128)(2,1)} %get-tuple-element.207.refs_1_.refs_0_), channel_id=1, source_target_pairs={{0,4},{2,6},{4,0},{6,2},{8,12},{10,14},{12,8},{14,10},{1,5},{3,7},... | collective-permute-start | bytes 3145736 | tf_op jit(solution)/shard_map/ppermute | solution.py:766
  62.0 63.3 %collective-permute-start.24 = (bf16[2,512,512]{2,1,0:T(8,128)(2,1)}, bf16[2,512,512]{2,1,0:T(8,128)(2,1)S(1)}, u32[]{:S(2)}, u32[]{:S(2)}) collective-permute-start(bf16[2,512,512]{2,1,0:T(8,128)(2,1)} %get-tuple-element.207.refs_1_.refs_0_), channel_id=1, source_target_pairs={{0,8},{2,10},{4,12},{6,14},{8,0},{10,2},{12,4},{14,6},{1,9},{3,11}... | collective-permute-start | bytes 3145736 | tf_op jit(solution)/shard_map/ppermute | solution.py:766
  63.4 29.7 %collective-permute-start.18 = (bf16[128,1024]{1,0:T(8,128)(2,1)S(1)}, bf16[128,1024]{1,0:T(8,128)(2,1)S(1)}, u32[]{:S(2)}, u32[]{:S(2)}) collective-permute-start(bf16[128,1024]{1,0:T(8,128)(2,1)S(1)} %slice.207), channel_id=1, source_target_pairs={{0,8},{2,10},{4,12},{6,14},{8,0},{10,2},{12,4},{14,6},{1,9},{3,11}... | collective-permute-start | bytes 786440 | tf_op jit(solution)/shard_map/ppermute | solution.py:766
  66.0 27.1 %collective-permute-start.17 = (bf16[128,1024]{1,0:T(8,128)(2,1)S(1)}, bf16[128,1024]{1,0:T(8,128)(2,1)S(1)}, u32[]{:S(2)}, u32[]{:S(2)}) collective-permute-start(bf16[128,1024]{1,0:T(8,128)(2,1)S(1)} %slice.206), channel_id=1, source_target_pairs={{0,4},{2,6},{4,0},{6,2},{8,12},{10,14},{12,8},{14,10},{1,5},{3,7},... | collective-permute-start | bytes 786440 | tf_op jit(solution)/shard_map/ppermute | solution.py:766
  75.1 24.9 %collective-permute-start.21 = (bf16[128,2048]{1,0:T(8,128)(2,1)}, bf16[128,2048]{1,0:T(8,128)(2,1)S(1)}, u32[]{:S(2)}, u32[]{:S(2)}) collective-permute-start(bf16[128,2048]{1,0:T(8,128)(2,1)} %collective-permute-done.16), channel_id=1, source_target_pairs={{0,2},{2,0},{4,6},{6,4},{8,10},{10,8},{12,14},{14,12},{1,3},{3,1},... | collective-permute-start | bytes 1572872 | tf_op jit(solution)/shard_map/ppermute | solution.py:766
  96.5 28.8 %collective-permute-start.6 = (bf16[64,4608]{1,0:T(8,128)(2,1)S(1)}, bf16[64,4608]{1,0:T(8,128)(2,1)S(1)}, u32[]{:S(2)}, u32[]{:S(2)}) collective-permute-start(bf16[64,4608]{1,0:T(8,128)(2,1)S(1)} %copy-done.32), channel_id=1, source_target_pairs={{0,16},{16,0},{1,17},{17,1},{2,18},{18,2},{3,19},{19,3},{4,20},{20... | collective-permute-start | bytes 1769480 | tf_op jit(solution)/shard_map/ppermute | solution.py:766
  100.0 27.5 %collective-permute-start.25 = (bf16[2,512,512]{2,1,0:T(8,128)(2,1)S(1)}, bf16[2,512,512]{2,1,0:T(8,128)(2,1)S(1)}, u32[]{:S(2)}, u32[]{:S(2)}) collective-permute-start(bf16[2,512,512]{2,1,0:T(8,128)(2,1)S(1)} %copy-done.5), channel_id=1, source_target_pairs={{0,2},{2,0},{4,6},{6,4},{8,10},{10,8},{12,14},{14,12},{1,3},{3,1},... | collective-permute-start | bytes 3145736 | tf_op jit(solution)/shard_map/ppermute | solution.py:766
  141.0 69.5 %collective-permute-start.28 = (bf16[2,512,512]{2,1,0:T(8,128)(2,1)S(1)}, bf16[2,512,512]{2,1,0:T(8,128)(2,1)}, u32[]{:S(2)}, u32[]{:S(2)}) collective-permute-start(bf16[2,512,512]{2,1,0:T(8,128)(2,1)S(1)} %pad_maximum_fusion.2.refs_7_.refs_5_.refs_0_), channel_id=1, source_target_pairs={{0,2},{2,0},{4,6},{6,4},{8,10},{10,8},{12,14},{14,12},{1,3},{3,1},... | collective-permute-start | bytes 3145736 | tf_op jit(solution)/shard_map/ppermute | solution.py:766
  141.1 70.5 %collective-permute-start.30 = (bf16[2,512,512]{2,1,0:T(8,128)(2,1)S(1)}, bf16[2,512,512]{2,1,0:T(8,128)(2,1)}, u32[]{:S(2)}, u32[]{:S(2)}) collective-permute-start(bf16[2,512,512]{2,1,0:T(8,128)(2,1)S(1)} %collective-permute-done.24.refs_4_.refs_2_.refs_3_.refs_1_), channel_id=1, source_target_pairs={{0,2},{2,0},{4,6},{6,4},{8,10},{10,8},{12,14},{14,12},{1,3},{3,1},... | collective-permute-start | bytes 3145736 | tf_op jit(solution)/shard_map/ppermute | solution.py:766
  141.6 70.0 %collective-permute-start.29 = (bf16[2,512,512]{2,1,0:T(8,128)(2,1)S(1)}, bf16[2,512,512]{2,1,0:T(8,128)(2,1)}, u32[]{:S(2)}, u32[]{:S(2)}) collective-permute-start(bf16[2,512,512]{2,1,0:T(8,128)(2,1)S(1)} %collective-permute-done.23.refs_3_.refs_1_.refs_2_.refs_0_), channel_id=1, source_target_pairs={{0,2},{2,0},{4,6},{6,4},{8,10},{10,8},{12,14},{14,12},{1,3},{3,1},... | collective-permute-start | bytes 3145736 | tf_op jit(solution)/shard_map/ppermute | solution.py:766
  141.7 82.6 %collective-permute-start.31 = (bf16[2,512,512]{2,1,0:T(8,128)(2,1)}, bf16[2,512,512]{2,1,0:T(8,128)(2,1)}, u32[]{:S(2)}, u32[]{:S(2)}) collective-permute-start(bf16[2,512,512]{2,1,0:T(8,128)(2,1)} %get-tuple-element.232.refs_3_.refs_0_), channel_id=1, source_target_pairs={{0,4},{2,6},{4,8},{6,10},{8,12},{10,14},{1,5},{3,7},{5,9},{7,11},{... | collective-permute-start | bytes 3145736 | tf_op jit(solution)/shard_map/ppermute | solution.py:771
  145.1 83.7 %collective-permute-start.35 = (bf16[128,4608]{1,0:T(8,128)(2,1)}, bf16[128,4608]{1,0:T(8,128)(2,1)}, u32[]{:S(2)}, u32[]{:S(2)}) collective-permute-start(bf16[128,4608]{1,0:T(8,128)(2,1)} %copy-done.15), channel_id=1, source_target_pairs={{0,8},{2,10},{4,12},{6,14},{8,0},{10,2},{12,4},{14,6},{1,9},{3,11}... | collective-permute-start | bytes 3538952 | tf_op jit(solution)/shard_map/ppermute | solution.py:766
  210.5 51.0 %collective-permute-start.36 = (bf16[128,4608]{1,0:T(8,128)(2,1)}, bf16[128,4608]{1,0:T(8,128)(2,1)}, u32[]{:S(2)}, u32[]{:S(2)}) collective-permute-start(bf16[128,4608]{1,0:T(8,128)(2,1)} %copy-done.15), channel_id=1, source_target_pairs={{0,4},{2,6},{4,0},{6,2},{8,12},{10,14},{12,8},{14,10},{1,5},{3,7},... | collective-permute-start | bytes 3538952 | tf_op jit(solution)/shard_map/ppermute | solution.py:766
  228.1 29.1 %collective-permute-start.33 = (bf16[512,1024]{1,0:T(8,128)(2,1)S(1)}, bf16[512,1024]{1,0:T(8,128)(2,1)S(1)}, u32[]{:S(2)}, u32[]{:S(2)}) collective-permute-start(bf16[512,1024]{1,0:T(8,128)(2,1)S(1)} %copy-done.14), channel_id=1, source_target_pairs={{0,1},{1,0},{2,3},{3,2},{4,5},{5,4},{6,7},{7,6},{8,9},{9,8},{10,11... | collective-permute-start | bytes 3145736 | tf_op jit(solution)/shard_map/ppermute | solution.py:766
  228.8 62.5 %collective-permute-start.39 = (bf16[128,4608]{1,0:T(8,128)(2,1)S(1)}, bf16[128,4608]{1,0:T(8,128)(2,1)}, u32[]{:S(2)}, u32[]{:S(2)}) collective-permute-start(bf16[128,4608]{1,0:T(8,128)(2,1)S(1)} %copy-done.16), channel_id=1, source_target_pairs={{0,2},{2,0},{4,6},{6,4},{8,10},{10,8},{12,14},{14,12},{1,3},{3,1},... | collective-permute-start | bytes 3538952 | tf_op jit(solution)/shard_map/ppermute | solution.py:766
  229.9 62.3 %collective-permute-start.40 = (bf16[128,4608]{1,0:T(8,128)(2,1)}, bf16[128,4608]{1,0:T(8,128)(2,1)}, u32[]{:S(2)}, u32[]{:S(2)}) collective-permute-start(bf16[128,4608]{1,0:T(8,128)(2,1)} %collective-permute-done.35.refs_1_), channel_id=1, source_target_pairs={{0,2},{2,0},{4,6},{6,4},{8,10},{10,8},{12,14},{14,12},{1,3},{3,1},... | collective-permute-start | bytes 3538952 | tf_op jit(solution)/shard_map/ppermute | solution.py:766
  230.5 49.8 %collective-permute-start.37 = (bf16[128,2304]{1,0:T(8,128)(2,1)S(1)}, bf16[128,2304]{1,0:T(8,128)(2,1)}, u32[]{:S(2)}, u32[]{:S(2)}) collective-permute-start(bf16[128,2304]{1,0:T(8,128)(2,1)S(1)} %slice.212), channel_id=1, source_target_pairs={{0,4},{2,6},{4,0},{6,2},{8,12},{10,14},{12,8},{14,10},{1,5},{3,7},... | collective-permute-start | bytes 1769480 | tf_op jit(solution)/shard_map/ppermute | solution.py:766
  262.6 28.0 %collective-permute-start.38 = (bf16[128,2304]{1,0:T(8,128)(2,1)S(1)}, bf16[128,2304]{1,0:T(8,128)(2,1)S(1)}, u32[]{:S(2)}, u32[]{:S(2)}) collective-permute-start(bf16[128,2304]{1,0:T(8,128)(2,1)S(1)} %slice.213), channel_id=1, source_target_pairs={{0,8},{2,10},{4,12},{6,14},{8,0},{10,2},{12,4},{14,6},{1,9},{3,11}... | collective-permute-start | bytes 1769480 | tf_op jit(solution)/shard_map/ppermute | solution.py:766
  291.3 309.0 %collective-permute-start.34 = (bf16[512,1024]{1,0:T(8,128)(2,1)}, bf16[512,1024]{1,0:T(8,128)(2,1)S(1)}, u32[]{:S(2)}, u32[]{:S(2)}) collective-permute-start(bf16[512,1024]{1,0:T(8,128)(2,1)} %out_projection.3.own_ref), channel_id=1, source_target_pairs={{0,1},{1,0},{2,3},{3,2},{4,5},{5,4},{6,7},{7,6},{8,9},{9,8},{10,11... | collective-permute-start | bytes 3145736 | tf_op jit(solution)/shard_map/ppermute | solution.py:766
  599.4 31.7 %collective-permute-start.45 = (bf16[512,1024]{1,0:T(8,128)(2,1)}, bf16[512,1024]{1,0:T(8,128)(2,1)S(1)}, u32[]{:S(2)}, u32[]{:S(2)}) collective-permute-start(bf16[512,1024]{1,0:T(8,128)(2,1)} %get-tuple-element.242.own_ref), channel_id=1, source_target_pairs={{0,1},{1,0},{2,3},{3,2},{4,5},{5,4},{6,7},{7,6},{8,9},{9,8},{10,11... | collective-permute-start | bytes 3145736 | tf_op jit(solution)/shard_map/ppermute | solution.py:766
  639.1 35.3 %collective-permute-start.44 = (bf16[512,1024]{1,0:T(8,128)(2,1)S(1)}, bf16[512,1024]{1,0:T(8,128)(2,1)S(1)}, u32[]{:S(2)}, u32[]{:S(2)}) collective-permute-start(bf16[512,1024]{1,0:T(8,128)(2,1)S(1)} %copy-done.21), channel_id=1, source_target_pairs={{0,1},{1,0},{2,3},{3,2},{4,5},{5,4},{6,7},{7,6},{8,9},{9,8},{10,11... | collective-permute-start | bytes 3145736 | tf_op jit(solution)/shard_map/ppermute | solution.py:766
  662.3 43.4 %collective-permute-start.47 = (bf16[128,2304]{1,0:T(8,128)(2,1)}, bf16[128,2304]{1,0:T(8,128)(2,1)}, u32[]{:S(2)}, u32[]{:S(2)}) collective-permute-start(bf16[128,2304]{1,0:T(8,128)(2,1)} %get-tuple-element.387), channel_id=1, source_target_pairs={{0,8},{2,10},{4,12},{6,14},{8,0},{10,2},{12,4},{14,6},{1,9},{3,11}... | collective-permute-start | bytes 1769480 | tf_op jit(solution)/shard_map/ppermute | solution.py:766
  673.3 32.4 %collective-permute-start.48 = (bf16[128,2304]{1,0:T(8,128)(2,1)}, bf16[128,2304]{1,0:T(8,128)(2,1)}, u32[]{:S(2)}, u32[]{:S(2)}) collective-permute-start(bf16[128,2304]{1,0:T(8,128)(2,1)} %get-tuple-element.385), channel_id=1, source_target_pairs={{0,4},{2,6},{4,0},{6,2},{8,12},{10,14},{12,8},{14,10},{1,5},{3,7},... | collective-permute-start | bytes 1769480 | tf_op jit(solution)/shard_map/ppermute | solution.py:766
  674.4 121.2 %collective-permute-start.59 = (bf16[512,1024]{1,0:T(8,128)(2,1)}, bf16[512,1024]{1,0:T(8,128)(2,1)}, u32[]{:S(2)}, u32[]{:S(2)}) collective-permute-start(bf16[512,1024]{1,0:T(8,128)(2,1)} %get-tuple-element.308.own_ref), channel_id=1, source_target_pairs={{0,1},{1,0},{2,3},{3,2},{4,5},{5,4},{6,7},{7,6},{8,9},{9,8},{10,11... | collective-permute-start | bytes 3145736 | tf_op jit(solution)/shard_map/ppermute | solution.py:766
  688.3 24.7 %collective-permute-start.49 = (bf16[512,1024]{1,0:T(8,128)(2,1)}, bf16[512,1024]{1,0:T(8,128)(2,1)}, u32[]{:S(2)}, u32[]{:S(2)}) collective-permute-start(bf16[512,1024]{1,0:T(8,128)(2,1)} %get-tuple-element.278), channel_id=1, source_target_pairs={{0,2},{2,0},{4,6},{6,4},{8,10},{10,8},{12,14},{14,12},{1,3},{3,1},... | collective-permute-start | bytes 3145736 | tf_op jit(solution)/shard_map/ppermute | solution.py:766
  698.9 30.9 %collective-permute-start.52 = (bf16[2,512,512]{2,1,0:T(8,128)(2,1)}, bf16[2,512,512]{2,1,0:T(8,128)(2,1)S(1)}, u32[]{:S(2)}, u32[]{:S(2)}) collective-permute-start(bf16[2,512,512]{2,1,0:T(8,128)(2,1)} %get-tuple-element.288), channel_id=1, source_target_pairs={{0,2},{2,0},{4,6},{6,4},{8,10},{10,8},{12,14},{14,12},{1,3},{3,1},... | collective-permute-start | bytes 3145736 | tf_op jit(solution)/shard_map/ppermute | solution.py:766
  707.2 54.9 %collective-permute-start.53 = (bf16[128,4608]{1,0:T(8,128)(2,1)S(1)}, bf16[128,4608]{1,0:T(8,128)(2,1)}, u32[]{:S(2)}, u32[]{:S(2)}) collective-permute-start(bf16[128,4608]{1,0:T(8,128)(2,1)S(1)} %pad_maximum_fusion), channel_id=1, source_target_pairs={{0,4},{2,6},{4,0},{6,2},{8,12},{10,14},{12,8},{14,10},{1,5},{3,7},... | collective-permute-start | bytes 3538952 | tf_op jit(solution)/shard_map/ppermute | solution.py:766
  708.3 58.0 %collective-permute-start.54 = (bf16[128,4608]{1,0:T(8,128)(2,1)S(1)}, bf16[128,4608]{1,0:T(8,128)(2,1)}, u32[]{:S(2)}, u32[]{:S(2)}) collective-permute-start(bf16[128,4608]{1,0:T(8,128)(2,1)S(1)} %pad_maximum_fusion.1), channel_id=1, source_target_pairs={{0,8},{2,10},{4,12},{6,14},{8,0},{10,2},{12,4},{14,6},{1,9},{3,11}... | collective-permute-start | bytes 3538952 | tf_op jit(solution)/shard_map/ppermute | solution.py:766
  742.6 17.1 %collective-permute-start.55 = (bf16[128,1024]{1,0:T(8,128)(2,1)S(1)}, bf16[128,1024]{1,0:T(8,128)(2,1)S(1)}, u32[]{:S(2)}, u32[]{:S(2)}) collective-permute-start(bf16[128,1024]{1,0:T(8,128)(2,1)S(1)} %pad_maximum_fusion.8), channel_id=1, source_target_pairs={{0,4},{2,6},{4,0},{6,2},{8,12},{10,14},{12,8},{14,10},{1,5},{3,7},... | collective-permute-start | bytes 786440 | tf_op jit(solution)/shard_map/ppermute | solution.py:766
  759.7 39.8 %collective-permute-start.58 = (bf16[512,1024]{1,0:T(8,128)(2,1)}, bf16[512,1024]{1,0:T(8,128)(2,1)}, u32[]{:S(2)}, u32[]{:S(2)}) collective-permute-start(bf16[512,1024]{1,0:T(8,128)(2,1)} %get-tuple-element.306.own_ref), channel_id=1, source_target_pairs={{0,1},{1,0},{2,3},{3,2},{4,5},{5,4},{6,7},{7,6},{8,9},{9,8},{10,11... | collective-permute-start | bytes 3145736 | tf_op jit(solution)/shard_map/ppermute | solution.py:766
  760.7 73.1 %collective-permute-start.60 = (bf16[2,512,512]{2,1,0:T(8,128)(2,1)}, bf16[2,512,512]{2,1,0:T(8,128)(2,1)S(1)}, u32[]{:S(2)}, u32[]{:S(2)}) collective-permute-start(bf16[2,512,512]{2,1,0:T(8,128)(2,1)} %add_convert_fusion.5), channel_id=1, source_target_pairs={{4,0},{6,2},{8,4},{10,6},{12,8},{14,10},{5,1},{7,3},{9,5},{11,7},{... | collective-permute-start | bytes 3145736 | tf_op jit(solution)/shard_map/ppermute | solution.py:771
  794.9 64.7 %collective-permute-start.64 = (bf16[2,512,512]{2,1,0:T(8,128)(2,1)}, bf16[2,512,512]{2,1,0:T(8,128)(2,1)S(1)}, u32[]{:S(2)}, u32[]{:S(2)}) collective-permute-start(bf16[2,512,512]{2,1,0:T(8,128)(2,1)} %get-tuple-element.318), channel_id=1, source_target_pairs={{0,2},{2,0},{4,6},{6,4},{8,10},{10,8},{12,14},{14,12},{1,3},{3,1},... | collective-permute-start | bytes 3145736 | tf_op jit(solution)/shard_map/ppermute | solution.py:766
  795.4 64.3 %collective-permute-start.61 = (bf16[2,512,512]{2,1,0:T(8,128)(2,1)}, bf16[2,512,512]{2,1,0:T(8,128)(2,1)S(1)}, u32[]{:S(2)}, u32[]{:S(2)}) collective-permute-start(bf16[2,512,512]{2,1,0:T(8,128)(2,1)} %get-tuple-element.315), channel_id=1, source_target_pairs={{0,2},{2,0},{4,6},{6,4},{8,10},{10,8},{12,14},{14,12},{1,3},{3,1},... | collective-permute-start | bytes 3145736 | tf_op jit(solution)/shard_map/ppermute | solution.py:766
  795.6 23.7 %collective-permute-start.63 = (bf16[64,1024]{1,0:T(8,128)(2,1)S(1)}, bf16[64,1024]{1,0:T(8,128)(2,1)S(1)}, u32[]{:S(2)}, u32[]{:S(2)}) collective-permute-start(bf16[64,1024]{1,0:T(8,128)(2,1)S(1)} %slice.277), channel_id=1, source_target_pairs={{0,16},{16,0},{1,17},{17,1},{2,18},{18,2},{3,19},{19,3},{4,20},{20... | collective-permute-start | bytes 393224 | tf_op jit(solution)/shard_map/ppermute | solution.py:766
  799.5 60.0 %collective-permute-start.62 = (bf16[64,4608]{1,0:T(8,128)(2,1)S(1)}, bf16[64,4608]{1,0:T(8,128)(2,1)S(1)}, u32[]{:S(2)}, u32[]{:S(2)}) collective-permute-start(bf16[64,4608]{1,0:T(8,128)(2,1)S(1)} %slice.276), channel_id=1, source_target_pairs={{0,16},{16,0},{1,17},{17,1},{2,18},{18,2},{3,19},{19,3},{4,20},{20... | collective-permute-start | bytes 1769480 | tf_op jit(solution)/shard_map/ppermute | solution.py:766
  819.3 40.4 %collective-permute-start.66 = (bf16[512,512]{1,0:T(8,128)(2,1)S(1)}, bf16[512,512]{1,0:T(8,128)(2,1)S(1)}, u32[]{:S(2)}, u32[]{:S(2)}) collective-permute-start(bf16[512,512]{1,0:T(8,128)(2,1)S(1)} %get-tuple-element.401), channel_id=1, source_target_pairs={{0,8},{2,10},{4,12},{6,14},{8,0},{10,2},{12,4},{14,6},{1,9},{3,11}... | collective-permute-start | bytes 1572872 | tf_op jit(solution)/shard_map/ppermute | solution.py:766
  833.8 25.9 %collective-permute-start.65 = (bf16[512,512]{1,0:T(8,128)(2,1)S(1)}, bf16[512,512]{1,0:T(8,128)(2,1)S(1)}, u32[]{:S(2)}, u32[]{:S(2)}) collective-permute-start(bf16[512,512]{1,0:T(8,128)(2,1)S(1)} %get-tuple-element.402), channel_id=1, source_target_pairs={{0,4},{2,6},{4,0},{6,2},{8,12},{10,14},{12,8},{14,10},{1,5},{3,7},... | collective-permute-start | bytes 1572872 | tf_op jit(solution)/shard_map/ppermute | solution.py:766
  859.6 35.1 %collective-permute-start.67 = (bf16[2,512,512]{2,1,0:T(8,128)(2,1)}, bf16[2,512,512]{2,1,0:T(8,128)(2,1)S(1)}, u32[]{:S(2)}, u32[]{:S(2)}) collective-permute-start(bf16[2,512,512]{2,1,0:T(8,128)(2,1)} %get-tuple-element.334), channel_id=1, source_target_pairs={{0,2},{2,0},{4,6},{6,4},{8,10},{10,8},{12,14},{14,12},{1,3},{3,1},... | collective-permute-start | bytes 3145736 | tf_op jit(solution)/shard_map/ppermute | solution.py:766
  865.2 29.5 %collective-permute-start.68 = (bf16[2,512,512]{2,1,0:T(8,128)(2,1)}, bf16[2,512,512]{2,1,0:T(8,128)(2,1)S(1)}, u32[]{:S(2)}, u32[]{:S(2)}) collective-permute-start(bf16[2,512,512]{2,1,0:T(8,128)(2,1)} %get-tuple-element.322), channel_id=1, source_target_pairs={{0,4},{2,6},{4,0},{6,2},{8,12},{10,14},{12,8},{14,10},{1,5},{3,7},... | collective-permute-start | bytes 3145736 | tf_op jit(solution)/shard_map/ppermute | solution.py:766
  865.3 29.5 %collective-permute-start.69 = (bf16[2,512,512]{2,1,0:T(8,128)(2,1)}, bf16[2,512,512]{2,1,0:T(8,128)(2,1)S(1)}, u32[]{:S(2)}, u32[]{:S(2)}) collective-permute-start(bf16[2,512,512]{2,1,0:T(8,128)(2,1)} %get-tuple-element.335), channel_id=1, source_target_pairs={{0,8},{2,10},{4,12},{6,14},{8,0},{10,2},{12,4},{14,6},{1,9},{3,11}... | collective-permute-start | bytes 3145736 | tf_op jit(solution)/shard_map/ppermute | solution.py:766
  894.2 26.3 %collective-permute-start.72 = (bf16[512,1024]{1,0:T(8,128)(2,1)}, bf16[512,1024]{1,0:T(8,128)(2,1)}, u32[]{:S(2)}, u32[]{:S(2)}) collective-permute-start(bf16[512,1024]{1,0:T(8,128)(2,1)} %get-tuple-element.329.own_ref), channel_id=1, source_target_pairs={{0,1},{1,0},{2,3},{3,2},{4,5},{5,4},{6,7},{7,6},{8,9},{9,8},{10,11... | collective-permute-start | bytes 3145736 | tf_op jit(solution)/shard_map/ppermute | solution.py:766
  910.1 35.0 %collective-permute-start.79 = (bf16[512,1024]{1,0:T(8,128)(2,1)S(1)}, bf16[512,1024]{1,0:T(8,128)(2,1)}, u32[]{:S(2)}, u32[]{:S(2)}) collective-permute-start(bf16[512,1024]{1,0:T(8,128)(2,1)S(1)} %copy-done.50), channel_id=1, source_target_pairs={{0,1},{1,0},{2,3},{3,2},{4,5},{5,4},{6,7},{7,6},{8,9},{9,8},{10,11... | collective-permute-start | bytes 3145736 | tf_op jit(solution)/shard_map/ppermute | solution.py:766
  (101 other events, 1023.6 us)

commit v4 on v2

--- a/solution.py
+++ b/solution.py
@@ -96,24 +96,24 @@
         q_ref[:, cols] = (turned * (SCALE * LOG2E)).astype(BF)
 
 
-def pack_kernel(chunk, key_ref, value_ref, out_ref, gate_ref, up_ref, down_ref, kv_ref, rest_ref):
+def pack_kernel(chunk, key_ref, value_ref, out_ref, down_ref, gate_ref, up_ref, kv_ref, od_ref, gu_ref):
     k_cols, o_cols, units = key_ref.shape[1], out_ref.shape[1], gate_ref.shape[1]
     kv_ref[:, :k_cols] = key_ref[...]
     kv_ref[:, k_cols:] = value_ref[...]
-    rest_ref[:, :o_cols] = out_ref[...]
+    od_ref[:, :o_cols] = out_ref[...]
+    od_ref[:, o_cols:] = down_ref[...]
     for at in range(0, units, chunk):
-        to = o_cols + 2 * at
-        rest_ref[:, to : to + chunk] = gate_ref[:, at : at + chunk]
-        rest_ref[:, to + chunk : to + 2 * chunk] = up_ref[:, at : at + chunk]
-    rest_ref[:, o_cols + 2 * units :] = down_ref[...]
+        gu_ref[:, 2 * at : 2 * at + chunk] = gate_ref[:, at : at + chunk]
+        gu_ref[:, 2 * at + chunk : 2 * at + 2 * chunk] = up_ref[:, at : at + chunk]
 
 
 def pack(chunk, *weights):
-    wide, k_cols = weights[0].shape
-    width = weights[2].shape[1] + 3 * weights[3].shape[1]
+    cols = [w.shape[1] for w in weights]
+    wide = weights[0].shape[0]
     whole = lambda f: (0, 0)
     ins = [(w, w.shape, whole) for w in weights]
-    outs = [(shaped((wide, cols), BF), (wide, cols), whole) for cols in (2 * k_cols, width)]
+    sums = (cols[0] + cols[1], cols[2] + cols[3], cols[4] + cols[5])
+    outs = [(shaped((wide, width), BF), (wide, width), whole) for width in sums]
     return call(functools.partial(pack_kernel, chunk), "pack", (1,), ins, outs)
 
 
@@ -413,17 +413,17 @@
         back_ref[...] = back_acc[...].astype(BF)
 
 
-def feed_forward(half, x, own, got, gain, dy, w_rest, o_cols, chunk, whole=None):
+def feed_forward(half, x, own, got, gain, dy, w_od, w_gu, chunk, whole=None):
     rows, model = own.shape
-    units = (w_rest.shape[1] - o_cols) // 3
+    units = w_gu.shape[1] // 2
     steps = units // chunk
     mine, once = lambda f: (half, 0), lambda f: (0, 0)
-    at_gu, at_down = o_cols // (2 * chunk), (o_cols + 2 * units) // chunk
+    at_down = (w_od.shape[1] - units) // chunk
     block = (rows, model)
     ins = [
         (x, block, mine), (own, block, once), (got, block, once), (gain, (1, model), once), (dy, block, mine),
-        (w_rest, (model, 2 * chunk), lambda f: (0, at_gu + f)),
-        (w_rest, (model, chunk), lambda f: (0, at_down + f)),
+        (w_gu, (model, 2 * chunk), lambda f: (0, f)),
+        (w_od, (model, chunk), lambda f: (0, at_down + f)),
     ]
     keep = {}
     if whole is not None:
@@ -446,6 +446,21 @@
     unit = values * scale
     inner = grad * gain
     return scale * (inner - unit * jnp.mean(inner * unit, axis=-1, keepdims=True)), grad * unit
+
+
+def lane_mean(values):
+    width = values.shape[-1]
+    ones = jnp.ones((width, width), BF)
+    high = values.astype(BF)
+    low = (values - high.astype(F32)).astype(BF)
+    return (mm(high, ones) + mm(low, ones)) * (1.0 / width)
+
+
+def head_norm_back(grad, values, gain):
+    scale = lax.rsqrt(lane_mean(values * values) + EPSILON)
+    unit = values * scale
+    inner = grad * gain
+    return scale * (inner - unit * lane_mean(inner * unit)), grad * unit
 
 
 def row_blocks(rows):
@@ -564,7 +579,7 @@
     total = jnp.zeros(cos.shape, F32)
     for h in range(heads):
         cols = slice(h * HEAD_SIZE, (h + 1) * HEAD_SIZE)
-        grad, summand = norm_back(turn_back(dq_ref[:, cols], cos, sin), lin_ref[:, cols], gain_ref[...])
+        grad, summand = head_norm_back(turn_back(dq_ref[:, cols], cos, sin), lin_ref[:, cols], gain_ref[...])
         d_ref[:, cols] = grad.astype(BF)
         total = total + summand
     part_ref[...] = mm(d_ref[...], w_ref[...], NT)
@@ -605,7 +620,7 @@
     gains = jnp.zeros(cos.shape, F32)
     for h in range(heads):
         cols = slice(h * HEAD_SIZE, (h + 1) * HEAD_SIZE)
-        grad, summand = norm_back(
+        grad, summand = head_norm_back(
             turn_back(total(key_refs, 0, cols), cos, sin), lin_ref[:, cols], gain_ref[...]
         )
         d_ref[:, cols] = grad.astype(BF)
@@ -776,18 +791,22 @@
     def gather_first(piece, *gate):
         return jnp.concatenate([piece, after(swap(piece, "shard", 1), *gate)]) if ctx_size == 8 else piece
 
-    def gather_rows(one, gates=((),) * 3):
+    def gather_near(one, *gate):
         if ctx_size != 8:
             for axis, bit in bits:
                 one = jnp.concatenate([one, swap(one, axis, bit)])
-            return one, (one,) * 3
-        by_x, by_y = (after(v, *gates[0]) for v in (swap(one, "ctx", 2), swap(one, "ctx", 4)))
+            return [one]
+        by_x, by_y = (after(v, *gate) for v in (swap(one, "ctx", 2), swap(one, "ctx", 4)))
         cut = one.shape[1] // 2
-        left, right = swap(by_y[:, :cut], "ctx", 2), swap(by_x[:, cut:], "ctx", 4)
-        far = jnp.concatenate([after(left, *gates[1]), after(right, *gates[1])], axis=1)
-        half = jnp.concatenate([one, by_x, by_y, far])
-        whole = jnp.concatenate([half, after(swap(half, "ctx", 1), *gates[2])])
-        return whole, (by_x, half, whole)
+        return [one, by_x, by_y, swap(by_y[:, :cut], "ctx", 2), swap(by_x[:, cut:], "ctx", 4)]
+
+    def gather_far(pieces, *gate):
+        if ctx_size != 8:
+            return pieces[0], pieces[0]
+        *near, left, right = pieces
+        far = jnp.concatenate([after(left, *gate), after(right, *gate)], axis=1)
+        near = [*near, far]
+        return jnp.concatenate(near + [after(swap(piece, "ctx", 1), *gate) for piece in near]), far
 
     def scatter_rows(low, high, late):
         total = add_low(low, after(swap(high, "ctx", 1), late))
@@ -818,16 +837,19 @@
         total, size = total.astype(BF), total.shape[0] // 2
         return total, swap(total[size:], "shard", 1)
 
-    kv_piece, rest_piece = pack(chunk, key_weight, value_weight, w_out.T, w_gate, w_up, w_down.T)
+    kv_piece, od_piece, gu_piece = pack(
+        chunk, key_weight, value_weight, w_out.T, w_down.T, w_gate, w_up
+    )
     kv_one = gather_first(kv_piece)
-    w_kv, stages = gather_rows(kv_one)
-    q_one = gather_first(after(w_query, kv_one), stages[1])
-    w_rest = lax.all_gather(rest_piece, weight_axes, axis=0, tiled=True)
+    kv_near = gather_near(kv_one)
+    w_kv, kv_far = gather_far(kv_near)
+    q_one = gather_first(after(w_query, kv_one), kv_far)
+    w_od = lax.all_gather(od_piece, weight_axes, axis=0, tiled=True)
     gains = jnp.concatenate([attn_gain, ffn_gain, query_gain, key_gain])[None]
     gains = jnp.where(jnp.arange(parts)[:, None] == part, gains, jnp.zeros((), BF))
     gains = gains + after(swap(gains, "ctx", 1), kv_piece)
     for at, (axis, bit) in enumerate(bits[:-1]):
-        gains = gains + after(swap(gains, axis, bit), (kv_one, *stages)[min(at, 2)])
+        gains = gains + after(swap(gains, axis, bit), (kv_one, kv_near[min(1, len(kv_near) - 1)], kv_far)[min(at, 2)])
     gains = gains.astype(F32)
     gain_one = gains[:, :wide].reshape(1, -1)
     gain_two = gains[:, wide : 2 * wide].reshape(1, -1)
@@ -870,9 +892,10 @@
         ]
         return call(functools.partial(kv_kernel, kv_heads), "keys_values", (1,), ins, outs, keep=keep)
 
-    normed, kv_p, k_lin_p = keys_values(0, gain_one_s)
+    q_near = gather_near(q_one, w_kv)
+    normed, kv_p, k_lin_p = keys_values(0, after(gain_one_s, *q_near[1:]))
     normed, kv_c, k_lin_c = keys_values(1, after(gain_one_s, kv_p), normed)
-    w_q, _ = gather_rows(q_one, ((w_kv,), (kv_p,), (kv_c,)))
+    w_q, _ = gather_far(q_near, kv_c)
     mine = lambda f: (f, 0)
     q, q_lin = call(
         functools.partial(q_kernel, heads), "queries", (2,),
@@ -905,7 +928,9 @@
         far_k, far_v = swap(slots[4][0], "ctx", 2), swap(slots[2][1], "ctx", 4)
         slots[3], slots[5] = swap(slots[2], "ctx", 1), swap(slots[4], "ctx", 1)
         halos[2] = shift(after(kv_c, slots[2]), 2)
+        gu_piece = after(gu_piece, slots[2], slots[4])
         ready = (slots[2], slots[4])
+    w_gu = lax.all_gather(after(gu_piece, w_od), weight_axes, axis=0, tiled=True)
     c_state = attention_forward(
         (1,), after(scalars, *ready), q, low_col, pick(slots, near), pick(halos, (0,))
     )
@@ -916,7 +941,7 @@
     attended, lse_p = attention_forward(
         (0,), after(scalars, c_state[0], *ready), q, low_col, slots, {}, None, (None,)
     )
-    part_p = out_projection(0, attended, w_rest)
+    part_p = out_projection(0, attended, w_od)
     got_p = swap(part_p, "tensor", 1)
     if ctx_size == 8:
         halos[1] = swap(jnp.where(odd, after(halos[2], part_p), kv_c), "ctx", 1)
@@ -924,15 +949,15 @@
         (1,), after(scalars, part_p), q, low_col, pick(slots, middle + far), pick(halos, range(1, n_halo)),
         c_state, (attended,),
     )
-    part_c = out_projection(1, attended, w_rest)
+    part_c = out_projection(1, attended, w_od)
     got_c = swap(part_c, "tensor", 1)
 
     resid_p, *whole, out_p, back_p = feed_forward(
-        0, tokens, part_p, got_p, after(gain_two, part_c), cotangent, w_rest, o_cols, chunk
+        0, tokens, part_p, got_p, after(gain_two, part_c), cotangent, w_od, w_gu, chunk
     )
     back_got_p = swap(back_p, "tensor", 1)
     resid_c, *whole, out_c, back_c = feed_forward(
-        1, tokens, part_c, got_c, after(gain_two, back_p), cotangent, w_rest, o_cols, chunk, whole
+        1, tokens, part_c, got_c, after(gain_two, back_p), cotangent, w_od, w_gu, chunk, whole
     )
     back_got_c = swap(back_c, "tensor", 1)
     normed_ffn, hidden, d_gu = whole
@@ -940,7 +965,7 @@
     rest_grads = weight_grad(normed_ffn, d_gu, o_cols, width, min(1024, o_cols))
     rest_grads = weight_grad(cotangent, hidden, o_cols + 2 * units, width, chunk, rest_grads)
     d_resid_p, d_mixed, d_att_p, delta_p, d_two_p = mixed_back(
-        0, back_p, back_got_p, resid_p, after(gain_two, rest_grads), cotangent, w_rest, o_cols, attended
+        0, back_p, back_got_p, resid_p, after(gain_two, rest_grads), cotangent, w_od, o_cols, attended
     )
     out_p, out_c = after(out_p, back_got_c), after(out_c, back_got_c)
     out_got_p, out_got_c = swap(out_p, "tensor", 1), swap(out_c, "tensor", 1)
@@ -955,7 +980,7 @@
 
     dq_p, prior, _ = back_rows(0, (d_att_p,), pick(slots, far), {}, None)
     d_resid_c, d_mixed, d_att_c, delta_c, d_two_c = mixed_back(
-        1, back_c, back_got_c, resid_c, after(gain_two, dq_p), cotangent, w_rest, o_cols, attended, d_mixed
+        1, back_c, back_got_c, resid_c, after(gain_two, dq_p), cotangent, w_od, o_cols, attended, d_mixed
     )
     of_rows.append((d_att_c, lse_c, delta_c))
     rest_grads = weight_grad(d_mixed, attended, 0, width, min(1024, o_cols), rest_grads)
@@ -977,12 +1002,13 @@
     if ctx_size == 8:
         g6 = add_low(g[6], after(got7, dq))
         far_k, far_v = swap(g6[0], "ctx", 2), swap(g6[1], "ctx", 4)
-        ready = (g6, halo_two)
+        ready = (g6,)
     dq_c, more, _ = back_rows(1, (dq, *ready), pick(slots, middle), {}, dq_c, prior)
     g.update(more)
     if ctx_size == 8:
         got3, got5 = swap(g[3], "ctx", 1), swap(g[5], "ctx", 1)
-    dq, more, _ = back_rows(1, (dq_c, out_got_p, out_got_c), pick(slots, near), {}, dq_c, prior, dq, True)
+        ready = (halo_two,)
+    dq, more, _ = back_rows(1, (dq_c, out_got_p, out_got_c, *ready), pick(slots, near), {}, dq_c, prior, dq, True)
     g.update(more)
     if ctx_size == 8:
         got1 = swap(g[1], "ctx", 1)

time: 576 us -> 561 us (0.974)
  starting transfers between devices: 137 us -> 113 us
  waiting for transfers between devices: 63.1 us -> 78.1 us
  Pallas kernels: 299 us -> 293 us
    ppermute x59 -> x65, starting transfers between devices: 132 us -> 109 us  [swap(): return lax.ppermute(value, axis, [(i, i ^ bit) for i in range(size)])]
    ppermute x2, waiting for transfers between devices: 7.45 us -> 21.2 us  [shift(): lax.ppermute(value, 'ctx', [(i, i + by) for i in range(size) if 0 <= i +...]
    unnamed x90 -> x94, local copies, waits for them, and re-layouts: 16.6 us -> 18 us
    ppermute x59 -> x65, waiting for transfers between devices: 55.6 us -> 56.8 us  [swap(): return lax.ppermute(value, axis, [(i, i ^ bit) for i in range(size)])]
  transfers between devices with their start and end apart: 63 -> 70, of which waited for: 16 -> 22; matrix products, arithmetic and copies ran while one was open for 7% -> 7% of each run, Pallas kernels for 50% -> 50%
where the time goes in v4:
time: 561 us; the launch traced here: 552 us
  Pallas kernels  293 us (52%)
  starting transfers between devices  113 us (20%)
  waiting for transfers between devices  78.1 us (14%)
  local copies, waits for them, and re-layouts  30.6 us (5%)
  other arithmetic  16.5 us (3%)
  between operations  15 us (3%)
    pallas_call x33, Pallas kernels, call(): pl.pallas_call(kernel, grid_spec=pltpu.PrefetchScalarGridSpec(num_scalar_...  293 us
    ppermute x65, starting transfers between devices, swap(): return lax.ppermute(value, axis, [(i, i ^ bit) for i in range(size)])  109 us
    ppermute x65, waiting for transfers between devices, swap(): return lax.ppermute(value, axis, [(i, i ^ bit) for i in range(size)])  56.8 us
    ppermute x2, waiting for transfers between devices, shift(): lax.ppermute(value, 'ctx', [(i, i + by) for i in range(size) if 0 <= i +...  21.2 us
    unnamed x94, local copies, waits for them, and re-layouts  18 us
  transfers between devices with their start and end apart: 70, of which 22 were waited for; matrix products, arithmetic and copies ran while one was open for 7% of the time, Pallas kernels for 50%

profile of v4, /device:TPU:0, one launch (start us, length us, event | category | flops | bytes accessed | tf_op | source)
XLA Modules:
  0.0 551.8 jit_solution(18207118043121713597)
XLA Ops:
  10.8 3.7 collective-permute-start
  27.1 5.1 collective-permute-done.4
  41.4 3.7 fusion.5.x_ref
  57.0 4.0 collective-permute-done.17
  60.9 5.5 %keys_values.2 = (bf16[1024,1024]{1,0:T(8,128)(2,1)}, bf16[2,512,512]{2,1,0:T(8,128)(2,1)}, f32[512,512]{1,0:T(8,128)}) custom-call(bf16[1024,1024]{1,0:T(8,128)(2,1)} %fusion.5.x_ref, f32[1,1024]{1,0:T(1,128)} %fusion.1.gain_ref, bf16[1024,1024]{1,0:T(8,128)(2,1)} %copy-done, f32[1,128]{1,0:T(1,128)} %reshape.120.hgain_ref.gain_ref, ...), custom_call_target="tpu_custom_call" | custom-call | tf_op jit(solution)/shard_map/keys_values/pallas_call | solution.py:46
  70.0 5.6 %keys_values.3 = (bf16[1024,1024]{1,0:T(8,128)(2,1)}, bf16[2,512,512]{2,1,0:T(8,128)(2,1)}, f32[512,512]{1,0:T(8,128)}) custom-call(bf16[1024,1024]{1,0:T(8,128)(2,1)} %fusion.5.x_ref, f32[1,1024]{1,0:T(1,128)} %fusion.1.gain_ref, bf16[1024,1024]{1,0:T(8,128)(2,1)} %copy-done, ...), custom_call_target="tpu_custom_call", output_to_operand_aliasing={{0}: (6, {})} | custom-call | tf_op jit(solution)/shard_map/keys_values/pallas_call | solution.py:46
  79.8 10.5 %queries.1 = (bf16[1024,1024]{1,0:T(8,128)(2,1)}, f32[1024,1024]{1,0:T(8,128)}) custom-call(bf16[1024,1024]{1,0:T(8,128)(2,1)} %get-tuple-element.187.normed_ref.left_ref, bf16[1024,1024]{1,0:T(8,128)(2,1)} %constant_dynamic-update-slice_fusion.11.w_ref, f32[1,128]{1,0:T(1,128)} %reshape.121.hgain_ref.gain_ref, f32[1024,128]{1,0:T(8,128)} %get-tuple-element.368.cos_ref, ...), custom_call_target="tpu_custom_call" | custom-call | tf_op jit(solution)/shard_map/queries/pallas_call | solution.py:46
  98.1 10.9 %attend.3 = (f32[512,1024]{1,0:T(8,128)}, f32[512,1024]{1,0:T(8,128)}) custom-call(s32[2]{0:T(128)} %pad_add_fusion.1.idx_ref, s32[512,128]{1,0:T(8,128)} %broadcast_in_dim.70.lo_ref, bf16[1024,1024]{1,0:T(8,128)(2,1)} %get-tuple-element.195.refs_0_.q_ref, bf16[2,512,512]{2,1,0:T(8,128)(2,1)} %get-tuple-element.184.refs_1_.refs_0_, ...), custom_call_target="tpu_custom_call" | custom-call | tf_op jit(solution)/shard_map/attend/pallas_call | solution.py:46
  111.5 3.3 collective-permute-start.30
  117.0 8.8 %attend.4 = (bf16[1024,1024]{1,0:T(8,128)(2,1)}, f32[4,8,512]{2,1,0:T(8,128)}) custom-call(s32[2]{0:T(128)} %pad_add_fusion.1.idx_ref, s32[512,128]{1,0:T(8,128)} %broadcast_in_dim.70.lo_ref, bf16[1024,1024]{1,0:T(8,128)(2,1)} %get-tuple-element.195.refs_0_.q_ref, bf16[2,512,512]{2,1,0:T(8,128)(2,1)} %get-tuple-element.184.refs_1_.refs_0_, ...), custom_call_target="tpu_custom_call" | custom-call | tf_op jit(solution)/shard_map/attend/pallas_call | solution.py:46
  125.8 3.9 out_projection.2.own_ref
  129.7 21.2 %collective-permute-done.30.refs_7_.refs_1_ = bf16[2,512,512]{2,1,0:T(8,128)(2,1)} collective-permute-done((bf16[2,512,512]{2,1,0:T(8,128)(2,1)}, bf16[2,512,512]{2,1,0:T(8,128)(2,1)}, u32[]{:S(2)}, u32[]{:S(2)}) %collective-permute-start.30) | collective-permute-done | bytes 1048608 | tf_op jit(solution)/shard_map/ppermute | solution.py:726
  156.2 20.0 %attend.5 = (bf16[1024,1024]{1,0:T(8,128)(2,1)}, f32[4,8,512]{2,1,0:T(8,128)}) custom-call(s32[2]{0:T(128)} %pad_add_fusion.1.idx_ref, s32[512,128]{1,0:T(8,128)} %broadcast_in_dim.70.lo_ref, bf16[1024,1024]{1,0:T(8,128)(2,1)} %get-tuple-element.195.refs_0_.q_ref, ...), custom_call_target="tpu_custom_call", output_to_operand_aliasing={{0}: (13, {})} | custom-call | tf_op jit(solution)/shard_map/attend/pallas_call | solution.py:46
  176.2 4.1 out_projection.3.own_ref
  184.0 18.3 %feed_forward.2 = (f32[512,1024]{1,0:T(8,128)}, bf16[1024,1024]{1,0:T(8,128)(2,1)}, bf16[1024,1536]{1,0:T(8,128)(2,1)}, bf16[1024,3072]{1,0:T(8,128)(2,1)}, bf16...) custom-call(bf16[1024,1024]{1,0:T(8,128)(2,1)} %x_ref.7, bf16[512,1024]{1,0:T(8,128)(2,1)} %out_projection.2.own_ref, ...), custom_call_target="tpu_custom_call" | custom-call | tf_op jit(solution)/shard_map/feed_forward/pallas_call | solution.py:46
  205.4 18.5 %feed_forward.3 = (f32[512,1024]{1,0:T(8,128)}, bf16[1024,1024]{1,0:T(8,128)(2,1)}, bf16[1024,1536]{1,0:T(8,128)(2,1)}, bf16[1024,3072]{1,0:T(8,128)(2,1)}, bf16...) custom-call(bf16[1024,1024]{1,0:T(8,128)(2,1)} %x_ref.7, ...), custom_call_target="tpu_custom_call", output_to_operand_aliasing={{1}: (7, {}), {2}: (8, {}), {3}: (9, {})} | custom-call | tf_op jit(solution)/shard_map/feed_forward/pallas_call | solution.py:46
  225.2 10.7 %weight_grad.3.refs_0_ = bf16[1024,5632]{1,0:T(8,128)(2,1)} custom-call(bf16[1024,1024]{1,0:T(8,128)(2,1)} %get-tuple-element.224.left_ref, bf16[1024,3072]{1,0:T(8,128)(2,1)} %get-tuple-element.225.right_ref), custom_call_target="tpu_custom_call" | custom-call | tf_op jit(solution)/shard_map/weight_grad/pallas_call | solution.py:46
  236.0 7.4 %weight_grad.4.refs_0_ = bf16[1024,5632]{1,0:T(8,128)(2,1)} custom-call(bf16[1024,1024]{1,0:T(8,128)(2,1)} %dy_ref.7, bf16[1024,1536]{1,0:T(8,128)(2,1)} %get-tuple-element.223.right_ref, bf16[1024,5632]{1,0:T(8,128)(2,1)} %weight_grad.3.refs_0_), custom_call_target="tpu_custom_call", output_to_operand_aliasing={{}: (2, {})} | custom-call | tf_op jit(solution)/shard_map/weight_grad/pallas_call | solution.py:46
  244.4 7.2 %mixed_back.2 = (f32[512,1024]{1,0:T(8,128)}, bf16[1024,1024]{1,0:T(8,128)(2,1)}, bf16[512,1024]{1,0:T(8,128)(2,1)}, f32[4,8,512]{2,1,0:T(8,128)}, f32[1,1024]{1,0:T(1,128)}) custom-call(bf16[512,1024]{1,0:T(8,128)(2,1)} %get-tuple-element.214.own_ref, bf16[512,1024]{1,0:T(8,128)(2,1)} %copy-done.18, f32[512,1024]{1,0:T(8,128)} %get-tuple-element.308.resid_ref, ...), custom_call_target="tpu_custom_call" | custom-call | tf_op jit(solution)/shard_map/mixed_back/pallas_call | solution.py:46
  252.1 5.8 %attend_back.6 = (f32[512,1024]{1,0:T(8,128)}, bf16[2,512,512]{2,1,0:T(8,128)(2,1)}, bf16[2,512,512]{2,1,0:T(8,128)(2,1)}) custom-call(s32[2]{0:T(128)} %pad_add_fusion.1.idx_ref, bf16[1024,1024]{1,0:T(8,128)(2,1)} %get-tuple-element.195.refs_0_.q_ref, bf16[512,1024]{1,0:T(8,128)(2,1)} %get-tuple-element.227.do_ref, ...), custom_call_target="tpu_custom_call" | custom-call | tf_op jit(solution)/shard_map/attend_back/pallas_call | solution.py:46
  258.9 6.8 %mixed_back.3 = (f32[512,1024]{1,0:T(8,128)}, bf16[1024,1024]{1,0:T(8,128)(2,1)}, bf16[512,1024]{1,0:T(8,128)(2,1)}, f32[4,8,512]{2,1,0:T(8,128)}, f32[1,1024]{1,0:T(1,128)}) custom-call(bf16[512,1024]{1,0:T(8,128)(2,1)} %get-tuple-element.221.own_ref, bf16[512,1024]{1,0:T(8,128)(2,1)} %copy-done.19, ...), custom_call_target="tpu_custom_call", output_to_operand_aliasing={{1}: (7, {})} | custom-call | tf_op jit(solution)/shard_map/mixed_back/pallas_call | solution.py:46
  265.8 6.0 %weight_grad.5 = bf16[1024,5632]{1,0:T(8,128)(2,1)} custom-call(bf16[1024,1024]{1,0:T(8,128)(2,1)} %get-tuple-element.234.left_ref, bf16[1024,1024]{1,0:T(8,128)(2,1)} %get-tuple-element.209.att_ref.right_ref, bf16[1024,5632]{1,0:T(8,128)(2,1)} %weight_grad.4.refs_0_), custom_call_target="tpu_custom_call", output_to_operand_aliasing={{}: (2, {})} | custom-call | tf_op jit(solution)/shard_map/weight_grad/pallas_call | solution.py:46
  273.9 10.4 %attend_back.7 = (f32[512,1024]{1,0:T(8,128)}, bf16[2,512,512]{2,1,0:T(8,128)(2,1)}, bf16[2,512,512]{2,1,0:T(8,128)(2,1)}, bf16[2,512,512]{2,1,0:T(8,128)(2,1)}) custom-call(s32[2]{0:T(128)} %pad_add_fusion.1.idx_ref, bf16[1024,1024]{1,0:T(8,128)(2,1)} %get-tuple-element.195.refs_0_.q_ref, bf16[512,1024]{1,0:T(8,128)(2,1)} %get-tuple-element.236.do_ref, ...), custom_call_target="tpu_custom_call" | custom-call | flops 65999998976 | tf_op jit(solution)/shard_map/attend_back/pallas_call | solution.py:46
  284.3 8.8 %collective-permute-start.36 = (bf16[2,512,512]{2,1,0:T(8,128)(2,1)}, bf16[2,512,512]{2,1,0:T(8,128)(2,1)S(1)}, u32[]{:S(2)}, u32[]{:S(2)}) collective-permute-start(bf16[2,512,512]{2,1,0:T(8,128)(2,1)} %get-tuple-element.245), channel_id=1, source_target_pairs={{0,2},{2,0},{4,6},{6,4},{8,10},{10,8},{12,14},{14,12},{1,3},{3,1},... | collective-permute-start | bytes 3145736 | tf_op jit(solution)/shard_map/ppermute | solution.py:721
  293.1 15.2 %attend_back.8 = (f32[512,1024]{1,0:T(8,128)}, bf16[2,512,512]{2,1,0:T(8,128)(2,1)}, bf16[2,512,512]{2,1,0:T(8,128)(2,1)}) custom-call(s32[2]{0:T(128)} %pad_add_fusion.1.idx_ref, bf16[1024,1024]{1,0:T(8,128)(2,1)} %get-tuple-element.195.refs_0_.q_ref, bf16[512,1024]{1,0:T(8,128)(2,1)} %get-tuple-element.236.do_ref, ...), custom_call_target="tpu_custom_call" | custom-call | flops 48000000000 | tf_op jit(solution)/shard_map/attend_back/pallas_call | solution.py:46
  312.5 12.6 %attend_back.9 = (f32[1024,1024]{1,0:T(8,128)}, bf16[2,512,512]{2,1,0:T(8,128)(2,1)}, bf16[2,512,512]{2,1,0:T(8,128)(2,1)}, bf16[2,512,512]{2,1,0:T(8,128)(2,1)}...) custom-call(s32[2]{0:T(128)} %pad_add_fusion.1.idx_ref, ...), custom_call_target="tpu_custom_call" | custom-call | flops 120000004096 | tf_op jit(solution)/shard_map/attend_back/pallas_call | solution.py:46
  325.5 26.6 %collective-permute-start.44 = (bf16[512,512]{1,0:T(8,128)(2,1)S(1)}, bf16[512,512]{1,0:T(8,128)(2,1)S(1)}, u32[]{:S(2)}, u32[]{:S(2)}) collective-permute-start(bf16[512,512]{1,0:T(8,128)(2,1)S(1)} %get-tuple-element.349), channel_id=1, source_target_pairs={{0,8},{2,10},{4,12},{6,14},{8,0},{10,2},{12,4},{14,6},{1,9},{3,11}... | collective-permute-start | bytes 1572872 | tf_op jit(solution)/shard_map/ppermute | solution.py:721
  352.1 13.9 %collective-permute-start.43 = (bf16[512,512]{1,0:T(8,128)(2,1)S(1)}, bf16[512,512]{1,0:T(8,128)(2,1)S(1)}, u32[]{:S(2)}, u32[]{:S(2)}) collective-permute-start(bf16[512,512]{1,0:T(8,128)(2,1)S(1)} %get-tuple-element.350), channel_id=1, source_target_pairs={{0,4},{2,6},{4,0},{6,2},{8,12},{10,14},{12,8},{14,10},{1,5},{3,7},... | collective-permute-start | bytes 1572872 | tf_op jit(solution)/shard_map/ppermute | solution.py:721
  366.0 25.9 %attend_back.10 = (f32[512,1024]{1,0:T(8,128)}, bf16[2,512,512]{2,1,0:T(8,128)(2,1)}, bf16[2,512,512]{2,1,0:T(8,128)(2,1)}, bf16[2,512,512]{2,1,0:T(8,128)(2,1)}, bf16[2,512,512]{2,1,0:T(8,128)(2,1)}) custom-call(s32[2]{0:T(128)} %pad_add_fusion.1.idx_ref, bf16[1024,1024]{1,0:T(8,128)(2,1)} %get-tuple-element.195.refs_0_.q_ref, ...), custom_call_target="tpu_custom_call" | custom-call | flops 83999997952 | tf_op jit(solution)/shard_map/attend_back/pallas_call | solution.py:46
  391.9 5.5 collective-permute-start.42
  397.5 15.1 %attend_back.11 = (f32[1024,1024]{1,0:T(8,128)}, bf16[2,512,512]{2,1,0:T(8,128)(2,1)}, bf16[2,512,512]{2,1,0:T(8,128)(2,1)}) custom-call(s32[2]{0:T(128)} %pad_add_fusion.1.idx_ref, bf16[1024,1024]{1,0:T(8,128)(2,1)} %get-tuple-element.195.refs_0_.q_ref, bf16[512,1024]{1,0:T(8,128)(2,1)} %get-tuple-element.236.do_ref, ...), custom_call_target="tpu_custom_call", output_to_operand_aliasing={{0}: (11, {})} | custom-call | flops 48000000000 | tf_op jit(solution)/shard_map/attend_back/pallas_call | solution.py:46
  414.3 3.9 merge.1
  421.2 11.7 %q_back.1 = (bf16[1024,1024]{1,0:T(8,128)(2,1)}, f32[1024,1024]{1,0:T(8,128)}, f32[1,128]{1,0:T(1,128)}) custom-call(f32[1024,1024]{1,0:T(8,128)} %get-tuple-element.265.dq_ref, f32[1024,1024]{1,0:T(8,128)} %get-tuple-element.266.lin_ref, f32[1,128]{1,0:T(1,128)} %reshape.121.hgain_ref.gain_ref, f32[1024,128]{1,0:T(8,128)} %get-tuple-element.368.cos_ref, ...), custom_call_target="tpu_custom_call" | custom-call | tf_op jit(solution)/shard_map/q_back/pallas_call | solution.py:46
  432.9 8.9 %kv_back.2 = (bf16[1024,1024]{1,0:T(8,128)(2,1)}, bf16[512,1024]{1,0:T(8,128)(2,1)}, f32[1,128]{1,0:T(1,128)}) custom-call(f32[512,512]{1,0:T(8,128)} %get-tuple-element.278.lin_ref, f32[1,128]{1,0:T(1,128)} %reshape.120.hgain_ref.gain_ref, f32[1024,128]{1,0:T(8,128)} %get-tuple-element.368.cos_ref, f32[1024,128]{1,0:T(8,128)} %get-tuple-element.369.sin_ref, ...), custom_call_target="tpu_custom_call" | custom-call | tf_op jit(solution)/shard_map/kv_back/pallas_call | solution.py:46
  441.8 5.9 %weight_halves.2 = (bf16[512,1024]{1,0:T(8,128)(2,1)}, bf16[512,1024]{1,0:T(8,128)(2,1)}) custom-call(bf16[1024,1024]{1,0:T(8,128)(2,1)} %get-tuple-element.187.normed_ref.left_ref, bf16[1024,1024]{1,0:T(8,128)(2,1)} %get-tuple-element.283.right_ref), custom_call_target="tpu_custom_call" | custom-call | tf_op jit(solution)/shard_map/weight_halves/pallas_call | solution.py:46
  448.5 18.3 %collective-permute-done.46.refs_2_.refs_6_ = bf16[2,512,512]{2,1,0:T(8,128)(2,1)S(1)} collective-permute-done((bf16[2,512,512]{2,1,0:T(8,128)(2,1)}, bf16[2,512,512]{2,1,0:T(8,128)(2,1)S(1)}, u32[]{:S(2)}, u32[]{:S(2)}) %collective-permute-start.46) | collective-permute-done | bytes 1048608 | tf_op jit(solution)/shard_map/ppermute | solution.py:721
  468.5 8.9 %kv_back.3 = (bf16[1024,1024]{1,0:T(8,128)(2,1)}, bf16[512,1024]{1,0:T(8,128)(2,1)}, f32[1,128]{1,0:T(1,128)}) custom-call(f32[512,512]{1,0:T(8,128)} %get-tuple-element.220.lin_ref, f32[1,128]{1,0:T(1,128)} %reshape.120.hgain_ref.gain_ref, f32[1024,128]{1,0:T(8,128)} %get-tuple-element.368.cos_ref, ...), custom_call_target="tpu_custom_call", output_to_operand_aliasing={{0}: (15, {})} | custom-call | flops 8999999488 | tf_op jit(solution)/shard_map/kv_back/pallas_call | solution.py:46
  478.0 4.4 collective-permute-start.51
  483.2 5.8 %weight_halves.3 = (bf16[512,1024]{1,0:T(8,128)(2,1)}, bf16[512,1024]{1,0:T(8,128)(2,1)}) custom-call(bf16[1024,1024]{1,0:T(8,128)(2,1)} %get-tuple-element.187.normed_ref.left_ref, bf16[1024,1024]{1,0:T(8,128)(2,1)} %get-tuple-element.294.right_ref), custom_call_target="tpu_custom_call" | custom-call | tf_op jit(solution)/shard_map/weight_halves/pallas_call | solution.py:46
  491.4 4.1 tokens_back.2
  495.5 2.2 unpack.1
  500.5 7.4 %collective-permute-start.60 = (bf16[64,1024]{1,0:T(8,128)(2,1)S(1)}, bf16[64,1024]{1,0:T(8,128)(2,1)S(1)}, u32[]{:S(2)}, u32[]{:S(2)}) collective-permute-start(bf16[64,1024]{1,0:T(8,128)(2,1)S(1)} %slice.189), channel_id=1, source_target_pairs={{0,16},{16,0},{1,17},{17,1},{2,18},{18,2},{3,19},{19,3},{4,20},{20... | collective-permute-start | bytes 393224 | tf_op jit(solution)/shard_map/ppermute | solution.py:721
  507.9 3.1 add_layer.2.refs_0_
  515.2 3.1 add_layer.3
  519.5 4.0 tokens_back.3
  527.0 7.0 %collective-permute-done.64 = bf16[64,1024]{1,0:T(8,128)(2,1)S(1)} collective-permute-done((bf16[64,1024]{1,0:T(8,128)(2,1)S(1)}, bf16[64,1024]{1,0:T(8,128)(2,1)S(1)}, u32[]{:S(2)}, u32[]{:S(2)}) %collective-permute-start.64) | collective-permute-done | bytes 131104 | tf_op jit(solution)/shard_map/ppermute | solution.py:721
  535.2 2.5 collective-permute-done.65
  538.6 3.8 collective-permute-done.66
  (316 shorter events, 106.6 us)
Async XLA Ops:
  7.2 83.7 %all-gather.3.cloned.1.call-start = ((), (), s32[]{:S(2)}) async-start(), calls=%async_computation.1 | async-start | bytes 5570560 | tf_op jit(solution)/shard_map/all_gather | solution.py:847
  9.4 173.5 %all-gather.5.cloned.1.call-start = ((), (), s32[]{:S(2)}) async-start(), calls=%async_computation.2 | async-start | bytes 6684672 | tf_op jit(solution)/shard_map/all_gather | solution.py:933
  10.4 9.3 %collective-permute-start.6 = (bf16[16,144]{1,0:T(8,128)(2,1)S(1)}, bf16[16,144]{1,0:T(8,128)(2,1)S(1)}, u32[]{:S(2)}, u32[]{:S(2)}) collective-permute-start(bf16[16,144]{1,0:T(8,128)(2,1)S(1)} %broadcast_select_fusion.2), channel_id=1, source_target_pairs={{0,2},{2,0},{4,6},{6,4},{8,10},{10,8},{12,14},{14,12},{1,3},{3,1},... | collective-permute-start | bytes 13832 | tf_op jit(solution)/shard_map/ppermute | solution.py:721
  10.8 10.8 %collective-permute-start = (bf16[64,1024]{1,0:T(8,128)(2,1)}, bf16[64,1024]{1,0:T(8,128)(2,1)S(1)}, u32[]{:S(2)}, u32[]{:S(2)}) collective-permute-start(bf16[64,1024]{1,0:T(8,128)(2,1)} %get-tuple-element.173), channel_id=1, source_target_pairs={{0,16},{16,0},{1,17},{17,1},{2,18},{18,2},{3,19},{19,3},{4,20},{20... | collective-permute-start | bytes 393224 | tf_op jit(solution)/shard_map/ppermute | solution.py:721
  21.6 10.6 %collective-permute-start.4 = (bf16[128,1024]{1,0:T(8,128)(2,1)S(1)}, bf16[128,1024]{1,0:T(8,128)(2,1)S(1)}, u32[]{:S(2)}, u32[]{:S(2)}) collective-permute-start(bf16[128,1024]{1,0:T(8,128)(2,1)S(1)} %pad_maximum_fusion.3), channel_id=1, source_target_pairs={{0,4},{2,6},{4,0},{6,2},{8,12},{10,14},{12,8},{14,10},{1,5},{3,7},... | collective-permute-start | bytes 786440 | tf_op jit(solution)/shard_map/ppermute | solution.py:721
  23.2 10.4 %collective-permute-start.2 = (bf16[128,1024]{1,0:T(8,128)(2,1)S(1)}, bf16[128,1024]{1,0:T(8,128)(2,1)S(1)}, u32[]{:S(2)}, u32[]{:S(2)}) collective-permute-start(bf16[128,1024]{1,0:T(8,128)(2,1)S(1)} %pad_maximum_fusion.3), channel_id=1, source_target_pairs={{0,8},{2,10},{4,12},{6,14},{8,0},{10,2},{12,4},{14,6},{1,9},{3,11}... | collective-permute-start | bytes 786440 | tf_op jit(solution)/shard_map/ppermute | solution.py:721
  24.7 10.0 %collective-permute-start.11 = (bf16[128,1024]{1,0:T(8,128)(2,1)S(1)}, bf16[128,1024]{1,0:T(8,128)(2,1)S(1)}, u32[]{:S(2)}, u32[]{:S(2)}) collective-permute-start(bf16[128,1024]{1,0:T(8,128)(2,1)S(1)} %pad_maximum_fusion.3), channel_id=1, source_target_pairs={{0,2},{2,0},{4,6},{6,4},{8,10},{10,8},{12,14},{14,12},{1,3},{3,1},... | collective-permute-start | bytes 786440 | tf_op jit(solution)/shard_map/ppermute | solution.py:721
  24.8 9.8 %collective-permute-start.8 = (bf16[16,144]{1,0:T(8,128)(2,1)S(1)}, bf16[16,144]{1,0:T(8,128)(2,1)S(1)}, u32[]{:S(2)}, u32[]{:S(2)}) collective-permute-start(bf16[16,144]{1,0:T(8,128)(2,1)S(1)} %fusion.24), channel_id=1, source_target_pairs={{0,4},{2,6},{4,0},{6,2},{8,12},{10,14},{12,8},{14,10},{1,5},{3,7},... | collective-permute-start | bytes 13832 | tf_op jit(solution)/shard_map/ppermute | solution.py:721
  25.8 13.0 %collective-permute-start.1 = (bf16[64,1024]{1,0:T(8,128)(2,1)S(1)}, bf16[64,1024]{1,0:T(8,128)(2,1)S(1)}, u32[]{:S(2)}, u32[]{:S(2)}) collective-permute-start(bf16[64,1024]{1,0:T(8,128)(2,1)S(1)} %copy-done.24), channel_id=1, source_target_pairs={{0,16},{16,0},{1,17},{17,1},{2,18},{18,2},{3,19},{19,3},{4,20},{20... | collective-permute-start | bytes 393224 | tf_op jit(solution)/shard_map/ppermute | solution.py:721
  34.7 11.9 %collective-permute-start.12 = (bf16[128,1024]{1,0:T(8,128)(2,1)S(1)}, bf16[128,1024]{1,0:T(8,128)(2,1)}, u32[]{:S(2)}, u32[]{:S(2)}) collective-permute-start(bf16[128,1024]{1,0:T(8,128)(2,1)S(1)} %collective-permute-done.4), channel_id=1, source_target_pairs={{0,2},{2,0},{4,6},{6,4},{8,10},{10,8},{12,14},{14,12},{1,3},{3,1},... | collective-permute-start | bytes 786440 | tf_op jit(solution)/shard_map/ppermute | solution.py:721
  34.8 12.8 %collective-permute-start.13 = (bf16[128,1024]{1,0:T(8,128)(2,1)S(1)}, bf16[128,1024]{1,0:T(8,128)(2,1)}, u32[]{:S(2)}, u32[]{:S(2)}) collective-permute-start(bf16[128,1024]{1,0:T(8,128)(2,1)S(1)} %collective-permute-done.2), channel_id=1, source_target_pairs={{0,2},{2,0},{4,6},{6,4},{8,10},{10,8},{12,14},{14,12},{1,3},{3,1},... | collective-permute-start | bytes 786440 | tf_op jit(solution)/shard_map/ppermute | solution.py:721
  38.7 9.8 %collective-permute-start.14 = (bf16[128,1024]{1,0:T(8,128)(2,1)S(1)}, bf16[128,1024]{1,0:T(8,128)(2,1)}, u32[]{:S(2)}, u32[]{:S(2)}) collective-permute-start(bf16[128,1024]{1,0:T(8,128)(2,1)S(1)} %get-tuple-element.354), channel_id=1, source_target_pairs={{0,2},{2,0},{4,6},{6,4},{8,10},{10,8},{12,14},{14,12},{1,3},{3,1},... | collective-permute-start | bytes 786440 | tf_op jit(solution)/shard_map/ppermute | solution.py:721
  39.6 11.9 %collective-permute-start.15 = (bf16[128,1024]{1,0:T(8,128)(2,1)}, bf16[128,1024]{1,0:T(8,128)(2,1)S(1)}, u32[]{:S(2)}, u32[]{:S(2)}) collective-permute-start(bf16[128,1024]{1,0:T(8,128)(2,1)} %get-tuple-element.356), channel_id=1, source_target_pairs={{0,8},{2,10},{4,12},{6,14},{8,0},{10,2},{12,4},{14,6},{1,9},{3,11}... | collective-permute-start | bytes 786440 | tf_op jit(solution)/shard_map/ppermute | solution.py:721
  41.1 11.9 %collective-permute-start.10 = (bf16[128,1024]{1,0:T(8,128)(2,1)}, bf16[128,1024]{1,0:T(8,128)(2,1)}, u32[]{:S(2)}, u32[]{:S(2)}) collective-permute-start(bf16[128,1024]{1,0:T(8,128)(2,1)} %get-tuple-element.356), channel_id=1, source_target_pairs={{0,4},{2,6},{4,0},{6,2},{8,12},{10,14},{12,8},{14,10},{1,5},{3,7},... | collective-permute-start | bytes 786440 | tf_op jit(solution)/shard_map/ppermute | solution.py:721
  46.6 29.7 %collective-permute-start.19 = (bf16[128,1024]{1,0:T(8,128)(2,1)}, bf16[128,1024]{1,0:T(8,128)(2,1)S(1)}, u32[]{:S(2)}, u32[]{:S(2)}) collective-permute-start(bf16[128,1024]{1,0:T(8,128)(2,1)} %get-tuple-element.356), channel_id=1, source_target_pairs={{0,2},{2,0},{4,6},{6,4},{8,10},{10,8},{12,14},{14,12},{1,3},{3,1},... | collective-permute-start | bytes 786440 | tf_op jit(solution)/shard_map/ppermute | solution.py:721
  55.9 21.7 %collective-permute-start.21 = (bf16[128,1024]{1,0:T(8,128)(2,1)S(1)}, bf16[128,1024]{1,0:T(8,128)(2,1)S(1)}, u32[]{:S(2)}, u32[]{:S(2)}) collective-permute-start(bf16[128,1024]{1,0:T(8,128)(2,1)S(1)} %collective-permute-done.15), channel_id=1, source_target_pairs={{0,2},{2,0},{4,6},{6,4},{8,10},{10,8},{12,14},{14,12},{1,3},{3,1},... | collective-permute-start | bytes 786440 | tf_op jit(solution)/shard_map/ppermute | solution.py:721
  55.9 21.7 %collective-permute-start.20 = (bf16[128,1024]{1,0:T(8,128)(2,1)}, bf16[128,1024]{1,0:T(8,128)(2,1)S(1)}, u32[]{:S(2)}, u32[]{:S(2)}) collective-permute-start(bf16[128,1024]{1,0:T(8,128)(2,1)} %collective-permute-done.10), channel_id=1, source_target_pairs={{0,2},{2,0},{4,6},{6,4},{8,10},{10,8},{12,14},{14,12},{1,3},{3,1},... | collective-permute-start | bytes 786440 | tf_op jit(solution)/shard_map/ppermute | solution.py:721
  66.5 24.4 %collective-permute-start.23 = (bf16[2,512,512]{2,1,0:T(8,128)(2,1)}, bf16[2,512,512]{2,1,0:T(8,128)(2,1)S(1)}, u32[]{:S(2)}, u32[]{:S(2)}) collective-permute-start(bf16[2,512,512]{2,1,0:T(8,128)(2,1)} %get-tuple-element.184.refs_1_.refs_0_), channel_id=1, source_target_pairs={{0,8},{2,10},{4,12},{6,14},{8,0},{10,2},{12,4},{14,6},{1,9},{3,11}... | collective-permute-start | bytes 3145736 | tf_op jit(solution)/shard_map/ppermute | solution.py:721
  67.6 23.3 %collective-permute-start.18 = (bf16[2,512,512]{2,1,0:T(8,128)(2,1)}, bf16[2,512,512]{2,1,0:T(8,128)(2,1)}, u32[]{:S(2)}, u32[]{:S(2)}) collective-permute-start(bf16[2,512,512]{2,1,0:T(8,128)(2,1)} %get-tuple-element.184.refs_1_.refs_0_), channel_id=1, source_target_pairs={{0,4},{2,6},{4,0},{6,2},{8,12},{10,14},{12,8},{14,10},{1,5},{3,7},... | collective-permute-start | bytes 3145736 | tf_op jit(solution)/shard_map/ppermute | solution.py:721
  90.9 404.6 %reduce-scatter.2.cloned.1.call-start = ((), (), s32[]{:S(2)}) async-start(), calls=%async_computation.3 | async-start | bytes 12255232 | tf_op jit(solution)/shard_map/reduce_scatter | solution.py:987
  91.1 17.9 %collective-permute-start.25 = (bf16[512,512]{1,0:T(8,128)(2,1)S(1)}, bf16[512,512]{1,0:T(8,128)(2,1)S(1)}, u32[]{:S(2)}, u32[]{:S(2)}) collective-permute-start(bf16[512,512]{1,0:T(8,128)(2,1)S(1)} %slice_bitcast_fusion.3), channel_id=1, source_target_pairs={{0,4},{2,6},{4,0},{6,2},{8,12},{10,14},{12,8},{14,10},{1,5},{3,7},... | collective-permute-start | bytes 1572872 | tf_op jit(solution)/shard_map/ppermute | solution.py:721
  94.3 16.4 %collective-permute-start.26 = (bf16[512,512]{1,0:T(8,128)(2,1)S(1)}, bf16[512,512]{1,0:T(8,128)(2,1)S(1)}, u32[]{:S(2)}, u32[]{:S(2)}) collective-permute-start(bf16[512,512]{1,0:T(8,128)(2,1)S(1)} %slice_bitcast_fusion.2), channel_id=1, source_target_pairs={{0,8},{2,10},{4,12},{6,14},{8,0},{10,2},{12,4},{14,6},{1,9},{3,11}... | collective-permute-start | bytes 1572872 | tf_op jit(solution)/shard_map/ppermute | solution.py:721
  111.5 39.3 %collective-permute-start.30 = (bf16[2,512,512]{2,1,0:T(8,128)(2,1)}, bf16[2,512,512]{2,1,0:T(8,128)(2,1)}, u32[]{:S(2)}, u32[]{:S(2)}) collective-permute-start(bf16[2,512,512]{2,1,0:T(8,128)(2,1)} %get-tuple-element.206.refs_3_.refs_0_), channel_id=1, source_target_pairs={{0,4},{2,6},{4,8},{6,10},{8,12},{10,14},{1,5},{3,7},{5,9},{7,11},{... | collective-permute-start | bytes 3145736 | tf_op jit(solution)/shard_map/ppermute | solution.py:726
  152.3 30.6 %collective-permute-start.33 = (bf16[512,1024]{1,0:T(8,128)(2,1)S(1)}, bf16[512,1024]{1,0:T(8,128)(2,1)S(1)}, u32[]{:S(2)}, u32[]{:S(2)}) collective-permute-start(bf16[512,1024]{1,0:T(8,128)(2,1)S(1)} %copy-done.7), channel_id=1, source_target_pairs={{0,1},{1,0},{2,3},{3,2},{4,5},{5,4},{6,7},{7,6},{8,9},{9,8},{10,11... | collective-permute-start | bytes 3145736 | tf_op jit(solution)/shard_map/ppermute | solution.py:721
  180.3 24.0 %collective-permute-start.32 = (bf16[512,1024]{1,0:T(8,128)(2,1)}, bf16[512,1024]{1,0:T(8,128)(2,1)S(1)}, u32[]{:S(2)}, u32[]{:S(2)}) collective-permute-start(bf16[512,1024]{1,0:T(8,128)(2,1)} %out_projection.3.own_ref), channel_id=1, source_target_pairs={{0,1},{1,0},{2,3},{3,2},{4,5},{5,4},{6,7},{7,6},{8,9},{9,8},{10,11... | collective-permute-start | bytes 3145736 | tf_op jit(solution)/shard_map/ppermute | solution.py:721
  202.2 41.1 %collective-permute-start.35 = (bf16[512,1024]{1,0:T(8,128)(2,1)}, bf16[512,1024]{1,0:T(8,128)(2,1)S(1)}, u32[]{:S(2)}, u32[]{:S(2)}) collective-permute-start(bf16[512,1024]{1,0:T(8,128)(2,1)} %get-tuple-element.214.own_ref), channel_id=1, source_target_pairs={{0,1},{1,0},{2,3},{3,2},{4,5},{5,4},{6,7},{7,6},{8,9},{9,8},{10,11... | collective-permute-start | bytes 3145736 | tf_op jit(solution)/shard_map/ppermute | solution.py:721
  223.8 34.1 %collective-permute-start.34 = (bf16[512,1024]{1,0:T(8,128)(2,1)}, bf16[512,1024]{1,0:T(8,128)(2,1)S(1)}, u32[]{:S(2)}, u32[]{:S(2)}) collective-permute-start(bf16[512,1024]{1,0:T(8,128)(2,1)} %get-tuple-element.221.own_ref), channel_id=1, source_target_pairs={{0,1},{1,0},{2,3},{3,2},{4,5},{5,4},{6,7},{7,6},{8,9},{9,8},{10,11... | collective-permute-start | bytes 3145736 | tf_op jit(solution)/shard_map/ppermute | solution.py:721
  271.8 120.1 %collective-permute-start.39 = (bf16[512,1024]{1,0:T(8,128)(2,1)}, bf16[512,1024]{1,0:T(8,128)(2,1)}, u32[]{:S(2)}, u32[]{:S(2)}) collective-permute-start(bf16[512,1024]{1,0:T(8,128)(2,1)} %get-tuple-element.261.own_ref), channel_id=1, source_target_pairs={{0,1},{1,0},{2,3},{3,2},{4,5},{5,4},{6,7},{7,6},{8,9},{9,8},{10,11... | collective-permute-start | bytes 3145736 | tf_op jit(solution)/shard_map/ppermute | solution.py:721
  272.5 124.9 %collective-permute-start.38 = (bf16[512,1024]{1,0:T(8,128)(2,1)}, bf16[512,1024]{1,0:T(8,128)(2,1)}, u32[]{:S(2)}, u32[]{:S(2)}) collective-permute-start(bf16[512,1024]{1,0:T(8,128)(2,1)} %get-tuple-element.259.own_ref), channel_id=1, source_target_pairs={{0,1},{1,0},{2,3},{3,2},{4,5},{5,4},{6,7},{7,6},{8,9},{9,8},{10,11... | collective-permute-start | bytes 3145736 | tf_op jit(solution)/shard_map/ppermute | solution.py:721
  284.3 24.3 %collective-permute-start.36 = (bf16[2,512,512]{2,1,0:T(8,128)(2,1)}, bf16[2,512,512]{2,1,0:T(8,128)(2,1)S(1)}, u32[]{:S(2)}, u32[]{:S(2)}) collective-permute-start(bf16[2,512,512]{2,1,0:T(8,128)(2,1)} %get-tuple-element.245), channel_id=1, source_target_pairs={{0,2},{2,0},{4,6},{6,4},{8,10},{10,8},{12,14},{14,12},{1,3},{3,1},... | collective-permute-start | bytes 3145736 | tf_op jit(solution)/shard_map/ppermute | solution.py:721
  308.4 16.7 %collective-permute-start.37 = (bf16[2,512,512]{2,1,0:T(8,128)(2,1)}, bf16[2,512,512]{2,1,0:T(8,128)(2,1)S(1)}, u32[]{:S(2)}, u32[]{:S(2)}) collective-permute-start(bf16[2,512,512]{2,1,0:T(8,128)(2,1)} %get-tuple-element.250), channel_id=1, source_target_pairs={{0,2},{2,0},{4,6},{6,4},{8,10},{10,8},{12,14},{14,12},{1,3},{3,1},... | collective-permute-start | bytes 3145736 | tf_op jit(solution)/shard_map/ppermute | solution.py:721
  311.1 86.4 %collective-permute-start.40 = (bf16[2,512,512]{2,1,0:T(8,128)(2,1)}, bf16[2,512,512]{2,1,0:T(8,128)(2,1)}, u32[]{:S(2)}, u32[]{:S(2)}) collective-permute-start(bf16[2,512,512]{2,1,0:T(8,128)(2,1)} %add_convert_fusion.3), channel_id=1, source_target_pairs={{4,0},{6,2},{8,4},{10,6},{12,8},{14,10},{5,1},{7,3},{9,5},{11,7},{... | collective-permute-start | bytes 3145736 | tf_op jit(solution)/shard_map/ppermute | solution.py:726
  325.5 87.1 %collective-permute-start.44 = (bf16[512,512]{1,0:T(8,128)(2,1)S(1)}, bf16[512,512]{1,0:T(8,128)(2,1)S(1)}, u32[]{:S(2)}, u32[]{:S(2)}) collective-permute-start(bf16[512,512]{1,0:T(8,128)(2,1)S(1)} %get-tuple-element.349), channel_id=1, source_target_pairs={{0,8},{2,10},{4,12},{6,14},{8,0},{10,2},{12,4},{14,6},{1,9},{3,11}... | collective-permute-start | bytes 1572872 | tf_op jit(solution)/shard_map/ppermute | solution.py:721
  352.1 60.5 %collective-permute-start.43 = (bf16[512,512]{1,0:T(8,128)(2,1)S(1)}, bf16[512,512]{1,0:T(8,128)(2,1)S(1)}, u32[]{:S(2)}, u32[]{:S(2)}) collective-permute-start(bf16[512,512]{1,0:T(8,128)(2,1)S(1)} %get-tuple-element.350), channel_id=1, source_target_pairs={{0,4},{2,6},{4,0},{6,2},{8,12},{10,14},{12,8},{14,10},{1,5},{3,7},... | collective-permute-start | bytes 1572872 | tf_op jit(solution)/shard_map/ppermute | solution.py:721
  391.9 20.7 %collective-permute-start.42 = (bf16[2,512,512]{2,1,0:T(8,128)(2,1)}, bf16[2,512,512]{2,1,0:T(8,128)(2,1)S(1)}, u32[]{:S(2)}, u32[]{:S(2)}) collective-permute-start(bf16[2,512,512]{2,1,0:T(8,128)(2,1)} %get-tuple-element.271), channel_id=1, source_target_pairs={{0,2},{2,0},{4,6},{6,4},{8,10},{10,8},{12,14},{14,12},{1,3},{3,1},... | collective-permute-start | bytes 3145736 | tf_op jit(solution)/shard_map/ppermute | solution.py:721
  397.4 15.2 %collective-permute-start.41 = (bf16[2,512,512]{2,1,0:T(8,128)(2,1)}, bf16[2,512,512]{2,1,0:T(8,128)(2,1)S(1)}, u32[]{:S(2)}, u32[]{:S(2)}) collective-permute-start(bf16[2,512,512]{2,1,0:T(8,128)(2,1)} %get-tuple-element.268), channel_id=1, source_target_pairs={{0,2},{2,0},{4,6},{6,4},{8,10},{10,8},{12,14},{14,12},{1,3},{3,1},... | collective-permute-start | bytes 3145736 | tf_op jit(solution)/shard_map/ppermute | solution.py:721
  418.2 48.6 %collective-permute-start.46 = (bf16[2,512,512]{2,1,0:T(8,128)(2,1)}, bf16[2,512,512]{2,1,0:T(8,128)(2,1)S(1)}, u32[]{:S(2)}, u32[]{:S(2)}) collective-permute-start(bf16[2,512,512]{2,1,0:T(8,128)(2,1)} %get-tuple-element.275), channel_id=1, source_target_pairs={{0,4},{2,6},{4,0},{6,2},{8,12},{10,14},{12,8},{14,10},{1,5},{3,7},... | collective-permute-start | bytes 3145736 | tf_op jit(solution)/shard_map/ppermute | solution.py:721
  418.5 48.3 %collective-permute-start.47 = (bf16[2,512,512]{2,1,0:T(8,128)(2,1)}, bf16[2,512,512]{2,1,0:T(8,128)(2,1)S(1)}, u32[]{:S(2)}, u32[]{:S(2)}) collective-permute-start(bf16[2,512,512]{2,1,0:T(8,128)(2,1)} %get-tuple-element.288), channel_id=1, source_target_pairs={{0,8},{2,10},{4,12},{6,14},{8,0},{10,2},{12,4},{14,6},{1,9},{3,11}... | collective-permute-start | bytes 3145736 | tf_op jit(solution)/shard_map/ppermute | solution.py:721
  418.9 47.9 %collective-permute-start.45 = (bf16[2,512,512]{2,1,0:T(8,128)(2,1)S(1)}, bf16[2,512,512]{2,1,0:T(8,128)(2,1)S(1)}, u32[]{:S(2)}, u32[]{:S(2)}) collective-permute-start(bf16[2,512,512]{2,1,0:T(8,128)(2,1)S(1)} %copy-done.32), channel_id=1, source_target_pairs={{0,2},{2,0},{4,6},{6,4},{8,10},{10,8},{12,14},{14,12},{1,3},{3,1},... | collective-permute-start | bytes 3145736 | tf_op jit(solution)/shard_map/ppermute | solution.py:721
  447.6 29.8 %collective-permute-start.48 = (bf16[512,1024]{1,0:T(8,128)(2,1)}, bf16[512,1024]{1,0:T(8,128)(2,1)S(1)}, u32[]{:S(2)}, u32[]{:S(2)}) collective-permute-start(bf16[512,1024]{1,0:T(8,128)(2,1)} %get-tuple-element.291), channel_id=1, source_target_pairs={{0,2},{2,0},{4,6},{6,4},{8,10},{10,8},{12,14},{14,12},{1,3},{3,1},... | collective-permute-start | bytes 3145736 | tf_op jit(solution)/shard_map/ppermute | solution.py:721
  448.1 43.3 %collective-permute-start.50 = (bf16[512,1024]{1,0:T(8,128)(2,1)}, bf16[512,1024]{1,0:T(8,128)(2,1)}, u32[]{:S(2)}, u32[]{:S(2)}) collective-permute-start(bf16[512,1024]{1,0:T(8,128)(2,1)} %get-tuple-element.282.own_ref), channel_id=1, source_target_pairs={{0,1},{1,0},{2,3},{3,2},{4,5},{5,4},{6,7},{7,6},{8,9},{9,8},{10,11... | collective-permute-start | bytes 3145736 | tf_op jit(solution)/shard_map/ppermute | solution.py:721
  478.0 11.0 %collective-permute-start.51 = (bf16[128,512]{1,0:T(8,128)(2,1)S(1)}, bf16[128,512]{1,0:T(8,128)(2,1)S(1)}, u32[]{:S(2)}, u32[]{:S(2)}) collective-permute-start(bf16[128,512]{1,0:T(8,128)(2,1)S(1)} %get-tuple-element.347), channel_id=1, source_target_pairs={{0,8},{2,10},{4,12},{6,14},{8,0},{10,2},{12,4},{14,6},{1,9},{3,11}... | collective-permute-start | bytes 393224 | tf_op jit(solution)/shard_map/ppermute | solution.py:721
  483.1 36.4 %collective-permute-start.57 = (bf16[512,1024]{1,0:T(8,128)(2,1)}, bf16[512,1024]{1,0:T(8,128)(2,1)}, u32[]{:S(2)}, u32[]{:S(2)}) collective-permute-start(bf16[512,1024]{1,0:T(8,128)(2,1)} %get-tuple-element.292.own_ref), channel_id=1, source_target_pairs={{0,1},{1,0},{2,3},{3,2},{4,5},{5,4},{6,7},{7,6},{8,9},{9,8},{10,11... | collective-permute-start | bytes 3145736 | tf_op jit(solution)/shard_map/ppermute | solution.py:721
  499.8 11.2 %collective-permute-start.53 = (bf16[128,512]{1,0:T(8,128)(2,1)S(1)}, bf16[128,512]{1,0:T(8,128)(2,1)S(1)}, u32[]{:S(2)}, u32[]{:S(2)}) collective-permute-start(bf16[128,512]{1,0:T(8,128)(2,1)S(1)} %get-tuple-element.341), channel_id=1, source_target_pairs={{0,8},{2,10},{4,12},{6,14},{8,0},{10,2},{12,4},{14,6},{1,9},{3,11}... | collective-permute-start | bytes 393224 | tf_op jit(solution)/shard_map/ppermute | solution.py:721
  500.2 10.8 %collective-permute-start.56 = (bf16[128,512]{1,0:T(8,128)(2,1)S(1)}, bf16[128,512]{1,0:T(8,128)(2,1)S(1)}, u32[]{:S(2)}, u32[]{:S(2)}) collective-permute-start(bf16[128,512]{1,0:T(8,128)(2,1)S(1)} %get-tuple-element.339), channel_id=1, source_target_pairs={{0,4},{2,6},{4,0},{6,2},{8,12},{10,14},{12,8},{14,10},{1,5},{3,7},... | collective-permute-start | bytes 393224 | tf_op jit(solution)/shard_map/ppermute | solution.py:721
  500.5 17.8 %collective-permute-start.60 = (bf16[64,1024]{1,0:T(8,128)(2,1)S(1)}, bf16[64,1024]{1,0:T(8,128)(2,1)S(1)}, u32[]{:S(2)}, u32[]{:S(2)}) collective-permute-start(bf16[64,1024]{1,0:T(8,128)(2,1)S(1)} %slice.189), channel_id=1, source_target_pairs={{0,16},{16,0},{1,17},{17,1},{2,18},{18,2},{3,19},{19,3},{4,20},{20... | collective-permute-start | bytes 393224 | tf_op jit(solution)/shard_map/ppermute | solution.py:721
  513.9 10.3 %collective-permute-start.61 = (f32[1,256]{1,0:T(1,128)S(1)}, f32[1,256]{1,0:T(1,128)S(1)}, u32[]{:S(2)}, u32[]{:S(2)}) collective-permute-start(f32[1,256]{1,0:T(1,128)S(1)} %pad_maximum_fusion.11), channel_id=1, source_target_pairs={{0,1},{1,0},{2,3},{3,2},{4,5},{5,4},{6,7},{7,6},{8,9},{9,8},{10,11... | collective-permute-start | bytes 3080 | tf_op jit(solution)/shard_map/ppermute | solution.py:721
  524.3 9.7 %collective-permute-start.64 = (bf16[64,1024]{1,0:T(8,128)(2,1)S(1)}, bf16[64,1024]{1,0:T(8,128)(2,1)S(1)}, u32[]{:S(2)}, u32[]{:S(2)}) collective-permute-start(bf16[64,1024]{1,0:T(8,128)(2,1)S(1)} %slice.191), channel_id=1, source_target_pairs={{0,16},{16,0},{1,17},{17,1},{2,18},{18,2},{3,19},{19,3},{4,20},{20... | collective-permute-start | bytes 393224 | tf_op jit(solution)/shard_map/ppermute | solution.py:721
  (63 other events, 400.9 us)
Sparse Core Ops, SparseCore 0:
  10.9 68.8 all-gather.2
  91.1 68.8 all-gather.4
  271.9 199.8 reduce-scatter.1

commit v5 on v4

--- a/solution.py
+++ b/solution.py
@@ -86,7 +86,8 @@
         kv_ref[0, :, cols] = turn(lin * rms(lin) * hgain_ref[...], cos_ref[...], sin_ref[...]).astype(BF)
 
 
-def q_kernel(heads, normed_ref, w_ref, hgain_ref, cos_ref, sin_ref, q_ref, lin_ref):
+def q_kernel(heads, normed_ref, w_ref, hgain_ref, cos_ref, sin_ref, *refs):
+    q_ref, lin_ref = refs[-2:]
     both = mm(normed_ref[...], w_ref[...])
     for h in range(heads):
         cols = slice(h * HEAD_SIZE, (h + 1) * HEAD_SIZE)
@@ -125,12 +126,29 @@
     return groups
 
 
+def slot_inputs(kv, rows):
+    if isinstance(kv, tuple):
+        return [(part, (rows, 128), lambda h, i: (0, h)) for part in kv]
+    return [(kv, (2, rows, 128), lambda h, i: (0, 0, h))]
+
+
+def take_slots(refs, pairs):
+    taken = []
+    for pair in pairs:
+        if pair:
+            taken.append((refs.pop(0), refs.pop(0)))
+        else:
+            ref = refs.pop(0)
+            taken.append((ref.at[0], ref.at[1]))
+    return taken
+
+
 def fwd_kernel(plan, idx_ref, lo_ref, *refs):
     halves, slots, halos = plan["halves"], plan["slots"], plan["halos"]
     refs = list(refs)
     q_refs = [refs.pop(0) for _ in halves]
-    slot_refs = [refs.pop(0) for _ in slots]
-    halo_refs = [refs.pop(0) for _ in halos]
+    slot_refs = take_slots(refs, plan["pairs"])
+    halo_refs = take_slots(refs, [False] * len(halos))
     prior = [refs.pop(0) for _ in range(2 * len(halves))] if plan["carry"] else None
     if plan["last"]:
         if plan["alias"]:
@@ -155,14 +173,14 @@
         empty = [prior is None]
 
         def add(kv_ref, mask=None):
-            scores = mm(qs[...], kv_ref[0], NT)
+            scores = mm(qs[...], kv_ref[0][...], NT)
             if mask is not None:
                 scores = jnp.where(mask, scores, MASKED)
             weights = jnp.exp2(scores)
             total = weights[:, :128]
             for at in range(128, weights.shape[1], 128):
                 total = total + weights[:, at : at + 128]
-            part = mm(weights.astype(BF), kv_ref[1])
+            part = mm(weights.astype(BF), kv_ref[1][...])
             if empty[0]:
                 acc[...] = part
                 tot[...] = total
@@ -209,14 +227,14 @@
 
 
 def attention_forward(halves, scalars, q, low, slots, halos, carry=None, last=None):
-    rows, heads = q.shape[0] // 2, q.shape[1] // 256
-    plan = dict(halves=halves, slots=list(slots), halos=list(halos), carry=carry is not None,
+    rows, heads = q[0].shape[0], q[0].shape[1] // 256
+    plan = dict(halves=halves, slots=list(slots), pairs=[isinstance(kv, tuple) for kv in slots.values()], halos=list(halos), carry=carry is not None,
                 last=last is not None, alias=last is not None and last[0] is not None)
     part = lambda h, i: (0, h)
     ins = [(low, (rows, 128), lambda h, i: (0, 0))]
-    ins += [(q, (rows, 256), lambda h, i, half=half: (half, h)) for half in halves]
+    ins += [(of_half, (rows, 256), part) for of_half in q]
     for kv in list(slots.values()) + list(halos.values()):
-        ins.append((kv, (2, rows, 128), lambda h, i: (0, 0, h)))
+        ins += slot_inputs(kv, rows)
     if carry is not None:
         ins += [(c, (rows, 256), part) for c in carry]
     scratch, keep = [], {}
@@ -254,8 +272,8 @@
 def bwd_kernel(plan, idx_ref, q_ref, do_ref, lse_ref, delta_ref, lo_ref, *refs):
     half, slots, halos = plan["half"], plan["slots"], plan["halos"]
     refs = list(refs)
-    slot_refs = [refs.pop(0) for _ in slots]
-    halo_refs = [refs.pop(0) for _ in halos]
+    slot_refs = take_slots(refs, plan["pairs"])
+    halo_refs = take_slots(refs, [False] * len(halos))
     prior_dq = refs.pop(0) if plan["carry"] else None
     prior = [refs.pop(0) for _ in slots] if plan["sum"] else None
     if plan["alias"]:
@@ -275,9 +293,9 @@
     dq[...] = jnp.zeros_like(dq) if prior_dq is None else prior_dq[...]
 
     def block(kv_ref, out_ref, mask=None, before=None):
-        keys = kv_ref[0]
+        keys = kv_ref[0][...]
         scores = mm(keys, qs[...], NT)
-        dp = mm(kv_ref[1], dos[...], NT)
+        dp = mm(kv_ref[1][...], dos[...], NT)
         scores = scores - lses[...]
         if mask is not None:
             scores = jnp.where(mask, scores, MASKED)
@@ -337,21 +355,22 @@
 
 
 def attention_backward(half, scalars, q, do, lse, delta, low, slots, halos, carry=None, prior=None, last=True, whole=None):
-    rows, heads = q.shape[0] // 2, q.shape[1] // 256
-    plan = dict(half=half, slots=list(slots), halos=list(halos), carry=carry is not None,
+    rows, heads = q.shape[0], q.shape[1] // 256
+    plan = dict(half=half, slots=list(slots), pairs=[isinstance(kv, tuple) for kv in slots.values()], halos=list(halos), carry=carry is not None,
                 sum=prior is not None, last=last, alias=whole is not None)
     part = lambda h, i: (0, h)
     stat = lambda h, i: (h, 0, 0)
     kv_map = lambda h, i: (0, 0, h)
     ins = [
-        (q, (rows, 256), lambda h, i: (half, h)),
+        (q, (rows, 256), part),
         (do, (rows, 256), part),
         (lse, (1, 8, rows), stat),
         (delta, (1, 8, rows), stat),
         (low, (8, 2 * rows), lambda h, i: (0, 0)),
     ]
     pieces = list(slots.values()) + list(halos.values())
-    ins += [(kv, (2, rows, 128), kv_map) for kv in pieces]
+    for kv in pieces:
+        ins += slot_inputs(kv, rows)
     if carry is not None:
         ins.append((carry, (128, 2 * rows), lambda h, i: (h, 0)))
     if prior is not None:
@@ -364,7 +383,7 @@
         outs = [(shaped((2 * rows, heads * 256), F32), (rows, 256), lambda h, i: (half, h))]
     else:
         outs = [(shaped((heads * 128, 2 * rows), F32), (128, 2 * rows), lambda h, i: (h, 0))]
-    outs += [(shaped(kv.shape, BF), (2, rows, 128), kv_map) for kv in pieces]
+    outs += [(shaped((2, rows, heads * 128), BF), (2, rows, 128), kv_map) for _ in pieces]
     scratch = [
         pltpu.VMEM((2 * rows, 128), BF),
         pltpu.VMEM((2 * rows, 128), BF),
@@ -372,7 +391,7 @@
         pltpu.VMEM((1, 2 * rows), F32),
         pltpu.VMEM((128, 2 * rows), F32),
     ]
-    us = 4 + 6 * (len(slots) + len(halos)) if carry is not None or halos else 0
+    us = 4 + 6 * (len(slots) + len(halos)) if carry is not None or halos else 0.1
     results = call(functools.partial(bwd_kernel, plan), "attend_back", (heads,), ins, outs, scratch,
                    scalars=scalars, us=us, keep=keep)
     n = len(slots)
@@ -556,6 +575,26 @@
     return call(weight_kernel, "weight_grad", (n // cols,), ins, outs, keep=keep)[0]
 
 
+def slot_weight_kernel(order, part_ref, left_ref, right_ref, low_ref, high_ref, total):
+    total[...] = mm(left_ref[...], right_ref[...], TN)
+    wide = total.shape[0] // len(order)
+    for at, slot in enumerate(order):
+        block = jnp.bitwise_xor(part_ref[0], slot)
+        piece = total[pl.ds(pl.multiple_of(block * wide, wide), wide), :].astype(BF)
+        out_ref, row = (low_ref, at) if at < len(order) // 2 else (high_ref, at - len(order) // 2)
+        out_ref[row * wide : (row + 1) * wide, :] = piece
+
+
+def slot_weight_grad(order, part, left, right):
+    tokens, model = left.shape
+    cols = right.shape[1]
+    once = lambda j, i: (0, 0)
+    ins = [(left, (tokens, model), once), (right, (tokens, cols), once)]
+    half = shaped((model // 2, cols), BF)
+    return call(functools.partial(slot_weight_kernel, order), "slot_weight_grad", (1,), ins,
+                [(half, half.shape, once)] * 2, [pltpu.VMEM((model, cols), F32)], scalars=part[None])
+
+
 def weight_halves_kernel(left_ref, right_ref, high_ref, low_ref):
     for half, out_ref in enumerate((high_ref, low_ref)):
 
@@ -681,22 +720,22 @@
     return call(tokens_kernel, "tokens_back", (steps,), ins, outs, keep=keep, us=20)
 
 
-def share_kernel(chunk, share_ref, out_ref, gate_ref, up_ref, down_ref):
-    o_cols, units = out_ref.shape[1], gate_ref.shape[1]
-    out_ref[...] = share_ref[:, :o_cols].astype(F32)
+def share_kernel(chunk, ffn_ref, own_ref, got_ref, out_ref, gate_ref, up_ref, down_ref):
+    units = gate_ref.shape[1]
+    out_ref[...] = own_ref[...].astype(F32) + got_ref[...].astype(F32)
     for at in range(0, units, chunk):
-        to = o_cols + 2 * at
-        gate_ref[:, at : at + chunk] = share_ref[:, to : to + chunk].astype(F32)
-        up_ref[:, at : at + chunk] = share_ref[:, to + chunk : to + 2 * chunk].astype(F32)
-    down_ref[...] = share_ref[:, o_cols + 2 * units :].astype(F32)
-
-
-def unpack(chunk, o_cols, share):
-    wide = share.shape[0]
-    units = (share.shape[1] - o_cols) // 3
+        gate_ref[:, at : at + chunk] = ffn_ref[:, 2 * at : 2 * at + chunk].astype(F32)
+        up_ref[:, at : at + chunk] = ffn_ref[:, 2 * at + chunk : 2 * at + 2 * chunk].astype(F32)
+    down_ref[...] = ffn_ref[:, 2 * units :].astype(F32)
+
+
+def unpack(chunk, ffn_share, out_grad):
+    wide, units = ffn_share.shape[0], ffn_share.shape[1] // 3
+    o_cols = out_grad[0].shape[1]
     whole = lambda f: (0, 0)
+    ins = [(ffn_share, ffn_share.shape, whole)] + [(grad, (wide, o_cols), whole) for grad in out_grad]
     outs = [(shaped((wide, cols), F32), (wide, cols), whole) for cols in (o_cols, units, units, units)]
-    return call(functools.partial(share_kernel, chunk), "unpack", (1,), [(share, share.shape, whole)], outs)
+    return call(functools.partial(share_kernel, chunk), "unpack", (1,), ins, outs)
 
 
 def layer_kernel(resid_ref, own_ref, got_ref, *refs):
@@ -843,7 +882,7 @@
     kv_one = gather_first(kv_piece)
     kv_near = gather_near(kv_one)
     w_kv, kv_far = gather_far(kv_near)
-    q_one = gather_first(after(w_query, kv_one), kv_far)
+    q_one = gather_first(after(w_query, kv_piece), kv_far)
     w_od = lax.all_gather(od_piece, weight_axes, axis=0, tiled=True)
     gains = jnp.concatenate([attn_gain, ffn_gain, query_gain, key_gain])[None]
     gains = jnp.where(jnp.arange(parts)[:, None] == part, gains, jnp.zeros((), BF))
@@ -896,16 +935,23 @@
     normed, kv_p, k_lin_p = keys_values(0, after(gain_one_s, *q_near[1:]))
     normed, kv_c, k_lin_c = keys_values(1, after(gain_one_s, kv_p), normed)
     w_q, _ = gather_far(q_near, kv_c)
-    mine = lambda f: (f, 0)
-    q, q_lin = call(
-        functools.partial(q_kernel, heads), "queries", (2,),
-        [
-            (normed, (rows, model), mine), (w_q, (model, q_cols), lambda f: (0, 0)),
-            (gain_q, (1, HEAD_SIZE), lambda f: (0, 0)),
+    def queries(half, gain, whole=None):
+        mine = lambda f: (half, 0)
+        ins = [
+            (normed, (rows, model), mine), (w_q, (model, q_cols), once), (gain, (1, HEAD_SIZE), once),
             (cos, (rows, HEAD_SIZE), mine), (sin, (rows, HEAD_SIZE), mine),
-        ],
-        [(shaped((2 * rows, q_cols), BF), (rows, q_cols), mine), (shaped((2 * rows, q_cols), F32), (rows, q_cols), mine)],
-    )
+        ]
+        keep = {}
+        if whole is not None:
+            keep = {len(ins): 1}
+            ins.append((whole, None, None))
+        outs = [
+            (shaped((rows, q_cols), BF), (rows, q_cols), once),
+            (shaped((2 * rows, q_cols), F32), (rows, q_cols), mine),
+        ]
+        return call(functools.partial(q_kernel, heads), "queries", (1,), ins, outs, keep=keep)
+
+    q_c, q_lin = queries(1, gain_q)
 
     def pick(source, wanted):
         return {s: source[s] for s in source if s in wanted}
@@ -924,7 +970,7 @@
         halos.update({d: shift(kv_c, d) for d in range(1, n_halo)})
     ready = ()
     if ctx_size == 8:
-        slots[2], slots[4] = after(slots[2], q), after(slots[4], q)
+        slots[2], slots[4] = after(slots[2], q_c), after(slots[4], q_c)
         far_k, far_v = swap(slots[4][0], "ctx", 2), swap(slots[2][1], "ctx", 4)
         slots[3], slots[5] = swap(slots[2], "ctx", 1), swap(slots[4], "ctx", 1)
         halos[2] = shift(after(kv_c, slots[2]), 2)
@@ -932,21 +978,21 @@
         ready = (slots[2], slots[4])
     w_gu = lax.all_gather(after(gu_piece, w_od), weight_axes, axis=0, tiled=True)
     c_state = attention_forward(
-        (1,), after(scalars, *ready), q, low_col, pick(slots, near), pick(halos, (0,))
+        (1,), after(scalars, *ready), (q_c,), low_col, pick(slots, near), pick(halos, (0,))
     )
+    q_p, q_lin = queries(0, after(gain_q, c_state[0]), q_lin)
     if ctx_size == 8:
-        slots[6] = jnp.stack([after(far_k, c_state[0]), after(far_v, c_state[0])])
-        slots[7] = swap(slots[6], "ctx", 1)
-        ready = (slots[7],)
+        slots[6] = after(far_k, c_state[0]), after(far_v, c_state[0])
+        slots[7] = tuple(swap(part, "ctx", 1) for part in slots[6])
     attended, lse_p = attention_forward(
-        (0,), after(scalars, c_state[0], *ready), q, low_col, slots, {}, None, (None,)
+        (0,), after(scalars, q_p), (q_p,), low_col, slots, {}, None, (None,)
     )
     part_p = out_projection(0, attended, w_od)
     got_p = swap(part_p, "tensor", 1)
     if ctx_size == 8:
         halos[1] = swap(jnp.where(odd, after(halos[2], part_p), kv_c), "ctx", 1)
     attended, lse_c = attention_forward(
-        (1,), after(scalars, part_p), q, low_col, pick(slots, middle + far), pick(halos, range(1, n_halo)),
+        (1,), after(scalars, part_p), (q_c,), low_col, pick(slots, middle + far), pick(halos, range(1, n_halo)),
         c_state, (attended,),
     )
     part_c = out_projection(1, attended, w_od)
@@ -961,21 +1007,19 @@
     )
     back_got_c = swap(back_c, "tensor", 1)
     normed_ffn, hidden, d_gu = whole
-    width = o_cols + 3 * units
-    rest_grads = weight_grad(normed_ffn, d_gu, o_cols, width, min(1024, o_cols))
-    rest_grads = weight_grad(cotangent, hidden, o_cols + 2 * units, width, chunk, rest_grads)
+    ffn_grads = weight_grad(normed_ffn, d_gu, 0, 3 * units, 2 * chunk)
+    ffn_grads = weight_grad(cotangent, hidden, 2 * units, 3 * units, chunk, ffn_grads)
+    ffn_share = lax.psum_scatter(ffn_grads, weight_axes, scatter_dimension=0, tiled=True)
     d_resid_p, d_mixed, d_att_p, delta_p, d_two_p = mixed_back(
-        0, back_p, back_got_p, resid_p, after(gain_two, rest_grads), cotangent, w_od, o_cols, attended
+        0, back_p, back_got_p, resid_p, after(gain_two, ffn_grads), cotangent, w_od, o_cols, attended
     )
-    out_p, out_c = after(out_p, back_got_c), after(out_c, back_got_c)
-    out_got_p, out_got_c = swap(out_p, "tensor", 1), swap(out_c, "tensor", 1)
 
     of_rows = [(d_att_p, lse_p, delta_p)]
 
     def back_rows(half, deps, slots, halos, carry, prior=None, whole=None, last=False):
         do, lse, delta = of_rows[half]
         return attention_backward(
-            half, after(scalars, *deps), q, do, lse, delta, low_row, slots, halos, carry, prior, last, whole
+            half, after(scalars, *deps), (q_p, q_c)[half], do, lse, delta, low_row, slots, halos, carry, prior, last, whole
         )
 
     dq_p, prior, _ = back_rows(0, (d_att_p,), pick(slots, far), {}, None)
@@ -983,12 +1027,15 @@
         1, back_c, back_got_c, resid_c, after(gain_two, dq_p), cotangent, w_od, o_cols, attended, d_mixed
     )
     of_rows.append((d_att_c, lse_c, delta_c))
-    rest_grads = weight_grad(d_mixed, attended, 0, width, min(1024, o_cols), rest_grads)
-    rest_share = lax.psum_scatter(rest_grads, weight_axes, scatter_dimension=0, tiled=True)
-    dq_c, _, g_halo = back_rows(1, (rest_grads,), {}, halos, None)
+    out_low, out_high = slot_weight_grad(order, part, d_mixed, attended)
+    out_p, out_c = after(out_p, out_low), after(out_c, out_low)
+    out_got_p, out_got_c = swap(out_p, "tensor", 1), swap(out_c, "tensor", 1)
+    dq_c, _, g_halo = back_rows(1, (out_low,), {}, halos, None)
+    out_grad = scatter_rows(out_low, out_high, dq_c)
     if ctx_size == 8:
         near_one = swap(g_halo[1], "ctx", 1)
-    dq_c, g, _ = back_rows(1, (dq_c,), pick(slots, far), {}, dq_c, prior)
+    dq_c, g, _ = back_rows(1, (dq_c, out_grad[0]), pick(slots, far), {}, dq_c, prior)
+    out_grad = scatter_more(out_grad, dq_c)
     zero = jnp.zeros((), BF)
     ready = ()
     if ctx_size == 8:
@@ -998,12 +1045,13 @@
         halo_two = shift(two_back, -2)
         halo_near = jnp.where(odd, zero, near_one)
         ready = (two_back, halo_near)
-    dq, prior, _ = back_rows(0, (dq_c, *ready), pick(slots, near + middle), {}, dq_p, None, None, True)
+    dq, prior, _ = back_rows(0, (dq_c, out_grad[0], *ready), pick(slots, near + middle), {}, dq_p, None, None, True)
     if ctx_size == 8:
         g6 = add_low(g[6], after(got7, dq))
         far_k, far_v = swap(g6[0], "ctx", 2), swap(g6[1], "ctx", 4)
         ready = (g6,)
-    dq_c, more, _ = back_rows(1, (dq, *ready), pick(slots, middle), {}, dq_c, prior)
+    out_grad = scatter_sum(out_grad, dq)
+    dq_c, more, _ = back_rows(1, (dq, out_grad[0], *ready), pick(slots, middle), {}, dq_c, prior)
     g.update(more)
     if ctx_size == 8:
         got3, got5 = swap(g[3], "ctx", 1), swap(g[5], "ctx", 1)
@@ -1012,7 +1060,7 @@
     g.update(more)
     if ctx_size == 8:
         got1 = swap(g[1], "ctx", 1)
-        far_k, far_v, got3, got5 = (after(v, dq) for v in (far_k, far_v, got3, got5))
+        far_k, far_v, got3, got5 = (after(v, dq, out_grad[1], ffn_share) for v in (far_k, far_v, got3, got5))
         to_x, to_y = merge(g[2], got3, g[4], got5, far_k, far_v)
         ready = (to_x,)
         keys_p = values_p = [g[0], got1, swap(to_x, "ctx", 2), swap(to_y, "ctx", 4)]
@@ -1041,7 +1089,7 @@
     heads = jnp.concatenate([q_heads, k_heads_c + k_heads_p], axis=1)
     heads_got = swap(heads, "tensor", 1)
     grad_tokens, d_one_c = tokens_back(1, into_c, into_got_c, tokens, after(gain_one, kv_low, q_grad[0]), d_resid_c)
-    out_share, gate_share, up_share, down_share = unpack(chunk, o_cols, after(rest_share, d_one_c))
+    out_share, gate_share, up_share, down_share = unpack(chunk, after(ffn_share, d_one_c), out_grad)
     q_grad = scatter_sum(q_grad, gate_share)
     kv_grad = scatter_rows(kv_low, kv_high, gate_share)
     layer_out = add_layer(0, after(resid_p, kv_grad[0], q_grad[0]), out_p, out_got_p)

time: 561 us -> 549 us (0.979)
  waiting for transfers between devices: 78.1 us -> 58.5 us
  starting transfers between devices: 113 us -> 122 us
    ppermute x2, waiting for transfers between devices: 21.2 us -> 10.6 us  [shift(): lax.ppermute(value, 'ctx', [(i, i + by) for i in range(size) if 0 <= i +...]
    ppermute x65 -> x72, waiting for transfers between devices: 56.8 us -> 47.9 us  [swap(): return lax.ppermute(value, axis, [(i, i ^ bit) for i in range(size)])]
    ppermute x65 -> x72, starting transfers between devices: 109 us -> 117 us  [swap(): return lax.ppermute(value, axis, [(i, i ^ bit) for i in range(size)])]
    pallas_call x33 -> x34, Pallas kernels: 293 us -> 296 us  [call(): pl.pallas_call(kernel, grid_spec=pltpu.PrefetchScalarGridSpec(num_scalar_...]
    unnamed x94 -> x100, local copies, waits for them, and re-layouts: 18 us -> 16.4 us
  transfers between devices with their start and end apart: 70 -> 77, of which waited for: 22 -> 21; matrix products, arithmetic and copies ran while one was open for 7% -> 7% of each run, Pallas kernels for 50% -> 55%
where the time goes in v5:
time: 549 us; the launch traced here: 540 us
  Pallas kernels  296 us (54%)
  starting transfers between devices  122 us (22%)
  waiting for transfers between devices  58.5 us (11%)
  local copies, waits for them, and re-layouts  27.9 us (5%)
  between operations  15.3 us (3%)
  other arithmetic  14.8 us (3%)
    pallas_call x34, Pallas kernels, call(): pl.pallas_call(kernel, grid_spec=pltpu.PrefetchScalarGridSpec(num_scalar_...  296 us
    ppermute x72, starting transfers between devices, swap(): return lax.ppermute(value, axis, [(i, i ^ bit) for i in range(size)])  117 us
    ppermute x72, waiting for transfers between devices, swap(): return lax.ppermute(value, axis, [(i, i ^ bit) for i in range(size)])  47.9 us
    unnamed x100, local copies, waits for them, and re-layouts  16.4 us
  transfers between devices with their start and end apart: 77, of which 21 were waited for; matrix products, arithmetic and copies ran while one was open for 7% of the time, Pallas kernels for 55%

profile of v5, /device:TPU:0, one launch (start us, length us, event | category | flops | bytes accessed | tf_op | source)
XLA Modules:
  0.0 539.7 jit_solution(367463080762980639)
XLA Ops:
  10.8 3.7 collective-permute-start.1
  28.0 3.9 collective-permute-done.7
  44.6 3.7 fusion.5.x_ref
  57.9 3.6 collective-permute-done.16
  62.8 5.6 %keys_values.2 = (bf16[1024,1024]{1,0:T(8,128)(2,1)}, bf16[2,512,512]{2,1,0:T(8,128)(2,1)}, f32[512,512]{1,0:T(8,128)}) custom-call(bf16[1024,1024]{1,0:T(8,128)(2,1)} %fusion.5.x_ref, f32[1,1024]{1,0:T(1,128)} %fusion.1.gain_ref, bf16[1024,1024]{1,0:T(8,128)(2,1)} %copy-done, f32[1,128]{1,0:T(1,128)} %reshape.120.hgain_ref.gain_ref, ...), custom_call_target="tpu_custom_call" | custom-call | tf_op jit(solution)/shard_map/keys_values/pallas_call | solution.py:46
  72.7 5.6 %keys_values.3 = (bf16[1024,1024]{1,0:T(8,128)(2,1)}, bf16[2,512,512]{2,1,0:T(8,128)(2,1)}, f32[512,512]{1,0:T(8,128)}) custom-call(bf16[1024,1024]{1,0:T(8,128)(2,1)} %fusion.5.x_ref, f32[1,1024]{1,0:T(1,128)} %fusion.1.gain_ref, bf16[1024,1024]{1,0:T(8,128)(2,1)} %copy-done, ...), custom_call_target="tpu_custom_call", output_to_operand_aliasing={{0}: (6, {})} | custom-call | tf_op jit(solution)/shard_map/keys_values/pallas_call | solution.py:46
  82.5 6.8 %queries.2 = (bf16[512,1024]{1,0:T(8,128)(2,1)}, f32[1024,1024]{1,0:T(8,128)}) custom-call(bf16[1024,1024]{1,0:T(8,128)(2,1)} %get-tuple-element.198.normed_ref.left_ref, bf16[1024,1024]{1,0:T(8,128)(2,1)} %constant_dynamic-update-slice_fusion.11.w_ref, f32[1,128]{1,0:T(1,128)} %reshape.121.hgain_ref.gain_ref, f32[1024,128]{1,0:T(8,128)} %get-tuple-element.396.cos_ref, ...), custom_call_target="tpu_custom_call" | custom-call | tf_op jit(solution)/shard_map/queries/pallas_call | solution.py:46
  89.3 4.2 collective-permute-done.23.refs_4_.refs_2_.refs_3_.refs_1_
  98.0 3.5 collective-permute-start.31
  104.1 10.8 %attend.3 = (f32[512,1024]{1,0:T(8,128)}, f32[512,1024]{1,0:T(8,128)}) custom-call(s32[2]{0:T(128)} %pad_add_fusion.1.idx_ref, s32[512,128]{1,0:T(8,128)} %broadcast_in_dim.73.lo_ref, bf16[512,1024]{1,0:T(8,128)(2,1)} %get-tuple-element.206.refs_0_.q_ref, bf16[2,512,512]{2,1,0:T(8,128)(2,1)} %get-tuple-element.195.refs_1_.refs_0_, ...), custom_call_target="tpu_custom_call" | custom-call | tf_op jit(solution)/shard_map/attend/pallas_call | solution.py:46
  115.5 6.4 %queries.3 = (bf16[512,1024]{1,0:T(8,128)(2,1)}, f32[1024,1024]{1,0:T(8,128)}) custom-call(bf16[1024,1024]{1,0:T(8,128)(2,1)} %get-tuple-element.198.normed_ref.left_ref, bf16[1024,1024]{1,0:T(8,128)(2,1)} %constant_dynamic-update-slice_fusion.11.w_ref, f32[1,128]{1,0:T(1,128)} %reshape.121.hgain_ref.gain_ref, ...), custom_call_target="tpu_custom_call", output_to_operand_aliasing={{1}: (5, {})} | custom-call | tf_op jit(solution)/shard_map/queries/pallas_call | solution.py:46
  121.9 8.8 %attend.4 = (bf16[1024,1024]{1,0:T(8,128)(2,1)}, f32[4,8,512]{2,1,0:T(8,128)}) custom-call(s32[2]{0:T(128)} %pad_add_fusion.1.idx_ref, s32[512,128]{1,0:T(8,128)} %broadcast_in_dim.73.lo_ref, bf16[512,1024]{1,0:T(8,128)(2,1)} %get-tuple-element.213.refs_0_.q_ref, bf16[2,512,512]{2,1,0:T(8,128)(2,1)} %get-tuple-element.195.refs_1_.refs_0_, ...), custom_call_target="tpu_custom_call" | custom-call | tf_op jit(solution)/shard_map/attend/pallas_call | solution.py:46
  130.8 4.0 out_projection.2.own_ref
  134.8 4.5 collective-permute-done.31.refs_9_.refs_1_
  140.1 6.5 %collective-permute-start.34 = (bf16[512,1024]{1,0:T(8,128)(2,1)S(1)}, bf16[512,1024]{1,0:T(8,128)(2,1)S(1)}, u32[]{:S(2)}, u32[]{:S(2)}) collective-permute-start(bf16[512,1024]{1,0:T(8,128)(2,1)S(1)} %copy-done.12), channel_id=1, source_target_pairs={{0,1},{1,0},{2,3},{3,2},{4,5},{5,4},{6,7},{7,6},{8,9},{9,8},{10,11... | collective-permute-start | bytes 3145736 | tf_op jit(solution)/shard_map/ppermute | solution.py:760
  147.6 19.5 %attend.5 = (bf16[1024,1024]{1,0:T(8,128)(2,1)}, f32[4,8,512]{2,1,0:T(8,128)}) custom-call(s32[2]{0:T(128)} %pad_add_fusion.1.idx_ref, s32[512,128]{1,0:T(8,128)} %broadcast_in_dim.73.lo_ref, bf16[512,1024]{1,0:T(8,128)(2,1)} %get-tuple-element.206.refs_0_.q_ref, bf16[2,512,512]{2,1,0:T(8,128)(2,1)} %copy-done.3, ...), custom_call_target="tpu_custom_call", output_to_operand_aliasing={{0}: (15, {})} | custom-call | tf_op jit(solution)/shard_map/attend/pallas_call | solution.py:46
  167.1 4.0 out_projection.3.own_ref
  174.9 5.9 %collective-permute-done.34.got_ref = bf16[512,1024]{1,0:T(8,128)(2,1)S(1)} collective-permute-done((bf16[512,1024]{1,0:T(8,128)(2,1)S(1)}, bf16[512,1024]{1,0:T(8,128)(2,1)S(1)}, u32[]{:S(2)}, u32[]{:S(2)}) %collective-permute-start.34) | collective-permute-done | bytes 1048608 | tf_op jit(solution)/shard_map/ppermute | solution.py:760
  181.8 18.4 %feed_forward.2 = (f32[512,1024]{1,0:T(8,128)}, bf16[1024,1024]{1,0:T(8,128)(2,1)}, bf16[1024,1536]{1,0:T(8,128)(2,1)}, bf16[1024,3072]{1,0:T(8,128)(2,1)}, bf16...) custom-call(bf16[1024,1024]{1,0:T(8,128)(2,1)} %x_ref.7, bf16[512,1024]{1,0:T(8,128)(2,1)} %out_projection.2.own_ref, ...), custom_call_target="tpu_custom_call" | custom-call | tf_op jit(solution)/shard_map/feed_forward/pallas_call | solution.py:46
  203.4 18.5 %feed_forward.3 = (f32[512,1024]{1,0:T(8,128)}, bf16[1024,1024]{1,0:T(8,128)(2,1)}, bf16[1024,1536]{1,0:T(8,128)(2,1)}, bf16[1024,3072]{1,0:T(8,128)(2,1)}, bf16...) custom-call(bf16[1024,1024]{1,0:T(8,128)(2,1)} %x_ref.7, ...), custom_call_target="tpu_custom_call", output_to_operand_aliasing={{1}: (7, {}), {2}: (8, {}), {3}: (9, {})} | custom-call | tf_op jit(solution)/shard_map/feed_forward/pallas_call | solution.py:46
  222.0 10.7 %weight_grad.2.refs_0_ = bf16[1024,4608]{1,0:T(8,128)(2,1)} custom-call(bf16[1024,1024]{1,0:T(8,128)(2,1)} %get-tuple-element.238.left_ref, bf16[1024,3072]{1,0:T(8,128)(2,1)} %get-tuple-element.239.right_ref), custom_call_target="tpu_custom_call" | custom-call | tf_op jit(solution)/shard_map/weight_grad/pallas_call | solution.py:46
  232.8 7.2 %weight_grad.3 = bf16[1024,4608]{1,0:T(8,128)(2,1)} custom-call(bf16[1024,1024]{1,0:T(8,128)(2,1)} %dy_ref.7, bf16[1024,1536]{1,0:T(8,128)(2,1)} %get-tuple-element.237.right_ref, bf16[1024,4608]{1,0:T(8,128)(2,1)} %weight_grad.2.refs_0_), custom_call_target="tpu_custom_call", output_to_operand_aliasing={{}: (2, {})} | custom-call | tf_op jit(solution)/shard_map/weight_grad/pallas_call | solution.py:46
  240.9 7.2 %mixed_back.2 = (f32[512,1024]{1,0:T(8,128)}, bf16[1024,1024]{1,0:T(8,128)(2,1)}, bf16[512,1024]{1,0:T(8,128)(2,1)}, f32[4,8,512]{2,1,0:T(8,128)}, f32[1,1024]{1,0:T(1,128)}) custom-call(bf16[512,1024]{1,0:T(8,128)(2,1)} %get-tuple-element.228.own_ref, bf16[512,1024]{1,0:T(8,128)(2,1)} %copy-done.19, f32[512,1024]{1,0:T(8,128)} %get-tuple-element.330.resid_ref, ...), custom_call_target="tpu_custom_call" | custom-call | tf_op jit(solution)/shard_map/mixed_back/pallas_call | solution.py:46
  248.7 6.0 %attend_back.6 = (f32[512,1024]{1,0:T(8,128)}, bf16[2,512,512]{2,1,0:T(8,128)(2,1)}, bf16[2,512,512]{2,1,0:T(8,128)(2,1)}) custom-call(s32[2]{0:T(128)} %pad_add_fusion.1.idx_ref, bf16[512,1024]{1,0:T(8,128)(2,1)} %get-tuple-element.213.refs_0_.q_ref, bf16[512,1024]{1,0:T(8,128)(2,1)} %get-tuple-element.241.do_ref, f32[4,8,512]{2,1,0:T(8,128)} %get-tuple-element.243.lse_ref, ...), custom_call_target="tpu_custom_call" | custom-call | flops 300000000 | tf_op jit(solution)/shard_map/attend_back/pallas_call | solution.py:46
  255.7 7.6 %mixed_back.3 = (f32[512,1024]{1,0:T(8,128)}, bf16[1024,1024]{1,0:T(8,128)(2,1)}, bf16[512,1024]{1,0:T(8,128)(2,1)}, f32[4,8,512]{2,1,0:T(8,128)}, f32[1,1024]{1,0:T(1,128)}) custom-call(bf16[512,1024]{1,0:T(8,128)(2,1)} %get-tuple-element.235.own_ref, bf16[512,1024]{1,0:T(8,128)(2,1)} %copy-done.20, ...), custom_call_target="tpu_custom_call", output_to_operand_aliasing={{1}: (7, {})} | custom-call | tf_op jit(solution)/shard_map/mixed_back/pallas_call | solution.py:46
  263.3 6.4 %slot_weight_grad.1 = (bf16[512,1024]{1,0:T(8,128)(2,1)}, bf16[512,1024]{1,0:T(8,128)(2,1)}) custom-call(s32[1]{0:T(128)} %bitcast.10.part_ref, bf16[1024,1024]{1,0:T(8,128)(2,1)} %get-tuple-element.248.left_ref, bf16[1024,1024]{1,0:T(8,128)(2,1)} %get-tuple-element.223.att_ref.right_ref), custom_call_target="tpu_custom_call" | custom-call | tf_op jit(solution)/shard_map/slot_weight_grad/pallas_call | solution.py:46
  271.8 10.6 %attend_back.7 = (f32[512,1024]{1,0:T(8,128)}, bf16[2,512,512]{2,1,0:T(8,128)(2,1)}, bf16[2,512,512]{2,1,0:T(8,128)(2,1)}, bf16[2,512,512]{2,1,0:T(8,128)(2,1)}) custom-call(s32[2]{0:T(128)} %pad_add_fusion.1.idx_ref, bf16[512,1024]{1,0:T(8,128)(2,1)} %get-tuple-element.206.refs_0_.q_ref, bf16[512,1024]{1,0:T(8,128)(2,1)} %get-tuple-element.251.do_ref, ...), custom_call_target="tpu_custom_call" | custom-call | flops 65999998976 | tf_op jit(solution)/shard_map/attend_back/pallas_call | solution.py:46
  282.4 6.6 %collective-permute-start.40 = (bf16[2,512,512]{2,1,0:T(8,128)(2,1)}, bf16[2,512,512]{2,1,0:T(8,128)(2,1)S(1)}, u32[]{:S(2)}, u32[]{:S(2)}) collective-permute-start(bf16[2,512,512]{2,1,0:T(8,128)(2,1)} %get-tuple-element.265), channel_id=1, source_target_pairs={{0,2},{2,0},{4,6},{6,4},{8,10},{10,8},{12,14},{14,12},{1,3},{3,1},... | collective-permute-start | bytes 3145736 | tf_op jit(solution)/shard_map/ppermute | solution.py:760
  289.4 15.2 %attend_back.8 = (f32[512,1024]{1,0:T(8,128)}, bf16[2,512,512]{2,1,0:T(8,128)(2,1)}, bf16[2,512,512]{2,1,0:T(8,128)(2,1)}) custom-call(s32[2]{0:T(128)} %pad_add_fusion.1.idx_ref, bf16[512,1024]{1,0:T(8,128)(2,1)} %get-tuple-element.206.refs_0_.q_ref, bf16[512,1024]{1,0:T(8,128)(2,1)} %get-tuple-element.251.do_ref, f32[4,8,512]{2,1,0:T(8,128)} %get-tuple-element.252.lse_ref, ...), custom_call_target="tpu_custom_call" | custom-call | flops 48000000000 | tf_op jit(solution)/shard_map/attend_back/pallas_call | solution.py:46
  304.6 16.7 %collective-permute-start.38 = (bf16[128,512]{1,0:T(8,128)(2,1)S(1)}, bf16[128,512]{1,0:T(8,128)(2,1)S(1)}, u32[]{:S(2)}, u32[]{:S(2)}) collective-permute-start(bf16[128,512]{1,0:T(8,128)(2,1)S(1)} %get-tuple-element.377), channel_id=1, source_target_pairs={{0,8},{2,10},{4,12},{6,14},{8,0},{10,2},{12,4},{14,6},{1,9},{3,11}... | collective-permute-start | bytes 393224 | tf_op jit(solution)/shard_map/ppermute | solution.py:760
  321.3 5.4 %collective-permute-start.39 = (bf16[128,512]{1,0:T(8,128)(2,1)S(1)}, bf16[128,512]{1,0:T(8,128)(2,1)S(1)}, u32[]{:S(2)}, u32[]{:S(2)}) collective-permute-start(bf16[128,512]{1,0:T(8,128)(2,1)S(1)} %get-tuple-element.375), channel_id=1, source_target_pairs={{0,4},{2,6},{4,0},{6,2},{8,12},{10,14},{12,8},{14,10},{1,5},{3,7},... | collective-permute-start | bytes 393224 | tf_op jit(solution)/shard_map/ppermute | solution.py:760
  332.8 12.4 %attend_back.9 = (f32[1024,1024]{1,0:T(8,128)}, bf16[2,512,512]{2,1,0:T(8,128)(2,1)}, bf16[2,512,512]{2,1,0:T(8,128)(2,1)}, bf16[2,512,512]{2,1,0:T(8,128)(2,1)}...) custom-call(s32[2]{0:T(128)} %pad_add_fusion.1.idx_ref, ...), custom_call_target="tpu_custom_call" | custom-call | flops 120000004096 | tf_op jit(solution)/shard_map/attend_back/pallas_call | solution.py:46
  346.7 4.7 collective-permute-start.48
  351.6 25.9 %attend_back.10 = (f32[512,1024]{1,0:T(8,128)}, bf16[2,512,512]{2,1,0:T(8,128)(2,1)}, bf16[2,512,512]{2,1,0:T(8,128)(2,1)}, bf16[2,512,512]{2,1,0:T(8,128)(2,1)}, bf16[2,512,512]{2,1,0:T(8,128)(2,1)}) custom-call(s32[2]{0:T(128)} %pad_add_fusion.1.idx_ref, bf16[512,1024]{1,0:T(8,128)(2,1)} %get-tuple-element.206.refs_0_.q_ref, ...), custom_call_target="tpu_custom_call" | custom-call | flops 83999997952 | tf_op jit(solution)/shard_map/attend_back/pallas_call | solution.py:46
  377.5 6.1 %collective-permute-done.46.refs_2_.refs_5_ = bf16[2,512,512]{2,1,0:T(8,128)(2,1)S(1)} collective-permute-done((bf16[2,512,512]{2,1,0:T(8,128)(2,1)S(1)}, bf16[2,512,512]{2,1,0:T(8,128)(2,1)S(1)}, u32[]{:S(2)}, u32[]{:S(2)}) %collective-permute-start.46) | collective-permute-done | bytes 1048608 | tf_op jit(solution)/shard_map/ppermute | solution.py:765
  384.6 8.5 %collective-permute-start.51 = (bf16[512,512]{1,0:T(8,128)(2,1)S(1)}, bf16[512,512]{1,0:T(8,128)(2,1)}, u32[]{:S(2)}, u32[]{:S(2)}) collective-permute-start(bf16[512,512]{1,0:T(8,128)(2,1)S(1)} %get-tuple-element.371), channel_id=1, source_target_pairs={{0,8},{2,10},{4,12},{6,14},{8,0},{10,2},{12,4},{14,6},{1,9},{3,11}... | collective-permute-start | bytes 1572872 | tf_op jit(solution)/shard_map/ppermute | solution.py:760
  393.2 10.9 %collective-permute-start.50 = (bf16[512,512]{1,0:T(8,128)(2,1)}, bf16[512,512]{1,0:T(8,128)(2,1)}, u32[]{:S(2)}, u32[]{:S(2)}) collective-permute-start(bf16[512,512]{1,0:T(8,128)(2,1)} %get-tuple-element.372), channel_id=1, source_target_pairs={{0,4},{2,6},{4,0},{6,2},{8,12},{10,14},{12,8},{14,10},{1,5},{3,7},... | collective-permute-start | bytes 1572872 | tf_op jit(solution)/shard_map/ppermute | solution.py:760
  406.2 15.1 %attend_back.11 = (f32[1024,1024]{1,0:T(8,128)}, bf16[2,512,512]{2,1,0:T(8,128)(2,1)}, bf16[2,512,512]{2,1,0:T(8,128)(2,1)}) custom-call(s32[2]{0:T(128)} %pad_add_fusion.1.idx_ref, bf16[512,1024]{1,0:T(8,128)(2,1)} %get-tuple-element.206.refs_0_.q_ref, bf16[512,1024]{1,0:T(8,128)(2,1)} %get-tuple-element.251.do_ref, ...), custom_call_target="tpu_custom_call", output_to_operand_aliasing={{0}: (11, {})} | custom-call | flops 48000000000 | tf_op jit(solution)/shard_map/attend_back/pallas_call | solution.py:46
  423.2 3.8 merge.1
  429.8 12.0 %q_back.1 = (bf16[1024,1024]{1,0:T(8,128)(2,1)}, f32[1024,1024]{1,0:T(8,128)}, f32[1,128]{1,0:T(1,128)}) custom-call(f32[1024,1024]{1,0:T(8,128)} %get-tuple-element.287.dq_ref, f32[1024,1024]{1,0:T(8,128)} %get-tuple-element.288.lin_ref, f32[1,128]{1,0:T(1,128)} %reshape.121.hgain_ref.gain_ref, f32[1024,128]{1,0:T(8,128)} %get-tuple-element.396.cos_ref, ...), custom_call_target="tpu_custom_call" | custom-call | tf_op jit(solution)/shard_map/q_back/pallas_call | solution.py:46
  441.8 8.5 %kv_back.2 = (bf16[1024,1024]{1,0:T(8,128)(2,1)}, bf16[512,1024]{1,0:T(8,128)(2,1)}, f32[1,128]{1,0:T(1,128)}) custom-call(f32[512,512]{1,0:T(8,128)} %get-tuple-element.300.lin_ref, f32[1,128]{1,0:T(1,128)} %reshape.120.hgain_ref.gain_ref, f32[1024,128]{1,0:T(8,128)} %get-tuple-element.396.cos_ref, f32[1024,128]{1,0:T(8,128)} %get-tuple-element.397.sin_ref, ...), custom_call_target="tpu_custom_call" | custom-call | tf_op jit(solution)/shard_map/kv_back/pallas_call | solution.py:46
  450.3 5.8 %weight_halves.2 = (bf16[512,1024]{1,0:T(8,128)(2,1)}, bf16[512,1024]{1,0:T(8,128)(2,1)}) custom-call(bf16[1024,1024]{1,0:T(8,128)(2,1)} %get-tuple-element.198.normed_ref.left_ref, bf16[1024,1024]{1,0:T(8,128)(2,1)} %get-tuple-element.305.right_ref), custom_call_target="tpu_custom_call" | custom-call | tf_op jit(solution)/shard_map/weight_halves/pallas_call | solution.py:46
  458.5 8.9 %kv_back.3 = (bf16[1024,1024]{1,0:T(8,128)(2,1)}, bf16[512,1024]{1,0:T(8,128)(2,1)}, f32[1,128]{1,0:T(1,128)}) custom-call(f32[512,512]{1,0:T(8,128)} %get-tuple-element.234.lin_ref, f32[1,128]{1,0:T(1,128)} %reshape.120.hgain_ref.gain_ref, f32[1024,128]{1,0:T(8,128)} %get-tuple-element.396.cos_ref, ...), custom_call_target="tpu_custom_call", output_to_operand_aliasing={{0}: (15, {})} | custom-call | flops 8999999488 | tf_op jit(solution)/shard_map/kv_back/pallas_call | solution.py:46
  473.6 5.9 %weight_halves.3 = (bf16[512,1024]{1,0:T(8,128)(2,1)}, bf16[512,1024]{1,0:T(8,128)(2,1)}) custom-call(bf16[1024,1024]{1,0:T(8,128)(2,1)} %get-tuple-element.198.normed_ref.left_ref, bf16[1024,1024]{1,0:T(8,128)(2,1)} %get-tuple-element.316.right_ref), custom_call_target="tpu_custom_call" | custom-call | tf_op jit(solution)/shard_map/weight_halves/pallas_call | solution.py:46
  482.4 4.3 tokens_back.2
  507.3 4.0 tokens_back.3
  516.4 5.4 collective-permute-done.71
  526.4 3.8 collective-permute-done.73
  (345 shorter events, 131.1 us)
Async XLA Ops:
  7.2 87.8 %all-gather.3.cloned.1.call-start = ((), (), s32[]{:S(2)}) async-start(), calls=%async_computation.1 | async-start | bytes 5570560 | tf_op jit(solution)/shard_map/all_gather | solution.py:886
  9.4 171.4 %all-gather.5.cloned.1.call-start = ((), (), s32[]{:S(2)}) async-start(), calls=%async_computation.2 | async-start | bytes 6684672 | tf_op jit(solution)/shard_map/all_gather | solution.py:979
  10.4 11.0 %collective-permute-start.6 = (bf16[16,144]{1,0:T(8,128)(2,1)S(1)}, bf16[16,144]{1,0:T(8,128)(2,1)S(1)}, u32[]{:S(2)}, u32[]{:S(2)}) collective-permute-start(bf16[16,144]{1,0:T(8,128)(2,1)S(1)} %broadcast_select_fusion.2), channel_id=1, source_target_pairs={{0,2},{2,0},{4,6},{6,4},{8,10},{10,8},{12,14},{14,12},{1,3},{3,1},... | collective-permute-start | bytes 13832 | tf_op jit(solution)/shard_map/ppermute | solution.py:760
  10.8 13.8 %collective-permute-start.1 = (bf16[64,1024]{1,0:T(8,128)(2,1)}, bf16[64,1024]{1,0:T(8,128)(2,1)S(1)}, u32[]{:S(2)}, u32[]{:S(2)}) collective-permute-start(bf16[64,1024]{1,0:T(8,128)(2,1)} %get-tuple-element.184), channel_id=1, source_target_pairs={{0,16},{16,0},{1,17},{17,1},{2,18},{18,2},{3,19},{19,3},{4,20},{20... | collective-permute-start | bytes 393224 | tf_op jit(solution)/shard_map/ppermute | solution.py:760
  14.5 28.3 %collective-permute-start = (bf16[64,1024]{1,0:T(8,128)(2,1)}, bf16[64,1024]{1,0:T(8,128)(2,1)S(1)}, u32[]{:S(2)}, u32[]{:S(2)}) collective-permute-start(bf16[64,1024]{1,0:T(8,128)(2,1)} %param.21), channel_id=1, source_target_pairs={{0,16},{16,0},{1,17},{17,1},{2,18},{18,2},{3,19},{19,3},{4,20},{20... | collective-permute-start | bytes 393224 | tf_op jit(solution)/shard_map/ppermute | solution.py:760
  21.4 10.5 %collective-permute-start.7 = (bf16[16,144]{1,0:T(8,128)(2,1)S(1)}, bf16[16,144]{1,0:T(8,128)(2,1)S(1)}, u32[]{:S(2)}, u32[]{:S(2)}) collective-permute-start(bf16[16,144]{1,0:T(8,128)(2,1)S(1)} %fusion.9), channel_id=1, source_target_pairs={{0,16},{16,0},{1,17},{17,1},{2,18},{18,2},{3,19},{19,3},{4,20},{20... | collective-permute-start | bytes 13832 | tf_op jit(solution)/shard_map/ppermute | solution.py:760
  36.1 13.6 %collective-permute-start.12 = (bf16[128,1024]{1,0:T(8,128)(2,1)S(1)}, bf16[128,1024]{1,0:T(8,128)(2,1)}, u32[]{:S(2)}, u32[]{:S(2)}) collective-permute-start(bf16[128,1024]{1,0:T(8,128)(2,1)S(1)} %collective-permute-done.4), channel_id=1, source_target_pairs={{0,2},{2,0},{4,6},{6,4},{8,10},{10,8},{12,14},{14,12},{1,3},{3,1},... | collective-permute-start | bytes 786440 | tf_op jit(solution)/shard_map/ppermute | solution.py:760
  36.2 14.7 %collective-permute-start.13 = (bf16[128,1024]{1,0:T(8,128)(2,1)S(1)}, bf16[128,1024]{1,0:T(8,128)(2,1)}, u32[]{:S(2)}, u32[]{:S(2)}) collective-permute-start(bf16[128,1024]{1,0:T(8,128)(2,1)S(1)} %collective-permute-done.2), channel_id=1, source_target_pairs={{0,2},{2,0},{4,6},{6,4},{8,10},{10,8},{12,14},{14,12},{1,3},{3,1},... | collective-permute-start | bytes 786440 | tf_op jit(solution)/shard_map/ppermute | solution.py:760
  43.8 10.3 %collective-permute-start.10 = (bf16[128,1024]{1,0:T(8,128)(2,1)}, bf16[128,1024]{1,0:T(8,128)(2,1)S(1)}, u32[]{:S(2)}, u32[]{:S(2)}) collective-permute-start(bf16[128,1024]{1,0:T(8,128)(2,1)} %get-tuple-element.384), channel_id=1, source_target_pairs={{0,4},{2,6},{4,0},{6,2},{8,12},{10,14},{12,8},{14,10},{1,5},{3,7},... | collective-permute-start | bytes 786440 | tf_op jit(solution)/shard_map/ppermute | solution.py:760
  49.8 29.2 %collective-permute-start.18 = (bf16[128,1024]{1,0:T(8,128)(2,1)}, bf16[128,1024]{1,0:T(8,128)(2,1)S(1)}, u32[]{:S(2)}, u32[]{:S(2)}) collective-permute-start(bf16[128,1024]{1,0:T(8,128)(2,1)} %get-tuple-element.384), channel_id=1, source_target_pairs={{0,2},{2,0},{4,6},{6,4},{8,10},{10,8},{12,14},{14,12},{1,3},{3,1},... | collective-permute-start | bytes 786440 | tf_op jit(solution)/shard_map/ppermute | solution.py:760
  57.4 22.9 %collective-permute-start.20 = (bf16[128,1024]{1,0:T(8,128)(2,1)S(1)}, bf16[128,1024]{1,0:T(8,128)(2,1)S(1)}, u32[]{:S(2)}, u32[]{:S(2)}) collective-permute-start(bf16[128,1024]{1,0:T(8,128)(2,1)S(1)} %collective-permute-done.15), channel_id=1, source_target_pairs={{0,2},{2,0},{4,6},{6,4},{8,10},{10,8},{12,14},{14,12},{1,3},{3,1},... | collective-permute-start | bytes 786440 | tf_op jit(solution)/shard_map/ppermute | solution.py:760
  57.4 22.9 %collective-permute-start.19 = (bf16[128,1024]{1,0:T(8,128)(2,1)S(1)}, bf16[128,1024]{1,0:T(8,128)(2,1)S(1)}, u32[]{:S(2)}, u32[]{:S(2)}) collective-permute-start(bf16[128,1024]{1,0:T(8,128)(2,1)S(1)} %collective-permute-done.10), channel_id=1, source_target_pairs={{0,2},{2,0},{4,6},{6,4},{8,10},{10,8},{12,14},{14,12},{1,3},{3,1},... | collective-permute-start | bytes 786440 | tf_op jit(solution)/shard_map/ppermute | solution.py:760
  68.3 25.2 %collective-permute-start.23 = (bf16[2,512,512]{2,1,0:T(8,128)(2,1)}, bf16[2,512,512]{2,1,0:T(8,128)(2,1)S(1)}, u32[]{:S(2)}, u32[]{:S(2)}) collective-permute-start(bf16[2,512,512]{2,1,0:T(8,128)(2,1)} %get-tuple-element.195.refs_1_.refs_0_), channel_id=1, source_target_pairs={{0,8},{2,10},{4,12},{6,14},{8,0},{10,2},{12,4},{14,6},{1,9},{3,11}... | collective-permute-start | bytes 3145736 | tf_op jit(solution)/shard_map/ppermute | solution.py:760
  70.5 24.5 %collective-permute-start.22 = (bf16[2,512,512]{2,1,0:T(8,128)(2,1)}, bf16[2,512,512]{2,1,0:T(8,128)(2,1)S(1)}, u32[]{:S(2)}, u32[]{:S(2)}) collective-permute-start(bf16[2,512,512]{2,1,0:T(8,128)(2,1)} %get-tuple-element.195.refs_1_.refs_0_), channel_id=1, source_target_pairs={{0,4},{2,6},{4,0},{6,2},{8,12},{10,14},{12,8},{14,10},{1,5},{3,7},... | collective-permute-start | bytes 3145736 | tf_op jit(solution)/shard_map/ppermute | solution.py:760
  95.0 326.9 %reduce-scatter.2.cloned.1.call-start = ((), (), s32[]{:S(2)}) async-start(), calls=%async_computation.3 | async-start | bytes 10027008 | tf_op jit(solution)/shard_map/reduce_scatter | solution.py:1012
  95.2 19.7 %collective-permute-start.28 = (bf16[512,512]{1,0:T(8,128)(2,1)S(1)}, bf16[512,512]{1,0:T(8,128)(2,1)S(1)}, u32[]{:S(2)}, u32[]{:S(2)}) collective-permute-start(bf16[512,512]{1,0:T(8,128)(2,1)S(1)} %slice_bitcast_fusion.2), channel_id=1, source_target_pairs={{0,8},{2,10},{4,12},{6,14},{8,0},{10,2},{12,4},{14,6},{1,9},{3,11}... | collective-permute-start | bytes 1572872 | tf_op jit(solution)/shard_map/ppermute | solution.py:760
  95.6 19.4 %collective-permute-start.27 = (bf16[512,512]{1,0:T(8,128)(2,1)S(1)}, bf16[512,512]{1,0:T(8,128)(2,1)S(1)}, u32[]{:S(2)}, u32[]{:S(2)}) collective-permute-start(bf16[512,512]{1,0:T(8,128)(2,1)S(1)} %slice_bitcast_fusion.3), channel_id=1, source_target_pairs={{0,4},{2,6},{4,0},{6,2},{8,12},{10,14},{12,8},{14,10},{1,5},{3,7},... | collective-permute-start | bytes 1572872 | tf_op jit(solution)/shard_map/ppermute | solution.py:760
  96.7 25.2 %collective-permute-start.26 = (bf16[2,512,512]{2,1,0:T(8,128)(2,1)S(1)}, bf16[2,512,512]{2,1,0:T(8,128)(2,1)}, u32[]{:S(2)}, u32[]{:S(2)}) collective-permute-start(bf16[2,512,512]{2,1,0:T(8,128)(2,1)S(1)} %collective-permute-done.23.refs_4_.refs_2_.refs_3_.refs_1_), channel_id=1, source_target_pairs={{0,2},{2,0},{4,6},{6,4},{8,10},{10,8},{12,14},{14,12},{1,3},{3,1},... | collective-permute-start | bytes 3145736 | tf_op jit(solution)/shard_map/ppermute | solution.py:760
  96.7 25.2 %collective-permute-start.25 = (bf16[2,512,512]{2,1,0:T(8,128)(2,1)S(1)}, bf16[2,512,512]{2,1,0:T(8,128)(2,1)}, u32[]{:S(2)}, u32[]{:S(2)}) collective-permute-start(bf16[2,512,512]{2,1,0:T(8,128)(2,1)S(1)} %collective-permute-done.22.refs_3_.refs_1_.refs_2_.refs_0_), channel_id=1, source_target_pairs={{0,2},{2,0},{4,6},{6,4},{8,10},{10,8},{12,14},{14,12},{1,3},{3,1},... | collective-permute-start | bytes 3145736 | tf_op jit(solution)/shard_map/ppermute | solution.py:760
  98.0 41.3 %collective-permute-start.31 = (bf16[2,512,512]{2,1,0:T(8,128)(2,1)}, bf16[2,512,512]{2,1,0:T(8,128)(2,1)}, u32[]{:S(2)}, u32[]{:S(2)}) collective-permute-start(bf16[2,512,512]{2,1,0:T(8,128)(2,1)} %get-tuple-element.220.refs_3_.refs_0_), channel_id=1, source_target_pairs={{0,4},{2,6},{4,8},{6,10},{8,12},{10,14},{1,5},{3,7},{5,9},{7,11},{... | collective-permute-start | bytes 3145736 | tf_op jit(solution)/shard_map/ppermute | solution.py:765
  140.1 40.8 %collective-permute-start.34 = (bf16[512,1024]{1,0:T(8,128)(2,1)S(1)}, bf16[512,1024]{1,0:T(8,128)(2,1)S(1)}, u32[]{:S(2)}, u32[]{:S(2)}) collective-permute-start(bf16[512,1024]{1,0:T(8,128)(2,1)S(1)} %copy-done.12), channel_id=1, source_target_pairs={{0,1},{1,0},{2,3},{3,2},{4,5},{5,4},{6,7},{7,6},{8,9},{9,8},{10,11... | collective-permute-start | bytes 3145736 | tf_op jit(solution)/shard_map/ppermute | solution.py:760
  171.1 32.3 %collective-permute-start.33 = (bf16[512,1024]{1,0:T(8,128)(2,1)}, bf16[512,1024]{1,0:T(8,128)(2,1)}, u32[]{:S(2)}, u32[]{:S(2)}) collective-permute-start(bf16[512,1024]{1,0:T(8,128)(2,1)} %out_projection.3.own_ref), channel_id=1, source_target_pairs={{0,1},{1,0},{2,3},{3,2},{4,5},{5,4},{6,7},{7,6},{8,9},{9,8},{10,11... | collective-permute-start | bytes 3145736 | tf_op jit(solution)/shard_map/ppermute | solution.py:760
  200.2 39.7 %collective-permute-start.36 = (bf16[512,1024]{1,0:T(8,128)(2,1)}, bf16[512,1024]{1,0:T(8,128)(2,1)S(1)}, u32[]{:S(2)}, u32[]{:S(2)}) collective-permute-start(bf16[512,1024]{1,0:T(8,128)(2,1)} %get-tuple-element.228.own_ref), channel_id=1, source_target_pairs={{0,1},{1,0},{2,3},{3,2},{4,5},{5,4},{6,7},{7,6},{8,9},{9,8},{10,11... | collective-permute-start | bytes 3145736 | tf_op jit(solution)/shard_map/ppermute | solution.py:760
  221.9 32.8 %collective-permute-start.35 = (bf16[512,1024]{1,0:T(8,128)(2,1)}, bf16[512,1024]{1,0:T(8,128)(2,1)S(1)}, u32[]{:S(2)}, u32[]{:S(2)}) collective-permute-start(bf16[512,1024]{1,0:T(8,128)(2,1)} %get-tuple-element.235.own_ref), channel_id=1, source_target_pairs={{0,1},{1,0},{2,3},{3,2},{4,5},{5,4},{6,7},{7,6},{8,9},{9,8},{10,11... | collective-permute-start | bytes 3145736 | tf_op jit(solution)/shard_map/ppermute | solution.py:760
  269.7 107.8 %collective-permute-start.45 = (bf16[512,1024]{1,0:T(8,128)(2,1)}, bf16[512,1024]{1,0:T(8,128)(2,1)}, u32[]{:S(2)}, u32[]{:S(2)}) collective-permute-start(bf16[512,1024]{1,0:T(8,128)(2,1)} %get-tuple-element.283.own_ref), channel_id=1, source_target_pairs={{0,1},{1,0},{2,3},{3,2},{4,5},{5,4},{6,7},{7,6},{8,9},{9,8},{10,11... | collective-permute-start | bytes 3145736 | tf_op jit(solution)/shard_map/ppermute | solution.py:760
  271.7 105.8 %collective-permute-start.44 = (bf16[512,1024]{1,0:T(8,128)(2,1)}, bf16[512,1024]{1,0:T(8,128)(2,1)}, u32[]{:S(2)}, u32[]{:S(2)}) collective-permute-start(bf16[512,1024]{1,0:T(8,128)(2,1)} %get-tuple-element.281.own_ref), channel_id=1, source_target_pairs={{0,1},{1,0},{2,3},{3,2},{4,5},{5,4},{6,7},{7,6},{8,9},{9,8},{10,11... | collective-permute-start | bytes 3145736 | tf_op jit(solution)/shard_map/ppermute | solution.py:760
  271.8 17.2 %collective-permute-start.37 = (bf16[512,1024]{1,0:T(8,128)(2,1)}, bf16[512,1024]{1,0:T(8,128)(2,1)S(1)}, u32[]{:S(2)}, u32[]{:S(2)}) collective-permute-start(bf16[512,1024]{1,0:T(8,128)(2,1)} %get-tuple-element.255), channel_id=1, source_target_pairs={{0,2},{2,0},{4,6},{6,4},{8,10},{10,8},{12,14},{14,12},{1,3},{3,1},... | collective-permute-start | bytes 3145736 | tf_op jit(solution)/shard_map/ppermute | solution.py:760
  282.4 22.2 %collective-permute-start.40 = (bf16[2,512,512]{2,1,0:T(8,128)(2,1)}, bf16[2,512,512]{2,1,0:T(8,128)(2,1)S(1)}, u32[]{:S(2)}, u32[]{:S(2)}) collective-permute-start(bf16[2,512,512]{2,1,0:T(8,128)(2,1)} %get-tuple-element.265), channel_id=1, source_target_pairs={{0,2},{2,0},{4,6},{6,4},{8,10},{10,8},{12,14},{14,12},{1,3},{3,1},... | collective-permute-start | bytes 3145736 | tf_op jit(solution)/shard_map/ppermute | solution.py:760
  304.6 23.5 %collective-permute-start.38 = (bf16[128,512]{1,0:T(8,128)(2,1)S(1)}, bf16[128,512]{1,0:T(8,128)(2,1)S(1)}, u32[]{:S(2)}, u32[]{:S(2)}) collective-permute-start(bf16[128,512]{1,0:T(8,128)(2,1)S(1)} %get-tuple-element.377), channel_id=1, source_target_pairs={{0,8},{2,10},{4,12},{6,14},{8,0},{10,2},{12,4},{14,6},{1,9},{3,11}... | collective-permute-start | bytes 393224 | tf_op jit(solution)/shard_map/ppermute | solution.py:760
  328.1 23.2 %collective-permute-start.43 = (bf16[2,512,512]{2,1,0:T(8,128)(2,1)S(1)}, bf16[2,512,512]{2,1,0:T(8,128)(2,1)S(1)}, u32[]{:S(2)}, u32[]{:S(2)}) collective-permute-start(bf16[2,512,512]{2,1,0:T(8,128)(2,1)S(1)} %copy-done.35), channel_id=1, source_target_pairs={{0,2},{2,0},{4,6},{6,4},{8,10},{10,8},{12,14},{14,12},{1,3},{3,1},... | collective-permute-start | bytes 3145736 | tf_op jit(solution)/shard_map/ppermute | solution.py:760
  330.5 14.6 %collective-permute-start.41 = (bf16[128,1024]{1,0:T(8,128)(2,1)S(1)}, bf16[128,1024]{1,0:T(8,128)(2,1)S(1)}, u32[]{:S(2)}, u32[]{:S(2)}) collective-permute-start(bf16[128,1024]{1,0:T(8,128)(2,1)S(1)} %pad_maximum_fusion.5), channel_id=1, source_target_pairs={{0,4},{2,6},{4,0},{6,2},{8,12},{10,14},{12,8},{14,10},{1,5},{3,7},... | collective-permute-start | bytes 786440 | tf_op jit(solution)/shard_map/ppermute | solution.py:760
  332.4 14.1 %collective-permute-start.42 = (bf16[128,1024]{1,0:T(8,128)(2,1)S(1)}, bf16[128,1024]{1,0:T(8,128)(2,1)S(1)}, u32[]{:S(2)}, u32[]{:S(2)}) collective-permute-start(bf16[128,1024]{1,0:T(8,128)(2,1)S(1)} %pad_maximum_fusion.6), channel_id=1, source_target_pairs={{0,8},{2,10},{4,12},{6,14},{8,0},{10,2},{12,4},{14,6},{1,9},{3,11}... | collective-permute-start | bytes 786440 | tf_op jit(solution)/shard_map/ppermute | solution.py:760
  345.2 38.5 %collective-permute-start.46 = (bf16[2,512,512]{2,1,0:T(8,128)(2,1)S(1)}, bf16[2,512,512]{2,1,0:T(8,128)(2,1)S(1)}, u32[]{:S(2)}, u32[]{:S(2)}) collective-permute-start(bf16[2,512,512]{2,1,0:T(8,128)(2,1)S(1)} %add_convert_fusion.3), channel_id=1, source_target_pairs={{4,0},{6,2},{8,4},{10,6},{12,8},{14,10},{5,1},{7,3},{9,5},{11,7},{... | collective-permute-start | bytes 3145736 | tf_op jit(solution)/shard_map/ppermute | solution.py:765
  346.7 74.6 %collective-permute-start.48 = (bf16[64,1024]{1,0:T(8,128)(2,1)S(1)}, bf16[64,1024]{1,0:T(8,128)(2,1)S(1)}, u32[]{:S(2)}, u32[]{:S(2)}) collective-permute-start(bf16[64,1024]{1,0:T(8,128)(2,1)S(1)} %slice.220), channel_id=1, source_target_pairs={{0,16},{16,0},{1,17},{17,1},{2,18},{18,2},{3,19},{19,3},{4,20},{20... | collective-permute-start | bytes 393224 | tf_op jit(solution)/shard_map/ppermute | solution.py:760
  384.6 37.3 %collective-permute-start.51 = (bf16[512,512]{1,0:T(8,128)(2,1)S(1)}, bf16[512,512]{1,0:T(8,128)(2,1)}, u32[]{:S(2)}, u32[]{:S(2)}) collective-permute-start(bf16[512,512]{1,0:T(8,128)(2,1)S(1)} %get-tuple-element.371), channel_id=1, source_target_pairs={{0,8},{2,10},{4,12},{6,14},{8,0},{10,2},{12,4},{14,6},{1,9},{3,11}... | collective-permute-start | bytes 1572872 | tf_op jit(solution)/shard_map/ppermute | solution.py:760
  393.2 28.7 %collective-permute-start.50 = (bf16[512,512]{1,0:T(8,128)(2,1)}, bf16[512,512]{1,0:T(8,128)(2,1)}, u32[]{:S(2)}, u32[]{:S(2)}) collective-permute-start(bf16[512,512]{1,0:T(8,128)(2,1)} %get-tuple-element.372), channel_id=1, source_target_pairs={{0,4},{2,6},{4,0},{6,2},{8,12},{10,14},{12,8},{14,10},{1,5},{3,7},... | collective-permute-start | bytes 1572872 | tf_op jit(solution)/shard_map/ppermute | solution.py:760
  404.0 17.9 %collective-permute-start.49 = (bf16[2,512,512]{2,1,0:T(8,128)(2,1)}, bf16[2,512,512]{2,1,0:T(8,128)(2,1)S(1)}, u32[]{:S(2)}, u32[]{:S(2)}) collective-permute-start(bf16[2,512,512]{2,1,0:T(8,128)(2,1)} %get-tuple-element.293), channel_id=1, source_target_pairs={{0,2},{2,0},{4,6},{6,4},{8,10},{10,8},{12,14},{14,12},{1,3},{3,1},... | collective-permute-start | bytes 3145736 | tf_op jit(solution)/shard_map/ppermute | solution.py:760
  406.2 15.7 %collective-permute-start.47 = (bf16[2,512,512]{2,1,0:T(8,128)(2,1)}, bf16[2,512,512]{2,1,0:T(8,128)(2,1)S(1)}, u32[]{:S(2)}, u32[]{:S(2)}) collective-permute-start(bf16[2,512,512]{2,1,0:T(8,128)(2,1)} %get-tuple-element.290), channel_id=1, source_target_pairs={{0,2},{2,0},{4,6},{6,4},{8,10},{10,8},{12,14},{14,12},{1,3},{3,1},... | collective-permute-start | bytes 3145736 | tf_op jit(solution)/shard_map/ppermute | solution.py:760
  421.3 35.5 %collective-permute-start.52 = (bf16[2,512,512]{2,1,0:T(8,128)(2,1)}, bf16[2,512,512]{2,1,0:T(8,128)(2,1)S(1)}, u32[]{:S(2)}, u32[]{:S(2)}) collective-permute-start(bf16[2,512,512]{2,1,0:T(8,128)(2,1)} %get-tuple-element.309), channel_id=1, source_target_pairs={{0,2},{2,0},{4,6},{6,4},{8,10},{10,8},{12,14},{14,12},{1,3},{3,1},... | collective-permute-start | bytes 3145736 | tf_op jit(solution)/shard_map/ppermute | solution.py:760
  427.0 29.8 %collective-permute-start.53 = (bf16[2,512,512]{2,1,0:T(8,128)(2,1)}, bf16[2,512,512]{2,1,0:T(8,128)(2,1)S(1)}, u32[]{:S(2)}, u32[]{:S(2)}) collective-permute-start(bf16[2,512,512]{2,1,0:T(8,128)(2,1)} %get-tuple-element.297), channel_id=1, source_target_pairs={{0,4},{2,6},{4,0},{6,2},{8,12},{10,14},{12,8},{14,10},{1,5},{3,7},... | collective-permute-start | bytes 3145736 | tf_op jit(solution)/shard_map/ppermute | solution.py:760
  427.3 29.5 %collective-permute-start.54 = (bf16[2,512,512]{2,1,0:T(8,128)(2,1)}, bf16[2,512,512]{2,1,0:T(8,128)(2,1)S(1)}, u32[]{:S(2)}, u32[]{:S(2)}) collective-permute-start(bf16[2,512,512]{2,1,0:T(8,128)(2,1)} %get-tuple-element.310), channel_id=1, source_target_pairs={{0,8},{2,10},{4,12},{6,14},{8,0},{10,2},{12,4},{14,6},{1,9},{3,11}... | collective-permute-start | bytes 3145736 | tf_op jit(solution)/shard_map/ppermute | solution.py:760
  456.1 11.3 %collective-permute-start.55 = (bf16[512,1024]{1,0:T(8,128)(2,1)}, bf16[512,1024]{1,0:T(8,128)(2,1)S(1)}, u32[]{:S(2)}, u32[]{:S(2)}) collective-permute-start(bf16[512,1024]{1,0:T(8,128)(2,1)} %get-tuple-element.313), channel_id=1, source_target_pairs={{0,2},{2,0},{4,6},{6,4},{8,10},{10,8},{12,14},{14,12},{1,3},{3,1},... | collective-permute-start | bytes 3145736 | tf_op jit(solution)/shard_map/ppermute | solution.py:760
  456.1 26.3 %collective-permute-start.57 = (bf16[512,1024]{1,0:T(8,128)(2,1)}, bf16[512,1024]{1,0:T(8,128)(2,1)}, u32[]{:S(2)}, u32[]{:S(2)}) collective-permute-start(bf16[512,1024]{1,0:T(8,128)(2,1)} %get-tuple-element.304.own_ref), channel_id=1, source_target_pairs={{0,1},{1,0},{2,3},{3,2},{4,5},{5,4},{6,7},{7,6},{8,9},{9,8},{10,11... | collective-permute-start | bytes 3145736 | tf_op jit(solution)/shard_map/ppermute | solution.py:760
  467.9 11.6 %collective-permute-start.58 = (bf16[128,512]{1,0:T(8,128)(2,1)S(1)}, bf16[128,512]{1,0:T(8,128)(2,1)S(1)}, u32[]{:S(2)}, u32[]{:S(2)}) collective-permute-start(bf16[128,512]{1,0:T(8,128)(2,1)S(1)} %get-tuple-element.369), channel_id=1, source_target_pairs={{0,8},{2,10},{4,12},{6,14},{8,0},{10,2},{12,4},{14,6},{1,9},{3,11}... | collective-permute-start | bytes 393224 | tf_op jit(solution)/shard_map/ppermute | solution.py:760
  469.7 9.8 %collective-permute-start.59 = (bf16[128,512]{1,0:T(8,128)(2,1)S(1)}, bf16[128,512]{1,0:T(8,128)(2,1)S(1)}, u32[]{:S(2)}, u32[]{:S(2)}) collective-permute-start(bf16[128,512]{1,0:T(8,128)(2,1)S(1)} %get-tuple-element.367), channel_id=1, source_target_pairs={{0,4},{2,6},{4,0},{6,2},{8,12},{10,14},{12,8},{14,10},{1,5},{3,7},... | collective-permute-start | bytes 393224 | tf_op jit(solution)/shard_map/ppermute | solution.py:760
  472.2 35.1 %collective-permute-start.64 = (bf16[512,1024]{1,0:T(8,128)(2,1)S(1)}, bf16[512,1024]{1,0:T(8,128)(2,1)}, u32[]{:S(2)}, u32[]{:S(2)}) collective-permute-start(bf16[512,1024]{1,0:T(8,128)(2,1)S(1)} %copy-done.34), channel_id=1, source_target_pairs={{0,1},{1,0},{2,3},{3,2},{4,5},{5,4},{6,7},{7,6},{8,9},{9,8},{10,11... | collective-permute-start | bytes 3145736 | tf_op jit(solution)/shard_map/ppermute | solution.py:760
  493.2 12.2 %collective-permute-start.67 = (bf16[64,1024]{1,0:T(8,128)(2,1)S(1)}, bf16[64,1024]{1,0:T(8,128)(2,1)S(1)}, u32[]{:S(2)}, u32[]{:S(2)}) collective-permute-start(bf16[64,1024]{1,0:T(8,128)(2,1)S(1)} %slice.238), channel_id=1, source_target_pairs={{0,16},{16,0},{1,17},{17,1},{2,18},{18,2},{3,19},{19,3},{4,20},{20... | collective-permute-start | bytes 393224 | tf_op jit(solution)/shard_map/ppermute | solution.py:760
  498.6 13.4 %collective-permute-start.68 = (f32[1,256]{1,0:T(1,128)S(1)}, f32[1,256]{1,0:T(1,128)S(1)}, u32[]{:S(2)}, u32[]{:S(2)}) collective-permute-start(f32[1,256]{1,0:T(1,128)S(1)} %pad_maximum_fusion.12), channel_id=1, source_target_pairs={{0,1},{1,0},{2,3},{3,2},{4,5},{5,4},{6,7},{7,6},{8,9},{9,8},{10,11... | collective-permute-start | bytes 3080 | tf_op jit(solution)/shard_map/ppermute | solution.py:760
  (74 other events, 647.6 us)
Sparse Core Ops, SparseCore 0:
  10.9 67.0 all-gather.2
  95.1 73.4 all-gather.4
  240.1 129.0 reduce-scatter.1

commit v6 on v5

--- a/solution.py
+++ b/solution.py
@@ -72,8 +72,19 @@
     return values * cos - pltpu.roll(values, HEAD_SIZE // 2, 1) * sin
 
 
-def kv_kernel(heads, x_ref, gain_ref, w_ref, hgain_ref, cos_ref, sin_ref, *refs):
-    normed_ref, kv_ref, lin_ref = refs[-3:]
+def put_together(pieces, whole_ref):
+    rows = whole_ref.shape[0] // len(pieces)
+    for at, piece in enumerate(pieces):
+        whole_ref[at * rows : (at + 1) * rows, :] = piece[...]
+
+
+def kv_kernel(heads, n_pieces, x_ref, gain_ref, hgain_ref, cos_ref, sin_ref, *refs):
+    pieces, refs = refs[:n_pieces], refs[n_pieces:]
+    if n_pieces == 1:
+        w_ref, (normed_ref, kv_ref, lin_ref) = pieces[0], refs[-3:]
+    else:
+        normed_ref, kv_ref, lin_ref, w_ref = refs[-4:]
+        put_together(pieces, w_ref)
     x = x_ref[...].astype(F32)
     normed_ref[...] = (x * rms(x) * gain_ref[...]).astype(BF)
     both = mm(normed_ref[...], w_ref[...])
@@ -86,8 +97,13 @@
         kv_ref[0, :, cols] = turn(lin * rms(lin) * hgain_ref[...], cos_ref[...], sin_ref[...]).astype(BF)
 
 
-def q_kernel(heads, normed_ref, w_ref, hgain_ref, cos_ref, sin_ref, *refs):
-    q_ref, lin_ref = refs[-2:]
+def q_kernel(heads, n_pieces, normed_ref, hgain_ref, cos_ref, sin_ref, *refs):
+    pieces, refs = refs[:n_pieces], refs[n_pieces:]
+    if n_pieces == 1:
+        w_ref, (q_ref, lin_ref) = pieces[0], refs[-2:]
+    else:
+        q_ref, lin_ref, w_ref = refs[-3:]
+        put_together(pieces, w_ref)
     both = mm(normed_ref[...], w_ref[...])
     for h in range(heads):
         cols = slice(h * HEAD_SIZE, (h + 1) * HEAD_SIZE)
@@ -835,17 +851,12 @@
             for axis, bit in bits:
                 one = jnp.concatenate([one, swap(one, axis, bit)])
             return [one]
-        by_x, by_y = (after(v, *gate) for v in (swap(one, "ctx", 2), swap(one, "ctx", 4)))
-        cut = one.shape[1] // 2
-        return [one, by_x, by_y, swap(by_y[:, :cut], "ctx", 2), swap(by_x[:, cut:], "ctx", 4)]
-
-    def gather_far(pieces, *gate):
+        return [one] + [after(swap(one, "ctx", bit), *gate) for bit in (2, 4, 6)]
+
+    def gather_far(near, *gate):
         if ctx_size != 8:
-            return pieces[0], pieces[0]
-        *near, left, right = pieces
-        far = jnp.concatenate([after(left, *gate), after(right, *gate)], axis=1)
-        near = [*near, far]
-        return jnp.concatenate(near + [after(swap(piece, "ctx", 1), *gate) for piece in near]), far
+            return near
+        return near + [after(swap(piece, "ctx", 1), *gate) for piece in near]
 
     def scatter_rows(low, high, late):
         total = add_low(low, after(swap(high, "ctx", 1), late))
@@ -881,14 +892,14 @@
     )
     kv_one = gather_first(kv_piece)
     kv_near = gather_near(kv_one)
-    w_kv, kv_far = gather_far(kv_near)
-    q_one = gather_first(after(w_query, kv_piece), kv_far)
+    kv_pieces = gather_far(kv_near)
+    q_one = gather_first(after(w_query, kv_one), kv_near[-1])
     w_od = lax.all_gather(od_piece, weight_axes, axis=0, tiled=True)
     gains = jnp.concatenate([attn_gain, ffn_gain, query_gain, key_gain])[None]
     gains = jnp.where(jnp.arange(parts)[:, None] == part, gains, jnp.zeros((), BF))
     gains = gains + after(swap(gains, "ctx", 1), kv_piece)
     for at, (axis, bit) in enumerate(bits[:-1]):
-        gains = gains + after(swap(gains, axis, bit), (kv_one, kv_near[min(1, len(kv_near) - 1)], kv_far)[min(at, 2)])
+        gains = gains + after(swap(gains, axis, bit), (kv_one, kv_near[-1], kv_near[-1])[min(at, 2)])
     gains = gains.astype(F32)
     gain_one = gains[:, :wide].reshape(1, -1)
     gain_two = gains[:, wide : 2 * wide].reshape(1, -1)
@@ -914,11 +925,14 @@
 
     once = lambda f: (0, 0)
 
-    def keys_values(half, gain, whole=None):
+    def weight_inputs(pieces):
+        return [(piece, piece.shape, once) for piece in pieces]
+
+    def keys_values(half, gain, pieces, whole=None):
         mine = lambda f: (half, 0)
         ins = [
-            (tokens_s, (rows, model), mine), (gain, (1, model), once), (w_kv, (model, 2 * k_cols), once),
-            (gain_k, (1, HEAD_SIZE), once), (cos, (rows, HEAD_SIZE), mine), (sin, (rows, HEAD_SIZE), mine),
+            (tokens_s, (rows, model), mine), (gain, (1, model), once), (gain_k, (1, HEAD_SIZE), once),
+            (cos, (rows, HEAD_SIZE), mine), (sin, (rows, HEAD_SIZE), mine), *weight_inputs(pieces),
         ]
         keep = {}
         if whole is not None:
@@ -929,17 +943,21 @@
             (shaped((2, rows, k_cols), BF), (2, rows, k_cols), lambda f: (0, 0, 0)),
             (shaped((rows, k_cols), F32), (rows, k_cols), once),
         ]
-        return call(functools.partial(kv_kernel, kv_heads), "keys_values", (1,), ins, outs, keep=keep)
-
-    q_near = gather_near(q_one, w_kv)
-    normed, kv_p, k_lin_p = keys_values(0, after(gain_one_s, *q_near[1:]))
-    normed, kv_c, k_lin_c = keys_values(1, after(gain_one_s, kv_p), normed)
-    w_q, _ = gather_far(q_near, kv_c)
-    def queries(half, gain, whole=None):
+        if len(pieces) > 1:
+            outs.append((shaped((model, 2 * k_cols), BF), (model, 2 * k_cols), once))
+        return call(functools.partial(kv_kernel, kv_heads, len(pieces)), "keys_values", (1,), ins, outs, keep=keep)
+
+    q_near = gather_near(q_one, kv_pieces[-1])
+    normed, kv_p, k_lin_p, *w_kv = keys_values(0, after(gain_one_s, *q_near[1:]), kv_pieces)
+    (w_kv,) = w_kv or kv_pieces
+    normed, kv_c, k_lin_c = keys_values(1, after(gain_one_s, kv_p), [w_kv], normed)
+    q_pieces = gather_far(q_near, kv_c)
+
+    def queries(half, gain, pieces, whole=None):
         mine = lambda f: (half, 0)
         ins = [
-            (normed, (rows, model), mine), (w_q, (model, q_cols), once), (gain, (1, HEAD_SIZE), once),
-            (cos, (rows, HEAD_SIZE), mine), (sin, (rows, HEAD_SIZE), mine),
+            (normed, (rows, model), mine), (gain, (1, HEAD_SIZE), once),
+            (cos, (rows, HEAD_SIZE), mine), (sin, (rows, HEAD_SIZE), mine), *weight_inputs(pieces),
         ]
         keep = {}
         if whole is not None:
@@ -949,9 +967,13 @@
             (shaped((rows, q_cols), BF), (rows, q_cols), once),
             (shaped((2 * rows, q_cols), F32), (rows, q_cols), mine),
         ]
-        return call(functools.partial(q_kernel, heads), "queries", (1,), ins, outs, keep=keep)
-
-    q_c, q_lin = queries(1, gain_q)
+        if len(pieces) > 1:
+            outs.append((shaped((model, q_cols), BF), (model, q_cols), once))
+        return call(functools.partial(q_kernel, heads, len(pieces)), "queries", (1,), ins, outs, keep=keep)
+
+    q_c, q_lin, *w_q = queries(1, gain_q, q_pieces)
+    (w_q,) = w_q or q_pieces
+    q_p, q_lin = queries(0, after(gain_q, q_c), [w_q], q_lin)
 
     def pick(source, wanted):
         return {s: source[s] for s in source if s in wanted}
@@ -970,7 +992,7 @@
         halos.update({d: shift(kv_c, d) for d in range(1, n_halo)})
     ready = ()
     if ctx_size == 8:
-        slots[2], slots[4] = after(slots[2], q_c), after(slots[4], q_c)
+        slots[2], slots[4] = after(slots[2], q_p), after(slots[4], q_p)
         far_k, far_v = swap(slots[4][0], "ctx", 2), swap(slots[2][1], "ctx", 4)
         slots[3], slots[5] = swap(slots[2], "ctx", 1), swap(slots[4], "ctx", 1)
         halos[2] = shift(after(kv_c, slots[2]), 2)
@@ -980,12 +1002,11 @@
     c_state = attention_forward(
         (1,), after(scalars, *ready), (q_c,), low_col, pick(slots, near), pick(halos, (0,))
     )
-    q_p, q_lin = queries(0, after(gain_q, c_state[0]), q_lin)
     if ctx_size == 8:
         slots[6] = after(far_k, c_state[0]), after(far_v, c_state[0])
         slots[7] = tuple(swap(part, "ctx", 1) for part in slots[6])
     attended, lse_p = attention_forward(
-        (0,), after(scalars, q_p), (q_p,), low_col, slots, {}, None, (None,)
+        (0,), after(scalars, c_state[0]), (q_p,), low_col, slots, {}, None, (None,)
     )
     part_p = out_projection(0, attended, w_od)
     got_p = swap(part_p, "tensor", 1)

time: 549 us -> 545 us (level)
  waiting for transfers between devices: 58.5 us -> 72.7 us
  starting transfers between devices: 122 us -> 112 us
  local copies, waits for them, and re-layouts: 27.9 us -> 18.5 us
    ppermute x72 -> x70, starting transfers between devices: 117 us -> 106 us  [swap(): return lax.ppermute(value, axis, [(i, i ^ bit) for i in range(size)])]
    ppermute x72 -> x70, waiting for transfers between devices: 47.9 us -> 58.5 us  [swap(): return lax.ppermute(value, axis, [(i, i ^ bit) for i in range(size)])]
    unnamed x100 -> x115, local copies, waits for them, and re-layouts: 16.4 us -> 8.78 us
  transfers between devices with their start and end apart: 77 -> 75, of which waited for: 21 -> 24; matrix products, arithmetic and copies ran while one was open for 7% -> 5% of each run, Pallas kernels for 55% -> 55%
where the time goes in v6:
time: 545 us; the launch traced here: 535 us
  Pallas kernels  297 us (54%)
  starting transfers between devices  112 us (21%)
  waiting for transfers between devices  72.7 us (13%)
  local copies, waits for them, and re-layouts  18.5 us (3%)
  other arithmetic  15.4 us (3%)
  between operations  15.3 us (3%)
    pallas_call x34, Pallas kernels, call(): pl.pallas_call(kernel, grid_spec=pltpu.PrefetchScalarGridSpec(num_scalar_...  297 us
    ppermute x70, starting transfers between devices, swap(): return lax.ppermute(value, axis, [(i, i ^ bit) for i in range(size)])  106 us
    ppermute x70, waiting for transfers between devices, swap(): return lax.ppermute(value, axis, [(i, i ^ bit) for i in range(size)])  58.5 us
    ppermute x2, waiting for transfers between devices, shift(): lax.ppermute(value, 'ctx', [(i, i + by) for i in range(size) if 0 <= i +...  14.1 us
  transfers between devices with their start and end apart: 75, of which 24 were waited for; matrix products, arithmetic and copies ran while one was open for 5% of the time, Pallas kernels for 55%

profile of v6, /device:TPU:0, one launch (start us, length us, event | category | flops | bytes accessed | tf_op | source)
XLA Modules:
  0.0 535.4 jit_solution(6605775541792465746)
XLA Ops:
  10.8 3.7 collective-permute-start
  28.9 4.4 collective-permute-done.2.refs_3_
  37.3 3.7 fusion.5.x_ref
  47.5 5.0 collective-permute-done.7.refs_1_
  52.5 6.1 %collective-permute-done.10.refs_3_ = bf16[128,1024]{1,0:T(8,128)(2,1)S(1)} collective-permute-done((bf16[128,1024]{1,0:T(8,128)(2,1)S(1)}, bf16[128,1024]{1,0:T(8,128)(2,1)S(1)}, u32[]{:S(2)}, u32[]{:S(2)}) %collective-permute-start.10) | collective-permute-done | bytes 262176 | tf_op jit(solution)/shard_map/ppermute | solution.py:776
  59.5 5.6 %keys_values.2 = (bf16[1024,1024]{1,0:T(8,128)(2,1)}, bf16[2,512,512]{2,1,0:T(8,128)(2,1)}, f32[512,512]{1,0:T(8,128)}, bf16[1024,1024]{1,0:T(8,128)(2,1)}) custom-call(bf16[1024,1024]{1,0:T(8,128)(2,1)} %fusion.5.x_ref, f32[1,1024]{1,0:T(1,128)} %fusion.1.gain_ref, f32[1,128]{1,0:T(1,128)} %reshape.120.hgain_ref.gain_ref, ...), custom_call_target="tpu_custom_call" | custom-call | tf_op jit(solution)/shard_map/keys_values/pallas_call | solution.py:46
  68.6 5.7 %keys_values.3 = (bf16[1024,1024]{1,0:T(8,128)(2,1)}, bf16[2,512,512]{2,1,0:T(8,128)(2,1)}, f32[512,512]{1,0:T(8,128)}) custom-call(bf16[1024,1024]{1,0:T(8,128)(2,1)} %fusion.5.x_ref, f32[1,1024]{1,0:T(1,128)} %fusion.1.gain_ref, f32[1,128]{1,0:T(1,128)} %reshape.120.hgain_ref.gain_ref, ...), custom_call_target="tpu_custom_call", output_to_operand_aliasing={{0}: (6, {})} | custom-call | tf_op jit(solution)/shard_map/keys_values/pallas_call | solution.py:46
  75.2 6.9 %queries.2 = (bf16[512,1024]{1,0:T(8,128)(2,1)}, f32[1024,1024]{1,0:T(8,128)}, bf16[1024,1024]{1,0:T(8,128)(2,1)}) custom-call(bf16[1024,1024]{1,0:T(8,128)(2,1)} %get-tuple-element.201.normed_ref.left_ref, f32[1,128]{1,0:T(1,128)} %reshape.121.hgain_ref.gain_ref, f32[1024,128]{1,0:T(8,128)} %get-tuple-element.392.cos_ref, ...), custom_call_target="tpu_custom_call" | custom-call | tf_op jit(solution)/shard_map/queries/pallas_call | solution.py:46
  82.0 6.5 %queries.3 = (bf16[512,1024]{1,0:T(8,128)(2,1)}, f32[1024,1024]{1,0:T(8,128)}) custom-call(bf16[1024,1024]{1,0:T(8,128)(2,1)} %get-tuple-element.201.normed_ref.left_ref, f32[1,128]{1,0:T(1,128)} %reshape.121.hgain_ref.gain_ref, f32[1024,128]{1,0:T(8,128)} %get-tuple-element.392.cos_ref, ...), custom_call_target="tpu_custom_call", output_to_operand_aliasing={{1}: (5, {})} | custom-call | tf_op jit(solution)/shard_map/queries/pallas_call | solution.py:46
  93.8 4.3 collective-permute-start.29
  100.7 10.9 %attend.3 = (f32[512,1024]{1,0:T(8,128)}, f32[512,1024]{1,0:T(8,128)}) custom-call(s32[2]{0:T(128)} %pad_add_fusion.1.idx_ref, s32[512,128]{1,0:T(8,128)} %broadcast_in_dim.73.lo_ref, bf16[512,1024]{1,0:T(8,128)(2,1)} %get-tuple-element.207.refs_0_.q_ref, bf16[2,512,512]{2,1,0:T(8,128)(2,1)} %get-tuple-element.197.refs_1_.refs_0_, ...), custom_call_target="tpu_custom_call" | custom-call | tf_op jit(solution)/shard_map/attend/pallas_call | solution.py:46
  114.5 8.8 %attend.4 = (bf16[1024,1024]{1,0:T(8,128)(2,1)}, f32[4,8,512]{2,1,0:T(8,128)}) custom-call(s32[2]{0:T(128)} %pad_add_fusion.1.idx_ref, s32[512,128]{1,0:T(8,128)} %broadcast_in_dim.73.lo_ref, bf16[512,1024]{1,0:T(8,128)(2,1)} %get-tuple-element.211.refs_0_.q_ref, bf16[2,512,512]{2,1,0:T(8,128)(2,1)} %get-tuple-element.197.refs_1_.refs_0_, ...), custom_call_target="tpu_custom_call" | custom-call | tf_op jit(solution)/shard_map/attend/pallas_call | solution.py:46
  123.3 4.0 out_projection.2.own_ref
  127.3 12.4 %collective-permute-done.29.refs_9_.refs_1_ = bf16[2,512,512]{2,1,0:T(8,128)(2,1)} collective-permute-done((bf16[2,512,512]{2,1,0:T(8,128)(2,1)}, bf16[2,512,512]{2,1,0:T(8,128)(2,1)}, u32[]{:S(2)}, u32[]{:S(2)}) %collective-permute-start.29) | collective-permute-done | bytes 1048608 | tf_op jit(solution)/shard_map/ppermute | solution.py:781
  143.6 19.5 %attend.5 = (bf16[1024,1024]{1,0:T(8,128)(2,1)}, f32[4,8,512]{2,1,0:T(8,128)}) custom-call(s32[2]{0:T(128)} %pad_add_fusion.1.idx_ref, s32[512,128]{1,0:T(8,128)} %broadcast_in_dim.73.lo_ref, bf16[512,1024]{1,0:T(8,128)(2,1)} %get-tuple-element.207.refs_0_.q_ref, bf16[2,512,512]{2,1,0:T(8,128)(2,1)} %copy-done.2, ...), custom_call_target="tpu_custom_call", output_to_operand_aliasing={{0}: (15, {})} | custom-call | tf_op jit(solution)/shard_map/attend/pallas_call | solution.py:46
  163.1 3.9 out_projection.3.own_ref
  170.0 6.2 %collective-permute-done.32.got_ref = bf16[512,1024]{1,0:T(8,128)(2,1)S(1)} collective-permute-done((bf16[512,1024]{1,0:T(8,128)(2,1)S(1)}, bf16[512,1024]{1,0:T(8,128)(2,1)S(1)}, u32[]{:S(2)}, u32[]{:S(2)}) %collective-permute-start.32) | collective-permute-done | bytes 1048608 | tf_op jit(solution)/shard_map/ppermute | solution.py:776
  177.2 18.3 %feed_forward.2 = (f32[512,1024]{1,0:T(8,128)}, bf16[1024,1024]{1,0:T(8,128)(2,1)}, bf16[1024,1536]{1,0:T(8,128)(2,1)}, bf16[1024,3072]{1,0:T(8,128)(2,1)}, bf16...) custom-call(bf16[1024,1024]{1,0:T(8,128)(2,1)} %x_ref.7, bf16[512,1024]{1,0:T(8,128)(2,1)} %out_projection.2.own_ref, ...), custom_call_target="tpu_custom_call" | custom-call | tf_op jit(solution)/shard_map/feed_forward/pallas_call | solution.py:46
  195.6 3.2 collective-permute-done.31.got_ref
  198.8 18.5 %feed_forward.3 = (f32[512,1024]{1,0:T(8,128)}, bf16[1024,1024]{1,0:T(8,128)(2,1)}, bf16[1024,1536]{1,0:T(8,128)(2,1)}, bf16[1024,3072]{1,0:T(8,128)(2,1)}, bf16...) custom-call(bf16[1024,1024]{1,0:T(8,128)(2,1)} %x_ref.7, ...), custom_call_target="tpu_custom_call", output_to_operand_aliasing={{1}: (7, {}), {2}: (8, {}), {3}: (9, {})} | custom-call | tf_op jit(solution)/shard_map/feed_forward/pallas_call | solution.py:46
  217.4 10.8 %weight_grad.2.refs_0_ = bf16[1024,4608]{1,0:T(8,128)(2,1)} custom-call(bf16[1024,1024]{1,0:T(8,128)(2,1)} %get-tuple-element.240.left_ref, bf16[1024,3072]{1,0:T(8,128)(2,1)} %get-tuple-element.241.right_ref), custom_call_target="tpu_custom_call" | custom-call | tf_op jit(solution)/shard_map/weight_grad/pallas_call | solution.py:46
  228.1 7.2 %weight_grad.3 = bf16[1024,4608]{1,0:T(8,128)(2,1)} custom-call(bf16[1024,1024]{1,0:T(8,128)(2,1)} %dy_ref.7, bf16[1024,1536]{1,0:T(8,128)(2,1)} %get-tuple-element.239.right_ref, bf16[1024,4608]{1,0:T(8,128)(2,1)} %weight_grad.2.refs_0_), custom_call_target="tpu_custom_call", output_to_operand_aliasing={{}: (2, {})} | custom-call | tf_op jit(solution)/shard_map/weight_grad/pallas_call | solution.py:46
  236.3 7.2 %mixed_back.2 = (f32[512,1024]{1,0:T(8,128)}, bf16[1024,1024]{1,0:T(8,128)(2,1)}, bf16[512,1024]{1,0:T(8,128)(2,1)}, f32[4,8,512]{2,1,0:T(8,128)}, f32[1,1024]{1,0:T(1,128)}) custom-call(bf16[512,1024]{1,0:T(8,128)(2,1)} %get-tuple-element.230.own_ref, bf16[512,1024]{1,0:T(8,128)(2,1)} %copy-done.18, f32[512,1024]{1,0:T(8,128)} %get-tuple-element.332.resid_ref, ...), custom_call_target="tpu_custom_call" | custom-call | tf_op jit(solution)/shard_map/mixed_back/pallas_call | solution.py:46
  244.1 6.1 %attend_back.6 = (f32[512,1024]{1,0:T(8,128)}, bf16[2,512,512]{2,1,0:T(8,128)(2,1)}, bf16[2,512,512]{2,1,0:T(8,128)(2,1)}) custom-call(s32[2]{0:T(128)} %pad_add_fusion.1.idx_ref, bf16[512,1024]{1,0:T(8,128)(2,1)} %get-tuple-element.211.refs_0_.q_ref, bf16[512,1024]{1,0:T(8,128)(2,1)} %get-tuple-element.243.do_ref, f32[4,8,512]{2,1,0:T(8,128)} %get-tuple-element.245.lse_ref, ...), custom_call_target="tpu_custom_call" | custom-call | flops 300000000 | tf_op jit(solution)/shard_map/attend_back/pallas_call | solution.py:46
  251.2 7.9 %mixed_back.3 = (f32[512,1024]{1,0:T(8,128)}, bf16[1024,1024]{1,0:T(8,128)(2,1)}, bf16[512,1024]{1,0:T(8,128)(2,1)}, f32[4,8,512]{2,1,0:T(8,128)}, f32[1,1024]{1,0:T(1,128)}) custom-call(bf16[512,1024]{1,0:T(8,128)(2,1)} %get-tuple-element.237.own_ref, bf16[512,1024]{1,0:T(8,128)(2,1)} %copy-done.19, ...), custom_call_target="tpu_custom_call", output_to_operand_aliasing={{1}: (7, {})} | custom-call | tf_op jit(solution)/shard_map/mixed_back/pallas_call | solution.py:46
  259.1 6.4 %slot_weight_grad.1 = (bf16[512,1024]{1,0:T(8,128)(2,1)}, bf16[512,1024]{1,0:T(8,128)(2,1)}) custom-call(s32[1]{0:T(128)} %bitcast.10.part_ref, bf16[1024,1024]{1,0:T(8,128)(2,1)} %get-tuple-element.250.left_ref, bf16[1024,1024]{1,0:T(8,128)(2,1)} %get-tuple-element.225.att_ref.right_ref), custom_call_target="tpu_custom_call" | custom-call | tf_op jit(solution)/shard_map/slot_weight_grad/pallas_call | solution.py:46
  267.5 10.3 %attend_back.7 = (f32[512,1024]{1,0:T(8,128)}, bf16[2,512,512]{2,1,0:T(8,128)(2,1)}, bf16[2,512,512]{2,1,0:T(8,128)(2,1)}, bf16[2,512,512]{2,1,0:T(8,128)(2,1)}) custom-call(s32[2]{0:T(128)} %pad_add_fusion.1.idx_ref, bf16[512,1024]{1,0:T(8,128)(2,1)} %get-tuple-element.207.refs_0_.q_ref, bf16[512,1024]{1,0:T(8,128)(2,1)} %get-tuple-element.253.do_ref, ...), custom_call_target="tpu_custom_call" | custom-call | flops 65999998976 | tf_op jit(solution)/shard_map/attend_back/pallas_call | solution.py:46
  277.8 6.7 %collective-permute-start.38 = (bf16[2,512,512]{2,1,0:T(8,128)(2,1)}, bf16[2,512,512]{2,1,0:T(8,128)(2,1)S(1)}, u32[]{:S(2)}, u32[]{:S(2)}) collective-permute-start(bf16[2,512,512]{2,1,0:T(8,128)(2,1)} %get-tuple-element.267), channel_id=1, source_target_pairs={{0,2},{2,0},{4,6},{6,4},{8,10},{10,8},{12,14},{14,12},{1,3},{3,1},... | collective-permute-start | bytes 3145736 | tf_op jit(solution)/shard_map/ppermute | solution.py:776
  285.0 15.1 %attend_back.8 = (f32[512,1024]{1,0:T(8,128)}, bf16[2,512,512]{2,1,0:T(8,128)(2,1)}, bf16[2,512,512]{2,1,0:T(8,128)(2,1)}) custom-call(s32[2]{0:T(128)} %pad_add_fusion.1.idx_ref, bf16[512,1024]{1,0:T(8,128)(2,1)} %get-tuple-element.207.refs_0_.q_ref, bf16[512,1024]{1,0:T(8,128)(2,1)} %get-tuple-element.253.do_ref, f32[4,8,512]{2,1,0:T(8,128)} %get-tuple-element.254.lse_ref, ...), custom_call_target="tpu_custom_call" | custom-call | flops 48000000000 | tf_op jit(solution)/shard_map/attend_back/pallas_call | solution.py:46
  300.1 12.1 %collective-permute-start.36 = (bf16[128,512]{1,0:T(8,128)(2,1)S(1)}, bf16[128,512]{1,0:T(8,128)(2,1)S(1)}, u32[]{:S(2)}, u32[]{:S(2)}) collective-permute-start(bf16[128,512]{1,0:T(8,128)(2,1)S(1)} %get-tuple-element.379), channel_id=1, source_target_pairs={{0,8},{2,10},{4,12},{6,14},{8,0},{10,2},{12,4},{14,6},{1,9},{3,11}... | collective-permute-start | bytes 393224 | tf_op jit(solution)/shard_map/ppermute | solution.py:776
  312.2 9.0 %collective-permute-start.37 = (bf16[128,512]{1,0:T(8,128)(2,1)S(1)}, bf16[128,512]{1,0:T(8,128)(2,1)S(1)}, u32[]{:S(2)}, u32[]{:S(2)}) collective-permute-start(bf16[128,512]{1,0:T(8,128)(2,1)S(1)} %get-tuple-element.377), channel_id=1, source_target_pairs={{0,4},{2,6},{4,0},{6,2},{8,12},{10,14},{12,8},{14,10},{1,5},{3,7},... | collective-permute-start | bytes 393224 | tf_op jit(solution)/shard_map/ppermute | solution.py:776
  322.6 5.6 %collective-permute-done.37 = bf16[128,512]{1,0:T(8,128)(2,1)S(1)} collective-permute-done((bf16[128,512]{1,0:T(8,128)(2,1)S(1)}, bf16[128,512]{1,0:T(8,128)(2,1)S(1)}, u32[]{:S(2)}, u32[]{:S(2)}) %collective-permute-start.37) | collective-permute-done | bytes 131104 | tf_op jit(solution)/shard_map/ppermute | solution.py:776
  330.5 12.5 %attend_back.9 = (f32[1024,1024]{1,0:T(8,128)}, bf16[2,512,512]{2,1,0:T(8,128)(2,1)}, bf16[2,512,512]{2,1,0:T(8,128)(2,1)}, bf16[2,512,512]{2,1,0:T(8,128)(2,1)}...) custom-call(s32[2]{0:T(128)} %pad_add_fusion.1.idx_ref, ...), custom_call_target="tpu_custom_call" | custom-call | flops 120000004096 | tf_op jit(solution)/shard_map/attend_back/pallas_call | solution.py:46
  347.3 25.9 %attend_back.10 = (f32[512,1024]{1,0:T(8,128)}, bf16[2,512,512]{2,1,0:T(8,128)(2,1)}, bf16[2,512,512]{2,1,0:T(8,128)(2,1)}, bf16[2,512,512]{2,1,0:T(8,128)(2,1)}, bf16[2,512,512]{2,1,0:T(8,128)(2,1)}) custom-call(s32[2]{0:T(128)} %pad_add_fusion.1.idx_ref, bf16[512,1024]{1,0:T(8,128)(2,1)} %get-tuple-element.207.refs_0_.q_ref, ...), custom_call_target="tpu_custom_call" | custom-call | flops 83999997952 | tf_op jit(solution)/shard_map/attend_back/pallas_call | solution.py:46
  375.9 12.3 %collective-permute-start.49 = (bf16[512,512]{1,0:T(8,128)(2,1)S(1)}, bf16[512,512]{1,0:T(8,128)(2,1)}, u32[]{:S(2)}, u32[]{:S(2)}) collective-permute-start(bf16[512,512]{1,0:T(8,128)(2,1)S(1)} %get-tuple-element.373), channel_id=1, source_target_pairs={{0,8},{2,10},{4,12},{6,14},{8,0},{10,2},{12,4},{14,6},{1,9},{3,11}... | collective-permute-start | bytes 1572872 | tf_op jit(solution)/shard_map/ppermute | solution.py:776
  388.2 9.4 %collective-permute-start.48 = (bf16[512,512]{1,0:T(8,128)(2,1)}, bf16[512,512]{1,0:T(8,128)(2,1)}, u32[]{:S(2)}, u32[]{:S(2)}) collective-permute-start(bf16[512,512]{1,0:T(8,128)(2,1)} %get-tuple-element.374), channel_id=1, source_target_pairs={{0,4},{2,6},{4,0},{6,2},{8,12},{10,14},{12,8},{14,10},{1,5},{3,7},... | collective-permute-start | bytes 1572872 | tf_op jit(solution)/shard_map/ppermute | solution.py:776
  397.7 4.1 collective-permute-start.47
  401.8 15.1 %attend_back.11 = (f32[1024,1024]{1,0:T(8,128)}, bf16[2,512,512]{2,1,0:T(8,128)(2,1)}, bf16[2,512,512]{2,1,0:T(8,128)(2,1)}) custom-call(s32[2]{0:T(128)} %pad_add_fusion.1.idx_ref, bf16[512,1024]{1,0:T(8,128)(2,1)} %get-tuple-element.207.refs_0_.q_ref, bf16[512,1024]{1,0:T(8,128)(2,1)} %get-tuple-element.253.do_ref, ...), custom_call_target="tpu_custom_call", output_to_operand_aliasing={{0}: (11, {})} | custom-call | flops 48000000000 | tf_op jit(solution)/shard_map/attend_back/pallas_call | solution.py:46
  418.8 3.8 merge.1
  425.4 12.0 %q_back.1 = (bf16[1024,1024]{1,0:T(8,128)(2,1)}, f32[1024,1024]{1,0:T(8,128)}, f32[1,128]{1,0:T(1,128)}) custom-call(f32[1024,1024]{1,0:T(8,128)} %get-tuple-element.289.dq_ref, f32[1024,1024]{1,0:T(8,128)} %get-tuple-element.290.lin_ref, f32[1,128]{1,0:T(1,128)} %reshape.121.hgain_ref.gain_ref, f32[1024,128]{1,0:T(8,128)} %get-tuple-element.392.cos_ref, ...), custom_call_target="tpu_custom_call" | custom-call | tf_op jit(solution)/shard_map/q_back/pallas_call | solution.py:46
  437.4 8.5 %kv_back.2 = (bf16[1024,1024]{1,0:T(8,128)(2,1)}, bf16[512,1024]{1,0:T(8,128)(2,1)}, f32[1,128]{1,0:T(1,128)}) custom-call(f32[512,512]{1,0:T(8,128)} %get-tuple-element.302.lin_ref, f32[1,128]{1,0:T(1,128)} %reshape.120.hgain_ref.gain_ref, f32[1024,128]{1,0:T(8,128)} %get-tuple-element.392.cos_ref, f32[1024,128]{1,0:T(8,128)} %get-tuple-element.393.sin_ref, ...), custom_call_target="tpu_custom_call" | custom-call | tf_op jit(solution)/shard_map/kv_back/pallas_call | solution.py:46
  445.9 5.8 %weight_halves.2 = (bf16[512,1024]{1,0:T(8,128)(2,1)}, bf16[512,1024]{1,0:T(8,128)(2,1)}) custom-call(bf16[1024,1024]{1,0:T(8,128)(2,1)} %get-tuple-element.201.normed_ref.left_ref, bf16[1024,1024]{1,0:T(8,128)(2,1)} %get-tuple-element.307.right_ref), custom_call_target="tpu_custom_call" | custom-call | tf_op jit(solution)/shard_map/weight_halves/pallas_call | solution.py:46
  453.9 8.9 %kv_back.3 = (bf16[1024,1024]{1,0:T(8,128)(2,1)}, bf16[512,1024]{1,0:T(8,128)(2,1)}, f32[1,128]{1,0:T(1,128)}) custom-call(f32[512,512]{1,0:T(8,128)} %get-tuple-element.236.lin_ref, f32[1,128]{1,0:T(1,128)} %reshape.120.hgain_ref.gain_ref, f32[1024,128]{1,0:T(8,128)} %get-tuple-element.392.cos_ref, ...), custom_call_target="tpu_custom_call", output_to_operand_aliasing={{0}: (15, {})} | custom-call | flops 8999999488 | tf_op jit(solution)/shard_map/kv_back/pallas_call | solution.py:46
  469.2 5.8 %weight_halves.3 = (bf16[512,1024]{1,0:T(8,128)(2,1)}, bf16[512,1024]{1,0:T(8,128)(2,1)}) custom-call(bf16[1024,1024]{1,0:T(8,128)(2,1)} %get-tuple-element.201.normed_ref.left_ref, bf16[1024,1024]{1,0:T(8,128)(2,1)} %get-tuple-element.318.right_ref), custom_call_target="tpu_custom_call" | custom-call | tf_op jit(solution)/shard_map/weight_halves/pallas_call | solution.py:46
  478.1 4.3 tokens_back.2
  503.0 4.0 tokens_back.3
  511.9 5.6 %collective-permute-done.69 = bf16[64,1024]{1,0:T(8,128)(2,1)S(1)} collective-permute-done((bf16[64,1024]{1,0:T(8,128)(2,1)S(1)}, bf16[64,1024]{1,0:T(8,128)(2,1)S(1)}, u32[]{:S(2)}, u32[]{:S(2)}) %collective-permute-start.69) | collective-permute-done | bytes 131104 | tf_op jit(solution)/shard_map/ppermute | solution.py:776
  522.1 3.8 collective-permute-done.71
  (349 shorter events, 116.2 us)
Async XLA Ops:
  7.2 83.6 %all-gather.3.cloned.1.call-start = ((), (), s32[]{:S(2)}) async-start(), calls=%async_computation.1 | async-start | bytes 5570560 | tf_op jit(solution)/shard_map/all_gather | solution.py:897
  9.4 166.8 %all-gather.5.cloned.1.call-start = ((), (), s32[]{:S(2)}) async-start(), calls=%async_computation.2 | async-start | bytes 6684672 | tf_op jit(solution)/shard_map/all_gather | solution.py:1001
  10.8 10.8 %collective-permute-start = (bf16[64,1024]{1,0:T(8,128)(2,1)}, bf16[64,1024]{1,0:T(8,128)(2,1)S(1)}, u32[]{:S(2)}, u32[]{:S(2)}) collective-permute-start(bf16[64,1024]{1,0:T(8,128)(2,1)} %get-tuple-element.185), channel_id=1, source_target_pairs={{0,16},{16,0},{1,17},{17,1},{2,18},{18,2},{3,19},{19,3},{4,20},{20... | collective-permute-start | bytes 393224 | tf_op jit(solution)/shard_map/ppermute | solution.py:776
  21.6 11.7 %collective-permute-start.2 = (bf16[128,1024]{1,0:T(8,128)(2,1)S(1)}, bf16[128,1024]{1,0:T(8,128)(2,1)S(1)}, u32[]{:S(2)}, u32[]{:S(2)}) collective-permute-start(bf16[128,1024]{1,0:T(8,128)(2,1)S(1)} %pad_maximum_fusion.2.refs_0_), channel_id=1, source_target_pairs={{0,12},{2,14},{4,8},{6,10},{8,4},{10,6},{12,0},{14,2},{1,13},{3,15... | collective-permute-start | bytes 786440 | tf_op jit(solution)/shard_map/ppermute | solution.py:776
  24.9 10.9 %collective-permute-start.1 = (bf16[64,1024]{1,0:T(8,128)(2,1)S(1)}, bf16[64,1024]{1,0:T(8,128)(2,1)S(1)}, u32[]{:S(2)}, u32[]{:S(2)}) collective-permute-start(bf16[64,1024]{1,0:T(8,128)(2,1)S(1)} %copy-done.41), channel_id=1, source_target_pairs={{0,16},{16,0},{1,17},{17,1},{2,18},{18,2},{3,19},{19,3},{4,20},{20... | collective-permute-start | bytes 393224 | tf_op jit(solution)/shard_map/ppermute | solution.py:776
  26.8 14.2 %collective-permute-start.11 = (bf16[128,1024]{1,0:T(8,128)(2,1)S(1)}, bf16[128,1024]{1,0:T(8,128)(2,1)S(1)}, u32[]{:S(2)}, u32[]{:S(2)}) collective-permute-start(bf16[128,1024]{1,0:T(8,128)(2,1)S(1)} %pad_maximum_fusion.2.refs_0_), channel_id=1, source_target_pairs={{0,4},{2,6},{4,0},{6,2},{8,12},{10,14},{12,8},{14,10},{1,5},{3,7},... | collective-permute-start | bytes 786440 | tf_op jit(solution)/shard_map/ppermute | solution.py:776
  28.0 14.6 %collective-permute-start.12 = (bf16[128,1024]{1,0:T(8,128)(2,1)S(1)}, bf16[128,1024]{1,0:T(8,128)(2,1)S(1)}, u32[]{:S(2)}, u32[]{:S(2)}) collective-permute-start(bf16[128,1024]{1,0:T(8,128)(2,1)S(1)} %pad_maximum_fusion.2.refs_0_), channel_id=1, source_target_pairs={{0,8},{2,10},{4,12},{6,14},{8,0},{10,2},{12,4},{14,6},{1,9},{3,11}... | collective-permute-start | bytes 786440 | tf_op jit(solution)/shard_map/ppermute | solution.py:776
  33.3 11.3 %collective-permute-start.8 = (bf16[128,1024]{1,0:T(8,128)(2,1)S(1)}, bf16[128,1024]{1,0:T(8,128)(2,1)S(1)}, u32[]{:S(2)}, u32[]{:S(2)}) collective-permute-start(bf16[128,1024]{1,0:T(8,128)(2,1)S(1)} %collective-permute-done.2.refs_3_), channel_id=1, source_target_pairs={{0,2},{2,0},{4,6},{6,4},{8,10},{10,8},{12,14},{14,12},{1,3},{3,1},... | collective-permute-start | bytes 786440 | tf_op jit(solution)/shard_map/ppermute | solution.py:776
  41.0 11.5 %collective-permute-start.7 = (bf16[128,1024]{1,0:T(8,128)(2,1)S(1)}, bf16[128,1024]{1,0:T(8,128)(2,1)S(1)}, u32[]{:S(2)}, u32[]{:S(2)}) collective-permute-start(bf16[128,1024]{1,0:T(8,128)(2,1)S(1)} %constant_dynamic-update-slice_fusion.refs_0_), channel_id=1, source_target_pairs={{0,4},{2,6},{4,0},{6,2},{8,12},{10,14},{12,8},{14,10},{1,5},{3,7},... | collective-permute-start | bytes 786440 | tf_op jit(solution)/shard_map/ppermute | solution.py:776
  43.1 15.5 %collective-permute-start.10 = (bf16[128,1024]{1,0:T(8,128)(2,1)S(1)}, bf16[128,1024]{1,0:T(8,128)(2,1)S(1)}, u32[]{:S(2)}, u32[]{:S(2)}) collective-permute-start(bf16[128,1024]{1,0:T(8,128)(2,1)S(1)} %constant_dynamic-update-slice_fusion.refs_0_), channel_id=1, source_target_pairs={{0,12},{2,14},{4,8},{6,10},{8,4},{10,6},{12,0},{14,2},{1,13},{3,15... | collective-permute-start | bytes 786440 | tf_op jit(solution)/shard_map/ppermute | solution.py:776
  44.6 14.1 %collective-permute-start.14 = (bf16[128,1024]{1,0:T(8,128)(2,1)S(1)}, bf16[128,1024]{1,0:T(8,128)(2,1)S(1)}, u32[]{:S(2)}, u32[]{:S(2)}) collective-permute-start(bf16[128,1024]{1,0:T(8,128)(2,1)S(1)} %collective-permute-done.11.refs_1_), channel_id=1, source_target_pairs={{0,2},{2,0},{4,6},{6,4},{8,10},{10,8},{12,14},{14,12},{1,3},{3,1},... | collective-permute-start | bytes 786440 | tf_op jit(solution)/shard_map/ppermute | solution.py:776
  44.6 14.0 %collective-permute-start.15 = (bf16[128,1024]{1,0:T(8,128)(2,1)S(1)}, bf16[128,1024]{1,0:T(8,128)(2,1)S(1)}, u32[]{:S(2)}, u32[]{:S(2)}) collective-permute-start(bf16[128,1024]{1,0:T(8,128)(2,1)S(1)} %collective-permute-done.12.refs_2_), channel_id=1, source_target_pairs={{0,2},{2,0},{4,6},{6,4},{8,10},{10,8},{12,14},{14,12},{1,3},{3,1},... | collective-permute-start | bytes 786440 | tf_op jit(solution)/shard_map/ppermute | solution.py:776
  65.1 25.6 %collective-permute-start.21 = (bf16[2,512,512]{2,1,0:T(8,128)(2,1)}, bf16[2,512,512]{2,1,0:T(8,128)(2,1)S(1)}, u32[]{:S(2)}, u32[]{:S(2)}) collective-permute-start(bf16[2,512,512]{2,1,0:T(8,128)(2,1)} %get-tuple-element.197.refs_1_.refs_0_), channel_id=1, source_target_pairs={{0,8},{2,10},{4,12},{6,14},{8,0},{10,2},{12,4},{14,6},{1,9},{3,11}... | collective-permute-start | bytes 3145736 | tf_op jit(solution)/shard_map/ppermute | solution.py:776
  65.7 25.0 %collective-permute-start.16 = (bf16[2,512,512]{2,1,0:T(8,128)(2,1)}, bf16[2,512,512]{2,1,0:T(8,128)(2,1)S(1)}, u32[]{:S(2)}, u32[]{:S(2)}) collective-permute-start(bf16[2,512,512]{2,1,0:T(8,128)(2,1)} %get-tuple-element.197.refs_1_.refs_0_), channel_id=1, source_target_pairs={{0,4},{2,6},{4,0},{6,2},{8,12},{10,14},{12,8},{14,10},{1,5},{3,7},... | collective-permute-start | bytes 3145736 | tf_op jit(solution)/shard_map/ppermute | solution.py:776
  90.8 326.7 %reduce-scatter.2.cloned.1.call-start = ((), (), s32[]{:S(2)}) async-start(), calls=%async_computation.3 | async-start | bytes 10027008 | tf_op jit(solution)/shard_map/reduce_scatter | solution.py:1033
  90.9 20.6 %collective-permute-start.26 = (bf16[512,512]{1,0:T(8,128)(2,1)S(1)}, bf16[512,512]{1,0:T(8,128)(2,1)S(1)}, u32[]{:S(2)}, u32[]{:S(2)}) collective-permute-start(bf16[512,512]{1,0:T(8,128)(2,1)S(1)} %slice_bitcast_fusion.2), channel_id=1, source_target_pairs={{0,8},{2,10},{4,12},{6,14},{8,0},{10,2},{12,4},{14,6},{1,9},{3,11}... | collective-permute-start | bytes 1572872 | tf_op jit(solution)/shard_map/ppermute | solution.py:776
  92.5 19.2 %collective-permute-start.25 = (bf16[512,512]{1,0:T(8,128)(2,1)S(1)}, bf16[512,512]{1,0:T(8,128)(2,1)S(1)}, u32[]{:S(2)}, u32[]{:S(2)}) collective-permute-start(bf16[512,512]{1,0:T(8,128)(2,1)S(1)} %slice_bitcast_fusion.3), channel_id=1, source_target_pairs={{0,4},{2,6},{4,0},{6,2},{8,12},{10,14},{12,8},{14,10},{1,5},{3,7},... | collective-permute-start | bytes 1572872 | tf_op jit(solution)/shard_map/ppermute | solution.py:776
  93.1 21.3 %collective-permute-start.24 = (bf16[2,512,512]{2,1,0:T(8,128)(2,1)S(1)}, bf16[2,512,512]{2,1,0:T(8,128)(2,1)}, u32[]{:S(2)}, u32[]{:S(2)}) collective-permute-start(bf16[2,512,512]{2,1,0:T(8,128)(2,1)S(1)} %collective-permute-done.21.refs_4_.refs_2_.refs_3_.refs_1_), channel_id=1, source_target_pairs={{0,2},{2,0},{4,6},{6,4},{8,10},{10,8},{12,14},{14,12},{1,3},{3,1},... | collective-permute-start | bytes 3145736 | tf_op jit(solution)/shard_map/ppermute | solution.py:776
  93.2 21.3 %collective-permute-start.23 = (bf16[2,512,512]{2,1,0:T(8,128)(2,1)S(1)}, bf16[2,512,512]{2,1,0:T(8,128)(2,1)}, u32[]{:S(2)}, u32[]{:S(2)}) collective-permute-start(bf16[2,512,512]{2,1,0:T(8,128)(2,1)S(1)} %collective-permute-done.16.refs_3_.refs_1_.refs_2_.refs_0_), channel_id=1, source_target_pairs={{0,2},{2,0},{4,6},{6,4},{8,10},{10,8},{12,14},{14,12},{1,3},{3,1},... | collective-permute-start | bytes 3145736 | tf_op jit(solution)/shard_map/ppermute | solution.py:776
  93.8 46.0 %collective-permute-start.29 = (bf16[2,512,512]{2,1,0:T(8,128)(2,1)}, bf16[2,512,512]{2,1,0:T(8,128)(2,1)}, u32[]{:S(2)}, u32[]{:S(2)}) collective-permute-start(bf16[2,512,512]{2,1,0:T(8,128)(2,1)} %get-tuple-element.222.refs_3_.refs_0_), channel_id=1, source_target_pairs={{0,4},{2,6},{4,8},{6,10},{8,12},{10,14},{1,5},{3,7},{5,9},{7,11},{... | collective-permute-start | bytes 3145736 | tf_op jit(solution)/shard_map/ppermute | solution.py:781
  140.0 36.2 %collective-permute-start.32 = (bf16[512,1024]{1,0:T(8,128)(2,1)S(1)}, bf16[512,1024]{1,0:T(8,128)(2,1)S(1)}, u32[]{:S(2)}, u32[]{:S(2)}) collective-permute-start(bf16[512,1024]{1,0:T(8,128)(2,1)S(1)} %copy-done.11), channel_id=1, source_target_pairs={{0,1},{1,0},{2,3},{3,2},{4,5},{5,4},{6,7},{7,6},{8,9},{9,8},{10,11... | collective-permute-start | bytes 3145736 | tf_op jit(solution)/shard_map/ppermute | solution.py:776
  167.0 31.8 %collective-permute-start.31 = (bf16[512,1024]{1,0:T(8,128)(2,1)}, bf16[512,1024]{1,0:T(8,128)(2,1)}, u32[]{:S(2)}, u32[]{:S(2)}) collective-permute-start(bf16[512,1024]{1,0:T(8,128)(2,1)} %out_projection.3.own_ref), channel_id=1, source_target_pairs={{0,1},{1,0},{2,3},{3,2},{4,5},{5,4},{6,7},{7,6},{8,9},{9,8},{10,11... | collective-permute-start | bytes 3145736 | tf_op jit(solution)/shard_map/ppermute | solution.py:776
  195.5 39.9 %collective-permute-start.34 = (bf16[512,1024]{1,0:T(8,128)(2,1)}, bf16[512,1024]{1,0:T(8,128)(2,1)S(1)}, u32[]{:S(2)}, u32[]{:S(2)}) collective-permute-start(bf16[512,1024]{1,0:T(8,128)(2,1)} %get-tuple-element.230.own_ref), channel_id=1, source_target_pairs={{0,1},{1,0},{2,3},{3,2},{4,5},{5,4},{6,7},{7,6},{8,9},{9,8},{10,11... | collective-permute-start | bytes 3145736 | tf_op jit(solution)/shard_map/ppermute | solution.py:776
  217.3 32.9 %collective-permute-start.33 = (bf16[512,1024]{1,0:T(8,128)(2,1)}, bf16[512,1024]{1,0:T(8,128)(2,1)S(1)}, u32[]{:S(2)}, u32[]{:S(2)}) collective-permute-start(bf16[512,1024]{1,0:T(8,128)(2,1)} %get-tuple-element.237.own_ref), channel_id=1, source_target_pairs={{0,1},{1,0},{2,3},{3,2},{4,5},{5,4},{6,7},{7,6},{8,9},{9,8},{10,11... | collective-permute-start | bytes 3145736 | tf_op jit(solution)/shard_map/ppermute | solution.py:776
  265.5 107.7 %collective-permute-start.43 = (bf16[512,1024]{1,0:T(8,128)(2,1)}, bf16[512,1024]{1,0:T(8,128)(2,1)}, u32[]{:S(2)}, u32[]{:S(2)}) collective-permute-start(bf16[512,1024]{1,0:T(8,128)(2,1)} %get-tuple-element.285.own_ref), channel_id=1, source_target_pairs={{0,1},{1,0},{2,3},{3,2},{4,5},{5,4},{6,7},{7,6},{8,9},{9,8},{10,11... | collective-permute-start | bytes 3145736 | tf_op jit(solution)/shard_map/ppermute | solution.py:776
  267.4 105.8 %collective-permute-start.42 = (bf16[512,1024]{1,0:T(8,128)(2,1)}, bf16[512,1024]{1,0:T(8,128)(2,1)}, u32[]{:S(2)}, u32[]{:S(2)}) collective-permute-start(bf16[512,1024]{1,0:T(8,128)(2,1)} %get-tuple-element.283.own_ref), channel_id=1, source_target_pairs={{0,1},{1,0},{2,3},{3,2},{4,5},{5,4},{6,7},{7,6},{8,9},{9,8},{10,11... | collective-permute-start | bytes 3145736 | tf_op jit(solution)/shard_map/ppermute | solution.py:776
  267.5 17.0 %collective-permute-start.35 = (bf16[512,1024]{1,0:T(8,128)(2,1)}, bf16[512,1024]{1,0:T(8,128)(2,1)S(1)}, u32[]{:S(2)}, u32[]{:S(2)}) collective-permute-start(bf16[512,1024]{1,0:T(8,128)(2,1)} %get-tuple-element.257), channel_id=1, source_target_pairs={{0,2},{2,0},{4,6},{6,4},{8,10},{10,8},{12,14},{14,12},{1,3},{3,1},... | collective-permute-start | bytes 3145736 | tf_op jit(solution)/shard_map/ppermute | solution.py:776
  277.8 22.3 %collective-permute-start.38 = (bf16[2,512,512]{2,1,0:T(8,128)(2,1)}, bf16[2,512,512]{2,1,0:T(8,128)(2,1)S(1)}, u32[]{:S(2)}, u32[]{:S(2)}) collective-permute-start(bf16[2,512,512]{2,1,0:T(8,128)(2,1)} %get-tuple-element.267), channel_id=1, source_target_pairs={{0,2},{2,0},{4,6},{6,4},{8,10},{10,8},{12,14},{14,12},{1,3},{3,1},... | collective-permute-start | bytes 3145736 | tf_op jit(solution)/shard_map/ppermute | solution.py:776
  300.1 22.4 %collective-permute-start.36 = (bf16[128,512]{1,0:T(8,128)(2,1)S(1)}, bf16[128,512]{1,0:T(8,128)(2,1)S(1)}, u32[]{:S(2)}, u32[]{:S(2)}) collective-permute-start(bf16[128,512]{1,0:T(8,128)(2,1)S(1)} %get-tuple-element.379), channel_id=1, source_target_pairs={{0,8},{2,10},{4,12},{6,14},{8,0},{10,2},{12,4},{14,6},{1,9},{3,11}... | collective-permute-start | bytes 393224 | tf_op jit(solution)/shard_map/ppermute | solution.py:776
  312.2 15.9 %collective-permute-start.37 = (bf16[128,512]{1,0:T(8,128)(2,1)S(1)}, bf16[128,512]{1,0:T(8,128)(2,1)S(1)}, u32[]{:S(2)}, u32[]{:S(2)}) collective-permute-start(bf16[128,512]{1,0:T(8,128)(2,1)S(1)} %get-tuple-element.377), channel_id=1, source_target_pairs={{0,4},{2,6},{4,0},{6,2},{8,12},{10,14},{12,8},{14,10},{1,5},{3,7},... | collective-permute-start | bytes 393224 | tf_op jit(solution)/shard_map/ppermute | solution.py:776
  322.5 24.5 %collective-permute-start.41 = (bf16[2,512,512]{2,1,0:T(8,128)(2,1)S(1)}, bf16[2,512,512]{2,1,0:T(8,128)(2,1)S(1)}, u32[]{:S(2)}, u32[]{:S(2)}) collective-permute-start(bf16[2,512,512]{2,1,0:T(8,128)(2,1)S(1)} %copy-done.51), channel_id=1, source_target_pairs={{0,2},{2,0},{4,6},{6,4},{8,10},{10,8},{12,14},{14,12},{1,3},{3,1},... | collective-permute-start | bytes 3145736 | tf_op jit(solution)/shard_map/ppermute | solution.py:776
  328.2 14.8 %collective-permute-start.39 = (bf16[128,1024]{1,0:T(8,128)(2,1)S(1)}, bf16[128,1024]{1,0:T(8,128)(2,1)S(1)}, u32[]{:S(2)}, u32[]{:S(2)}) collective-permute-start(bf16[128,1024]{1,0:T(8,128)(2,1)S(1)} %pad_maximum_fusion.3), channel_id=1, source_target_pairs={{0,4},{2,6},{4,0},{6,2},{8,12},{10,14},{12,8},{14,10},{1,5},{3,7},... | collective-permute-start | bytes 786440 | tf_op jit(solution)/shard_map/ppermute | solution.py:776
  330.3 14.1 %collective-permute-start.40 = (bf16[128,1024]{1,0:T(8,128)(2,1)S(1)}, bf16[128,1024]{1,0:T(8,128)(2,1)S(1)}, u32[]{:S(2)}, u32[]{:S(2)}) collective-permute-start(bf16[128,1024]{1,0:T(8,128)(2,1)S(1)} %pad_maximum_fusion.4), channel_id=1, source_target_pairs={{0,8},{2,10},{4,12},{6,14},{8,0},{10,2},{12,4},{14,6},{1,9},{3,11}... | collective-permute-start | bytes 786440 | tf_op jit(solution)/shard_map/ppermute | solution.py:776
  343.1 31.9 %collective-permute-start.44 = (bf16[2,512,512]{2,1,0:T(8,128)(2,1)S(1)}, bf16[2,512,512]{2,1,0:T(8,128)(2,1)S(1)}, u32[]{:S(2)}, u32[]{:S(2)}) collective-permute-start(bf16[2,512,512]{2,1,0:T(8,128)(2,1)S(1)} %add_convert_fusion.3), channel_id=1, source_target_pairs={{4,0},{6,2},{8,4},{10,6},{12,8},{14,10},{5,1},{7,3},{9,5},{11,7},{... | collective-permute-start | bytes 3145736 | tf_op jit(solution)/shard_map/ppermute | solution.py:781
  344.6 72.3 %collective-permute-start.46 = (bf16[64,1024]{1,0:T(8,128)(2,1)S(1)}, bf16[64,1024]{1,0:T(8,128)(2,1)S(1)}, u32[]{:S(2)}, u32[]{:S(2)}) collective-permute-start(bf16[64,1024]{1,0:T(8,128)(2,1)S(1)} %slice.202), channel_id=1, source_target_pairs={{0,16},{16,0},{1,17},{17,1},{2,18},{18,2},{3,19},{19,3},{4,20},{20... | collective-permute-start | bytes 393224 | tf_op jit(solution)/shard_map/ppermute | solution.py:776
  375.9 41.5 %collective-permute-start.49 = (bf16[512,512]{1,0:T(8,128)(2,1)S(1)}, bf16[512,512]{1,0:T(8,128)(2,1)}, u32[]{:S(2)}, u32[]{:S(2)}) collective-permute-start(bf16[512,512]{1,0:T(8,128)(2,1)S(1)} %get-tuple-element.373), channel_id=1, source_target_pairs={{0,8},{2,10},{4,12},{6,14},{8,0},{10,2},{12,4},{14,6},{1,9},{3,11}... | collective-permute-start | bytes 1572872 | tf_op jit(solution)/shard_map/ppermute | solution.py:776
  388.2 29.2 %collective-permute-start.48 = (bf16[512,512]{1,0:T(8,128)(2,1)}, bf16[512,512]{1,0:T(8,128)(2,1)}, u32[]{:S(2)}, u32[]{:S(2)}) collective-permute-start(bf16[512,512]{1,0:T(8,128)(2,1)} %get-tuple-element.374), channel_id=1, source_target_pairs={{0,4},{2,6},{4,0},{6,2},{8,12},{10,14},{12,8},{14,10},{1,5},{3,7},... | collective-permute-start | bytes 1572872 | tf_op jit(solution)/shard_map/ppermute | solution.py:776
  397.7 19.8 %collective-permute-start.47 = (bf16[2,512,512]{2,1,0:T(8,128)(2,1)}, bf16[2,512,512]{2,1,0:T(8,128)(2,1)S(1)}, u32[]{:S(2)}, u32[]{:S(2)}) collective-permute-start(bf16[2,512,512]{2,1,0:T(8,128)(2,1)} %get-tuple-element.295), channel_id=1, source_target_pairs={{0,2},{2,0},{4,6},{6,4},{8,10},{10,8},{12,14},{14,12},{1,3},{3,1},... | collective-permute-start | bytes 3145736 | tf_op jit(solution)/shard_map/ppermute | solution.py:776
  401.8 15.7 %collective-permute-start.45 = (bf16[2,512,512]{2,1,0:T(8,128)(2,1)}, bf16[2,512,512]{2,1,0:T(8,128)(2,1)S(1)}, u32[]{:S(2)}, u32[]{:S(2)}) collective-permute-start(bf16[2,512,512]{2,1,0:T(8,128)(2,1)} %get-tuple-element.292), channel_id=1, source_target_pairs={{0,2},{2,0},{4,6},{6,4},{8,10},{10,8},{12,14},{14,12},{1,3},{3,1},... | collective-permute-start | bytes 3145736 | tf_op jit(solution)/shard_map/ppermute | solution.py:776
  416.9 35.4 %collective-permute-start.50 = (bf16[2,512,512]{2,1,0:T(8,128)(2,1)}, bf16[2,512,512]{2,1,0:T(8,128)(2,1)S(1)}, u32[]{:S(2)}, u32[]{:S(2)}) collective-permute-start(bf16[2,512,512]{2,1,0:T(8,128)(2,1)} %get-tuple-element.311), channel_id=1, source_target_pairs={{0,2},{2,0},{4,6},{6,4},{8,10},{10,8},{12,14},{14,12},{1,3},{3,1},... | collective-permute-start | bytes 3145736 | tf_op jit(solution)/shard_map/ppermute | solution.py:776
  422.6 29.7 %collective-permute-start.51 = (bf16[2,512,512]{2,1,0:T(8,128)(2,1)}, bf16[2,512,512]{2,1,0:T(8,128)(2,1)S(1)}, u32[]{:S(2)}, u32[]{:S(2)}) collective-permute-start(bf16[2,512,512]{2,1,0:T(8,128)(2,1)} %get-tuple-element.299), channel_id=1, source_target_pairs={{0,4},{2,6},{4,0},{6,2},{8,12},{10,14},{12,8},{14,10},{1,5},{3,7},... | collective-permute-start | bytes 3145736 | tf_op jit(solution)/shard_map/ppermute | solution.py:776
  422.9 29.4 %collective-permute-start.52 = (bf16[2,512,512]{2,1,0:T(8,128)(2,1)}, bf16[2,512,512]{2,1,0:T(8,128)(2,1)S(1)}, u32[]{:S(2)}, u32[]{:S(2)}) collective-permute-start(bf16[2,512,512]{2,1,0:T(8,128)(2,1)} %get-tuple-element.312), channel_id=1, source_target_pairs={{0,8},{2,10},{4,12},{6,14},{8,0},{10,2},{12,4},{14,6},{1,9},{3,11}... | collective-permute-start | bytes 3145736 | tf_op jit(solution)/shard_map/ppermute | solution.py:776
  451.8 11.0 %collective-permute-start.53 = (bf16[512,1024]{1,0:T(8,128)(2,1)}, bf16[512,1024]{1,0:T(8,128)(2,1)S(1)}, u32[]{:S(2)}, u32[]{:S(2)}) collective-permute-start(bf16[512,1024]{1,0:T(8,128)(2,1)} %get-tuple-element.315), channel_id=1, source_target_pairs={{0,2},{2,0},{4,6},{6,4},{8,10},{10,8},{12,14},{14,12},{1,3},{3,1},... | collective-permute-start | bytes 3145736 | tf_op jit(solution)/shard_map/ppermute | solution.py:776
  451.8 26.3 %collective-permute-start.55 = (bf16[512,1024]{1,0:T(8,128)(2,1)}, bf16[512,1024]{1,0:T(8,128)(2,1)}, u32[]{:S(2)}, u32[]{:S(2)}) collective-permute-start(bf16[512,1024]{1,0:T(8,128)(2,1)} %get-tuple-element.306.own_ref), channel_id=1, source_target_pairs={{0,1},{1,0},{2,3},{3,2},{4,5},{5,4},{6,7},{7,6},{8,9},{9,8},{10,11... | collective-permute-start | bytes 3145736 | tf_op jit(solution)/shard_map/ppermute | solution.py:776
  463.3 11.8 %collective-permute-start.56 = (bf16[128,512]{1,0:T(8,128)(2,1)S(1)}, bf16[128,512]{1,0:T(8,128)(2,1)S(1)}, u32[]{:S(2)}, u32[]{:S(2)}) collective-permute-start(bf16[128,512]{1,0:T(8,128)(2,1)S(1)} %get-tuple-element.371), channel_id=1, source_target_pairs={{0,8},{2,10},{4,12},{6,14},{8,0},{10,2},{12,4},{14,6},{1,9},{3,11}... | collective-permute-start | bytes 393224 | tf_op jit(solution)/shard_map/ppermute | solution.py:776
  467.5 35.4 %collective-permute-start.62 = (bf16[512,1024]{1,0:T(8,128)(2,1)S(1)}, bf16[512,1024]{1,0:T(8,128)(2,1)}, u32[]{:S(2)}, u32[]{:S(2)}) collective-permute-start(bf16[512,1024]{1,0:T(8,128)(2,1)S(1)} %copy-done.50), channel_id=1, source_target_pairs={{0,1},{1,0},{2,3},{3,2},{4,5},{5,4},{6,7},{7,6},{8,9},{9,8},{10,11... | collective-permute-start | bytes 3145736 | tf_op jit(solution)/shard_map/ppermute | solution.py:776
  488.9 12.0 %collective-permute-start.65 = (bf16[64,1024]{1,0:T(8,128)(2,1)S(1)}, bf16[64,1024]{1,0:T(8,128)(2,1)S(1)}, u32[]{:S(2)}, u32[]{:S(2)}) collective-permute-start(bf16[64,1024]{1,0:T(8,128)(2,1)S(1)} %slice.220), channel_id=1, source_target_pairs={{0,16},{16,0},{1,17},{17,1},{2,18},{18,2},{3,19},{19,3},{4,20},{20... | collective-permute-start | bytes 393224 | tf_op jit(solution)/shard_map/ppermute | solution.py:776
  494.2 13.4 %collective-permute-start.66 = (f32[1,256]{1,0:T(1,128)S(1)}, f32[1,256]{1,0:T(1,128)S(1)}, u32[]{:S(2)}, u32[]{:S(2)}) collective-permute-start(f32[1,256]{1,0:T(1,128)S(1)} %pad_maximum_fusion.10), channel_id=1, source_target_pairs={{0,1},{1,0},{2,3},{3,2},{4,5},{5,4},{6,7},{7,6},{8,9},{9,8},{10,11... | collective-permute-start | bytes 3080 | tf_op jit(solution)/shard_map/ppermute | solution.py:776
  (87 other events, 757.1 us)
Sparse Core Ops, SparseCore 0:
  10.9 69.4 all-gather.2
  90.9 68.7 all-gather.4
  235.5 127.1 reduce-scatter.1

commit v7 on v6

--- a/solution.py
+++ b/solution.py
@@ -396,7 +396,7 @@
         keep = {len(ins): 0}
         ins.append((whole, None, None))
     if last:
-        outs = [(shaped((2 * rows, heads * 256), F32), (rows, 256), lambda h, i: (half, h))]
+        outs = [(shaped((rows, heads * 256), F32), (rows, 256), part)]
     else:
         outs = [(shaped((heads * 128, 2 * rows), F32), (128, 2 * rows), lambda h, i: (h, 0))]
     outs += [(shaped((2, rows, heads * 128), BF), (2, rows, 128), kv_map) for _ in pieces]
@@ -412,6 +412,108 @@
                    scalars=scalars, us=us, keep=keep)
     n = len(slots)
     return results[0], dict(zip(slots, results[1 : 1 + n])), dict(zip(halos, results[1 + n :]))
+
+
+def prompt_back_kernel(plan, idx_ref, qa_ref, qb_ref, doa_ref, dob_ref, lse_ref, lse_b_ref, delta_ref, delta_b_ref, *refs):
+    slots, last = plan["slots"], plan["ctx"] - 1
+    refs = list(refs)
+    slot_refs = take_slots(refs, plan["pairs"])
+    prior = {s: refs.pop(0) for s in plan["prior"]}
+    dqa_ref, dqb_ref = refs.pop(0), refs.pop(0)
+    outs = [refs.pop(0) for _ in slots]
+    qs, dos, lses, deltas, dq, dkv = refs
+    me = idx_ref[0]
+    half = qa_ref.shape[0]
+    rows = 2 * half
+    for part, (q_ref, do_ref) in enumerate(((qa_ref, doa_ref), (qb_ref, dob_ref))):
+        for g in range(2):
+            cols = slice(g * HEAD_SIZE, (g + 1) * HEAD_SIZE)
+            at = slice(part * rows + g * half, part * rows + (g + 1) * half)
+            qs[at, :] = q_ref[:, cols]
+            dos[at, :] = do_ref[:, cols]
+            for total, own, got in ((lses, lse_ref, lse_b_ref), (deltas, delta_ref, delta_b_ref)):
+                total[:, at] = (got if part else own)[0, g : g + 1, :half]
+    dq[...] = jnp.zeros_like(dq)
+    lane = lax.broadcasted_iota(jnp.int32, (1, rows), 1)
+    lane = jnp.where(lane >= half, lane - half, lane)
+    key = lax.broadcasted_iota(jnp.int32, (rows, 1), 0)
+
+    def block(kv_ref, part, mask=None):
+        at = slice(part * rows, (part + 1) * rows)
+        keys = kv_ref[0][...]
+        scores = mm(keys, qs[at, :], NT)
+        dp = mm(kv_ref[1][...], dos[at, :], NT)
+        scores = scores - lses[:, at]
+        if mask is not None:
+            scores = jnp.where(mask, scores, MASKED)
+        probs = jnp.exp2(scores)
+        ds = (probs * (dp - deltas[:, at])).astype(BF)
+        dq[:, at] += mm(keys.T, ds)
+        dkv[0] += mm(ds, qs[at, :])
+        dkv[1] += mm(probs.astype(BF), dos[at, :])
+
+    def top(s):
+        return 1 << (s.bit_length() - 1)
+
+    for s, kv_ref, out_ref in zip(slots, slot_refs, outs):
+        dkv[...] = jnp.zeros_like(dkv)
+        if s == 0:
+            block(kv_ref, 0, key <= lane)
+        else:
+
+            @pl.when(jnp.bitwise_and(me, top(s)) != 0)
+            def _(kv_ref=kv_ref):
+                block(kv_ref, 0)
+
+        if s == last:
+            block(kv_ref, 1, key <= lane + half)
+        else:
+
+            @pl.when(jnp.bitwise_and(me, top(s ^ last)) == 0)
+            def _(kv_ref=kv_ref):
+                block(kv_ref, 1)
+
+        for which, factor in ((0, LN2), (1, 1.0)):
+            total = dkv[which] * factor
+            if s in prior:
+                total = total + prior[s][which].astype(F32)
+            out_ref[which] = total.astype(BF)
+    for part, out_ref in enumerate((dqa_ref, dqb_ref)):
+        for g in range(2):
+            at = slice(part * rows + g * half, part * rows + (g + 1) * half)
+            cols = slice(g * HEAD_SIZE, (g + 1) * HEAD_SIZE)
+            out_ref[:, cols] = (dq[:, at].T * SCALE).astype(out_ref.dtype)
+
+
+def prompt_backward(scalars, ctx, own, got, slots, prior):
+    rows, heads = own[0].shape[0], own[0].shape[1] // 256
+    half = rows // 2
+    plan = dict(slots=list(slots), prior=list(prior), ctx=ctx,
+                pairs=[isinstance(kv, tuple) for kv in slots.values()])
+    part = lambda h, i: (0, h)
+    stat = lambda h, i: (h, 0, 0)
+    kv_map = lambda h, i: (0, 0, h)
+    ins = []
+    for mine, other in zip(own[:2], got[:2]):
+        ins += [(mine, (half, 256), part), (other, (half, 256), part)]
+    for mine, other in zip(own[2:], got[2:]):
+        ins += [(mine, (1, 8, rows), stat), (other, (1, 8, half), stat)]
+    for kv in slots.values():
+        ins += slot_inputs(kv, rows)
+    ins += [(grad, (2, rows, 128), kv_map) for grad in prior.values()]
+    outs = [(shaped((half, heads * 256), kind), (half, 256), part) for kind in (F32, BF)]
+    outs += [(shaped((2, rows, heads * 128), BF), (2, rows, 128), kv_map) for _ in slots]
+    scratch = [
+        pltpu.VMEM((2 * rows, 128), BF),
+        pltpu.VMEM((2 * rows, 128), BF),
+        pltpu.VMEM((1, 2 * rows), F32),
+        pltpu.VMEM((1, 2 * rows), F32),
+        pltpu.VMEM((128, 2 * rows), F32),
+        pltpu.VMEM((2, rows, 128), F32),
+    ]
+    results = call(functools.partial(prompt_back_kernel, plan), "prompt_back", (heads,), ins, outs, scratch,
+                   scalars=scalars, us=16)
+    return results[0], results[1], dict(zip(slots, results[2:]))
 
 
 def ffn_kernel(x_ref, own_ref, got_ref, gain_ref, dy_ref, gu_ref, down_ref, *refs):
@@ -628,8 +730,22 @@
     return call(weight_halves_kernel, "weight_halves", (2,), ins, [(half, half.shape, once)] * 2)
 
 
-def q_back_kernel(heads, dq_ref, lin_ref, gain_ref, cos_ref, sin_ref, w_ref, *refs):
-    d_ref, part_ref, gains_ref = refs[-3:]
+def q_back_kernel(heads, dqa_ref, dqb_ref, dqc_ref, lin_ref, gain_ref, cos_ref, sin_ref, w_ref, *refs):
+    d_ref, part_ref, gains_ref, dq_ref = refs[-4:]
+    step = pl.program_id(0)
+
+    @pl.when(step == 0)
+    def _():
+        dq_ref[...] = dqa_ref[...]
+
+    @pl.when(step == 1)
+    def _():
+        dq_ref[...] = dqb_ref[...].astype(F32)
+
+    @pl.when(step > 1)
+    def _():
+        dq_ref[...] = dqc_ref[...]
+
     cos, sin = cos_ref[...], sin_ref[...]
     total = jnp.zeros(cos.shape, F32)
     for h in range(heads):
@@ -641,13 +757,14 @@
     add_up(gains_ref, total)
 
 
-def q_back(dq, lin, gain, cos, sin, w):
-    rows, cols = dq.shape
+def q_back(dq_a, dq_b, dq_c, lin, gain, cos, sin, w):
+    rows, cols = lin.shape
     model = w.shape[0]
-    size, steps = row_blocks(rows)
+    size = rows // 4
     here, once = lambda f: (f, 0), lambda f: (0, 0)
     ins = [
-        (dq, (size, cols), here), (lin, (size, cols), here), (gain, (1, HEAD_SIZE), once),
+        (dq_a, (size, cols), once), (dq_b, (size, cols), once), (dq_c, (size, cols), lambda f: (jnp.maximum(f - 2, 0), 0)),
+        (lin, (size, cols), here), (gain, (1, HEAD_SIZE), once),
         (cos, (size, HEAD_SIZE), here), (sin, (size, HEAD_SIZE), here), (w, (model, cols), once),
     ]
     outs = [
@@ -656,7 +773,7 @@
         (shaped((1, HEAD_SIZE), F32), (1, HEAD_SIZE), once),
     ]
     kernel = functools.partial(q_back_kernel, cols // HEAD_SIZE)
-    return call(kernel, "q_back", (steps,), ins, outs)
+    return call(kernel, "q_back", (4,), ins, outs, [pltpu.VMEM((size, cols), F32)])
 
 
 def kv_back_kernel(heads, n_keys, n_values, lin_ref, gain_ref, cos_ref, sin_ref, w_ref, slots_ref, q_part_ref, *refs):
@@ -865,23 +982,12 @@
                 size = total.shape[0] // 2
                 total = add_low(total[:size], swap(total[size:], axis, bit))
             return (total,)
-        size, cut = total.shape[0] // 4, total.shape[1] // 2
-        own, by_x, by_y, far = (total[i * size : (i + 1) * size] for i in range(4))
-        left, right = swap(far[:, :cut], "ctx", 2), swap(far[:, cut:], "ctx", 4)
-        return own, by_x, by_y, left, right
-
-    def scatter_more(stage, late):
-        if ctx_size != 8:
-            return stage
-        own, by_x, by_y, left, right = stage
-        left, right = after(left, late), after(right, late)
-        cut = left.shape[1]
-        by_x = jnp.concatenate([by_x[:, :cut], add_low(by_x[:, cut:], right)], axis=1)
-        by_y = jnp.concatenate([add_low(by_y[:, :cut], left), by_y[:, cut:]], axis=1)
-        return lax.optimization_barrier((own, by_x, by_y))[0], swap(by_x, "ctx", 2), swap(by_y, "ctx", 4)
+        size = total.shape[0] // 4
+        by_x, by_y, far = (total[i * size : (i + 1) * size] for i in (1, 2, 3))
+        return total, swap(by_x, "ctx", 2), swap(by_y, "ctx", 4), swap(far, "ctx", 6)
 
     def scatter_sum(stage, late):
-        total = stage[0].astype(F32)
+        total = stage[0].astype(F32)[: stage[-1].shape[0]]
         for piece in stage[1:]:
             total = total + after(piece, late).astype(F32)
         total, size = total.astype(BF), total.shape[0] // 2
@@ -1035,53 +1141,58 @@
         0, back_p, back_got_p, resid_p, after(gain_two, ffn_grads), cotangent, w_od, o_cols, attended
     )
 
-    of_rows = [(d_att_p, lse_p, delta_p)]
-
-    def back_rows(half, deps, slots, halos, carry, prior=None, whole=None, last=False):
-        do, lse, delta = of_rows[half]
-        return attention_backward(
-            half, after(scalars, *deps), (q_p, q_c)[half], do, lse, delta, low_row, slots, halos, carry, prior, last, whole
-        )
-
-    dq_p, prior, _ = back_rows(0, (d_att_p,), pick(slots, far), {}, None)
+    def mirror(value):
+        return lax.ppermute(value, "ctx", [(i, i ^ (ctx_size - 1)) for i in range(ctx_size)])
+
+    half = rows // 2
+    q_b, lse_b = mirror(after(q_p, part_c)[half:]), mirror(after(lse_p, part_c)[:, :, half:])
+    do_b, delta_b = mirror(d_att_p[half:]), mirror(delta_p[:, :, half:])
     d_resid_c, d_mixed, d_att_c, delta_c, d_two_c = mixed_back(
-        1, back_c, back_got_c, resid_c, after(gain_two, dq_p), cotangent, w_od, o_cols, attended, d_mixed
-    )
-    of_rows.append((d_att_c, lse_c, delta_c))
+        1, back_c, back_got_c, resid_c, after(gain_two, d_att_p), cotangent, w_od, o_cols, attended, d_mixed
+    )
     out_low, out_high = slot_weight_grad(order, part, d_mixed, attended)
     out_p, out_c = after(out_p, out_low), after(out_c, out_low)
     out_got_p, out_got_c = swap(out_p, "tensor", 1), swap(out_c, "tensor", 1)
-    dq_c, _, g_halo = back_rows(1, (out_low,), {}, halos, None)
+
+    def back_c_rows(deps, slots, halos, carry, prior=None, last=False):
+        return attention_backward(
+            1, after(scalars, *deps), q_c, d_att_c, lse_c, delta_c, low_row, slots, halos, carry, prior, last
+        )
+
+    dq_c, from_c, g_halo = back_c_rows((out_low,), pick(slots, far), halos, None)
     out_grad = scatter_rows(out_low, out_high, dq_c)
     if ctx_size == 8:
         near_one = swap(g_halo[1], "ctx", 1)
-    dq_c, g, _ = back_rows(1, (dq_c, out_grad[0]), pick(slots, far), {}, dq_c, prior)
-    out_grad = scatter_more(out_grad, dq_c)
+    dq_a, dq_b, from_p = prompt_backward(
+        after(scalars, dq_c, out_grad[0]), ctx_size, (q_p, d_att_p, lse_p, delta_p),
+        (q_b, do_b, lse_b, delta_b), slots, from_c,
+    )
+    dq_b = mirror(dq_b)
+    g = pick(from_p, far)
     zero = jnp.zeros((), BF)
     ready = ()
     if ctx_size == 8:
         got7 = swap(g[7], "ctx", 1)
-        near_one = after(near_one, dq_c)
+        near_one = after(near_one, dq_a)
         two_back = add_low(g_halo[2], jnp.where(odd, near_one, zero))
         halo_two = shift(two_back, -2)
         halo_near = jnp.where(odd, zero, near_one)
         ready = (two_back, halo_near)
-    dq, prior, _ = back_rows(0, (dq_c, out_grad[0], *ready), pick(slots, near + middle), {}, dq_p, None, None, True)
+    dq_c, more, _ = back_c_rows((dq_a, out_grad[0], *ready), pick(slots, middle), {}, dq_c, from_p)
+    g.update(more)
+    out_grad = scatter_sum(out_grad, dq_c)
     if ctx_size == 8:
-        g6 = add_low(g[6], after(got7, dq))
+        g6 = add_low(g[6], after(got7, dq_c))
         far_k, far_v = swap(g6[0], "ctx", 2), swap(g6[1], "ctx", 4)
+        got3, got5 = swap(g[3], "ctx", 1), swap(g[5], "ctx", 1)
         ready = (g6,)
-    out_grad = scatter_sum(out_grad, dq)
-    dq_c, more, _ = back_rows(1, (dq, out_grad[0], *ready), pick(slots, middle), {}, dq_c, prior)
-    g.update(more)
-    if ctx_size == 8:
-        got3, got5 = swap(g[3], "ctx", 1), swap(g[5], "ctx", 1)
-        ready = (halo_two,)
-    dq, more, _ = back_rows(1, (dq_c, out_got_p, out_got_c, *ready), pick(slots, near), {}, dq_c, prior, dq, True)
+    dq_c, more, _ = back_c_rows(
+        (dq_c, out_got_p, out_got_c, out_grad[0], dq_b, *ready), pick(slots, near), {}, dq_c, from_p, True
+    )
     g.update(more)
     if ctx_size == 8:
         got1 = swap(g[1], "ctx", 1)
-        far_k, far_v, got3, got5 = (after(v, dq, out_grad[1], ffn_share) for v in (far_k, far_v, got3, got5))
+        far_k, far_v, got3, got5 = (after(v, dq_c, halo_two, ffn_share) for v in (far_k, far_v, got3, got5))
         to_x, to_y = merge(g[2], got3, g[4], got5, far_k, far_v)
         ready = (to_x,)
         keys_p = values_p = [g[0], got1, swap(to_x, "ctx", 2), swap(to_y, "ctx", 4)]
@@ -1094,7 +1205,7 @@
         keys_p = values_p = [both[0]]
         keys_c = values_c = [g_halo[0]] + [shift(g_halo[d], -d) for d in range(1, n_halo)]
 
-    d_q, q_part, q_heads = q_back(dq, q_lin, after(gain_q, dq, *ready), cos, sin, w_q)
+    d_q, q_part, q_heads = q_back(dq_a, dq_b, dq_c, q_lin, after(gain_q, dq_c, *ready), cos, sin, w_q)
     d_kv, into_c, k_heads_c = kv_back(
         1, keys_c, values_c, k_lin_c, after(gain_k, q_part), cos, sin, w_kv, to_slots, q_part
     )
@@ -1106,7 +1217,6 @@
     into_got_p = swap(into_p, "tensor", 1)
     q_grad = scatter_rows(q_low, q_high, into_p)
     kv_high, kv_low = weight_halves(normed, after(d_kv, q_grad[0]))
-    q_grad = scatter_more(q_grad, kv_low)
     heads = jnp.concatenate([q_heads, k_heads_c + k_heads_p], axis=1)
     heads_got = swap(heads, "tensor", 1)
     grad_tokens, d_one_c = tokens_back(1, into_c, into_got_c, tokens, after(gain_one, kv_low, q_grad[0]), d_resid_c)
@@ -1114,7 +1224,6 @@
     q_grad = scatter_sum(q_grad, gate_share)
     kv_grad = scatter_rows(kv_low, kv_high, gate_share)
     layer_out = add_layer(0, after(resid_p, kv_grad[0], q_grad[0]), out_p, out_got_p)
-    kv_grad = scatter_more(kv_grad, layer_out)
     layer_out = add_layer(1, after(resid_c, kv_grad[0]), out_c, out_got_c, layer_out)
     q_share = add_low(q_grad[0][:wide], after(q_grad[1], layer_out)).astype(F32)
     kv_grad = scatter_sum(kv_grad, layer_out)

time: 545 us -> 588 us (1.079)
  waiting for transfers between devices: 72.7 us -> 123 us
  starting transfers between devices: 112 us -> 82.3 us
  Pallas kernels: 297 us -> 314 us
    ppermute x70 -> x67, starting transfers between devices: 106 us -> 67.1 us  [swap(): return lax.ppermute(value, axis, [(i, i ^ bit) for i in range(size)])]
    ppermute x0 -> x5, waiting for transfers between devices: none -> 31.1 us  [mirror(): lax.ppermute(value, 'ctx', [(i, i ^ ctx_size - 1) for i in range(ctx_size)])]
    ppermute x70 -> x67, waiting for transfers between devices: 58.5 us -> 78.4 us  [swap(): return lax.ppermute(value, axis, [(i, i ^ bit) for i in range(size)])]
    pallas_call x34 -> x32, Pallas kernels: 297 us -> 314 us  [call(): pl.pallas_call(kernel, grid_spec=pltpu.PrefetchScalarGridSpec(num_scalar_...]
    ppermute x0 -> x5, starting transfers between devices: none -> 10.3 us  [mirror(): lax.ppermute(value, 'ctx', [(i, i ^ ctx_size - 1) for i in range(ctx_size)])]
  transfers between devices with their start and end apart: 75 -> 77, of which waited for: 24 -> 22; matrix products, arithmetic and copies ran while one was open for 5% -> 5% of each run, Pallas kernels for 55% -> 54%
where the time goes in v7:
time: 588 us; the launch traced here: 579 us
  Pallas kernels  314 us (53%)
  waiting for transfers between devices  123 us (21%)
  starting transfers between devices  82.3 us (14%)
  local copies, waits for them, and re-layouts  22.8 us (4%)
  other arithmetic  16.8 us (3%)
  between operations  15 us (3%)
    pallas_call x32, Pallas kernels, call(): pl.pallas_call(kernel, grid_spec=pltpu.PrefetchScalarGridSpec(num_scalar_...  314 us
    ppermute x67, waiting for transfers between devices, swap(): return lax.ppermute(value, axis, [(i, i ^ bit) for i in range(size)])  78.4 us
    ppermute x67, starting transfers between devices, swap(): return lax.ppermute(value, axis, [(i, i ^ bit) for i in range(size)])  67.1 us
    ppermute x5, waiting for transfers between devices, mirror(): lax.ppermute(value, 'ctx', [(i, i ^ ctx_size - 1) for i in range(ctx_size)])  31.1 us
    ppermute x2, waiting for transfers between devices, shift(): lax.ppermute(value, 'ctx', [(i, i + by) for i in range(size) if 0 <= i +...  13.4 us
  transfers between devices with their start and end apart: 77, of which 22 were waited for; matrix products, arithmetic and copies ran while one was open for 5% of the time, Pallas kernels for 54%

profile of v7, /device:TPU:0, one launch (start us, length us, event | category | flops | bytes accessed | tf_op | source)
XLA Modules:
  0.0 578.7 jit_solution(12177437600743353624)
XLA Ops:
  10.8 3.7 collective-permute-start
  28.9 4.4 collective-permute-done.2.refs_3_
  37.3 3.7 fusion.5.x_ref
  47.5 5.2 collective-permute-done.7.refs_1_
  52.6 6.0 %collective-permute-done.10.refs_3_ = bf16[128,1024]{1,0:T(8,128)(2,1)S(1)} collective-permute-done((bf16[128,1024]{1,0:T(8,128)(2,1)S(1)}, bf16[128,1024]{1,0:T(8,128)(2,1)S(1)}, u32[]{:S(2)}, u32[]{:S(2)}) %collective-permute-start.10) | collective-permute-done | bytes 262176 | tf_op jit(solution)/shard_map/ppermute | solution.py:893
  59.5 5.6 keys_values.2
  68.7 5.7 keys_values.3
  75.2 7.0 %queries.2 = (bf16[512,1024]{1,0:T(8,128)(2,1)}, f32[1024,1024]{1,0:T(8,128)}, bf16[1024,1024]{1,0:T(8,128)(2,1)}) custom-call(bf16[1024,1024]{1,0:T(8,128)(2,1)} %get-tuple-element.194.normed_ref.left_ref, f32[1,128]{1,0:T(1,128)} %reshape.121.hgain_ref.gain_ref, f32[1024,128]{1,0:T(8,128)} %get-tuple-element.369.cos_ref, ...), custom_call_target="tpu_custom_call" | custom-call | tf_op jit(solution)/shard_map/queries/pallas_call | solution.py:46
  82.2 6.6 %queries.3 = (bf16[512,1024]{1,0:T(8,128)(2,1)}, f32[1024,1024]{1,0:T(8,128)}) custom-call(bf16[1024,1024]{1,0:T(8,128)(2,1)} %get-tuple-element.194.normed_ref.left_ref, f32[1,128]{1,0:T(1,128)} %reshape.121.hgain_ref.gain_ref, f32[1024,128]{1,0:T(8,128)} %get-tuple-element.369.cos_ref, ...), custom_call_target="tpu_custom_call", output_to_operand_aliasing={{1}: (5, {})} | custom-call | tf_op jit(solution)/shard_map/queries/pallas_call | solution.py:46
  93.7 3.4 collective-permute-start.29
  99.7 10.9 %attend.3 = (f32[512,1024]{1,0:T(8,128)}, f32[512,1024]{1,0:T(8,128)}) custom-call(s32[2]{0:T(128)} %pad_add_fusion.1.idx_ref, s32[512,128]{1,0:T(8,128)} %broadcast_in_dim.73.lo_ref, bf16[512,1024]{1,0:T(8,128)(2,1)} %get-tuple-element.200.refs_0_.q_ref, bf16[2,512,512]{2,1,0:T(8,128)(2,1)} %get-tuple-element.190.refs_1_.refs_0_, ...), custom_call_target="tpu_custom_call" | custom-call | tf_op jit(solution)/shard_map/attend/pallas_call | solution.py:46
  113.7 8.8 %attend.4 = (bf16[1024,1024]{1,0:T(8,128)(2,1)}, f32[4,8,512]{2,1,0:T(8,128)}) custom-call(s32[2]{0:T(128)} %pad_add_fusion.1.idx_ref, s32[512,128]{1,0:T(8,128)} %broadcast_in_dim.73.lo_ref, bf16[512,1024]{1,0:T(8,128)(2,1)} %get-tuple-element.249.refs_0_.qa_ref, bf16[2,512,512]{2,1,0:T(8,128)(2,1)} %get-tuple-element.190.refs_1_.refs_0_, ...), custom_call_target="tpu_custom_call" | custom-call | tf_op jit(solution)/shard_map/attend/pallas_call | solution.py:46
  122.5 3.9 out_projection.2.own_ref
  126.4 13.4 %collective-permute-done.29.refs_9_.refs_5_ = bf16[2,512,512]{2,1,0:T(8,128)(2,1)S(1)} collective-permute-done((bf16[2,512,512]{2,1,0:T(8,128)(2,1)}, bf16[2,512,512]{2,1,0:T(8,128)(2,1)S(1)}, u32[]{:S(2)}, u32[]{:S(2)}) %collective-permute-start.29) | collective-permute-done | bytes 1048608 | tf_op jit(solution)/shard_map/ppermute | solution.py:898
  145.2 19.5 %attend.5 = (bf16[1024,1024]{1,0:T(8,128)(2,1)}, f32[4,8,512]{2,1,0:T(8,128)}) custom-call(s32[2]{0:T(128)} %pad_add_fusion.1.idx_ref, s32[512,128]{1,0:T(8,128)} %broadcast_in_dim.73.lo_ref, bf16[512,1024]{1,0:T(8,128)(2,1)} %get-tuple-element.200.refs_0_.q_ref, bf16[2,512,512]{2,1,0:T(8,128)(2,1)} %copy-done.2, ...), custom_call_target="tpu_custom_call", output_to_operand_aliasing={{0}: (15, {})} | custom-call | tf_op jit(solution)/shard_map/attend/pallas_call | solution.py:46
  164.7 3.9 out_projection.3.own_ref
  171.2 6.7 %collective-permute-done.32.got_ref = bf16[512,1024]{1,0:T(8,128)(2,1)} collective-permute-done((bf16[512,1024]{1,0:T(8,128)(2,1)S(1)}, bf16[512,1024]{1,0:T(8,128)(2,1)}, u32[]{:S(2)}, u32[]{:S(2)}) %collective-permute-start.32) | collective-permute-done | bytes 1048608 | tf_op jit(solution)/shard_map/ppermute | solution.py:893
  177.9 18.3 %feed_forward.2 = (f32[512,1024]{1,0:T(8,128)}, bf16[1024,1024]{1,0:T(8,128)(2,1)}, bf16[1024,1536]{1,0:T(8,128)(2,1)}, bf16[1024,3072]{1,0:T(8,128)(2,1)}, bf16...) custom-call(bf16[1024,1024]{1,0:T(8,128)(2,1)} %x_ref.7, bf16[512,1024]{1,0:T(8,128)(2,1)} %out_projection.2.own_ref, ...), custom_call_target="tpu_custom_call" | custom-call | tf_op jit(solution)/shard_map/feed_forward/pallas_call | solution.py:46
  196.3 4.0 collective-permute-done.31.got_ref
  201.3 18.7 %feed_forward.3 = (f32[512,1024]{1,0:T(8,128)}, bf16[1024,1024]{1,0:T(8,128)(2,1)}, bf16[1024,1536]{1,0:T(8,128)(2,1)}, bf16[1024,3072]{1,0:T(8,128)(2,1)}, bf16...) custom-call(bf16[1024,1024]{1,0:T(8,128)(2,1)} %x_ref.7, ...), custom_call_target="tpu_custom_call", output_to_operand_aliasing={{1}: (7, {}), {2}: (8, {}), {3}: (9, {})} | custom-call | tf_op jit(solution)/shard_map/feed_forward/pallas_call | solution.py:46
  220.1 3.5 collective-permute-start.38
  224.5 10.7 %weight_grad.2.refs_0_ = bf16[1024,4608]{1,0:T(8,128)(2,1)} custom-call(bf16[1024,1024]{1,0:T(8,128)(2,1)} %get-tuple-element.233.left_ref, bf16[1024,3072]{1,0:T(8,128)(2,1)} %get-tuple-element.234.right_ref), custom_call_target="tpu_custom_call" | custom-call | tf_op jit(solution)/shard_map/weight_grad/pallas_call | solution.py:46
  235.2 7.1 %weight_grad.3 = bf16[1024,4608]{1,0:T(8,128)(2,1)} custom-call(bf16[1024,1024]{1,0:T(8,128)(2,1)} %dy_ref.7, bf16[1024,1536]{1,0:T(8,128)(2,1)} %get-tuple-element.232.right_ref, bf16[1024,4608]{1,0:T(8,128)(2,1)} %weight_grad.2.refs_0_), custom_call_target="tpu_custom_call", output_to_operand_aliasing={{}: (2, {})} | custom-call | tf_op jit(solution)/shard_map/weight_grad/pallas_call | solution.py:46
  243.4 7.2 %mixed_back.2 = (f32[512,1024]{1,0:T(8,128)}, bf16[1024,1024]{1,0:T(8,128)(2,1)}, bf16[512,1024]{1,0:T(8,128)(2,1)}, f32[4,8,512]{2,1,0:T(8,128)}, f32[1,1024]{1,0:T(1,128)}) custom-call(bf16[512,1024]{1,0:T(8,128)(2,1)} %get-tuple-element.223.own_ref, bf16[512,1024]{1,0:T(8,128)(2,1)} %copy-done.15, f32[512,1024]{1,0:T(8,128)} %get-tuple-element.321.resid_ref, ...), custom_call_target="tpu_custom_call" | custom-call | tf_op jit(solution)/shard_map/mixed_back/pallas_call | solution.py:46
  252.6 7.8 %mixed_back.3 = (f32[512,1024]{1,0:T(8,128)}, bf16[1024,1024]{1,0:T(8,128)(2,1)}, bf16[512,1024]{1,0:T(8,128)(2,1)}, f32[4,8,512]{2,1,0:T(8,128)}, f32[1,1024]{1,0:T(1,128)}) custom-call(bf16[512,1024]{1,0:T(8,128)(2,1)} %get-tuple-element.230.own_ref, bf16[512,1024]{1,0:T(8,128)(2,1)} %copy-done.17, ...), custom_call_target="tpu_custom_call", output_to_operand_aliasing={{1}: (7, {})} | custom-call | tf_op jit(solution)/shard_map/mixed_back/pallas_call | solution.py:46
  260.5 6.4 %slot_weight_grad.1 = (bf16[512,1024]{1,0:T(8,128)(2,1)}, bf16[512,1024]{1,0:T(8,128)(2,1)}) custom-call(s32[1]{0:T(128)} %bitcast.10.part_ref, bf16[1024,1024]{1,0:T(8,128)(2,1)} %get-tuple-element.239.left_ref, bf16[1024,1024]{1,0:T(8,128)(2,1)} %get-tuple-element.218.att_ref.right_ref), custom_call_target="tpu_custom_call" | custom-call | tf_op jit(solution)/shard_map/slot_weight_grad/pallas_call | solution.py:46
  270.2 21.6 %attend_back.3 = (f32[512,1024]{1,0:T(8,128)}, bf16[2,512,512]{2,1,0:T(8,128)(2,1)}, bf16[2,512,512]{2,1,0:T(8,128)(2,1)}, bf16[2,512,512]{2,1,0:T(8,128)(2,1)},...) custom-call(s32[2]{0:T(128)} %pad_add_fusion.1.idx_ref, bf16[512,1024]{1,0:T(8,128)(2,1)} %get-tuple-element.200.refs_0_.q_ref, ...), custom_call_target="tpu_custom_call" | custom-call | flops 102000001024 | tf_op jit(solution)/shard_map/attend_back/pallas_call | solution.py:46
  291.9 6.6 %collective-permute-start.41 = (bf16[2,512,512]{2,1,0:T(8,128)(2,1)}, bf16[2,512,512]{2,1,0:T(8,128)(2,1)S(1)}, u32[]{:S(2)}, u32[]{:S(2)}) collective-permute-start(bf16[2,512,512]{2,1,0:T(8,128)(2,1)} %get-tuple-element.258), channel_id=1, source_target_pairs={{0,2},{2,0},{4,6},{6,4},{8,10},{10,8},{12,14},{14,12},{1,3},{3,1},... | collective-permute-start | bytes 3145736 | tf_op jit(solution)/shard_map/ppermute | solution.py:893
  301.9 39.3 %prompt_back.1 = (f32[256,1024]{1,0:T(8,128)}, bf16[256,1024]{1,0:T(8,128)(2,1)}, bf16[2,512,512]{2,1,0:T(8,128)(2,1)}, bf16[2,512,512]{2,1,0:T(8,128)(2,1)}, bf...) custom-call(s32[2]{0:T(128)} %pad_add_fusion.1.idx_ref, ...), custom_call_target="tpu_custom_call" | custom-call | flops 48000000000 | tf_op jit(solution)/shard_map/prompt_back/pallas_call | solution.py:46
  341.3 8.7 %collective-permute-start.44 = (bf16[128,1024]{1,0:T(8,128)(2,1)S(1)}, bf16[128,1024]{1,0:T(8,128)(2,1)S(1)}, u32[]{:S(2)}, u32[]{:S(2)}) collective-permute-start(bf16[128,1024]{1,0:T(8,128)(2,1)S(1)} %get-tuple-element.355), channel_id=1, source_target_pairs={{0,4},{2,6},{4,0},{6,2},{8,12},{10,14},{12,8},{14,10},{1,5},{3,7},... | collective-permute-start | bytes 786440 | tf_op jit(solution)/shard_map/ppermute | solution.py:893
  351.4 8.8 %collective-permute-done.44 = bf16[128,1024]{1,0:T(8,128)(2,1)S(1)} collective-permute-done((bf16[128,1024]{1,0:T(8,128)(2,1)S(1)}, bf16[128,1024]{1,0:T(8,128)(2,1)S(1)}, u32[]{:S(2)}, u32[]{:S(2)}) %collective-permute-start.44) | collective-permute-done | bytes 262176 | tf_op jit(solution)/shard_map/ppermute | solution.py:893
  360.2 25.8 %attend_back.4 = (f32[512,1024]{1,0:T(8,128)}, bf16[2,512,512]{2,1,0:T(8,128)(2,1)}, bf16[2,512,512]{2,1,0:T(8,128)(2,1)}, bf16[2,512,512]{2,1,0:T(8,128)(2,1)}, bf16[2,512,512]{2,1,0:T(8,128)(2,1)}) custom-call(s32[2]{0:T(128)} %pad_add_fusion.1.idx_ref, bf16[512,1024]{1,0:T(8,128)(2,1)} %get-tuple-element.200.refs_0_.q_ref, ...), custom_call_target="tpu_custom_call" | custom-call | flops 83999997952 | tf_op jit(solution)/shard_map/attend_back/pallas_call | solution.py:46
  387.4 4.1 collective-permute-start.40
  393.5 31.0 %collective-permute-done.40.dqb_ref = bf16[256,1024]{1,0:T(8,128)(2,1)S(1)} collective-permute-done((bf16[256,1024]{1,0:T(8,128)(2,1)}, bf16[256,1024]{1,0:T(8,128)(2,1)S(1)}, u32[]{:S(2)}, u32[]{:S(2)}) %collective-permute-start.40) | collective-permute-done | bytes 524320 | tf_op jit(solution)/shard_map/ppermute | solution.py:1145
  427.4 15.1 %attend_back.5 = (f32[512,1024]{1,0:T(8,128)}, bf16[2,512,512]{2,1,0:T(8,128)(2,1)}, bf16[2,512,512]{2,1,0:T(8,128)(2,1)}) custom-call(s32[2]{0:T(128)} %pad_add_fusion.1.idx_ref, bf16[512,1024]{1,0:T(8,128)(2,1)} %get-tuple-element.200.refs_0_.q_ref, bf16[512,1024]{1,0:T(8,128)(2,1)} %get-tuple-element.242.do_ref, f32[4,8,512]{2,1,0:T(8,128)} %get-tuple-element.243.lse_ref, ...), custom_call_target="tpu_custom_call" | custom-call | flops 48000000000 | tf_op jit(solution)/shard_map/attend_back/pallas_call | solution.py:46
  444.1 3.8 merge.1
  453.1 12.0 %q_back.1 = (bf16[1024,1024]{1,0:T(8,128)(2,1)}, f32[1024,1024]{1,0:T(8,128)}, f32[1,128]{1,0:T(1,128)}) custom-call(f32[256,1024]{1,0:T(8,128)} %get-tuple-element.255.dqa_ref, bf16[256,1024]{1,0:T(8,128)(2,1)} %copy-done.24, f32[512,1024]{1,0:T(8,128)} %get-tuple-element.279.dqc_ref, f32[1024,1024]{1,0:T(8,128)} %get-tuple-element.280.lin_ref, ...), custom_call_target="tpu_custom_call" | custom-call | tf_op jit(solution)/shard_map/q_back/pallas_call | solution.py:46
  465.1 8.5 %kv_back.2 = (bf16[1024,1024]{1,0:T(8,128)(2,1)}, bf16[512,1024]{1,0:T(8,128)(2,1)}, f32[1,128]{1,0:T(1,128)}) custom-call(f32[512,512]{1,0:T(8,128)} %get-tuple-element.292.lin_ref, f32[1,128]{1,0:T(1,128)} %reshape.120.hgain_ref.gain_ref, f32[1024,128]{1,0:T(8,128)} %get-tuple-element.369.cos_ref, f32[1024,128]{1,0:T(8,128)} %get-tuple-element.370.sin_ref, ...), custom_call_target="tpu_custom_call" | custom-call | tf_op jit(solution)/shard_map/kv_back/pallas_call | solution.py:46
  473.6 5.9 %weight_halves.2 = (bf16[512,1024]{1,0:T(8,128)(2,1)}, bf16[512,1024]{1,0:T(8,128)(2,1)}) custom-call(bf16[1024,1024]{1,0:T(8,128)(2,1)} %get-tuple-element.194.normed_ref.left_ref, bf16[1024,1024]{1,0:T(8,128)(2,1)} %get-tuple-element.297.right_ref), custom_call_target="tpu_custom_call" | custom-call | tf_op jit(solution)/shard_map/weight_halves/pallas_call | solution.py:46
  484.3 8.9 %kv_back.3 = (bf16[1024,1024]{1,0:T(8,128)(2,1)}, bf16[512,1024]{1,0:T(8,128)(2,1)}, f32[1,128]{1,0:T(1,128)}) custom-call(f32[512,512]{1,0:T(8,128)} %get-tuple-element.229.lin_ref, f32[1,128]{1,0:T(1,128)} %reshape.120.hgain_ref.gain_ref, f32[1024,128]{1,0:T(8,128)} %get-tuple-element.369.cos_ref, ...), custom_call_target="tpu_custom_call", output_to_operand_aliasing={{0}: (15, {})} | custom-call | flops 8999999488 | tf_op jit(solution)/shard_map/kv_back/pallas_call | solution.py:46
  493.6 6.0 %weight_halves.3 = (bf16[512,1024]{1,0:T(8,128)(2,1)}, bf16[512,1024]{1,0:T(8,128)(2,1)}) custom-call(bf16[1024,1024]{1,0:T(8,128)(2,1)} %get-tuple-element.194.normed_ref.left_ref, bf16[1024,1024]{1,0:T(8,128)(2,1)} %get-tuple-element.308.right_ref), custom_call_target="tpu_custom_call" | custom-call | tf_op jit(solution)/shard_map/weight_halves/pallas_call | solution.py:46
  503.2 6.9 %collective-permute-done.58.got_ref = bf16[512,1024]{1,0:T(8,128)(2,1)S(1)} collective-permute-done((bf16[512,1024]{1,0:T(8,128)(2,1)S(1)}, bf16[512,1024]{1,0:T(8,128)(2,1)S(1)}, u32[]{:S(2)}, u32[]{:S(2)}) %collective-permute-start.58) | collective-permute-done | bytes 1048608 | tf_op jit(solution)/shard_map/ppermute | solution.py:893
  511.1 4.1 tokens_back.2
  524.4 3.1 add_layer.2.refs_0_
  530.6 11.9 %collective-permute-done.67 = bf16[64,1024]{1,0:T(8,128)(2,1)S(1)} collective-permute-done((bf16[64,1024]{1,0:T(8,128)(2,1)S(1)}, bf16[64,1024]{1,0:T(8,128)(2,1)S(1)}, u32[]{:S(2)}, u32[]{:S(2)}) %collective-permute-start.67) | collective-permute-done | bytes 131104 | tf_op jit(solution)/shard_map/ppermute | solution.py:893
  546.6 4.0 tokens_back.3
  554.1 7.0 %collective-permute-done.71 = bf16[64,1024]{1,0:T(8,128)(2,1)S(1)} collective-permute-done((bf16[64,1024]{1,0:T(8,128)(2,1)S(1)}, bf16[64,1024]{1,0:T(8,128)(2,1)S(1)}, u32[]{:S(2)}, u32[]{:S(2)}) %collective-permute-start.71) | collective-permute-done | bytes 131104 | tf_op jit(solution)/shard_map/ppermute | solution.py:893
  565.7 3.8 collective-permute-done.73
  (346 shorter events, 114.6 us)
Async XLA Ops:
  7.2 83.6 %all-gather.3.cloned.1.call-start = ((), (), s32[]{:S(2)}) async-start(), calls=%async_computation.1 | async-start | bytes 5570560 | tf_op jit(solution)/shard_map/all_gather | solution.py:1003
  9.4 168.5 %all-gather.5.cloned.1.call-start = ((), (), s32[]{:S(2)}) async-start(), calls=%async_computation.2 | async-start | bytes 6684672 | tf_op jit(solution)/shard_map/all_gather | solution.py:1107
  26.8 14.2 %collective-permute-start.11 = (bf16[128,1024]{1,0:T(8,128)(2,1)S(1)}, bf16[128,1024]{1,0:T(8,128)(2,1)S(1)}, u32[]{:S(2)}, u32[]{:S(2)}) collective-permute-start(bf16[128,1024]{1,0:T(8,128)(2,1)S(1)} %pad_maximum_fusion.2.refs_0_), channel_id=1, source_target_pairs={{0,4},{2,6},{4,0},{6,2},{8,12},{10,14},{12,8},{14,10},{1,5},{3,7},... | collective-permute-start | bytes 786440 | tf_op jit(solution)/shard_map/ppermute | solution.py:893
  28.0 14.6 %collective-permute-start.12 = (bf16[128,1024]{1,0:T(8,128)(2,1)S(1)}, bf16[128,1024]{1,0:T(8,128)(2,1)S(1)}, u32[]{:S(2)}, u32[]{:S(2)}) collective-permute-start(bf16[128,1024]{1,0:T(8,128)(2,1)S(1)} %pad_maximum_fusion.2.refs_0_), channel_id=1, source_target_pairs={{0,8},{2,10},{4,12},{6,14},{8,0},{10,2},{12,4},{14,6},{1,9},{3,11}... | collective-permute-start | bytes 786440 | tf_op jit(solution)/shard_map/ppermute | solution.py:893
  43.1 15.5 %collective-permute-start.10 = (bf16[128,1024]{1,0:T(8,128)(2,1)S(1)}, bf16[128,1024]{1,0:T(8,128)(2,1)S(1)}, u32[]{:S(2)}, u32[]{:S(2)}) collective-permute-start(bf16[128,1024]{1,0:T(8,128)(2,1)S(1)} %constant_dynamic-update-slice_fusion.refs_0_), channel_id=1, source_target_pairs={{0,12},{2,14},{4,8},{6,10},{8,4},{10,6},{12,0},{14,2},{1,13},{3,15... | collective-permute-start | bytes 786440 | tf_op jit(solution)/shard_map/ppermute | solution.py:893
  65.2 25.5 %collective-permute-start.21 = (bf16[2,512,512]{2,1,0:T(8,128)(2,1)}, bf16[2,512,512]{2,1,0:T(8,128)(2,1)S(1)}, u32[]{:S(2)}, u32[]{:S(2)}) collective-permute-start(bf16[2,512,512]{2,1,0:T(8,128)(2,1)} %get-tuple-element.190.refs_1_.refs_0_), channel_id=1, source_target_pairs={{0,8},{2,10},{4,12},{6,14},{8,0},{10,2},{12,4},{14,6},{1,9},{3,11}... | collective-permute-start | bytes 3145736 | tf_op jit(solution)/shard_map/ppermute | solution.py:893
  65.7 25.0 %collective-permute-start.16 = (bf16[2,512,512]{2,1,0:T(8,128)(2,1)}, bf16[2,512,512]{2,1,0:T(8,128)(2,1)S(1)}, u32[]{:S(2)}, u32[]{:S(2)}) collective-permute-start(bf16[2,512,512]{2,1,0:T(8,128)(2,1)} %get-tuple-element.190.refs_1_.refs_0_), channel_id=1, source_target_pairs={{0,4},{2,6},{4,0},{6,2},{8,12},{10,14},{12,8},{14,10},{1,5},{3,7},... | collective-permute-start | bytes 3145736 | tf_op jit(solution)/shard_map/ppermute | solution.py:893
  90.8 351.8 %reduce-scatter.2.cloned.1.call-start = ((), (), s32[]{:S(2)}) async-start(), calls=%async_computation.3 | async-start | bytes 10027008 | tf_op jit(solution)/shard_map/reduce_scatter | solution.py:1139
  91.0 19.6 %collective-permute-start.26 = (bf16[512,512]{1,0:T(8,128)(2,1)S(1)}, bf16[512,512]{1,0:T(8,128)(2,1)}, u32[]{:S(2)}, u32[]{:S(2)}) collective-permute-start(bf16[512,512]{1,0:T(8,128)(2,1)S(1)} %slice_bitcast_fusion.2), channel_id=1, source_target_pairs={{0,8},{2,10},{4,12},{6,14},{8,0},{10,2},{12,4},{14,6},{1,9},{3,11}... | collective-permute-start | bytes 1572872 | tf_op jit(solution)/shard_map/ppermute | solution.py:893
  92.5 18.2 %collective-permute-start.25 = (bf16[512,512]{1,0:T(8,128)(2,1)S(1)}, bf16[512,512]{1,0:T(8,128)(2,1)}, u32[]{:S(2)}, u32[]{:S(2)}) collective-permute-start(bf16[512,512]{1,0:T(8,128)(2,1)S(1)} %slice_bitcast_fusion.3), channel_id=1, source_target_pairs={{0,4},{2,6},{4,0},{6,2},{8,12},{10,14},{12,8},{14,10},{1,5},{3,7},... | collective-permute-start | bytes 1572872 | tf_op jit(solution)/shard_map/ppermute | solution.py:893
  93.2 20.5 %collective-permute-start.24 = (bf16[2,512,512]{2,1,0:T(8,128)(2,1)S(1)}, bf16[2,512,512]{2,1,0:T(8,128)(2,1)}, u32[]{:S(2)}, u32[]{:S(2)}) collective-permute-start(bf16[2,512,512]{2,1,0:T(8,128)(2,1)S(1)} %collective-permute-done.21.refs_4_.refs_2_.refs_3_.refs_1_), channel_id=1, source_target_pairs={{0,2},{2,0},{4,6},{6,4},{8,10},{10,8},{12,14},{14,12},{1,3},{3,1},... | collective-permute-start | bytes 3145736 | tf_op jit(solution)/shard_map/ppermute | solution.py:893
  93.2 20.5 %collective-permute-start.23 = (bf16[2,512,512]{2,1,0:T(8,128)(2,1)S(1)}, bf16[2,512,512]{2,1,0:T(8,128)(2,1)}, u32[]{:S(2)}, u32[]{:S(2)}) collective-permute-start(bf16[2,512,512]{2,1,0:T(8,128)(2,1)S(1)} %collective-permute-done.16.refs_3_.refs_1_.refs_2_.refs_0_), channel_id=1, source_target_pairs={{0,2},{2,0},{4,6},{6,4},{8,10},{10,8},{12,14},{14,12},{1,3},{3,1},... | collective-permute-start | bytes 3145736 | tf_op jit(solution)/shard_map/ppermute | solution.py:893
  93.7 46.1 %collective-permute-start.29 = (bf16[2,512,512]{2,1,0:T(8,128)(2,1)}, bf16[2,512,512]{2,1,0:T(8,128)(2,1)S(1)}, u32[]{:S(2)}, u32[]{:S(2)}) collective-permute-start(bf16[2,512,512]{2,1,0:T(8,128)(2,1)} %get-tuple-element.215.refs_3_.refs_4_), channel_id=1, source_target_pairs={{0,4},{2,6},{4,8},{6,10},{8,12},{10,14},{1,5},{3,7},{5,9},{7,11},{... | collective-permute-start | bytes 3145736 | tf_op jit(solution)/shard_map/ppermute | solution.py:898
  141.6 36.3 %collective-permute-start.32 = (bf16[512,1024]{1,0:T(8,128)(2,1)S(1)}, bf16[512,1024]{1,0:T(8,128)(2,1)}, u32[]{:S(2)}, u32[]{:S(2)}) collective-permute-start(bf16[512,1024]{1,0:T(8,128)(2,1)S(1)} %copy-done.7), channel_id=1, source_target_pairs={{0,1},{1,0},{2,3},{3,2},{4,5},{5,4},{6,7},{7,6},{8,9},{9,8},{10,11... | collective-permute-start | bytes 3145736 | tf_op jit(solution)/shard_map/ppermute | solution.py:893
  168.6 31.7 %collective-permute-start.31 = (bf16[512,1024]{1,0:T(8,128)(2,1)}, bf16[512,1024]{1,0:T(8,128)(2,1)S(1)}, u32[]{:S(2)}, u32[]{:S(2)}) collective-permute-start(bf16[512,1024]{1,0:T(8,128)(2,1)} %out_projection.3.own_ref), channel_id=1, source_target_pairs={{0,1},{1,0},{2,3},{3,2},{4,5},{5,4},{6,7},{7,6},{8,9},{9,8},{10,11... | collective-permute-start | bytes 3145736 | tf_op jit(solution)/shard_map/ppermute | solution.py:893
  196.2 46.1 %collective-permute-start.34 = (bf16[512,1024]{1,0:T(8,128)(2,1)}, bf16[512,1024]{1,0:T(8,128)(2,1)S(1)}, u32[]{:S(2)}, u32[]{:S(2)}) collective-permute-start(bf16[512,1024]{1,0:T(8,128)(2,1)} %get-tuple-element.223.own_ref), channel_id=1, source_target_pairs={{0,1},{1,0},{2,3},{3,2},{4,5},{5,4},{6,7},{7,6},{8,9},{9,8},{10,11... | collective-permute-start | bytes 3145736 | tf_op jit(solution)/shard_map/ppermute | solution.py:893
  220.0 31.7 %collective-permute-start.33 = (bf16[512,1024]{1,0:T(8,128)(2,1)}, bf16[512,1024]{1,0:T(8,128)(2,1)S(1)}, u32[]{:S(2)}, u32[]{:S(2)}) collective-permute-start(bf16[512,1024]{1,0:T(8,128)(2,1)} %get-tuple-element.230.own_ref), channel_id=1, source_target_pairs={{0,1},{1,0},{2,3},{3,2},{4,5},{5,4},{6,7},{7,6},{8,9},{9,8},{10,11... | collective-permute-start | bytes 3145736 | tf_op jit(solution)/shard_map/ppermute | solution.py:893
  220.1 78.9 %collective-permute-start.38 = (f32[4,8,256]{2,1,0:T(8,128)S(1)}, f32[4,8,256]{2,1,0:T(8,128)S(1)}, u32[]{:S(2)}, u32[]{:S(2)}) collective-permute-start(f32[4,8,256]{2,1,0:T(8,128)S(1)} %slice.126), channel_id=1, source_target_pairs={{0,14},{2,12},{4,10},{6,8},{8,6},{10,4},{12,2},{14,0},{1,15},{3,13... | collective-permute-start | bytes 98312 | tf_op jit(solution)/shard_map/ppermute | solution.py:1145
  224.4 76.3 %collective-permute-start.36 = (bf16[256,1024]{1,0:T(8,128)(2,1)}, bf16[256,1024]{1,0:T(8,128)(2,1)S(1)}, u32[]{:S(2)}, u32[]{:S(2)}) collective-permute-start(bf16[256,1024]{1,0:T(8,128)(2,1)} %slice.124), channel_id=1, source_target_pairs={{0,14},{2,12},{4,10},{6,8},{8,6},{10,4},{12,2},{14,0},{1,15},{3,13... | collective-permute-start | bytes 1572872 | tf_op jit(solution)/shard_map/ppermute | solution.py:1145
  266.9 25.0 %collective-permute-start.35 = (bf16[512,1024]{1,0:T(8,128)(2,1)}, bf16[512,1024]{1,0:T(8,128)(2,1)S(1)}, u32[]{:S(2)}, u32[]{:S(2)}) collective-permute-start(bf16[512,1024]{1,0:T(8,128)(2,1)} %get-tuple-element.246), channel_id=1, source_target_pairs={{0,2},{2,0},{4,6},{6,4},{8,10},{10,8},{12,14},{14,12},{1,3},{3,1},... | collective-permute-start | bytes 3145736 | tf_op jit(solution)/shard_map/ppermute | solution.py:893
  266.9 34.2 %collective-permute-start.37 = (bf16[256,1024]{1,0:T(8,128)(2,1)S(1)}, bf16[256,1024]{1,0:T(8,128)(2,1)S(1)}, u32[]{:S(2)}, u32[]{:S(2)}) collective-permute-start(bf16[256,1024]{1,0:T(8,128)(2,1)S(1)} %slice.125), channel_id=1, source_target_pairs={{0,14},{2,12},{4,10},{6,8},{8,6},{10,4},{12,2},{14,0},{1,15},{3,13... | collective-permute-start | bytes 1572872 | tf_op jit(solution)/shard_map/ppermute | solution.py:1145
  269.5 31.5 %collective-permute-start.39 = (f32[4,8,256]{2,1,0:T(8,128)S(1)}, f32[4,8,256]{2,1,0:T(8,128)S(1)}, u32[]{:S(2)}, u32[]{:S(2)}) collective-permute-start(f32[4,8,256]{2,1,0:T(8,128)S(1)} %slice.127), channel_id=1, source_target_pairs={{0,14},{2,12},{4,10},{6,8},{8,6},{10,4},{12,2},{14,0},{1,15},{3,13... | collective-permute-start | bytes 98312 | tf_op jit(solution)/shard_map/ppermute | solution.py:1145
  291.9 49.4 %collective-permute-start.41 = (bf16[2,512,512]{2,1,0:T(8,128)(2,1)}, bf16[2,512,512]{2,1,0:T(8,128)(2,1)S(1)}, u32[]{:S(2)}, u32[]{:S(2)}) collective-permute-start(bf16[2,512,512]{2,1,0:T(8,128)(2,1)} %get-tuple-element.258), channel_id=1, source_target_pairs={{0,2},{2,0},{4,6},{6,4},{8,10},{10,8},{12,14},{14,12},{1,3},{3,1},... | collective-permute-start | bytes 3145736 | tf_op jit(solution)/shard_map/ppermute | solution.py:893
  299.0 94.4 %collective-permute-start.43 = (bf16[512,1024]{1,0:T(8,128)(2,1)S(1)}, bf16[512,1024]{1,0:T(8,128)(2,1)}, u32[]{:S(2)}, u32[]{:S(2)}) collective-permute-start(bf16[512,1024]{1,0:T(8,128)(2,1)S(1)} %copy-done.22), channel_id=1, source_target_pairs={{0,1},{1,0},{2,3},{3,2},{4,5},{5,4},{6,7},{7,6},{8,9},{9,8},{10,11... | collective-permute-start | bytes 3145736 | tf_op jit(solution)/shard_map/ppermute | solution.py:893
  300.8 92.7 %collective-permute-start.42 = (bf16[512,1024]{1,0:T(8,128)(2,1)}, bf16[512,1024]{1,0:T(8,128)(2,1)}, u32[]{:S(2)}, u32[]{:S(2)}) collective-permute-start(bf16[512,1024]{1,0:T(8,128)(2,1)} %get-tuple-element.267.own_ref), channel_id=1, source_target_pairs={{0,1},{1,0},{2,3},{3,2},{4,5},{5,4},{6,7},{7,6},{8,9},{9,8},{10,11... | collective-permute-start | bytes 3145736 | tf_op jit(solution)/shard_map/ppermute | solution.py:893
  341.3 18.9 %collective-permute-start.44 = (bf16[128,1024]{1,0:T(8,128)(2,1)S(1)}, bf16[128,1024]{1,0:T(8,128)(2,1)S(1)}, u32[]{:S(2)}, u32[]{:S(2)}) collective-permute-start(bf16[128,1024]{1,0:T(8,128)(2,1)S(1)} %get-tuple-element.355), channel_id=1, source_target_pairs={{0,4},{2,6},{4,0},{6,2},{8,12},{10,14},{12,8},{14,10},{1,5},{3,7},... | collective-permute-start | bytes 786440 | tf_op jit(solution)/shard_map/ppermute | solution.py:893
  351.4 40.3 %collective-permute-start.47 = (bf16[2,512,512]{2,1,0:T(8,128)(2,1)}, bf16[2,512,512]{2,1,0:T(8,128)(2,1)S(1)}, u32[]{:S(2)}, u32[]{:S(2)}) collective-permute-start(bf16[2,512,512]{2,1,0:T(8,128)(2,1)} %get-tuple-element.274), channel_id=1, source_target_pairs={{0,2},{2,0},{4,6},{6,4},{8,10},{10,8},{12,14},{14,12},{1,3},{3,1},... | collective-permute-start | bytes 3145736 | tf_op jit(solution)/shard_map/ppermute | solution.py:893
  351.4 34.7 %collective-permute-start.45 = (bf16[128,1024]{1,0:T(8,128)(2,1)S(1)}, bf16[128,1024]{1,0:T(8,128)(2,1)S(1)}, u32[]{:S(2)}, u32[]{:S(2)}) collective-permute-start(bf16[128,1024]{1,0:T(8,128)(2,1)S(1)} %get-tuple-element.357), channel_id=1, source_target_pairs={{0,8},{2,10},{4,12},{6,14},{8,0},{10,2},{12,4},{14,6},{1,9},{3,11}... | collective-permute-start | bytes 786440 | tf_op jit(solution)/shard_map/ppermute | solution.py:893
  360.2 27.2 %collective-permute-start.46 = (bf16[128,1024]{1,0:T(8,128)(2,1)S(1)}, bf16[128,1024]{1,0:T(8,128)(2,1)S(1)}, u32[]{:S(2)}, u32[]{:S(2)}) collective-permute-start(bf16[128,1024]{1,0:T(8,128)(2,1)S(1)} %get-tuple-element.356), channel_id=1, source_target_pairs={{0,12},{2,14},{4,8},{6,10},{8,4},{10,6},{12,0},{14,2},{1,13},{3,15... | collective-permute-start | bytes 786440 | tf_op jit(solution)/shard_map/ppermute | solution.py:893
  386.1 56.4 %collective-permute-start.49 = (bf16[2,512,512]{2,1,0:T(8,128)(2,1)S(1)}, bf16[2,512,512]{2,1,0:T(8,128)(2,1)S(1)}, u32[]{:S(2)}, u32[]{:S(2)}) collective-permute-start(bf16[2,512,512]{2,1,0:T(8,128)(2,1)S(1)} %add_convert_fusion.3), channel_id=1, source_target_pairs={{4,0},{6,2},{8,4},{10,6},{12,8},{14,10},{5,1},{7,3},{9,5},{11,7},{... | collective-permute-start | bytes 3145736 | tf_op jit(solution)/shard_map/ppermute | solution.py:898
  387.4 37.2 %collective-permute-start.40 = (bf16[256,1024]{1,0:T(8,128)(2,1)}, bf16[256,1024]{1,0:T(8,128)(2,1)S(1)}, u32[]{:S(2)}, u32[]{:S(2)}) collective-permute-start(bf16[256,1024]{1,0:T(8,128)(2,1)} %get-tuple-element.256), channel_id=1, source_target_pairs={{0,14},{2,12},{4,10},{6,8},{8,6},{10,4},{12,2},{14,0},{1,15},{3,13... | collective-permute-start | bytes 1572872 | tf_op jit(solution)/shard_map/ppermute | solution.py:1145
  391.6 51.0 %collective-permute-start.50 = (bf16[2,512,512]{2,1,0:T(8,128)(2,1)}, bf16[2,512,512]{2,1,0:T(8,128)(2,1)S(1)}, u32[]{:S(2)}, u32[]{:S(2)}) collective-permute-start(bf16[2,512,512]{2,1,0:T(8,128)(2,1)} %get-tuple-element.285), channel_id=1, source_target_pairs={{0,2},{2,0},{4,6},{6,4},{8,10},{10,8},{12,14},{14,12},{1,3},{3,1},... | collective-permute-start | bytes 3145736 | tf_op jit(solution)/shard_map/ppermute | solution.py:893
  393.4 49.2 %collective-permute-start.48 = (bf16[2,512,512]{2,1,0:T(8,128)(2,1)}, bf16[2,512,512]{2,1,0:T(8,128)(2,1)S(1)}, u32[]{:S(2)}, u32[]{:S(2)}) collective-permute-start(bf16[2,512,512]{2,1,0:T(8,128)(2,1)} %get-tuple-element.282), channel_id=1, source_target_pairs={{0,2},{2,0},{4,6},{6,4},{8,10},{10,8},{12,14},{14,12},{1,3},{3,1},... | collective-permute-start | bytes 3145736 | tf_op jit(solution)/shard_map/ppermute | solution.py:893
  425.5 17.0 %collective-permute-start.52 = (bf16[512,512]{1,0:T(8,128)(2,1)S(1)}, bf16[512,512]{1,0:T(8,128)(2,1)}, u32[]{:S(2)}, u32[]{:S(2)}) collective-permute-start(bf16[512,512]{1,0:T(8,128)(2,1)S(1)} %get-tuple-element.353), channel_id=1, source_target_pairs={{0,8},{2,10},{4,12},{6,14},{8,0},{10,2},{12,4},{14,6},{1,9},{3,11}... | collective-permute-start | bytes 1572872 | tf_op jit(solution)/shard_map/ppermute | solution.py:893
  425.7 16.9 %collective-permute-start.51 = (bf16[512,512]{1,0:T(8,128)(2,1)}, bf16[512,512]{1,0:T(8,128)(2,1)}, u32[]{:S(2)}, u32[]{:S(2)}) collective-permute-start(bf16[512,512]{1,0:T(8,128)(2,1)} %get-tuple-element.354), channel_id=1, source_target_pairs={{0,4},{2,6},{4,0},{6,2},{8,12},{10,14},{12,8},{14,10},{1,5},{3,7},... | collective-permute-start | bytes 1572872 | tf_op jit(solution)/shard_map/ppermute | solution.py:893
  442.5 40.5 %collective-permute-start.53 = (bf16[2,512,512]{2,1,0:T(8,128)(2,1)}, bf16[2,512,512]{2,1,0:T(8,128)(2,1)}, u32[]{:S(2)}, u32[]{:S(2)}) collective-permute-start(bf16[2,512,512]{2,1,0:T(8,128)(2,1)} %get-tuple-element.301), channel_id=1, source_target_pairs={{0,2},{2,0},{4,6},{6,4},{8,10},{10,8},{12,14},{14,12},{1,3},{3,1},... | collective-permute-start | bytes 3145736 | tf_op jit(solution)/shard_map/ppermute | solution.py:893
  447.9 35.4 %collective-permute-start.54 = (bf16[2,512,512]{2,1,0:T(8,128)(2,1)}, bf16[2,512,512]{2,1,0:T(8,128)(2,1)S(1)}, u32[]{:S(2)}, u32[]{:S(2)}) collective-permute-start(bf16[2,512,512]{2,1,0:T(8,128)(2,1)} %get-tuple-element.289), channel_id=1, source_target_pairs={{0,4},{2,6},{4,0},{6,2},{8,12},{10,14},{12,8},{14,10},{1,5},{3,7},... | collective-permute-start | bytes 3145736 | tf_op jit(solution)/shard_map/ppermute | solution.py:893
  449.1 34.2 %collective-permute-start.55 = (bf16[2,512,512]{2,1,0:T(8,128)(2,1)}, bf16[2,512,512]{2,1,0:T(8,128)(2,1)}, u32[]{:S(2)}, u32[]{:S(2)}) collective-permute-start(bf16[2,512,512]{2,1,0:T(8,128)(2,1)} %get-tuple-element.302), channel_id=1, source_target_pairs={{0,8},{2,10},{4,12},{6,14},{8,0},{10,2},{12,4},{14,6},{1,9},{3,11}... | collective-permute-start | bytes 3145736 | tf_op jit(solution)/shard_map/ppermute | solution.py:893
  480.3 35.0 %collective-permute-start.59 = (bf16[64,1024]{1,0:T(8,128)(2,1)S(1)}, bf16[64,1024]{1,0:T(8,128)(2,1)S(1)}, u32[]{:S(2)}, u32[]{:S(2)}) collective-permute-start(bf16[64,1024]{1,0:T(8,128)(2,1)S(1)} %slice.166), channel_id=1, source_target_pairs={{0,16},{16,0},{1,17},{17,1},{2,18},{18,2},{3,19},{19,3},{4,20},{20... | collective-permute-start | bytes 393224 | tf_op jit(solution)/shard_map/ppermute | solution.py:893
  483.0 27.1 %collective-permute-start.58 = (bf16[512,1024]{1,0:T(8,128)(2,1)S(1)}, bf16[512,1024]{1,0:T(8,128)(2,1)S(1)}, u32[]{:S(2)}, u32[]{:S(2)}) collective-permute-start(bf16[512,1024]{1,0:T(8,128)(2,1)S(1)} %copy-done.51), channel_id=1, source_target_pairs={{0,1},{1,0},{2,3},{3,2},{4,5},{5,4},{6,7},{7,6},{8,9},{9,8},{10,11... | collective-permute-start | bytes 3145736 | tf_op jit(solution)/shard_map/ppermute | solution.py:893
  499.7 19.2 %collective-permute-start.60 = (bf16[128,1024]{1,0:T(8,128)(2,1)S(1)}, bf16[128,1024]{1,0:T(8,128)(2,1)S(1)}, u32[]{:S(2)}, u32[]{:S(2)}) collective-permute-start(bf16[128,1024]{1,0:T(8,128)(2,1)S(1)} %get-tuple-element.350), channel_id=1, source_target_pairs={{0,4},{2,6},{4,0},{6,2},{8,12},{10,14},{12,8},{14,10},{1,5},{3,7},... | collective-permute-start | bytes 786440 | tf_op jit(solution)/shard_map/ppermute | solution.py:893
  500.8 18.1 %collective-permute-start.61 = (bf16[128,1024]{1,0:T(8,128)(2,1)S(1)}, bf16[128,1024]{1,0:T(8,128)(2,1)S(1)}, u32[]{:S(2)}, u32[]{:S(2)}) collective-permute-start(bf16[128,1024]{1,0:T(8,128)(2,1)S(1)} %get-tuple-element.352), channel_id=1, source_target_pairs={{0,8},{2,10},{4,12},{6,14},{8,0},{10,2},{12,4},{14,6},{1,9},{3,11}... | collective-permute-start | bytes 786440 | tf_op jit(solution)/shard_map/ppermute | solution.py:893
  501.8 17.1 %collective-permute-start.62 = (bf16[128,1024]{1,0:T(8,128)(2,1)S(1)}, bf16[128,1024]{1,0:T(8,128)(2,1)S(1)}, u32[]{:S(2)}, u32[]{:S(2)}) collective-permute-start(bf16[128,1024]{1,0:T(8,128)(2,1)S(1)} %get-tuple-element.351), channel_id=1, source_target_pairs={{0,12},{2,14},{4,8},{6,10},{8,4},{10,6},{12,0},{14,2},{1,13},{3,15... | collective-permute-start | bytes 786440 | tf_op jit(solution)/shard_map/ppermute | solution.py:893
  515.2 30.4 %collective-permute-start.63 = (bf16[512,1024]{1,0:T(8,128)(2,1)S(1)}, bf16[512,1024]{1,0:T(8,128)(2,1)S(1)}, u32[]{:S(2)}, u32[]{:S(2)}) collective-permute-start(bf16[512,1024]{1,0:T(8,128)(2,1)S(1)} %copy-done.49), channel_id=1, source_target_pairs={{0,1},{1,0},{2,3},{3,2},{4,5},{5,4},{6,7},{7,6},{8,9},{9,8},{10,11... | collective-permute-start | bytes 3145736 | tf_op jit(solution)/shard_map/ppermute | solution.py:893
  519.1 23.4 %collective-permute-start.67 = (bf16[64,1024]{1,0:T(8,128)(2,1)S(1)}, bf16[64,1024]{1,0:T(8,128)(2,1)S(1)}, u32[]{:S(2)}, u32[]{:S(2)}) collective-permute-start(bf16[64,1024]{1,0:T(8,128)(2,1)S(1)} %slice.176), channel_id=1, source_target_pairs={{0,16},{16,0},{1,17},{17,1},{2,18},{18,2},{3,19},{19,3},{4,20},{20... | collective-permute-start | bytes 393224 | tf_op jit(solution)/shard_map/ppermute | solution.py:893
  520.8 24.6 %collective-permute-start.64 = (bf16[128,1024]{1,0:T(8,128)(2,1)S(1)}, bf16[128,1024]{1,0:T(8,128)(2,1)S(1)}, u32[]{:S(2)}, u32[]{:S(2)}) collective-permute-start(bf16[128,1024]{1,0:T(8,128)(2,1)S(1)} %get-tuple-element.347), channel_id=1, source_target_pairs={{0,4},{2,6},{4,0},{6,2},{8,12},{10,14},{12,8},{14,10},{1,5},{3,7},... | collective-permute-start | bytes 786440 | tf_op jit(solution)/shard_map/ppermute | solution.py:893
  521.4 24.0 %collective-permute-start.65 = (bf16[128,1024]{1,0:T(8,128)(2,1)S(1)}, bf16[128,1024]{1,0:T(8,128)(2,1)S(1)}, u32[]{:S(2)}, u32[]{:S(2)}) collective-permute-start(bf16[128,1024]{1,0:T(8,128)(2,1)S(1)} %get-tuple-element.349), channel_id=1, source_target_pairs={{0,8},{2,10},{4,12},{6,14},{8,0},{10,2},{12,4},{14,6},{1,9},{3,11}... | collective-permute-start | bytes 786440 | tf_op jit(solution)/shard_map/ppermute | solution.py:893
  522.3 23.2 %collective-permute-start.66 = (bf16[128,1024]{1,0:T(8,128)(2,1)S(1)}, bf16[128,1024]{1,0:T(8,128)(2,1)S(1)}, u32[]{:S(2)}, u32[]{:S(2)}) collective-permute-start(bf16[128,1024]{1,0:T(8,128)(2,1)S(1)} %get-tuple-element.348), channel_id=1, source_target_pairs={{0,12},{2,14},{4,8},{6,10},{8,4},{10,6},{12,0},{14,2},{1,13},{3,15... | collective-permute-start | bytes 786440 | tf_op jit(solution)/shard_map/ppermute | solution.py:893
  (89 other events, 803.4 us)
Sparse Core Ops, SparseCore 0:
  10.9 69.4 all-gather.2
  90.9 68.7 all-gather.4
  242.5 119.1 reduce-scatter.1

commit v8 on v7

--- a/solution.py
+++ b/solution.py
@@ -421,7 +421,7 @@
     prior = {s: refs.pop(0) for s in plan["prior"]}
     dqa_ref, dqb_ref = refs.pop(0), refs.pop(0)
     outs = [refs.pop(0) for _ in slots]
-    qs, dos, lses, deltas, dq, dkv = refs
+    qs, dos, lses, deltas, dq = refs
     me = idx_ref[0]
     half = qa_ref.shape[0]
     rows = 2 * half
@@ -438,7 +438,8 @@
     lane = jnp.where(lane >= half, lane - half, lane)
     key = lax.broadcasted_iota(jnp.int32, (rows, 1), 0)
 
-    def block(kv_ref, part, mask=None):
+    def block(s, part, mask=None):
+        kv_ref, out_ref = slot_refs[slots.index(s)], outs[slots.index(s)]
         at = slice(part * rows, (part + 1) * rows)
         keys = kv_ref[0][...]
         scores = mm(keys, qs[at, :], NT)
@@ -449,35 +450,35 @@
         probs = jnp.exp2(scores)
         ds = (probs * (dp - deltas[:, at])).astype(BF)
         dq[:, at] += mm(keys.T, ds)
-        dkv[0] += mm(ds, qs[at, :])
-        dkv[1] += mm(probs.astype(BF), dos[at, :])
-
-    def top(s):
-        return 1 << (s.bit_length() - 1)
-
-    for s, kv_ref, out_ref in zip(slots, slot_refs, outs):
-        dkv[...] = jnp.zeros_like(dkv)
-        if s == 0:
-            block(kv_ref, 0, key <= lane)
-        else:
-
-            @pl.when(jnp.bitwise_and(me, top(s)) != 0)
-            def _(kv_ref=kv_ref):
-                block(kv_ref, 0)
-
-        if s == last:
-            block(kv_ref, 1, key <= lane + half)
-        else:
-
-            @pl.when(jnp.bitwise_and(me, top(s ^ last)) == 0)
-            def _(kv_ref=kv_ref):
-                block(kv_ref, 1)
-
-        for which, factor in ((0, LN2), (1, 1.0)):
-            total = dkv[which] * factor
-            if s in prior:
-                total = total + prior[s][which].astype(F32)
-            out_ref[which] = total.astype(BF)
+        before = out_ref if part else prior.get(s)
+        for which, value in enumerate((mm(ds, qs[at, :]) * LN2, mm(probs.astype(BF), dos[at, :]))):
+            if before is not None:
+                value = value + before[which].astype(F32)
+            out_ref[which] = value.astype(BF)
+
+    block(0, 0, key <= lane)
+    for bit, group in by_top_bit(slots).items():
+        group = [slots[at] for at in group]
+
+        @pl.when(jnp.bitwise_and(me, bit) != 0)
+        def _(group=group):
+            for s in group:
+                block(s, 0)
+
+        @pl.when(jnp.bitwise_and(me, bit) == 0)
+        def _(group=group):
+            for s in group:
+                out_ref = outs[slots.index(s)]
+                out_ref[...] = prior[s][...] if s in prior else jnp.zeros_like(out_ref)
+
+    block(last, 1, key <= lane + half)
+    for bit, group in by_top_bit(slots).items():
+
+        @pl.when(jnp.bitwise_and(me, bit) == 0)
+        def _(group=[slots[at] ^ last for at in group]):
+            for s in group:
+                block(s, 1)
+
     for part, out_ref in enumerate((dqa_ref, dqb_ref)):
         for g in range(2):
             at = slice(part * rows + g * half, part * rows + (g + 1) * half)
@@ -509,7 +510,6 @@
         pltpu.VMEM((1, 2 * rows), F32),
         pltpu.VMEM((1, 2 * rows), F32),
         pltpu.VMEM((128, 2 * rows), F32),
-        pltpu.VMEM((2, rows, 128), F32),
     ]
     results = call(functools.partial(prompt_back_kernel, plan), "prompt_back", (heads,), ins, outs, scratch,
                    scalars=scalars, us=16)
@@ -986,6 +986,25 @@
         by_x, by_y, far = (total[i * size : (i + 1) * size] for i in (1, 2, 3))
         return total, swap(by_x, "ctx", 2), swap(by_y, "ctx", 4), swap(far, "ctx", 6)
 
+    def scatter_first(low, high, late):
+        if ctx_size != 8:
+            return scatter_rows(low, high, late)
+        total = add_low(low, after(swap(high, "ctx", 1), late))
+        size, cut = total.shape[0] // 4, total.shape[1] // 2
+        own, by_x, by_y, far = (total[i * size : (i + 1) * size] for i in range(4))
+        left, right = swap(far[:, :cut], "ctx", 2), swap(far[:, cut:], "ctx", 4)
+        return own, by_x, by_y, left, right
+
+    def scatter_more(stage, late):
+        if ctx_size != 8:
+            return stage
+        own, by_x, by_y, left, right = stage
+        left, right = after(left, late), after(right, late)
+        cut = left.shape[1]
+        by_x = jnp.concatenate([by_x[:, :cut], add_low(by_x[:, cut:], right)], axis=1)
+        by_y = jnp.concatenate([add_low(by_y[:, :cut], left), by_y[:, cut:]], axis=1)
+        return lax.optimization_barrier((own, by_x, by_y))[0], swap(by_x, "ctx", 2), swap(by_y, "ctx", 4)
+
     def scatter_sum(stage, late):
         total = stage[0].astype(F32)[: stage[-1].shape[0]]
         for piece in stage[1:]:
@@ -1137,22 +1156,22 @@
     ffn_grads = weight_grad(normed_ffn, d_gu, 0, 3 * units, 2 * chunk)
     ffn_grads = weight_grad(cotangent, hidden, 2 * units, 3 * units, chunk, ffn_grads)
     ffn_share = lax.psum_scatter(ffn_grads, weight_axes, scatter_dimension=0, tiled=True)
-    d_resid_p, d_mixed, d_att_p, delta_p, d_two_p = mixed_back(
-        0, back_p, back_got_p, resid_p, after(gain_two, ffn_grads), cotangent, w_od, o_cols, attended
-    )
-
     def mirror(value):
         return lax.ppermute(value, "ctx", [(i, i ^ (ctx_size - 1)) for i in range(ctx_size)])
 
     half = rows // 2
     q_b, lse_b = mirror(after(q_p, part_c)[half:]), mirror(after(lse_p, part_c)[:, :, half:])
+    d_resid_p, d_mixed, d_att_p, delta_p, d_two_p = mixed_back(
+        0, back_p, back_got_p, resid_p, after(gain_two, ffn_grads, q_b, lse_b), cotangent, w_od, o_cols, attended
+    )
+
     do_b, delta_b = mirror(d_att_p[half:]), mirror(delta_p[:, :, half:])
     d_resid_c, d_mixed, d_att_c, delta_c, d_two_c = mixed_back(
         1, back_c, back_got_c, resid_c, after(gain_two, d_att_p), cotangent, w_od, o_cols, attended, d_mixed
     )
     out_low, out_high = slot_weight_grad(order, part, d_mixed, attended)
-    out_p, out_c = after(out_p, out_low), after(out_c, out_low)
-    out_got_p, out_got_c = swap(out_p, "tensor", 1), swap(out_c, "tensor", 1)
+    out_p = after(out_p, out_low)
+    out_got_p = swap(out_p, "tensor", 1)
 
     def back_c_rows(deps, slots, halos, carry, prior=None, last=False):
         return attention_backward(
@@ -1160,14 +1179,15 @@
         )
 
     dq_c, from_c, g_halo = back_c_rows((out_low,), pick(slots, far), halos, None)
+    out_c = after(out_c, dq_c)
+    out_got_c = swap(out_c, "tensor", 1)
     out_grad = scatter_rows(out_low, out_high, dq_c)
     if ctx_size == 8:
         near_one = swap(g_halo[1], "ctx", 1)
     dq_a, dq_b, from_p = prompt_backward(
-        after(scalars, dq_c, out_grad[0]), ctx_size, (q_p, d_att_p, lse_p, delta_p),
+        after(scalars, dq_c, out_got_p, out_grad[0]), ctx_size, (q_p, d_att_p, lse_p, delta_p),
         (q_b, do_b, lse_b, delta_b), slots, from_c,
     )
-    dq_b = mirror(dq_b)
     g = pick(from_p, far)
     zero = jnp.zeros((), BF)
     ready = ()
@@ -1178,21 +1198,22 @@
         halo_two = shift(two_back, -2)
         halo_near = jnp.where(odd, zero, near_one)
         ready = (two_back, halo_near)
-    dq_c, more, _ = back_c_rows((dq_a, out_grad[0], *ready), pick(slots, middle), {}, dq_c, from_p)
+    dq_c, more, _ = back_c_rows((dq_a, out_got_c, *ready), pick(slots, middle), {}, dq_c, from_p)
     g.update(more)
+    dq_b = mirror(after(dq_b, dq_c))
     out_grad = scatter_sum(out_grad, dq_c)
     if ctx_size == 8:
         g6 = add_low(g[6], after(got7, dq_c))
         far_k, far_v = swap(g6[0], "ctx", 2), swap(g6[1], "ctx", 4)
         got3, got5 = swap(g[3], "ctx", 1), swap(g[5], "ctx", 1)
-        ready = (g6,)
+        ready = (g6, halo_two)
     dq_c, more, _ = back_c_rows(
-        (dq_c, out_got_p, out_got_c, out_grad[0], dq_b, *ready), pick(slots, near), {}, dq_c, from_p, True
+        (dq_c, out_grad[0], *ready), pick(slots, near), {}, dq_c, from_p, True
     )
     g.update(more)
     if ctx_size == 8:
         got1 = swap(g[1], "ctx", 1)
-        far_k, far_v, got3, got5 = (after(v, dq_c, halo_two, ffn_share) for v in (far_k, far_v, got3, got5))
+        far_k, far_v, got3, got5 = (after(v, dq_c, dq_b, ffn_share) for v in (far_k, far_v, got3, got5))
         to_x, to_y = merge(g[2], got3, g[4], got5, far_k, far_v)
         ready = (to_x,)
         keys_p = values_p = [g[0], got1, swap(to_x, "ctx", 2), swap(to_y, "ctx", 4)]
@@ -1215,15 +1236,17 @@
         0, keys_p, values_p, k_lin_p, after(gain_k, q_low), cos, sin, w_kv, to_slots, q_part, d_kv
     )
     into_got_p = swap(into_p, "tensor", 1)
-    q_grad = scatter_rows(q_low, q_high, into_p)
+    q_grad = scatter_first(q_low, q_high, into_p)
     kv_high, kv_low = weight_halves(normed, after(d_kv, q_grad[0]))
+    q_grad = scatter_more(q_grad, kv_low)
     heads = jnp.concatenate([q_heads, k_heads_c + k_heads_p], axis=1)
     heads_got = swap(heads, "tensor", 1)
     grad_tokens, d_one_c = tokens_back(1, into_c, into_got_c, tokens, after(gain_one, kv_low, q_grad[0]), d_resid_c)
     out_share, gate_share, up_share, down_share = unpack(chunk, after(ffn_share, d_one_c), out_grad)
     q_grad = scatter_sum(q_grad, gate_share)
-    kv_grad = scatter_rows(kv_low, kv_high, gate_share)
+    kv_grad = scatter_first(kv_low, kv_high, gate_share)
     layer_out = add_layer(0, after(resid_p, kv_grad[0], q_grad[0]), out_p, out_got_p)
+    kv_grad = scatter_more(kv_grad, layer_out)
     layer_out = add_layer(1, after(resid_c, kv_grad[0]), out_c, out_got_c, layer_out)
     q_share = add_low(q_grad[0][:wide], after(q_grad[1], layer_out)).astype(F32)
     kv_grad = scatter_sum(kv_grad, layer_out)

time: 588 us -> 551 us (0.937)
  waiting for transfers between devices: 123 us -> 78.9 us
  Pallas kernels: 314 us -> 321 us
    ppermute x5, waiting for transfers between devices: 31.1 us -> 0.01 us  [mirror(): lax.ppermute(value, 'ctx', [(i, i ^ ctx_size - 1) for i in range(ctx_size)])]
    ppermute x67 -> x69, waiting for transfers between devices: 78.4 us -> 63.7 us  [swap(): return lax.ppermute(value, axis, [(i, i ^ bit) for i in range(size)])]
    pallas_call x32, Pallas kernels: 314 us -> 321 us  [call(): pl.pallas_call(kernel, grid_spec=pltpu.PrefetchScalarGridSpec(num_scalar_...]
    ppermute x67 -> x69, starting transfers between devices: 67.1 us -> 69.6 us  [swap(): return lax.ppermute(value, axis, [(i, i ^ bit) for i in range(size)])]
  transfers between devices with their start and end apart: 77 -> 79, of which waited for: 22 -> 21; matrix products, arithmetic and copies ran while one was open for 5% -> 6% of each run, Pallas kernels for 54% -> 59%
where the time goes in v8:
time: 551 us; the launch traced here: 541 us
  Pallas kernels  321 us (58%)
  starting transfers between devices  79.4 us (14%)
  waiting for transfers between devices  78.9 us (14%)
  local copies, waits for them, and re-layouts  24.1 us (4%)
  other arithmetic  18 us (3%)
  between operations  15.1 us (3%)
    pallas_call x32, Pallas kernels, call(): pl.pallas_call(kernel, grid_spec=pltpu.PrefetchScalarGridSpec(num_scalar_...  321 us
    ppermute x69, starting transfers between devices, swap(): return lax.ppermute(value, axis, [(i, i ^ bit) for i in range(size)])  69.6 us
    ppermute x69, waiting for transfers between devices, swap(): return lax.ppermute(value, axis, [(i, i ^ bit) for i in range(size)])  63.7 us
    ppermute x2, waiting for transfers between devices, shift(): lax.ppermute(value, 'ctx', [(i, i + by) for i in range(size) if 0 <= i +...  15.1 us
    unnamed x133, local copies, waits for them, and re-layouts  11.6 us
  transfers between devices with their start and end apart: 79, of which 21 were waited for; matrix products, arithmetic and copies ran while one was open for 6% of the time, Pallas kernels for 59%

profile of v8, /device:TPU:0, one launch (start us, length us, event | category | flops | bytes accessed | tf_op | source)
XLA Modules:
  0.0 541.4 jit_solution(11445307980623940977)
XLA Ops:
  10.8 3.7 collective-permute-start
  21.6 2.6 collective-permute-start.2
  28.9 4.4 collective-permute-done.2.refs_3_
  37.3 3.7 fusion.5.x_ref
  47.6 5.0 collective-permute-done.7.refs_1_
  52.5 6.1 %collective-permute-done.10.refs_3_ = bf16[128,1024]{1,0:T(8,128)(2,1)S(1)} collective-permute-done((bf16[128,1024]{1,0:T(8,128)(2,1)S(1)}, bf16[128,1024]{1,0:T(8,128)(2,1)S(1)}, u32[]{:S(2)}, u32[]{:S(2)}) %collective-permute-start.10) | collective-permute-done | bytes 262176 | tf_op jit(solution)/shard_map/ppermute | solution.py:893
  59.5 5.6 %keys_values.2 = (bf16[1024,1024]{1,0:T(8,128)(2,1)}, bf16[2,512,512]{2,1,0:T(8,128)(2,1)}, f32[512,512]{1,0:T(8,128)}, bf16[1024,1024]{1,0:T(8,128)(2,1)}) custom-call(bf16[1024,1024]{1,0:T(8,128)(2,1)} %fusion.5.x_ref, f32[1,1024]{1,0:T(1,128)} %fusion.1.gain_ref, f32[1,128]{1,0:T(1,128)} %reshape.120.hgain_ref.gain_ref, ...), custom_call_target="tpu_custom_call" | custom-call | tf_op jit(solution)/shard_map/keys_values/pallas_call | solution.py:46
  68.6 5.7 %keys_values.3 = (bf16[1024,1024]{1,0:T(8,128)(2,1)}, bf16[2,512,512]{2,1,0:T(8,128)(2,1)}, f32[512,512]{1,0:T(8,128)}) custom-call(bf16[1024,1024]{1,0:T(8,128)(2,1)} %fusion.5.x_ref, f32[1,1024]{1,0:T(1,128)} %fusion.1.gain_ref, f32[1,128]{1,0:T(1,128)} %reshape.120.hgain_ref.gain_ref, ...), custom_call_target="tpu_custom_call", output_to_operand_aliasing={{0}: (6, {})} | custom-call | tf_op jit(solution)/shard_map/keys_values/pallas_call | solution.py:46
  75.2 16.5 %queries.2 = (bf16[512,1024]{1,0:T(8,128)(2,1)}, f32[1024,1024]{1,0:T(8,128)}, bf16[1024,1024]{1,0:T(8,128)(2,1)}) custom-call(bf16[1024,1024]{1,0:T(8,128)(2,1)} %get-tuple-element.199.normed_ref.left_ref, f32[1,128]{1,0:T(1,128)} %reshape.121.hgain_ref.gain_ref, f32[1024,128]{1,0:T(8,128)} %get-tuple-element.385.cos_ref, ...), custom_call_target="tpu_custom_call" | custom-call | tf_op jit(solution)/shard_map/queries/pallas_call | solution.py:46
  91.6 6.6 %queries.3 = (bf16[512,1024]{1,0:T(8,128)(2,1)}, f32[1024,1024]{1,0:T(8,128)}) custom-call(bf16[1024,1024]{1,0:T(8,128)(2,1)} %get-tuple-element.199.normed_ref.left_ref, f32[1,128]{1,0:T(1,128)} %reshape.121.hgain_ref.gain_ref, f32[1024,128]{1,0:T(8,128)} %get-tuple-element.385.cos_ref, ...), custom_call_target="tpu_custom_call", output_to_operand_aliasing={{1}: (5, {})} | custom-call | tf_op jit(solution)/shard_map/queries/pallas_call | solution.py:46
  102.5 2.6 collective-permute-start.29
  107.7 10.9 %attend.3 = (f32[512,1024]{1,0:T(8,128)}, f32[512,1024]{1,0:T(8,128)}) custom-call(s32[2]{0:T(128)} %pad_add_fusion.1.idx_ref, s32[512,128]{1,0:T(8,128)} %broadcast_in_dim.73.lo_ref, bf16[512,1024]{1,0:T(8,128)(2,1)} %get-tuple-element.205.refs_0_.q_ref, bf16[2,512,512]{2,1,0:T(8,128)(2,1)} %get-tuple-element.195.refs_1_.refs_0_, ...), custom_call_target="tpu_custom_call" | custom-call | tf_op jit(solution)/shard_map/attend/pallas_call | solution.py:46
  121.6 8.8 %attend.4 = (bf16[1024,1024]{1,0:T(8,128)(2,1)}, f32[4,8,512]{2,1,0:T(8,128)}) custom-call(s32[2]{0:T(128)} %pad_add_fusion.1.idx_ref, s32[512,128]{1,0:T(8,128)} %broadcast_in_dim.73.lo_ref, bf16[512,1024]{1,0:T(8,128)(2,1)} %get-tuple-element.240.refs_0_.qa_ref, bf16[2,512,512]{2,1,0:T(8,128)(2,1)} %get-tuple-element.195.refs_1_.refs_0_, ...), custom_call_target="tpu_custom_call" | custom-call | tf_op jit(solution)/shard_map/attend/pallas_call | solution.py:46
  130.5 3.9 out_projection.2.own_ref
  134.4 15.1 %collective-permute-done.29.refs_9_.refs_5_ = bf16[2,512,512]{2,1,0:T(8,128)(2,1)S(1)} collective-permute-done((bf16[2,512,512]{2,1,0:T(8,128)(2,1)}, bf16[2,512,512]{2,1,0:T(8,128)(2,1)S(1)}, u32[]{:S(2)}, u32[]{:S(2)}) %collective-permute-start.29) | collective-permute-done | bytes 1048608 | tf_op jit(solution)/shard_map/ppermute | solution.py:898
  154.9 19.6 %attend.5 = (bf16[1024,1024]{1,0:T(8,128)(2,1)}, f32[4,8,512]{2,1,0:T(8,128)}) custom-call(s32[2]{0:T(128)} %pad_add_fusion.1.idx_ref, s32[512,128]{1,0:T(8,128)} %broadcast_in_dim.73.lo_ref, bf16[512,1024]{1,0:T(8,128)(2,1)} %get-tuple-element.205.refs_0_.q_ref, bf16[2,512,512]{2,1,0:T(8,128)(2,1)} %copy-done.2, ...), custom_call_target="tpu_custom_call", output_to_operand_aliasing={{0}: (15, {})} | custom-call | tf_op jit(solution)/shard_map/attend/pallas_call | solution.py:46
  174.4 3.9 out_projection.3.own_ref
  179.6 7.9 %collective-permute-done.32.got_ref = bf16[512,1024]{1,0:T(8,128)(2,1)} collective-permute-done((bf16[512,1024]{1,0:T(8,128)(2,1)S(1)}, bf16[512,1024]{1,0:T(8,128)(2,1)}, u32[]{:S(2)}, u32[]{:S(2)}) %collective-permute-start.32) | collective-permute-done | bytes 1048608 | tf_op jit(solution)/shard_map/ppermute | solution.py:893
  187.5 18.4 %feed_forward.2 = (f32[512,1024]{1,0:T(8,128)}, bf16[1024,1024]{1,0:T(8,128)(2,1)}, bf16[1024,1536]{1,0:T(8,128)(2,1)}, bf16[1024,3072]{1,0:T(8,128)(2,1)}, bf16...) custom-call(bf16[1024,1024]{1,0:T(8,128)(2,1)} %x_ref.7, bf16[512,1024]{1,0:T(8,128)(2,1)} %out_projection.2.own_ref, ...), custom_call_target="tpu_custom_call" | custom-call | tf_op jit(solution)/shard_map/feed_forward/pallas_call | solution.py:46
  206.0 3.9 collective-permute-done.31.got_ref
  210.8 18.8 %feed_forward.3 = (f32[512,1024]{1,0:T(8,128)}, bf16[1024,1024]{1,0:T(8,128)(2,1)}, bf16[1024,1536]{1,0:T(8,128)(2,1)}, bf16[1024,3072]{1,0:T(8,128)(2,1)}, bf16...) custom-call(bf16[1024,1024]{1,0:T(8,128)(2,1)} %x_ref.7, ...), custom_call_target="tpu_custom_call", output_to_operand_aliasing={{1}: (7, {}), {2}: (8, {}), {3}: (9, {})} | custom-call | tf_op jit(solution)/shard_map/feed_forward/pallas_call | solution.py:46
  233.2 10.8 %weight_grad.2.refs_0_ = bf16[1024,4608]{1,0:T(8,128)(2,1)} custom-call(bf16[1024,1024]{1,0:T(8,128)(2,1)} %get-tuple-element.238.left_ref, bf16[1024,3072]{1,0:T(8,128)(2,1)} %get-tuple-element.239.right_ref), custom_call_target="tpu_custom_call" | custom-call | tf_op jit(solution)/shard_map/weight_grad/pallas_call | solution.py:46
  244.0 7.2 %weight_grad.3 = bf16[1024,4608]{1,0:T(8,128)(2,1)} custom-call(bf16[1024,1024]{1,0:T(8,128)(2,1)} %dy_ref.7, bf16[1024,1536]{1,0:T(8,128)(2,1)} %get-tuple-element.237.right_ref, bf16[1024,4608]{1,0:T(8,128)(2,1)} %weight_grad.2.refs_0_), custom_call_target="tpu_custom_call", output_to_operand_aliasing={{}: (2, {})} | custom-call | tf_op jit(solution)/shard_map/weight_grad/pallas_call | solution.py:46
  252.2 7.2 %mixed_back.2 = (f32[512,1024]{1,0:T(8,128)}, bf16[1024,1024]{1,0:T(8,128)(2,1)}, bf16[512,1024]{1,0:T(8,128)(2,1)}, f32[4,8,512]{2,1,0:T(8,128)}, f32[1,1024]{1,0:T(1,128)}) custom-call(bf16[512,1024]{1,0:T(8,128)(2,1)} %get-tuple-element.228.own_ref, bf16[512,1024]{1,0:T(8,128)(2,1)} %copy-done.17, f32[512,1024]{1,0:T(8,128)} %get-tuple-element.328.resid_ref, ...), custom_call_target="tpu_custom_call" | custom-call | tf_op jit(solution)/shard_map/mixed_back/pallas_call | solution.py:46
  262.4 7.5 %mixed_back.3 = (f32[512,1024]{1,0:T(8,128)}, bf16[1024,1024]{1,0:T(8,128)(2,1)}, bf16[512,1024]{1,0:T(8,128)(2,1)}, f32[4,8,512]{2,1,0:T(8,128)}, f32[1,1024]{1,0:T(1,128)}) custom-call(bf16[512,1024]{1,0:T(8,128)(2,1)} %get-tuple-element.235.own_ref, bf16[512,1024]{1,0:T(8,128)(2,1)} %copy-done.18, ...), custom_call_target="tpu_custom_call", output_to_operand_aliasing={{1}: (7, {})} | custom-call | tf_op jit(solution)/shard_map/mixed_back/pallas_call | solution.py:46
  269.9 6.5 %slot_weight_grad.1 = (bf16[512,1024]{1,0:T(8,128)(2,1)}, bf16[512,1024]{1,0:T(8,128)(2,1)}) custom-call(s32[1]{0:T(128)} %bitcast.10.part_ref, bf16[1024,1024]{1,0:T(8,128)(2,1)} %get-tuple-element.247.left_ref, bf16[1024,1024]{1,0:T(8,128)(2,1)} %get-tuple-element.223.att_ref.right_ref), custom_call_target="tpu_custom_call" | custom-call | tf_op jit(solution)/shard_map/slot_weight_grad/pallas_call | solution.py:46
  281.7 21.5 %attend_back.3 = (f32[512,1024]{1,0:T(8,128)}, bf16[2,512,512]{2,1,0:T(8,128)(2,1)}, bf16[2,512,512]{2,1,0:T(8,128)(2,1)}, bf16[2,512,512]{2,1,0:T(8,128)(2,1)},...) custom-call(s32[2]{0:T(128)} %pad_add_fusion.1.idx_ref, bf16[512,1024]{1,0:T(8,128)(2,1)} %get-tuple-element.205.refs_0_.q_ref, ...), custom_call_target="tpu_custom_call" | custom-call | flops 102000001024 | tf_op jit(solution)/shard_map/attend_back/pallas_call | solution.py:46
  303.2 6.4 %collective-permute-start.42 = (bf16[2,512,512]{2,1,0:T(8,128)(2,1)}, bf16[2,512,512]{2,1,0:T(8,128)(2,1)S(1)}, u32[]{:S(2)}, u32[]{:S(2)}) collective-permute-start(bf16[2,512,512]{2,1,0:T(8,128)(2,1)} %get-tuple-element.267), channel_id=1, source_target_pairs={{0,2},{2,0},{4,6},{6,4},{8,10},{10,8},{12,14},{14,12},{1,3},{3,1},... | collective-permute-start | bytes 3145736 | tf_op jit(solution)/shard_map/ppermute | solution.py:893
  310.3 5.4 %collective-permute-done.37.got_ref = bf16[512,1024]{1,0:T(8,128)(2,1)S(1)} collective-permute-done((bf16[512,1024]{1,0:T(8,128)(2,1)S(1)}, bf16[512,1024]{1,0:T(8,128)(2,1)S(1)}, u32[]{:S(2)}, u32[]{:S(2)}) %collective-permute-start.37) | collective-permute-done | bytes 1048608 | tf_op jit(solution)/shard_map/ppermute | solution.py:893
  316.4 37.0 %prompt_back.1 = (f32[256,1024]{1,0:T(8,128)}, bf16[256,1024]{1,0:T(8,128)(2,1)}, bf16[2,512,512]{2,1,0:T(8,128)(2,1)}, bf16[2,512,512]{2,1,0:T(8,128)(2,1)}, bf...) custom-call(s32[2]{0:T(128)} %pad_add_fusion.1.idx_ref, ...), custom_call_target="tpu_custom_call" | custom-call | flops 48000000000 | tf_op jit(solution)/shard_map/prompt_back/pallas_call | solution.py:46
  356.6 2.6 collective-permute-start.44
  362.1 25.8 %attend_back.4 = (f32[512,1024]{1,0:T(8,128)}, bf16[2,512,512]{2,1,0:T(8,128)(2,1)}, bf16[2,512,512]{2,1,0:T(8,128)(2,1)}, bf16[2,512,512]{2,1,0:T(8,128)(2,1)}, bf16[2,512,512]{2,1,0:T(8,128)(2,1)}) custom-call(s32[2]{0:T(128)} %pad_add_fusion.1.idx_ref, bf16[512,1024]{1,0:T(8,128)(2,1)} %get-tuple-element.205.refs_0_.q_ref, ...), custom_call_target="tpu_custom_call" | custom-call | flops 83999997952 | tf_op jit(solution)/shard_map/attend_back/pallas_call | solution.py:46
  387.8 3.0 collective-permute-done.44
  401.7 15.1 %attend_back.5 = (f32[512,1024]{1,0:T(8,128)}, bf16[2,512,512]{2,1,0:T(8,128)(2,1)}, bf16[2,512,512]{2,1,0:T(8,128)(2,1)}) custom-call(s32[2]{0:T(128)} %pad_add_fusion.1.idx_ref, bf16[512,1024]{1,0:T(8,128)(2,1)} %get-tuple-element.205.refs_0_.q_ref, bf16[512,1024]{1,0:T(8,128)(2,1)} %get-tuple-element.250.do_ref, f32[4,8,512]{2,1,0:T(8,128)} %get-tuple-element.251.lse_ref, ...), custom_call_target="tpu_custom_call" | custom-call | flops 48000000000 | tf_op jit(solution)/shard_map/attend_back/pallas_call | solution.py:46
  419.3 3.8 merge.1
  428.0 12.0 %q_back.1 = (bf16[1024,1024]{1,0:T(8,128)(2,1)}, f32[1024,1024]{1,0:T(8,128)}, f32[1,128]{1,0:T(1,128)}) custom-call(f32[256,1024]{1,0:T(8,128)} %get-tuple-element.262.dqa_ref, bf16[256,1024]{1,0:T(8,128)(2,1)} %copy-done.28, f32[512,1024]{1,0:T(8,128)} %get-tuple-element.285.dqc_ref, f32[1024,1024]{1,0:T(8,128)} %get-tuple-element.286.lin_ref, ...), custom_call_target="tpu_custom_call" | custom-call | tf_op jit(solution)/shard_map/q_back/pallas_call | solution.py:46
  440.0 8.6 %kv_back.2 = (bf16[1024,1024]{1,0:T(8,128)(2,1)}, bf16[512,1024]{1,0:T(8,128)(2,1)}, f32[1,128]{1,0:T(1,128)}) custom-call(f32[512,512]{1,0:T(8,128)} %get-tuple-element.298.lin_ref, f32[1,128]{1,0:T(1,128)} %reshape.120.hgain_ref.gain_ref, f32[1024,128]{1,0:T(8,128)} %get-tuple-element.385.cos_ref, f32[1024,128]{1,0:T(8,128)} %get-tuple-element.386.sin_ref, ...), custom_call_target="tpu_custom_call" | custom-call | tf_op jit(solution)/shard_map/kv_back/pallas_call | solution.py:46
  448.6 5.9 %weight_halves.2 = (bf16[512,1024]{1,0:T(8,128)(2,1)}, bf16[512,1024]{1,0:T(8,128)(2,1)}) custom-call(bf16[1024,1024]{1,0:T(8,128)(2,1)} %get-tuple-element.199.normed_ref.left_ref, bf16[1024,1024]{1,0:T(8,128)(2,1)} %get-tuple-element.303.right_ref), custom_call_target="tpu_custom_call" | custom-call | tf_op jit(solution)/shard_map/weight_halves/pallas_call | solution.py:46
  457.9 8.9 %kv_back.3 = (bf16[1024,1024]{1,0:T(8,128)(2,1)}, bf16[512,1024]{1,0:T(8,128)(2,1)}, f32[1,128]{1,0:T(1,128)}) custom-call(f32[512,512]{1,0:T(8,128)} %get-tuple-element.234.lin_ref, f32[1,128]{1,0:T(1,128)} %reshape.120.hgain_ref.gain_ref, f32[1024,128]{1,0:T(8,128)} %get-tuple-element.385.cos_ref, ...), custom_call_target="tpu_custom_call", output_to_operand_aliasing={{0}: (15, {})} | custom-call | flops 8999999488 | tf_op jit(solution)/shard_map/kv_back/pallas_call | solution.py:46
  472.6 5.8 %weight_halves.3 = (bf16[512,1024]{1,0:T(8,128)(2,1)}, bf16[512,1024]{1,0:T(8,128)(2,1)}) custom-call(bf16[1024,1024]{1,0:T(8,128)(2,1)} %get-tuple-element.199.normed_ref.left_ref, bf16[1024,1024]{1,0:T(8,128)(2,1)} %get-tuple-element.314.right_ref), custom_call_target="tpu_custom_call" | custom-call | tf_op jit(solution)/shard_map/weight_halves/pallas_call | solution.py:46
  480.7 2.9 collective-permute-done.58.got_ref
  485.0 4.1 tokens_back.2
  495.2 3.1 add_layer.2.refs_0_
  503.4 3.1 add_layer.3
  508.6 4.0 tokens_back.3
  513.4 3.4 collective-permute-start.73
  518.1 5.7 %collective-permute-done.73 = bf16[64,1024]{1,0:T(8,128)(2,1)S(1)} collective-permute-done((bf16[64,1024]{1,0:T(8,128)(2,1)S(1)}, bf16[64,1024]{1,0:T(8,128)(2,1)S(1)}, u32[]{:S(2)}, u32[]{:S(2)}) %collective-permute-start.73) | collective-permute-done | bytes 131104 | tf_op jit(solution)/shard_map/ppermute | solution.py:893
  528.4 3.8 collective-permute-done.75
  (372 shorter events, 121.7 us)
Async XLA Ops:
  7.2 91.2 %all-gather.3.cloned.1.call-start = ((), (), s32[]{:S(2)}) async-start(), calls=%async_computation.1 | async-start | bytes 5570560 | tf_op jit(solution)/shard_map/all_gather | solution.py:1022
  9.4 178.1 %all-gather.5.cloned.1.call-start = ((), (), s32[]{:S(2)}) async-start(), calls=%async_computation.2 | async-start | bytes 6684672 | tf_op jit(solution)/shard_map/all_gather | solution.py:1126
  26.7 14.3 %collective-permute-start.11 = (bf16[128,1024]{1,0:T(8,128)(2,1)S(1)}, bf16[128,1024]{1,0:T(8,128)(2,1)S(1)}, u32[]{:S(2)}, u32[]{:S(2)}) collective-permute-start(bf16[128,1024]{1,0:T(8,128)(2,1)S(1)} %pad_maximum_fusion.2.refs_0_), channel_id=1, source_target_pairs={{0,4},{2,6},{4,0},{6,2},{8,12},{10,14},{12,8},{14,10},{1,5},{3,7},... | collective-permute-start | bytes 786440 | tf_op jit(solution)/shard_map/ppermute | solution.py:893
  27.9 14.6 %collective-permute-start.12 = (bf16[128,1024]{1,0:T(8,128)(2,1)S(1)}, bf16[128,1024]{1,0:T(8,128)(2,1)S(1)}, u32[]{:S(2)}, u32[]{:S(2)}) collective-permute-start(bf16[128,1024]{1,0:T(8,128)(2,1)S(1)} %pad_maximum_fusion.2.refs_0_), channel_id=1, source_target_pairs={{0,8},{2,10},{4,12},{6,14},{8,0},{10,2},{12,4},{14,6},{1,9},{3,11}... | collective-permute-start | bytes 786440 | tf_op jit(solution)/shard_map/ppermute | solution.py:893
  43.1 15.5 %collective-permute-start.10 = (bf16[128,1024]{1,0:T(8,128)(2,1)S(1)}, bf16[128,1024]{1,0:T(8,128)(2,1)S(1)}, u32[]{:S(2)}, u32[]{:S(2)}) collective-permute-start(bf16[128,1024]{1,0:T(8,128)(2,1)S(1)} %constant_dynamic-update-slice_fusion.refs_0_), channel_id=1, source_target_pairs={{0,12},{2,14},{4,8},{6,10},{8,4},{10,6},{12,0},{14,2},{1,13},{3,15... | collective-permute-start | bytes 786440 | tf_op jit(solution)/shard_map/ppermute | solution.py:893
  44.6 14.1 %collective-permute-start.14 = (bf16[128,1024]{1,0:T(8,128)(2,1)S(1)}, bf16[128,1024]{1,0:T(8,128)(2,1)S(1)}, u32[]{:S(2)}, u32[]{:S(2)}) collective-permute-start(bf16[128,1024]{1,0:T(8,128)(2,1)S(1)} %collective-permute-done.11.refs_1_), channel_id=1, source_target_pairs={{0,2},{2,0},{4,6},{6,4},{8,10},{10,8},{12,14},{14,12},{1,3},{3,1},... | collective-permute-start | bytes 786440 | tf_op jit(solution)/shard_map/ppermute | solution.py:893
  44.6 14.0 %collective-permute-start.15 = (bf16[128,1024]{1,0:T(8,128)(2,1)S(1)}, bf16[128,1024]{1,0:T(8,128)(2,1)S(1)}, u32[]{:S(2)}, u32[]{:S(2)}) collective-permute-start(bf16[128,1024]{1,0:T(8,128)(2,1)S(1)} %collective-permute-done.12.refs_2_), channel_id=1, source_target_pairs={{0,2},{2,0},{4,6},{6,4},{8,10},{10,8},{12,14},{14,12},{1,3},{3,1},... | collective-permute-start | bytes 786440 | tf_op jit(solution)/shard_map/ppermute | solution.py:893
  65.1 33.2 %collective-permute-start.21 = (bf16[2,512,512]{2,1,0:T(8,128)(2,1)}, bf16[2,512,512]{2,1,0:T(8,128)(2,1)S(1)}, u32[]{:S(2)}, u32[]{:S(2)}) collective-permute-start(bf16[2,512,512]{2,1,0:T(8,128)(2,1)} %get-tuple-element.195.refs_1_.refs_0_), channel_id=1, source_target_pairs={{0,8},{2,10},{4,12},{6,14},{8,0},{10,2},{12,4},{14,6},{1,9},{3,11}... | collective-permute-start | bytes 3145736 | tf_op jit(solution)/shard_map/ppermute | solution.py:893
  65.7 32.6 %collective-permute-start.16 = (bf16[2,512,512]{2,1,0:T(8,128)(2,1)}, bf16[2,512,512]{2,1,0:T(8,128)(2,1)S(1)}, u32[]{:S(2)}, u32[]{:S(2)}) collective-permute-start(bf16[2,512,512]{2,1,0:T(8,128)(2,1)} %get-tuple-element.195.refs_1_.refs_0_), channel_id=1, source_target_pairs={{0,4},{2,6},{4,0},{6,2},{8,12},{10,14},{12,8},{14,10},{1,5},{3,7},... | collective-permute-start | bytes 3145736 | tf_op jit(solution)/shard_map/ppermute | solution.py:893
  98.4 319.5 %reduce-scatter.2.cloned.1.call-start = ((), (), s32[]{:S(2)}) async-start(), calls=%async_computation.3 | async-start | bytes 10027008 | tf_op jit(solution)/shard_map/reduce_scatter | solution.py:1158
  98.9 19.6 %collective-permute-start.26 = (bf16[512,512]{1,0:T(8,128)(2,1)S(1)}, bf16[512,512]{1,0:T(8,128)(2,1)}, u32[]{:S(2)}, u32[]{:S(2)}) collective-permute-start(bf16[512,512]{1,0:T(8,128)(2,1)S(1)} %slice_bitcast_fusion.2), channel_id=1, source_target_pairs={{0,8},{2,10},{4,12},{6,14},{8,0},{10,2},{12,4},{14,6},{1,9},{3,11}... | collective-permute-start | bytes 1572872 | tf_op jit(solution)/shard_map/ppermute | solution.py:893
  100.5 18.2 %collective-permute-start.25 = (bf16[512,512]{1,0:T(8,128)(2,1)S(1)}, bf16[512,512]{1,0:T(8,128)(2,1)}, u32[]{:S(2)}, u32[]{:S(2)}) collective-permute-start(bf16[512,512]{1,0:T(8,128)(2,1)S(1)} %slice_bitcast_fusion.3), channel_id=1, source_target_pairs={{0,4},{2,6},{4,0},{6,2},{8,12},{10,14},{12,8},{14,10},{1,5},{3,7},... | collective-permute-start | bytes 1572872 | tf_op jit(solution)/shard_map/ppermute | solution.py:893
  102.0 19.7 %collective-permute-start.24 = (bf16[2,512,512]{2,1,0:T(8,128)(2,1)S(1)}, bf16[2,512,512]{2,1,0:T(8,128)(2,1)}, u32[]{:S(2)}, u32[]{:S(2)}) collective-permute-start(bf16[2,512,512]{2,1,0:T(8,128)(2,1)S(1)} %collective-permute-done.21.refs_4_.refs_2_.refs_3_.refs_1_), channel_id=1, source_target_pairs={{0,2},{2,0},{4,6},{6,4},{8,10},{10,8},{12,14},{14,12},{1,3},{3,1},... | collective-permute-start | bytes 3145736 | tf_op jit(solution)/shard_map/ppermute | solution.py:893
  102.0 19.7 %collective-permute-start.23 = (bf16[2,512,512]{2,1,0:T(8,128)(2,1)S(1)}, bf16[2,512,512]{2,1,0:T(8,128)(2,1)}, u32[]{:S(2)}, u32[]{:S(2)}) collective-permute-start(bf16[2,512,512]{2,1,0:T(8,128)(2,1)S(1)} %collective-permute-done.16.refs_3_.refs_1_.refs_2_.refs_0_), channel_id=1, source_target_pairs={{0,2},{2,0},{4,6},{6,4},{8,10},{10,8},{12,14},{14,12},{1,3},{3,1},... | collective-permute-start | bytes 3145736 | tf_op jit(solution)/shard_map/ppermute | solution.py:893
  102.5 47.0 %collective-permute-start.29 = (bf16[2,512,512]{2,1,0:T(8,128)(2,1)}, bf16[2,512,512]{2,1,0:T(8,128)(2,1)S(1)}, u32[]{:S(2)}, u32[]{:S(2)}) collective-permute-start(bf16[2,512,512]{2,1,0:T(8,128)(2,1)} %get-tuple-element.220.refs_3_.refs_4_), channel_id=1, source_target_pairs={{0,4},{2,6},{4,8},{6,10},{8,12},{10,14},{1,5},{3,7},{5,9},{7,11},{... | collective-permute-start | bytes 3145736 | tf_op jit(solution)/shard_map/ppermute | solution.py:898
  151.3 36.2 %collective-permute-start.32 = (bf16[512,1024]{1,0:T(8,128)(2,1)S(1)}, bf16[512,1024]{1,0:T(8,128)(2,1)}, u32[]{:S(2)}, u32[]{:S(2)}) collective-permute-start(bf16[512,1024]{1,0:T(8,128)(2,1)S(1)} %copy-done.9), channel_id=1, source_target_pairs={{0,1},{1,0},{2,3},{3,2},{4,5},{5,4},{6,7},{7,6},{8,9},{9,8},{10,11... | collective-permute-start | bytes 3145736 | tf_op jit(solution)/shard_map/ppermute | solution.py:893
  178.4 31.5 %collective-permute-start.31 = (bf16[512,1024]{1,0:T(8,128)(2,1)}, bf16[512,1024]{1,0:T(8,128)(2,1)S(1)}, u32[]{:S(2)}, u32[]{:S(2)}) collective-permute-start(bf16[512,1024]{1,0:T(8,128)(2,1)} %out_projection.3.own_ref), channel_id=1, source_target_pairs={{0,1},{1,0},{2,3},{3,2},{4,5},{5,4},{6,7},{7,6},{8,9},{9,8},{10,11... | collective-permute-start | bytes 3145736 | tf_op jit(solution)/shard_map/ppermute | solution.py:893
  205.9 45.3 %collective-permute-start.34 = (bf16[512,1024]{1,0:T(8,128)(2,1)}, bf16[512,1024]{1,0:T(8,128)(2,1)S(1)}, u32[]{:S(2)}, u32[]{:S(2)}) collective-permute-start(bf16[512,1024]{1,0:T(8,128)(2,1)} %get-tuple-element.228.own_ref), channel_id=1, source_target_pairs={{0,1},{1,0},{2,3},{3,2},{4,5},{5,4},{6,7},{7,6},{8,9},{9,8},{10,11... | collective-permute-start | bytes 3145736 | tf_op jit(solution)/shard_map/ppermute | solution.py:893
  229.6 31.7 %collective-permute-start.33 = (bf16[512,1024]{1,0:T(8,128)(2,1)}, bf16[512,1024]{1,0:T(8,128)(2,1)S(1)}, u32[]{:S(2)}, u32[]{:S(2)}) collective-permute-start(bf16[512,1024]{1,0:T(8,128)(2,1)} %get-tuple-element.235.own_ref), channel_id=1, source_target_pairs={{0,1},{1,0},{2,3},{3,2},{4,5},{5,4},{6,7},{7,6},{8,9},{9,8},{10,11... | collective-permute-start | bytes 3145736 | tf_op jit(solution)/shard_map/ppermute | solution.py:893
  230.6 20.6 %collective-permute-start.35 = (bf16[256,1024]{1,0:T(8,128)(2,1)}, bf16[256,1024]{1,0:T(8,128)(2,1)S(1)}, u32[]{:S(2)}, u32[]{:S(2)}) collective-permute-start(bf16[256,1024]{1,0:T(8,128)(2,1)} %slice.154), channel_id=1, source_target_pairs={{0,14},{2,12},{4,10},{6,8},{8,6},{10,4},{12,2},{14,0},{1,15},{3,13... | collective-permute-start | bytes 1572872 | tf_op jit(solution)/shard_map/ppermute | solution.py:1160
  232.5 18.7 %collective-permute-start.36 = (f32[4,8,256]{2,1,0:T(8,128)S(1)}, f32[4,8,256]{2,1,0:T(8,128)S(1)}, u32[]{:S(2)}, u32[]{:S(2)}) collective-permute-start(f32[4,8,256]{2,1,0:T(8,128)S(1)} %slice.155), channel_id=1, source_target_pairs={{0,14},{2,12},{4,10},{6,8},{8,6},{10,4},{12,2},{14,0},{1,15},{3,13... | collective-permute-start | bytes 98312 | tf_op jit(solution)/shard_map/ppermute | solution.py:1160
  276.4 33.2 %collective-permute-start.38 = (bf16[512,1024]{1,0:T(8,128)(2,1)}, bf16[512,1024]{1,0:T(8,128)(2,1)S(1)}, u32[]{:S(2)}, u32[]{:S(2)}) collective-permute-start(bf16[512,1024]{1,0:T(8,128)(2,1)} %get-tuple-element.256), channel_id=1, source_target_pairs={{0,2},{2,0},{4,6},{6,4},{8,10},{10,8},{12,14},{14,12},{1,3},{3,1},... | collective-permute-start | bytes 3145736 | tf_op jit(solution)/shard_map/ppermute | solution.py:893
  276.4 39.3 %collective-permute-start.37 = (bf16[512,1024]{1,0:T(8,128)(2,1)S(1)}, bf16[512,1024]{1,0:T(8,128)(2,1)S(1)}, u32[]{:S(2)}, u32[]{:S(2)}) collective-permute-start(bf16[512,1024]{1,0:T(8,128)(2,1)S(1)} %copy-done.24), channel_id=1, source_target_pairs={{0,1},{1,0},{2,3},{3,2},{4,5},{5,4},{6,7},{7,6},{8,9},{9,8},{10,11... | collective-permute-start | bytes 3145736 | tf_op jit(solution)/shard_map/ppermute | solution.py:893
  278.4 37.3 %collective-permute-start.39 = (bf16[256,1024]{1,0:T(8,128)(2,1)}, bf16[256,1024]{1,0:T(8,128)(2,1)}, u32[]{:S(2)}, u32[]{:S(2)}) collective-permute-start(bf16[256,1024]{1,0:T(8,128)(2,1)} %slice.156), channel_id=1, source_target_pairs={{0,14},{2,12},{4,10},{6,8},{8,6},{10,4},{12,2},{14,0},{1,15},{3,13... | collective-permute-start | bytes 1572872 | tf_op jit(solution)/shard_map/ppermute | solution.py:1160
  279.8 35.9 %collective-permute-start.40 = (f32[4,8,256]{2,1,0:T(8,128)S(1)}, f32[4,8,256]{2,1,0:T(8,128)S(1)}, u32[]{:S(2)}, u32[]{:S(2)}) collective-permute-start(f32[4,8,256]{2,1,0:T(8,128)S(1)} %slice.157), channel_id=1, source_target_pairs={{0,14},{2,12},{4,10},{6,8},{8,6},{10,4},{12,2},{14,0},{1,15},{3,13... | collective-permute-start | bytes 98312 | tf_op jit(solution)/shard_map/ppermute | solution.py:1160
  303.2 50.2 %collective-permute-start.42 = (bf16[2,512,512]{2,1,0:T(8,128)(2,1)}, bf16[2,512,512]{2,1,0:T(8,128)(2,1)S(1)}, u32[]{:S(2)}, u32[]{:S(2)}) collective-permute-start(bf16[2,512,512]{2,1,0:T(8,128)(2,1)} %get-tuple-element.267), channel_id=1, source_target_pairs={{0,2},{2,0},{4,6},{6,4},{8,10},{10,8},{12,14},{14,12},{1,3},{3,1},... | collective-permute-start | bytes 3145736 | tf_op jit(solution)/shard_map/ppermute | solution.py:893
  309.6 47.0 %collective-permute-start.41 = (bf16[512,1024]{1,0:T(8,128)(2,1)S(1)}, bf16[512,1024]{1,0:T(8,128)(2,1)}, u32[]{:S(2)}, u32[]{:S(2)}) collective-permute-start(bf16[512,1024]{1,0:T(8,128)(2,1)S(1)} %copy-done.26), channel_id=1, source_target_pairs={{0,1},{1,0},{2,3},{3,2},{4,5},{5,4},{6,7},{7,6},{8,9},{9,8},{10,11... | collective-permute-start | bytes 3145736 | tf_op jit(solution)/shard_map/ppermute | solution.py:893
  353.8 43.7 %collective-permute-start.48 = (bf16[2,512,512]{2,1,0:T(8,128)(2,1)S(1)}, bf16[2,512,512]{2,1,0:T(8,128)(2,1)S(1)}, u32[]{:S(2)}, u32[]{:S(2)}) collective-permute-start(bf16[2,512,512]{2,1,0:T(8,128)(2,1)S(1)} %add_convert_fusion.3), channel_id=1, source_target_pairs={{4,0},{6,2},{8,4},{10,6},{12,8},{14,10},{5,1},{7,3},{9,5},{11,7},{... | collective-permute-start | bytes 3145736 | tf_op jit(solution)/shard_map/ppermute | solution.py:898
  356.6 40.5 %collective-permute-start.47 = (bf16[2,512,512]{2,1,0:T(8,128)(2,1)}, bf16[2,512,512]{2,1,0:T(8,128)(2,1)S(1)}, u32[]{:S(2)}, u32[]{:S(2)}) collective-permute-start(bf16[2,512,512]{2,1,0:T(8,128)(2,1)} %get-tuple-element.280), channel_id=1, source_target_pairs={{0,2},{2,0},{4,6},{6,4},{8,10},{10,8},{12,14},{14,12},{1,3},{3,1},... | collective-permute-start | bytes 3145736 | tf_op jit(solution)/shard_map/ppermute | solution.py:893
  356.6 34.2 %collective-permute-start.44 = (bf16[128,1024]{1,0:T(8,128)(2,1)S(1)}, bf16[128,1024]{1,0:T(8,128)(2,1)}, u32[]{:S(2)}, u32[]{:S(2)}) collective-permute-start(bf16[128,1024]{1,0:T(8,128)(2,1)S(1)} %get-tuple-element.371), channel_id=1, source_target_pairs={{0,4},{2,6},{4,0},{6,2},{8,12},{10,14},{12,8},{14,10},{1,5},{3,7},... | collective-permute-start | bytes 786440 | tf_op jit(solution)/shard_map/ppermute | solution.py:893
  359.3 31.6 %collective-permute-start.45 = (bf16[128,1024]{1,0:T(8,128)(2,1)S(1)}, bf16[128,1024]{1,0:T(8,128)(2,1)S(1)}, u32[]{:S(2)}, u32[]{:S(2)}) collective-permute-start(bf16[128,1024]{1,0:T(8,128)(2,1)S(1)} %get-tuple-element.373), channel_id=1, source_target_pairs={{0,8},{2,10},{4,12},{6,14},{8,0},{10,2},{12,4},{14,6},{1,9},{3,11}... | collective-permute-start | bytes 786440 | tf_op jit(solution)/shard_map/ppermute | solution.py:893
  360.7 34.5 %collective-permute-start.46 = (bf16[128,1024]{1,0:T(8,128)(2,1)S(1)}, bf16[128,1024]{1,0:T(8,128)(2,1)S(1)}, u32[]{:S(2)}, u32[]{:S(2)}) collective-permute-start(bf16[128,1024]{1,0:T(8,128)(2,1)S(1)} %get-tuple-element.372), channel_id=1, source_target_pairs={{0,12},{2,14},{4,8},{6,10},{8,4},{10,6},{12,0},{14,2},{1,13},{3,15... | collective-permute-start | bytes 786440 | tf_op jit(solution)/shard_map/ppermute | solution.py:893
  390.9 26.0 %collective-permute-start.43 = (bf16[256,1024]{1,0:T(8,128)(2,1)}, bf16[256,1024]{1,0:T(8,128)(2,1)S(1)}, u32[]{:S(2)}, u32[]{:S(2)}) collective-permute-start(bf16[256,1024]{1,0:T(8,128)(2,1)} %get-tuple-element.275), channel_id=1, source_target_pairs={{0,14},{2,12},{4,10},{6,8},{8,6},{10,4},{12,2},{14,0},{1,15},{3,13... | collective-permute-start | bytes 1572872 | tf_op jit(solution)/shard_map/ppermute | solution.py:1160
  390.9 27.0 %collective-permute-start.50 = (bf16[2,512,512]{2,1,0:T(8,128)(2,1)}, bf16[2,512,512]{2,1,0:T(8,128)(2,1)S(1)}, u32[]{:S(2)}, u32[]{:S(2)}) collective-permute-start(bf16[2,512,512]{2,1,0:T(8,128)(2,1)} %get-tuple-element.291), channel_id=1, source_target_pairs={{0,2},{2,0},{4,6},{6,4},{8,10},{10,8},{12,14},{14,12},{1,3},{3,1},... | collective-permute-start | bytes 3145736 | tf_op jit(solution)/shard_map/ppermute | solution.py:893
  395.8 22.1 %collective-permute-start.49 = (bf16[2,512,512]{2,1,0:T(8,128)(2,1)}, bf16[2,512,512]{2,1,0:T(8,128)(2,1)S(1)}, u32[]{:S(2)}, u32[]{:S(2)}) collective-permute-start(bf16[2,512,512]{2,1,0:T(8,128)(2,1)} %get-tuple-element.288), channel_id=1, source_target_pairs={{0,2},{2,0},{4,6},{6,4},{8,10},{10,8},{12,14},{14,12},{1,3},{3,1},... | collective-permute-start | bytes 3145736 | tf_op jit(solution)/shard_map/ppermute | solution.py:893
  398.4 19.5 %collective-permute-start.52 = (bf16[512,512]{1,0:T(8,128)(2,1)S(1)}, bf16[512,512]{1,0:T(8,128)(2,1)}, u32[]{:S(2)}, u32[]{:S(2)}) collective-permute-start(bf16[512,512]{1,0:T(8,128)(2,1)S(1)} %get-tuple-element.369), channel_id=1, source_target_pairs={{0,8},{2,10},{4,12},{6,14},{8,0},{10,2},{12,4},{14,6},{1,9},{3,11}... | collective-permute-start | bytes 1572872 | tf_op jit(solution)/shard_map/ppermute | solution.py:893
  399.8 18.1 %collective-permute-start.51 = (bf16[512,512]{1,0:T(8,128)(2,1)}, bf16[512,512]{1,0:T(8,128)(2,1)}, u32[]{:S(2)}, u32[]{:S(2)}) collective-permute-start(bf16[512,512]{1,0:T(8,128)(2,1)} %get-tuple-element.370), channel_id=1, source_target_pairs={{0,4},{2,6},{4,0},{6,2},{8,12},{10,14},{12,8},{14,10},{1,5},{3,7},... | collective-permute-start | bytes 1572872 | tf_op jit(solution)/shard_map/ppermute | solution.py:893
  417.7 38.6 %collective-permute-start.53 = (bf16[2,512,512]{2,1,0:T(8,128)(2,1)}, bf16[2,512,512]{2,1,0:T(8,128)(2,1)S(1)}, u32[]{:S(2)}, u32[]{:S(2)}) collective-permute-start(bf16[2,512,512]{2,1,0:T(8,128)(2,1)} %get-tuple-element.307), channel_id=1, source_target_pairs={{0,2},{2,0},{4,6},{6,4},{8,10},{10,8},{12,14},{14,12},{1,3},{3,1},... | collective-permute-start | bytes 3145736 | tf_op jit(solution)/shard_map/ppermute | solution.py:893
  423.0 33.3 %collective-permute-start.54 = (bf16[2,512,512]{2,1,0:T(8,128)(2,1)}, bf16[2,512,512]{2,1,0:T(8,128)(2,1)S(1)}, u32[]{:S(2)}, u32[]{:S(2)}) collective-permute-start(bf16[2,512,512]{2,1,0:T(8,128)(2,1)} %get-tuple-element.295), channel_id=1, source_target_pairs={{0,4},{2,6},{4,0},{6,2},{8,12},{10,14},{12,8},{14,10},{1,5},{3,7},... | collective-permute-start | bytes 3145736 | tf_op jit(solution)/shard_map/ppermute | solution.py:893
  425.1 31.2 %collective-permute-start.55 = (bf16[2,512,512]{2,1,0:T(8,128)(2,1)}, bf16[2,512,512]{2,1,0:T(8,128)(2,1)S(1)}, u32[]{:S(2)}, u32[]{:S(2)}) collective-permute-start(bf16[2,512,512]{2,1,0:T(8,128)(2,1)} %get-tuple-element.308), channel_id=1, source_target_pairs={{0,8},{2,10},{4,12},{6,14},{8,0},{10,2},{12,4},{14,6},{1,9},{3,11}... | collective-permute-start | bytes 3145736 | tf_op jit(solution)/shard_map/ppermute | solution.py:893
  454.5 12.3 %collective-permute-start.56 = (bf16[512,1024]{1,0:T(8,128)(2,1)}, bf16[512,1024]{1,0:T(8,128)(2,1)S(1)}, u32[]{:S(2)}, u32[]{:S(2)}) collective-permute-start(bf16[512,1024]{1,0:T(8,128)(2,1)} %get-tuple-element.311), channel_id=1, source_target_pairs={{0,2},{2,0},{4,6},{6,4},{8,10},{10,8},{12,14},{14,12},{1,3},{3,1},... | collective-permute-start | bytes 3145736 | tf_op jit(solution)/shard_map/ppermute | solution.py:893
  454.5 29.1 %collective-permute-start.58 = (bf16[512,1024]{1,0:T(8,128)(2,1)}, bf16[512,1024]{1,0:T(8,128)(2,1)}, u32[]{:S(2)}, u32[]{:S(2)}) collective-permute-start(bf16[512,1024]{1,0:T(8,128)(2,1)} %get-tuple-element.302.own_ref), channel_id=1, source_target_pairs={{0,1},{1,0},{2,3},{3,2},{4,5},{5,4},{6,7},{7,6},{8,9},{9,8},{10,11... | collective-permute-start | bytes 3145736 | tf_op jit(solution)/shard_map/ppermute | solution.py:893
  469.8 19.3 %collective-permute-start.61 = (bf16[64,1024]{1,0:T(8,128)(2,1)S(1)}, bf16[64,1024]{1,0:T(8,128)(2,1)S(1)}, u32[]{:S(2)}, u32[]{:S(2)}) collective-permute-start(bf16[64,1024]{1,0:T(8,128)(2,1)S(1)} %slice.207), channel_id=1, source_target_pairs={{0,16},{16,0},{1,17},{17,1},{2,18},{18,2},{3,19},{19,3},{4,20},{20... | collective-permute-start | bytes 393224 | tf_op jit(solution)/shard_map/ppermute | solution.py:893
  471.0 37.6 %collective-permute-start.66 = (bf16[512,1024]{1,0:T(8,128)(2,1)S(1)}, bf16[512,1024]{1,0:T(8,128)(2,1)}, u32[]{:S(2)}, u32[]{:S(2)}) collective-permute-start(bf16[512,1024]{1,0:T(8,128)(2,1)S(1)} %copy-done.57), channel_id=1, source_target_pairs={{0,1},{1,0},{2,3},{3,2},{4,5},{5,4},{6,7},{7,6},{8,9},{9,8},{10,11... | collective-permute-start | bytes 3145736 | tf_op jit(solution)/shard_map/ppermute | solution.py:893
  478.4 13.6 %collective-permute-start.57 = (bf16[512,1024]{1,0:T(8,128)(2,1)}, bf16[512,1024]{1,0:T(8,128)(2,1)S(1)}, u32[]{:S(2)}, u32[]{:S(2)}) collective-permute-start(bf16[512,1024]{1,0:T(8,128)(2,1)} %get-tuple-element.316), channel_id=1, source_target_pairs={{0,2},{2,0},{4,6},{6,4},{8,10},{10,8},{12,14},{14,12},{1,3},{3,1},... | collective-permute-start | bytes 3145736 | tf_op jit(solution)/shard_map/ppermute | solution.py:893
  478.6 13.4 %collective-permute-start.63 = (bf16[128,1024]{1,0:T(8,128)(2,1)S(1)}, bf16[128,1024]{1,0:T(8,128)(2,1)S(1)}, u32[]{:S(2)}, u32[]{:S(2)}) collective-permute-start(bf16[128,1024]{1,0:T(8,128)(2,1)S(1)} %pad_maximum_fusion.3), channel_id=1, source_target_pairs={{0,4},{2,6},{4,0},{6,2},{8,12},{10,14},{12,8},{14,10},{1,5},{3,7},... | collective-permute-start | bytes 786440 | tf_op jit(solution)/shard_map/ppermute | solution.py:893
  494.5 13.2 %collective-permute-start.69 = (bf16[64,1024]{1,0:T(8,128)(2,1)S(1)}, bf16[64,1024]{1,0:T(8,128)(2,1)S(1)}, u32[]{:S(2)}, u32[]{:S(2)}) collective-permute-start(bf16[64,1024]{1,0:T(8,128)(2,1)S(1)} %slice.216), channel_id=1, source_target_pairs={{0,16},{16,0},{1,17},{17,1},{2,18},{18,2},{3,19},{19,3},{4,20},{20... | collective-permute-start | bytes 393224 | tf_op jit(solution)/shard_map/ppermute | solution.py:893
  500.9 12.4 %collective-permute-start.70 = (f32[1,256]{1,0:T(1,128)S(1)}, f32[1,256]{1,0:T(1,128)S(1)}, u32[]{:S(2)}, u32[]{:S(2)}) collective-permute-start(f32[1,256]{1,0:T(1,128)S(1)} %pad_maximum_fusion.8), channel_id=1, source_target_pairs={{0,1},{1,0},{2,3},{3,2},{4,5},{5,4},{6,7},{7,6},{8,9},{9,8},{10,11... | collective-permute-start | bytes 3080 | tf_op jit(solution)/shard_map/ppermute | solution.py:893
  (99 other events, 937.5 us)
Sparse Core Ops, SparseCore 0:
  10.9 69.4 all-gather.2
  98.5 68.8 all-gather.4
  251.3 117.5 reduce-scatter.1

commit v9 on v6

--- a/solution.py
+++ b/solution.py
@@ -1051,33 +1051,30 @@
     out_low, out_high = slot_weight_grad(order, part, d_mixed, attended)
     out_p, out_c = after(out_p, out_low), after(out_c, out_low)
     out_got_p, out_got_c = swap(out_p, "tensor", 1), swap(out_c, "tensor", 1)
-    dq_c, _, g_halo = back_rows(1, (out_low,), {}, halos, None)
+    dq_c, g, g_halo = back_rows(1, (out_low,), pick(slots, far), halos, None, prior)
     out_grad = scatter_rows(out_low, out_high, dq_c)
-    if ctx_size == 8:
-        near_one = swap(g_halo[1], "ctx", 1)
-    dq_c, g, _ = back_rows(1, (dq_c, out_grad[0]), pick(slots, far), {}, dq_c, prior)
-    out_grad = scatter_more(out_grad, dq_c)
     zero = jnp.zeros((), BF)
     ready = ()
     if ctx_size == 8:
-        got7 = swap(g[7], "ctx", 1)
-        near_one = after(near_one, dq_c)
+        near_one, got7 = swap(g_halo[1], "ctx", 1), swap(g[7], "ctx", 1)
+    dq, prior, _ = back_rows(0, (dq_c, out_got_p, out_grad[0]), pick(slots, near + middle), {}, dq_p, None, None, True)
+    out_grad = scatter_more(out_grad, dq)
+    if ctx_size == 8:
+        g6 = add_low(g[6], after(got7, dq))
+        far_k, far_v = swap(g6[0], "ctx", 2), swap(g6[1], "ctx", 4)
+        near_one = after(near_one, dq)
         two_back = add_low(g_halo[2], jnp.where(odd, near_one, zero))
         halo_two = shift(two_back, -2)
         halo_near = jnp.where(odd, zero, near_one)
-        ready = (two_back, halo_near)
-    dq, prior, _ = back_rows(0, (dq_c, out_grad[0], *ready), pick(slots, near + middle), {}, dq_p, None, None, True)
-    if ctx_size == 8:
-        g6 = add_low(g[6], after(got7, dq))
-        far_k, far_v = swap(g6[0], "ctx", 2), swap(g6[1], "ctx", 4)
-        ready = (g6,)
-    out_grad = scatter_sum(out_grad, dq)
-    dq_c, more, _ = back_rows(1, (dq, out_grad[0], *ready), pick(slots, middle), {}, dq_c, prior)
+        ready = (g6, two_back, halo_near)
+    dq_c, more, _ = back_rows(1, (dq, out_got_p, out_got_c, *ready), pick(slots, middle), {}, dq_c, prior)
     g.update(more)
+    out_grad = scatter_sum(out_grad, dq_c)
+    ready = (out_grad[0],)
     if ctx_size == 8:
         got3, got5 = swap(g[3], "ctx", 1), swap(g[5], "ctx", 1)
-        ready = (halo_two,)
-    dq, more, _ = back_rows(1, (dq_c, out_got_p, out_got_c, *ready), pick(slots, near), {}, dq_c, prior, dq, True)
+        ready = (out_grad[0], halo_two)
+    dq, more, _ = back_rows(1, (dq_c, *ready), pick(slots, near), {}, dq_c, prior, dq, True)
     g.update(more)
     if ctx_size == 8:
         got1 = swap(g[1], "ctx", 1)

time: 545 us -> 546 us (level)
    pallas_call x34 -> x33, Pallas kernels: 297 us -> 293 us  [call(): pl.pallas_call(kernel, grid_spec=pltpu.PrefetchScalarGridSpec(num_scalar_...]
  transfers between devices with their start and end apart: 75 -> 75, of which waited for: 24 -> 23; matrix products, arithmetic and copies ran while one was open for 5% -> 5% of each run, Pallas kernels for 55% -> 54%
where the time goes in v9:
time: 546 us; the launch traced here: 536 us
  Pallas kernels  293 us (54%)
  starting transfers between devices  113 us (21%)
  waiting for transfers between devices  75.4 us (14%)
  local copies, waits for them, and re-layouts  18.5 us (3%)
  other arithmetic  16.4 us (3%)
  between operations  15.4 us (3%)
    pallas_call x33, Pallas kernels, call(): pl.pallas_call(kernel, grid_spec=pltpu.PrefetchScalarGridSpec(num_scalar_...  293 us
    ppermute x70, starting transfers between devices, swap(): return lax.ppermute(value, axis, [(i, i ^ bit) for i in range(size)])  107 us
    ppermute x70, waiting for transfers between devices, swap(): return lax.ppermute(value, axis, [(i, i ^ bit) for i in range(size)])  62.9 us
    ppermute x2, waiting for transfers between devices, shift(): lax.ppermute(value, 'ctx', [(i, i + by) for i in range(size) if 0 <= i +...  12.4 us
  transfers between devices with their start and end apart: 75, of which 23 were waited for; matrix products, arithmetic and copies ran while one was open for 5% of the time, Pallas kernels for 54%

profile of v9, /device:TPU:0, one launch (start us, length us, event | category | flops | bytes accessed | tf_op | source)
XLA Modules:
  0.0 536.1 jit_solution(16431348237194158645)
XLA Ops:
  10.8 3.7 collective-permute-start
  28.9 4.4 collective-permute-done.2.refs_3_
  37.3 3.7 fusion.5.x_ref
  47.5 5.0 collective-permute-done.7.refs_1_
  52.5 6.1 %collective-permute-done.10.refs_3_ = bf16[128,1024]{1,0:T(8,128)(2,1)S(1)} collective-permute-done((bf16[128,1024]{1,0:T(8,128)(2,1)S(1)}, bf16[128,1024]{1,0:T(8,128)(2,1)S(1)}, u32[]{:S(2)}, u32[]{:S(2)}) %collective-permute-start.10) | collective-permute-done | bytes 262176 | tf_op jit(solution)/shard_map/ppermute | solution.py:776
  59.5 5.6 %keys_values.2 = (bf16[1024,1024]{1,0:T(8,128)(2,1)}, bf16[2,512,512]{2,1,0:T(8,128)(2,1)}, f32[512,512]{1,0:T(8,128)}, bf16[1024,1024]{1,0:T(8,128)(2,1)}) custom-call(bf16[1024,1024]{1,0:T(8,128)(2,1)} %fusion.5.x_ref, f32[1,1024]{1,0:T(1,128)} %fusion.1.gain_ref, f32[1,128]{1,0:T(1,128)} %reshape.120.hgain_ref.gain_ref, ...), custom_call_target="tpu_custom_call" | custom-call | tf_op jit(solution)/shard_map/keys_values/pallas_call | solution.py:46
  68.6 5.7 %keys_values.3 = (bf16[1024,1024]{1,0:T(8,128)(2,1)}, bf16[2,512,512]{2,1,0:T(8,128)(2,1)}, f32[512,512]{1,0:T(8,128)}) custom-call(bf16[1024,1024]{1,0:T(8,128)(2,1)} %fusion.5.x_ref, f32[1,1024]{1,0:T(1,128)} %fusion.1.gain_ref, f32[1,128]{1,0:T(1,128)} %reshape.120.hgain_ref.gain_ref, ...), custom_call_target="tpu_custom_call", output_to_operand_aliasing={{0}: (6, {})} | custom-call | tf_op jit(solution)/shard_map/keys_values/pallas_call | solution.py:46
  75.2 6.9 %queries.2 = (bf16[512,1024]{1,0:T(8,128)(2,1)}, f32[1024,1024]{1,0:T(8,128)}, bf16[1024,1024]{1,0:T(8,128)(2,1)}) custom-call(bf16[1024,1024]{1,0:T(8,128)(2,1)} %get-tuple-element.199.normed_ref.left_ref, f32[1,128]{1,0:T(1,128)} %reshape.121.hgain_ref.gain_ref, f32[1024,128]{1,0:T(8,128)} %get-tuple-element.388.cos_ref, ...), custom_call_target="tpu_custom_call" | custom-call | tf_op jit(solution)/shard_map/queries/pallas_call | solution.py:46
  82.1 6.5 %queries.3 = (bf16[512,1024]{1,0:T(8,128)(2,1)}, f32[1024,1024]{1,0:T(8,128)}) custom-call(bf16[1024,1024]{1,0:T(8,128)(2,1)} %get-tuple-element.199.normed_ref.left_ref, f32[1,128]{1,0:T(1,128)} %reshape.121.hgain_ref.gain_ref, f32[1024,128]{1,0:T(8,128)} %get-tuple-element.388.cos_ref, ...), custom_call_target="tpu_custom_call", output_to_operand_aliasing={{1}: (5, {})} | custom-call | tf_op jit(solution)/shard_map/queries/pallas_call | solution.py:46
  93.8 4.3 collective-permute-start.29
  100.7 10.9 %attend.3 = (f32[512,1024]{1,0:T(8,128)}, f32[512,1024]{1,0:T(8,128)}) custom-call(s32[2]{0:T(128)} %pad_add_fusion.1.idx_ref, s32[512,128]{1,0:T(8,128)} %broadcast_in_dim.73.lo_ref, bf16[512,1024]{1,0:T(8,128)(2,1)} %get-tuple-element.205.refs_0_.q_ref, bf16[2,512,512]{2,1,0:T(8,128)(2,1)} %get-tuple-element.195.refs_1_.refs_0_, ...), custom_call_target="tpu_custom_call" | custom-call | tf_op jit(solution)/shard_map/attend/pallas_call | solution.py:46
  114.5 8.8 %attend.4 = (bf16[1024,1024]{1,0:T(8,128)(2,1)}, f32[4,8,512]{2,1,0:T(8,128)}) custom-call(s32[2]{0:T(128)} %pad_add_fusion.1.idx_ref, s32[512,128]{1,0:T(8,128)} %broadcast_in_dim.73.lo_ref, bf16[512,1024]{1,0:T(8,128)(2,1)} %get-tuple-element.209.refs_0_.q_ref, bf16[2,512,512]{2,1,0:T(8,128)(2,1)} %get-tuple-element.195.refs_1_.refs_0_, ...), custom_call_target="tpu_custom_call" | custom-call | tf_op jit(solution)/shard_map/attend/pallas_call | solution.py:46
  123.3 4.0 out_projection.2.own_ref
  127.3 12.4 %collective-permute-done.29.refs_9_.refs_5_ = bf16[2,512,512]{2,1,0:T(8,128)(2,1)} collective-permute-done((bf16[2,512,512]{2,1,0:T(8,128)(2,1)}, bf16[2,512,512]{2,1,0:T(8,128)(2,1)}, u32[]{:S(2)}, u32[]{:S(2)}) %collective-permute-start.29) | collective-permute-done | bytes 1048608 | tf_op jit(solution)/shard_map/ppermute | solution.py:781
  143.6 19.5 %attend.5 = (bf16[1024,1024]{1,0:T(8,128)(2,1)}, f32[4,8,512]{2,1,0:T(8,128)}) custom-call(s32[2]{0:T(128)} %pad_add_fusion.1.idx_ref, s32[512,128]{1,0:T(8,128)} %broadcast_in_dim.73.lo_ref, bf16[512,1024]{1,0:T(8,128)(2,1)} %get-tuple-element.205.refs_0_.q_ref, bf16[2,512,512]{2,1,0:T(8,128)(2,1)} %copy-done.2, ...), custom_call_target="tpu_custom_call", output_to_operand_aliasing={{0}: (15, {})} | custom-call | tf_op jit(solution)/shard_map/attend/pallas_call | solution.py:46
  163.1 3.9 out_projection.3.own_ref
  170.0 6.2 %collective-permute-done.32.got_ref = bf16[512,1024]{1,0:T(8,128)(2,1)S(1)} collective-permute-done((bf16[512,1024]{1,0:T(8,128)(2,1)S(1)}, bf16[512,1024]{1,0:T(8,128)(2,1)S(1)}, u32[]{:S(2)}, u32[]{:S(2)}) %collective-permute-start.32) | collective-permute-done | bytes 1048608 | tf_op jit(solution)/shard_map/ppermute | solution.py:776
  177.2 18.3 %feed_forward.2 = (f32[512,1024]{1,0:T(8,128)}, bf16[1024,1024]{1,0:T(8,128)(2,1)}, bf16[1024,1536]{1,0:T(8,128)(2,1)}, bf16[1024,3072]{1,0:T(8,128)(2,1)}, bf16...) custom-call(bf16[1024,1024]{1,0:T(8,128)(2,1)} %x_ref.7, bf16[512,1024]{1,0:T(8,128)(2,1)} %out_projection.2.own_ref, ...), custom_call_target="tpu_custom_call" | custom-call | tf_op jit(solution)/shard_map/feed_forward/pallas_call | solution.py:46
  198.8 18.5 %feed_forward.3 = (f32[512,1024]{1,0:T(8,128)}, bf16[1024,1024]{1,0:T(8,128)(2,1)}, bf16[1024,1536]{1,0:T(8,128)(2,1)}, bf16[1024,3072]{1,0:T(8,128)(2,1)}, bf16...) custom-call(bf16[1024,1024]{1,0:T(8,128)(2,1)} %x_ref.7, ...), custom_call_target="tpu_custom_call", output_to_operand_aliasing={{1}: (7, {}), {2}: (8, {}), {3}: (9, {})} | custom-call | tf_op jit(solution)/shard_map/feed_forward/pallas_call | solution.py:46
  217.4 10.8 %weight_grad.2.refs_0_ = bf16[1024,4608]{1,0:T(8,128)(2,1)} custom-call(bf16[1024,1024]{1,0:T(8,128)(2,1)} %get-tuple-element.238.left_ref, bf16[1024,3072]{1,0:T(8,128)(2,1)} %get-tuple-element.239.right_ref), custom_call_target="tpu_custom_call" | custom-call | tf_op jit(solution)/shard_map/weight_grad/pallas_call | solution.py:46
  228.1 7.2 %weight_grad.3 = bf16[1024,4608]{1,0:T(8,128)(2,1)} custom-call(bf16[1024,1024]{1,0:T(8,128)(2,1)} %dy_ref.7, bf16[1024,1536]{1,0:T(8,128)(2,1)} %get-tuple-element.237.right_ref, bf16[1024,4608]{1,0:T(8,128)(2,1)} %weight_grad.2.refs_0_), custom_call_target="tpu_custom_call", output_to_operand_aliasing={{}: (2, {})} | custom-call | tf_op jit(solution)/shard_map/weight_grad/pallas_call | solution.py:46
  236.3 7.2 %mixed_back.2 = (f32[512,1024]{1,0:T(8,128)}, bf16[1024,1024]{1,0:T(8,128)(2,1)}, bf16[512,1024]{1,0:T(8,128)(2,1)}, f32[4,8,512]{2,1,0:T(8,128)}, f32[1,1024]{1,0:T(1,128)}) custom-call(bf16[512,1024]{1,0:T(8,128)(2,1)} %get-tuple-element.228.own_ref, bf16[512,1024]{1,0:T(8,128)(2,1)} %copy-done.19, f32[512,1024]{1,0:T(8,128)} %get-tuple-element.328.resid_ref, ...), custom_call_target="tpu_custom_call" | custom-call | tf_op jit(solution)/shard_map/mixed_back/pallas_call | solution.py:46
  244.1 6.1 %attend_back.5 = (f32[512,1024]{1,0:T(8,128)}, bf16[2,512,512]{2,1,0:T(8,128)(2,1)}, bf16[2,512,512]{2,1,0:T(8,128)(2,1)}) custom-call(s32[2]{0:T(128)} %pad_add_fusion.1.idx_ref, bf16[512,1024]{1,0:T(8,128)(2,1)} %get-tuple-element.209.refs_0_.q_ref, bf16[512,1024]{1,0:T(8,128)(2,1)} %get-tuple-element.241.do_ref, f32[4,8,512]{2,1,0:T(8,128)} %get-tuple-element.243.lse_ref, ...), custom_call_target="tpu_custom_call" | custom-call | flops 300000000 | tf_op jit(solution)/shard_map/attend_back/pallas_call | solution.py:46
  251.3 7.8 %mixed_back.3 = (f32[512,1024]{1,0:T(8,128)}, bf16[1024,1024]{1,0:T(8,128)(2,1)}, bf16[512,1024]{1,0:T(8,128)(2,1)}, f32[4,8,512]{2,1,0:T(8,128)}, f32[1,1024]{1,0:T(1,128)}) custom-call(bf16[512,1024]{1,0:T(8,128)(2,1)} %get-tuple-element.235.own_ref, bf16[512,1024]{1,0:T(8,128)(2,1)} %copy-done.20, ...), custom_call_target="tpu_custom_call", output_to_operand_aliasing={{1}: (7, {})} | custom-call | tf_op jit(solution)/shard_map/mixed_back/pallas_call | solution.py:46
  259.1 6.4 %slot_weight_grad.1 = (bf16[512,1024]{1,0:T(8,128)(2,1)}, bf16[512,1024]{1,0:T(8,128)(2,1)}) custom-call(s32[1]{0:T(128)} %bitcast.10.part_ref, bf16[1024,1024]{1,0:T(8,128)(2,1)} %get-tuple-element.248.left_ref, bf16[1024,1024]{1,0:T(8,128)(2,1)} %get-tuple-element.223.att_ref.right_ref), custom_call_target="tpu_custom_call" | custom-call | tf_op jit(solution)/shard_map/slot_weight_grad/pallas_call | solution.py:46
  267.5 21.5 %attend_back.6 = (f32[512,1024]{1,0:T(8,128)}, bf16[2,512,512]{2,1,0:T(8,128)(2,1)}, bf16[2,512,512]{2,1,0:T(8,128)(2,1)}, bf16[2,512,512]{2,1,0:T(8,128)(2,1)},...) custom-call(s32[2]{0:T(128)} %pad_add_fusion.1.idx_ref, bf16[512,1024]{1,0:T(8,128)(2,1)} %get-tuple-element.205.refs_0_.q_ref, ...), custom_call_target="tpu_custom_call" | custom-call | flops 102000001024 | tf_op jit(solution)/shard_map/attend_back/pallas_call | solution.py:46
  289.0 6.4 %collective-permute-start.39 = (bf16[2,512,512]{2,1,0:T(8,128)(2,1)}, bf16[2,512,512]{2,1,0:T(8,128)(2,1)S(1)}, u32[]{:S(2)}, u32[]{:S(2)}) collective-permute-start(bf16[2,512,512]{2,1,0:T(8,128)(2,1)} %get-tuple-element.269), channel_id=1, source_target_pairs={{0,2},{2,0},{4,6},{6,4},{8,10},{10,8},{12,14},{14,12},{1,3},{3,1},... | collective-permute-start | bytes 3145736 | tf_op jit(solution)/shard_map/ppermute | solution.py:776
  296.2 9.9 %collective-permute-done.35.got_ref = bf16[512,1024]{1,0:T(8,128)(2,1)S(1)} collective-permute-done((bf16[512,1024]{1,0:T(8,128)(2,1)S(1)}, bf16[512,1024]{1,0:T(8,128)(2,1)S(1)}, u32[]{:S(2)}, u32[]{:S(2)}) %collective-permute-start.35) | collective-permute-done | bytes 1048608 | tf_op jit(solution)/shard_map/ppermute | solution.py:776
  308.3 13.5 %collective-permute-start.40 = (bf16[128,512]{1,0:T(8,128)(2,1)S(1)}, bf16[128,512]{1,0:T(8,128)(2,1)S(1)}, u32[]{:S(2)}, u32[]{:S(2)}) collective-permute-start(bf16[128,512]{1,0:T(8,128)(2,1)S(1)} %get-tuple-element.374), channel_id=1, source_target_pairs={{0,8},{2,10},{4,12},{6,14},{8,0},{10,2},{12,4},{14,6},{1,9},{3,11}... | collective-permute-start | bytes 393224 | tf_op jit(solution)/shard_map/ppermute | solution.py:776
  321.8 12.4 %attend_back.7 = (f32[1024,1024]{1,0:T(8,128)}, bf16[2,512,512]{2,1,0:T(8,128)(2,1)}, bf16[2,512,512]{2,1,0:T(8,128)(2,1)}, bf16[2,512,512]{2,1,0:T(8,128)(2,1)}...) custom-call(s32[2]{0:T(128)} %pad_add_fusion.1.idx_ref, ...), custom_call_target="tpu_custom_call" | custom-call | flops 120000004096 | tf_op jit(solution)/shard_map/attend_back/pallas_call | solution.py:46
  339.2 14.0 %collective-permute-start.49 = (bf16[512,512]{1,0:T(8,128)(2,1)S(1)}, bf16[512,512]{1,0:T(8,128)(2,1)}, u32[]{:S(2)}, u32[]{:S(2)}) collective-permute-start(bf16[512,512]{1,0:T(8,128)(2,1)S(1)} %get-tuple-element.369), channel_id=1, source_target_pairs={{0,8},{2,10},{4,12},{6,14},{8,0},{10,2},{12,4},{14,6},{1,9},{3,11}... | collective-permute-start | bytes 1572872 | tf_op jit(solution)/shard_map/ppermute | solution.py:776
  353.1 7.7 %collective-permute-start.48 = (bf16[512,512]{1,0:T(8,128)(2,1)}, bf16[512,512]{1,0:T(8,128)(2,1)}, u32[]{:S(2)}, u32[]{:S(2)}) collective-permute-start(bf16[512,512]{1,0:T(8,128)(2,1)} %get-tuple-element.370), channel_id=1, source_target_pairs={{0,4},{2,6},{4,0},{6,2},{8,12},{10,14},{12,8},{14,10},{1,5},{3,7},... | collective-permute-start | bytes 1572872 | tf_op jit(solution)/shard_map/ppermute | solution.py:776
  361.2 26.0 %attend_back.8 = (f32[512,1024]{1,0:T(8,128)}, bf16[2,512,512]{2,1,0:T(8,128)(2,1)}, bf16[2,512,512]{2,1,0:T(8,128)(2,1)}, bf16[2,512,512]{2,1,0:T(8,128)(2,1)}, bf16[2,512,512]{2,1,0:T(8,128)(2,1)}) custom-call(s32[2]{0:T(128)} %pad_add_fusion.1.idx_ref, bf16[512,1024]{1,0:T(8,128)(2,1)} %get-tuple-element.205.refs_0_.q_ref, ...), custom_call_target="tpu_custom_call" | custom-call | flops 83999997952 | tf_op jit(solution)/shard_map/attend_back/pallas_call | solution.py:46
  387.2 4.8 collective-permute-start.47
  394.3 15.1 %attend_back.9 = (f32[1024,1024]{1,0:T(8,128)}, bf16[2,512,512]{2,1,0:T(8,128)(2,1)}, bf16[2,512,512]{2,1,0:T(8,128)(2,1)}) custom-call(s32[2]{0:T(128)} %pad_add_fusion.1.idx_ref, bf16[512,1024]{1,0:T(8,128)(2,1)} %get-tuple-element.205.refs_0_.q_ref, bf16[512,1024]{1,0:T(8,128)(2,1)} %get-tuple-element.251.do_ref, ...), custom_call_target="tpu_custom_call", output_to_operand_aliasing={{0}: (11, {})} | custom-call | flops 48000000000 | tf_op jit(solution)/shard_map/attend_back/pallas_call | solution.py:46
  411.0 3.8 merge.1
  416.5 6.1 %collective-permute-start.52 = (bf16[2,512,512]{2,1,0:T(8,128)(2,1)}, bf16[2,512,512]{2,1,0:T(8,128)(2,1)S(1)}, u32[]{:S(2)}, u32[]{:S(2)}) collective-permute-start(bf16[2,512,512]{2,1,0:T(8,128)(2,1)} %get-tuple-element.308), channel_id=1, source_target_pairs={{0,8},{2,10},{4,12},{6,14},{8,0},{10,2},{12,4},{14,6},{1,9},{3,11}... | collective-permute-start | bytes 3145736 | tf_op jit(solution)/shard_map/ppermute | solution.py:776
  424.9 12.0 %q_back.1 = (bf16[1024,1024]{1,0:T(8,128)(2,1)}, f32[1024,1024]{1,0:T(8,128)}, f32[1,128]{1,0:T(1,128)}) custom-call(f32[1024,1024]{1,0:T(8,128)} %get-tuple-element.285.dq_ref, f32[1024,1024]{1,0:T(8,128)} %get-tuple-element.286.lin_ref, f32[1,128]{1,0:T(1,128)} %reshape.121.hgain_ref.gain_ref, f32[1024,128]{1,0:T(8,128)} %get-tuple-element.388.cos_ref, ...), custom_call_target="tpu_custom_call" | custom-call | tf_op jit(solution)/shard_map/q_back/pallas_call | solution.py:46
  436.9 8.5 %kv_back.2 = (bf16[1024,1024]{1,0:T(8,128)(2,1)}, bf16[512,1024]{1,0:T(8,128)(2,1)}, f32[1,128]{1,0:T(1,128)}) custom-call(f32[512,512]{1,0:T(8,128)} %get-tuple-element.298.lin_ref, f32[1,128]{1,0:T(1,128)} %reshape.120.hgain_ref.gain_ref, f32[1024,128]{1,0:T(8,128)} %get-tuple-element.388.cos_ref, f32[1024,128]{1,0:T(8,128)} %get-tuple-element.389.sin_ref, ...), custom_call_target="tpu_custom_call" | custom-call | tf_op jit(solution)/shard_map/kv_back/pallas_call | solution.py:46
  445.4 5.9 %weight_halves.2 = (bf16[512,1024]{1,0:T(8,128)(2,1)}, bf16[512,1024]{1,0:T(8,128)(2,1)}) custom-call(bf16[1024,1024]{1,0:T(8,128)(2,1)} %get-tuple-element.199.normed_ref.left_ref, bf16[1024,1024]{1,0:T(8,128)(2,1)} %get-tuple-element.303.right_ref), custom_call_target="tpu_custom_call" | custom-call | tf_op jit(solution)/shard_map/weight_halves/pallas_call | solution.py:46
  455.4 8.9 %kv_back.3 = (bf16[1024,1024]{1,0:T(8,128)(2,1)}, bf16[512,1024]{1,0:T(8,128)(2,1)}, f32[1,128]{1,0:T(1,128)}) custom-call(f32[512,512]{1,0:T(8,128)} %get-tuple-element.234.lin_ref, f32[1,128]{1,0:T(1,128)} %reshape.120.hgain_ref.gain_ref, f32[1024,128]{1,0:T(8,128)} %get-tuple-element.388.cos_ref, ...), custom_call_target="tpu_custom_call", output_to_operand_aliasing={{0}: (15, {})} | custom-call | flops 8999999488 | tf_op jit(solution)/shard_map/kv_back/pallas_call | solution.py:46
  467.7 5.8 %weight_halves.3 = (bf16[512,1024]{1,0:T(8,128)(2,1)}, bf16[512,1024]{1,0:T(8,128)(2,1)}) custom-call(bf16[1024,1024]{1,0:T(8,128)(2,1)} %get-tuple-element.199.normed_ref.left_ref, bf16[1024,1024]{1,0:T(8,128)(2,1)} %get-tuple-element.314.right_ref), custom_call_target="tpu_custom_call" | custom-call | tf_op jit(solution)/shard_map/weight_halves/pallas_call | solution.py:46
  478.1 4.3 tokens_back.2
  503.2 4.0 tokens_back.3
  508.1 3.4 collective-permute-start.69
  513.5 4.7 collective-permute-done.69
  518.4 3.6 collective-permute-done.70
  522.9 3.8 collective-permute-done.71
  (350 shorter events, 114.8 us)
Async XLA Ops:
  7.2 83.6 %all-gather.3.cloned.1.call-start = ((), (), s32[]{:S(2)}) async-start(), calls=%async_computation.1 | async-start | bytes 5570560 | tf_op jit(solution)/shard_map/all_gather | solution.py:897
  9.4 166.8 %all-gather.5.cloned.1.call-start = ((), (), s32[]{:S(2)}) async-start(), calls=%async_computation.2 | async-start | bytes 6684672 | tf_op jit(solution)/shard_map/all_gather | solution.py:1001
  21.6 11.7 %collective-permute-start.2 = (bf16[128,1024]{1,0:T(8,128)(2,1)S(1)}, bf16[128,1024]{1,0:T(8,128)(2,1)S(1)}, u32[]{:S(2)}, u32[]{:S(2)}) collective-permute-start(bf16[128,1024]{1,0:T(8,128)(2,1)S(1)} %pad_maximum_fusion.2.refs_0_), channel_id=1, source_target_pairs={{0,12},{2,14},{4,8},{6,10},{8,4},{10,6},{12,0},{14,2},{1,13},{3,15... | collective-permute-start | bytes 786440 | tf_op jit(solution)/shard_map/ppermute | solution.py:776
  26.8 14.2 %collective-permute-start.11 = (bf16[128,1024]{1,0:T(8,128)(2,1)S(1)}, bf16[128,1024]{1,0:T(8,128)(2,1)S(1)}, u32[]{:S(2)}, u32[]{:S(2)}) collective-permute-start(bf16[128,1024]{1,0:T(8,128)(2,1)S(1)} %pad_maximum_fusion.2.refs_0_), channel_id=1, source_target_pairs={{0,4},{2,6},{4,0},{6,2},{8,12},{10,14},{12,8},{14,10},{1,5},{3,7},... | collective-permute-start | bytes 786440 | tf_op jit(solution)/shard_map/ppermute | solution.py:776
  28.0 14.6 %collective-permute-start.12 = (bf16[128,1024]{1,0:T(8,128)(2,1)S(1)}, bf16[128,1024]{1,0:T(8,128)(2,1)S(1)}, u32[]{:S(2)}, u32[]{:S(2)}) collective-permute-start(bf16[128,1024]{1,0:T(8,128)(2,1)S(1)} %pad_maximum_fusion.2.refs_0_), channel_id=1, source_target_pairs={{0,8},{2,10},{4,12},{6,14},{8,0},{10,2},{12,4},{14,6},{1,9},{3,11}... | collective-permute-start | bytes 786440 | tf_op jit(solution)/shard_map/ppermute | solution.py:776
  33.3 11.3 %collective-permute-start.8 = (bf16[128,1024]{1,0:T(8,128)(2,1)S(1)}, bf16[128,1024]{1,0:T(8,128)(2,1)S(1)}, u32[]{:S(2)}, u32[]{:S(2)}) collective-permute-start(bf16[128,1024]{1,0:T(8,128)(2,1)S(1)} %collective-permute-done.2.refs_3_), channel_id=1, source_target_pairs={{0,2},{2,0},{4,6},{6,4},{8,10},{10,8},{12,14},{14,12},{1,3},{3,1},... | collective-permute-start | bytes 786440 | tf_op jit(solution)/shard_map/ppermute | solution.py:776
  41.0 11.5 %collective-permute-start.7 = (bf16[128,1024]{1,0:T(8,128)(2,1)S(1)}, bf16[128,1024]{1,0:T(8,128)(2,1)S(1)}, u32[]{:S(2)}, u32[]{:S(2)}) collective-permute-start(bf16[128,1024]{1,0:T(8,128)(2,1)S(1)} %constant_dynamic-update-slice_fusion.refs_0_), channel_id=1, source_target_pairs={{0,4},{2,6},{4,0},{6,2},{8,12},{10,14},{12,8},{14,10},{1,5},{3,7},... | collective-permute-start | bytes 786440 | tf_op jit(solution)/shard_map/ppermute | solution.py:776
  43.1 15.5 %collective-permute-start.10 = (bf16[128,1024]{1,0:T(8,128)(2,1)S(1)}, bf16[128,1024]{1,0:T(8,128)(2,1)S(1)}, u32[]{:S(2)}, u32[]{:S(2)}) collective-permute-start(bf16[128,1024]{1,0:T(8,128)(2,1)S(1)} %constant_dynamic-update-slice_fusion.refs_0_), channel_id=1, source_target_pairs={{0,12},{2,14},{4,8},{6,10},{8,4},{10,6},{12,0},{14,2},{1,13},{3,15... | collective-permute-start | bytes 786440 | tf_op jit(solution)/shard_map/ppermute | solution.py:776
  44.6 14.1 %collective-permute-start.14 = (bf16[128,1024]{1,0:T(8,128)(2,1)S(1)}, bf16[128,1024]{1,0:T(8,128)(2,1)S(1)}, u32[]{:S(2)}, u32[]{:S(2)}) collective-permute-start(bf16[128,1024]{1,0:T(8,128)(2,1)S(1)} %collective-permute-done.11.refs_1_), channel_id=1, source_target_pairs={{0,2},{2,0},{4,6},{6,4},{8,10},{10,8},{12,14},{14,12},{1,3},{3,1},... | collective-permute-start | bytes 786440 | tf_op jit(solution)/shard_map/ppermute | solution.py:776
  44.6 14.0 %collective-permute-start.15 = (bf16[128,1024]{1,0:T(8,128)(2,1)S(1)}, bf16[128,1024]{1,0:T(8,128)(2,1)S(1)}, u32[]{:S(2)}, u32[]{:S(2)}) collective-permute-start(bf16[128,1024]{1,0:T(8,128)(2,1)S(1)} %collective-permute-done.12.refs_2_), channel_id=1, source_target_pairs={{0,2},{2,0},{4,6},{6,4},{8,10},{10,8},{12,14},{14,12},{1,3},{3,1},... | collective-permute-start | bytes 786440 | tf_op jit(solution)/shard_map/ppermute | solution.py:776
  65.1 25.6 %collective-permute-start.21 = (bf16[2,512,512]{2,1,0:T(8,128)(2,1)}, bf16[2,512,512]{2,1,0:T(8,128)(2,1)S(1)}, u32[]{:S(2)}, u32[]{:S(2)}) collective-permute-start(bf16[2,512,512]{2,1,0:T(8,128)(2,1)} %get-tuple-element.195.refs_1_.refs_0_), channel_id=1, source_target_pairs={{0,8},{2,10},{4,12},{6,14},{8,0},{10,2},{12,4},{14,6},{1,9},{3,11}... | collective-permute-start | bytes 3145736 | tf_op jit(solution)/shard_map/ppermute | solution.py:776
  65.7 25.0 %collective-permute-start.16 = (bf16[2,512,512]{2,1,0:T(8,128)(2,1)}, bf16[2,512,512]{2,1,0:T(8,128)(2,1)S(1)}, u32[]{:S(2)}, u32[]{:S(2)}) collective-permute-start(bf16[2,512,512]{2,1,0:T(8,128)(2,1)} %get-tuple-element.195.refs_1_.refs_0_), channel_id=1, source_target_pairs={{0,4},{2,6},{4,0},{6,2},{8,12},{10,14},{12,8},{14,10},{1,5},{3,7},... | collective-permute-start | bytes 3145736 | tf_op jit(solution)/shard_map/ppermute | solution.py:776
  90.8 318.9 %reduce-scatter.2.cloned.1.call-start = ((), (), s32[]{:S(2)}) async-start(), calls=%async_computation.3 | async-start | bytes 10027008 | tf_op jit(solution)/shard_map/reduce_scatter | solution.py:1033
  90.9 20.6 %collective-permute-start.26 = (bf16[512,512]{1,0:T(8,128)(2,1)S(1)}, bf16[512,512]{1,0:T(8,128)(2,1)S(1)}, u32[]{:S(2)}, u32[]{:S(2)}) collective-permute-start(bf16[512,512]{1,0:T(8,128)(2,1)S(1)} %slice_bitcast_fusion.2), channel_id=1, source_target_pairs={{0,8},{2,10},{4,12},{6,14},{8,0},{10,2},{12,4},{14,6},{1,9},{3,11}... | collective-permute-start | bytes 1572872 | tf_op jit(solution)/shard_map/ppermute | solution.py:776
  92.5 19.2 %collective-permute-start.25 = (bf16[512,512]{1,0:T(8,128)(2,1)S(1)}, bf16[512,512]{1,0:T(8,128)(2,1)S(1)}, u32[]{:S(2)}, u32[]{:S(2)}) collective-permute-start(bf16[512,512]{1,0:T(8,128)(2,1)S(1)} %slice_bitcast_fusion.3), channel_id=1, source_target_pairs={{0,4},{2,6},{4,0},{6,2},{8,12},{10,14},{12,8},{14,10},{1,5},{3,7},... | collective-permute-start | bytes 1572872 | tf_op jit(solution)/shard_map/ppermute | solution.py:776
  93.1 21.3 %collective-permute-start.24 = (bf16[2,512,512]{2,1,0:T(8,128)(2,1)S(1)}, bf16[2,512,512]{2,1,0:T(8,128)(2,1)}, u32[]{:S(2)}, u32[]{:S(2)}) collective-permute-start(bf16[2,512,512]{2,1,0:T(8,128)(2,1)S(1)} %collective-permute-done.21.refs_4_.refs_2_.refs_3_.refs_1_), channel_id=1, source_target_pairs={{0,2},{2,0},{4,6},{6,4},{8,10},{10,8},{12,14},{14,12},{1,3},{3,1},... | collective-permute-start | bytes 3145736 | tf_op jit(solution)/shard_map/ppermute | solution.py:776
  93.2 21.3 %collective-permute-start.23 = (bf16[2,512,512]{2,1,0:T(8,128)(2,1)S(1)}, bf16[2,512,512]{2,1,0:T(8,128)(2,1)}, u32[]{:S(2)}, u32[]{:S(2)}) collective-permute-start(bf16[2,512,512]{2,1,0:T(8,128)(2,1)S(1)} %collective-permute-done.16.refs_3_.refs_1_.refs_2_.refs_0_), channel_id=1, source_target_pairs={{0,2},{2,0},{4,6},{6,4},{8,10},{10,8},{12,14},{14,12},{1,3},{3,1},... | collective-permute-start | bytes 3145736 | tf_op jit(solution)/shard_map/ppermute | solution.py:776
  93.8 46.0 %collective-permute-start.29 = (bf16[2,512,512]{2,1,0:T(8,128)(2,1)}, bf16[2,512,512]{2,1,0:T(8,128)(2,1)}, u32[]{:S(2)}, u32[]{:S(2)}) collective-permute-start(bf16[2,512,512]{2,1,0:T(8,128)(2,1)} %get-tuple-element.220.refs_3_.refs_4_), channel_id=1, source_target_pairs={{0,4},{2,6},{4,8},{6,10},{8,12},{10,14},{1,5},{3,7},{5,9},{7,11},{... | collective-permute-start | bytes 3145736 | tf_op jit(solution)/shard_map/ppermute | solution.py:781
  140.0 36.2 %collective-permute-start.32 = (bf16[512,1024]{1,0:T(8,128)(2,1)S(1)}, bf16[512,1024]{1,0:T(8,128)(2,1)S(1)}, u32[]{:S(2)}, u32[]{:S(2)}) collective-permute-start(bf16[512,1024]{1,0:T(8,128)(2,1)S(1)} %copy-done.11), channel_id=1, source_target_pairs={{0,1},{1,0},{2,3},{3,2},{4,5},{5,4},{6,7},{7,6},{8,9},{9,8},{10,11... | collective-permute-start | bytes 3145736 | tf_op jit(solution)/shard_map/ppermute | solution.py:776
  167.0 31.8 %collective-permute-start.31 = (bf16[512,1024]{1,0:T(8,128)(2,1)}, bf16[512,1024]{1,0:T(8,128)(2,1)}, u32[]{:S(2)}, u32[]{:S(2)}) collective-permute-start(bf16[512,1024]{1,0:T(8,128)(2,1)} %out_projection.3.own_ref), channel_id=1, source_target_pairs={{0,1},{1,0},{2,3},{3,2},{4,5},{5,4},{6,7},{7,6},{8,9},{9,8},{10,11... | collective-permute-start | bytes 3145736 | tf_op jit(solution)/shard_map/ppermute | solution.py:776
  195.5 39.9 %collective-permute-start.34 = (bf16[512,1024]{1,0:T(8,128)(2,1)}, bf16[512,1024]{1,0:T(8,128)(2,1)S(1)}, u32[]{:S(2)}, u32[]{:S(2)}) collective-permute-start(bf16[512,1024]{1,0:T(8,128)(2,1)} %get-tuple-element.228.own_ref), channel_id=1, source_target_pairs={{0,1},{1,0},{2,3},{3,2},{4,5},{5,4},{6,7},{7,6},{8,9},{9,8},{10,11... | collective-permute-start | bytes 3145736 | tf_op jit(solution)/shard_map/ppermute | solution.py:776
  217.3 33.0 %collective-permute-start.33 = (bf16[512,1024]{1,0:T(8,128)(2,1)}, bf16[512,1024]{1,0:T(8,128)(2,1)S(1)}, u32[]{:S(2)}, u32[]{:S(2)}) collective-permute-start(bf16[512,1024]{1,0:T(8,128)(2,1)} %get-tuple-element.235.own_ref), channel_id=1, source_target_pairs={{0,1},{1,0},{2,3},{3,2},{4,5},{5,4},{6,7},{7,6},{8,9},{9,8},{10,11... | collective-permute-start | bytes 3145736 | tf_op jit(solution)/shard_map/ppermute | solution.py:776
  265.6 30.2 %collective-permute-start.36 = (bf16[512,1024]{1,0:T(8,128)(2,1)}, bf16[512,1024]{1,0:T(8,128)(2,1)S(1)}, u32[]{:S(2)}, u32[]{:S(2)}) collective-permute-start(bf16[512,1024]{1,0:T(8,128)(2,1)} %get-tuple-element.259), channel_id=1, source_target_pairs={{0,2},{2,0},{4,6},{6,4},{8,10},{10,8},{12,14},{14,12},{1,3},{3,1},... | collective-permute-start | bytes 3145736 | tf_op jit(solution)/shard_map/ppermute | solution.py:776
  265.6 40.6 %collective-permute-start.35 = (bf16[512,1024]{1,0:T(8,128)(2,1)S(1)}, bf16[512,1024]{1,0:T(8,128)(2,1)S(1)}, u32[]{:S(2)}, u32[]{:S(2)}) collective-permute-start(bf16[512,1024]{1,0:T(8,128)(2,1)S(1)} %copy-done.25), channel_id=1, source_target_pairs={{0,1},{1,0},{2,3},{3,2},{4,5},{5,4},{6,7},{7,6},{8,9},{9,8},{10,11... | collective-permute-start | bytes 3145736 | tf_op jit(solution)/shard_map/ppermute | solution.py:776
  289.0 45.2 %collective-permute-start.39 = (bf16[2,512,512]{2,1,0:T(8,128)(2,1)}, bf16[2,512,512]{2,1,0:T(8,128)(2,1)S(1)}, u32[]{:S(2)}, u32[]{:S(2)}) collective-permute-start(bf16[2,512,512]{2,1,0:T(8,128)(2,1)} %get-tuple-element.269), channel_id=1, source_target_pairs={{0,2},{2,0},{4,6},{6,4},{8,10},{10,8},{12,14},{14,12},{1,3},{3,1},... | collective-permute-start | bytes 3145736 | tf_op jit(solution)/shard_map/ppermute | solution.py:776
  295.4 38.9 %collective-permute-start.38 = (bf16[2,512,512]{2,1,0:T(8,128)(2,1)}, bf16[2,512,512]{2,1,0:T(8,128)(2,1)S(1)}, u32[]{:S(2)}, u32[]{:S(2)}) collective-permute-start(bf16[2,512,512]{2,1,0:T(8,128)(2,1)} %get-tuple-element.266), channel_id=1, source_target_pairs={{0,2},{2,0},{4,6},{6,4},{8,10},{10,8},{12,14},{14,12},{1,3},{3,1},... | collective-permute-start | bytes 3145736 | tf_op jit(solution)/shard_map/ppermute | solution.py:776
  295.4 43.7 %collective-permute-start.37 = (bf16[512,1024]{1,0:T(8,128)(2,1)}, bf16[512,1024]{1,0:T(8,128)(2,1)}, u32[]{:S(2)}, u32[]{:S(2)}) collective-permute-start(bf16[512,1024]{1,0:T(8,128)(2,1)} %get-tuple-element.264.own_ref), channel_id=1, source_target_pairs={{0,1},{1,0},{2,3},{3,2},{4,5},{5,4},{6,7},{7,6},{8,9},{9,8},{10,11... | collective-permute-start | bytes 3145736 | tf_op jit(solution)/shard_map/ppermute | solution.py:776
  306.2 54.7 %collective-permute-start.41 = (bf16[128,512]{1,0:T(8,128)(2,1)S(1)}, bf16[128,512]{1,0:T(8,128)(2,1)S(1)}, u32[]{:S(2)}, u32[]{:S(2)}) collective-permute-start(bf16[128,512]{1,0:T(8,128)(2,1)S(1)} %get-tuple-element.373), channel_id=1, source_target_pairs={{0,4},{2,6},{4,0},{6,2},{8,12},{10,14},{12,8},{14,10},{1,5},{3,7},... | collective-permute-start | bytes 393224 | tf_op jit(solution)/shard_map/ppermute | solution.py:776
  308.3 52.6 %collective-permute-start.40 = (bf16[128,512]{1,0:T(8,128)(2,1)S(1)}, bf16[128,512]{1,0:T(8,128)(2,1)S(1)}, u32[]{:S(2)}, u32[]{:S(2)}) collective-permute-start(bf16[128,512]{1,0:T(8,128)(2,1)S(1)} %get-tuple-element.374), channel_id=1, source_target_pairs={{0,8},{2,10},{4,12},{6,14},{8,0},{10,2},{12,4},{14,6},{1,9},{3,11}... | collective-permute-start | bytes 393224 | tf_op jit(solution)/shard_map/ppermute | solution.py:776
  335.5 56.8 %collective-permute-start.44 = (bf16[2,512,512]{2,1,0:T(8,128)(2,1)}, bf16[2,512,512]{2,1,0:T(8,128)(2,1)S(1)}, u32[]{:S(2)}, u32[]{:S(2)}) collective-permute-start(bf16[2,512,512]{2,1,0:T(8,128)(2,1)} %add_convert_fusion.2), channel_id=1, source_target_pairs={{4,0},{6,2},{8,4},{10,6},{12,8},{14,10},{5,1},{7,3},{9,5},{11,7},{... | collective-permute-start | bytes 3145736 | tf_op jit(solution)/shard_map/ppermute | solution.py:781
  339.2 70.5 %collective-permute-start.49 = (bf16[512,512]{1,0:T(8,128)(2,1)S(1)}, bf16[512,512]{1,0:T(8,128)(2,1)}, u32[]{:S(2)}, u32[]{:S(2)}) collective-permute-start(bf16[512,512]{1,0:T(8,128)(2,1)S(1)} %get-tuple-element.369), channel_id=1, source_target_pairs={{0,8},{2,10},{4,12},{6,14},{8,0},{10,2},{12,4},{14,6},{1,9},{3,11}... | collective-permute-start | bytes 1572872 | tf_op jit(solution)/shard_map/ppermute | solution.py:776
  353.1 56.5 %collective-permute-start.48 = (bf16[512,512]{1,0:T(8,128)(2,1)}, bf16[512,512]{1,0:T(8,128)(2,1)}, u32[]{:S(2)}, u32[]{:S(2)}) collective-permute-start(bf16[512,512]{1,0:T(8,128)(2,1)} %get-tuple-element.370), channel_id=1, source_target_pairs={{0,4},{2,6},{4,0},{6,2},{8,12},{10,14},{12,8},{14,10},{1,5},{3,7},... | collective-permute-start | bytes 1572872 | tf_op jit(solution)/shard_map/ppermute | solution.py:776
  361.0 26.2 %collective-permute-start.42 = (bf16[128,1024]{1,0:T(8,128)(2,1)S(1)}, bf16[128,1024]{1,0:T(8,128)(2,1)S(1)}, u32[]{:S(2)}, u32[]{:S(2)}) collective-permute-start(bf16[128,1024]{1,0:T(8,128)(2,1)S(1)} %pad_maximum_fusion.3), channel_id=1, source_target_pairs={{0,4},{2,6},{4,0},{6,2},{8,12},{10,14},{12,8},{14,10},{1,5},{3,7},... | collective-permute-start | bytes 786440 | tf_op jit(solution)/shard_map/ppermute | solution.py:776
  361.1 31.0 %collective-permute-start.43 = (bf16[128,1024]{1,0:T(8,128)(2,1)S(1)}, bf16[128,1024]{1,0:T(8,128)(2,1)S(1)}, u32[]{:S(2)}, u32[]{:S(2)}) collective-permute-start(bf16[128,1024]{1,0:T(8,128)(2,1)S(1)} %pad_maximum_fusion.4), channel_id=1, source_target_pairs={{0,8},{2,10},{4,12},{6,14},{8,0},{10,2},{12,4},{14,6},{1,9},{3,11}... | collective-permute-start | bytes 786440 | tf_op jit(solution)/shard_map/ppermute | solution.py:776
  387.2 22.4 %collective-permute-start.47 = (bf16[2,512,512]{2,1,0:T(8,128)(2,1)}, bf16[2,512,512]{2,1,0:T(8,128)(2,1)S(1)}, u32[]{:S(2)}, u32[]{:S(2)}) collective-permute-start(bf16[2,512,512]{2,1,0:T(8,128)(2,1)} %get-tuple-element.291), channel_id=1, source_target_pairs={{0,2},{2,0},{4,6},{6,4},{8,10},{10,8},{12,14},{14,12},{1,3},{3,1},... | collective-permute-start | bytes 3145736 | tf_op jit(solution)/shard_map/ppermute | solution.py:776
  392.1 17.6 %collective-permute-start.45 = (bf16[2,512,512]{2,1,0:T(8,128)(2,1)}, bf16[2,512,512]{2,1,0:T(8,128)(2,1)S(1)}, u32[]{:S(2)}, u32[]{:S(2)}) collective-permute-start(bf16[2,512,512]{2,1,0:T(8,128)(2,1)} %get-tuple-element.288), channel_id=1, source_target_pairs={{0,2},{2,0},{4,6},{6,4},{8,10},{10,8},{12,14},{14,12},{1,3},{3,1},... | collective-permute-start | bytes 3145736 | tf_op jit(solution)/shard_map/ppermute | solution.py:776
  392.3 17.1 %collective-permute-start.46 = (bf16[64,1024]{1,0:T(8,128)(2,1)S(1)}, bf16[64,1024]{1,0:T(8,128)(2,1)S(1)}, u32[]{:S(2)}, u32[]{:S(2)}) collective-permute-start(bf16[64,1024]{1,0:T(8,128)(2,1)S(1)} %slice.202), channel_id=1, source_target_pairs={{0,16},{16,0},{1,17},{17,1},{2,18},{18,2},{3,19},{19,3},{4,20},{20... | collective-permute-start | bytes 393224 | tf_op jit(solution)/shard_map/ppermute | solution.py:776
  409.4 44.3 %collective-permute-start.50 = (bf16[2,512,512]{2,1,0:T(8,128)(2,1)}, bf16[2,512,512]{2,1,0:T(8,128)(2,1)S(1)}, u32[]{:S(2)}, u32[]{:S(2)}) collective-permute-start(bf16[2,512,512]{2,1,0:T(8,128)(2,1)} %get-tuple-element.307), channel_id=1, source_target_pairs={{0,2},{2,0},{4,6},{6,4},{8,10},{10,8},{12,14},{14,12},{1,3},{3,1},... | collective-permute-start | bytes 3145736 | tf_op jit(solution)/shard_map/ppermute | solution.py:776
  414.8 38.9 %collective-permute-start.51 = (bf16[2,512,512]{2,1,0:T(8,128)(2,1)}, bf16[2,512,512]{2,1,0:T(8,128)(2,1)S(1)}, u32[]{:S(2)}, u32[]{:S(2)}) collective-permute-start(bf16[2,512,512]{2,1,0:T(8,128)(2,1)} %get-tuple-element.295), channel_id=1, source_target_pairs={{0,4},{2,6},{4,0},{6,2},{8,12},{10,14},{12,8},{14,10},{1,5},{3,7},... | collective-permute-start | bytes 3145736 | tf_op jit(solution)/shard_map/ppermute | solution.py:776
  416.5 37.2 %collective-permute-start.52 = (bf16[2,512,512]{2,1,0:T(8,128)(2,1)}, bf16[2,512,512]{2,1,0:T(8,128)(2,1)S(1)}, u32[]{:S(2)}, u32[]{:S(2)}) collective-permute-start(bf16[2,512,512]{2,1,0:T(8,128)(2,1)} %get-tuple-element.308), channel_id=1, source_target_pairs={{0,8},{2,10},{4,12},{6,14},{8,0},{10,2},{12,4},{14,6},{1,9},{3,11}... | collective-permute-start | bytes 3145736 | tf_op jit(solution)/shard_map/ppermute | solution.py:776
  451.2 13.1 %collective-permute-start.53 = (bf16[512,1024]{1,0:T(8,128)(2,1)}, bf16[512,1024]{1,0:T(8,128)(2,1)S(1)}, u32[]{:S(2)}, u32[]{:S(2)}) collective-permute-start(bf16[512,1024]{1,0:T(8,128)(2,1)} %get-tuple-element.311), channel_id=1, source_target_pairs={{0,2},{2,0},{4,6},{6,4},{8,10},{10,8},{12,14},{14,12},{1,3},{3,1},... | collective-permute-start | bytes 3145736 | tf_op jit(solution)/shard_map/ppermute | solution.py:776
  451.3 26.8 %collective-permute-start.55 = (bf16[512,1024]{1,0:T(8,128)(2,1)}, bf16[512,1024]{1,0:T(8,128)(2,1)}, u32[]{:S(2)}, u32[]{:S(2)}) collective-permute-start(bf16[512,1024]{1,0:T(8,128)(2,1)} %get-tuple-element.302.own_ref), channel_id=1, source_target_pairs={{0,1},{1,0},{2,3},{3,2},{4,5},{5,4},{6,7},{7,6},{8,9},{9,8},{10,11... | collective-permute-start | bytes 3145736 | tf_op jit(solution)/shard_map/ppermute | solution.py:776
  467.6 35.6 %collective-permute-start.62 = (bf16[512,1024]{1,0:T(8,128)(2,1)S(1)}, bf16[512,1024]{1,0:T(8,128)(2,1)}, u32[]{:S(2)}, u32[]{:S(2)}) collective-permute-start(bf16[512,1024]{1,0:T(8,128)(2,1)S(1)} %copy-done.52), channel_id=1, source_target_pairs={{0,1},{1,0},{2,3},{3,2},{4,5},{5,4},{6,7},{7,6},{8,9},{9,8},{10,11... | collective-permute-start | bytes 3145736 | tf_op jit(solution)/shard_map/ppermute | solution.py:776
  473.6 11.1 %collective-permute-start.54 = (bf16[512,1024]{1,0:T(8,128)(2,1)}, bf16[512,1024]{1,0:T(8,128)(2,1)S(1)}, u32[]{:S(2)}, u32[]{:S(2)}) collective-permute-start(bf16[512,1024]{1,0:T(8,128)(2,1)} %get-tuple-element.316), channel_id=1, source_target_pairs={{0,2},{2,0},{4,6},{6,4},{8,10},{10,8},{12,14},{14,12},{1,3},{3,1},... | collective-permute-start | bytes 3145736 | tf_op jit(solution)/shard_map/ppermute | solution.py:776
  473.7 10.9 %collective-permute-start.59 = (bf16[128,1024]{1,0:T(8,128)(2,1)S(1)}, bf16[128,1024]{1,0:T(8,128)(2,1)S(1)}, u32[]{:S(2)}, u32[]{:S(2)}) collective-permute-start(bf16[128,1024]{1,0:T(8,128)(2,1)S(1)} %pad_maximum_fusion.5), channel_id=1, source_target_pairs={{0,4},{2,6},{4,0},{6,2},{8,12},{10,14},{12,8},{14,10},{1,5},{3,7},... | collective-permute-start | bytes 786440 | tf_op jit(solution)/shard_map/ppermute | solution.py:776
  487.4 14.9 %collective-permute-start.65 = (bf16[64,1024]{1,0:T(8,128)(2,1)S(1)}, bf16[64,1024]{1,0:T(8,128)(2,1)S(1)}, u32[]{:S(2)}, u32[]{:S(2)}) collective-permute-start(bf16[64,1024]{1,0:T(8,128)(2,1)S(1)} %slice.220), channel_id=1, source_target_pairs={{0,16},{16,0},{1,17},{17,1},{2,18},{18,2},{3,19},{19,3},{4,20},{20... | collective-permute-start | bytes 393224 | tf_op jit(solution)/shard_map/ppermute | solution.py:776
  491.0 12.1 %collective-permute-start.63 = (bf16[128,1024]{1,0:T(8,128)(2,1)S(1)}, bf16[128,1024]{1,0:T(8,128)(2,1)S(1)}, u32[]{:S(2)}, u32[]{:S(2)}) collective-permute-start(bf16[128,1024]{1,0:T(8,128)(2,1)S(1)} %pad_maximum_fusion.7), channel_id=1, source_target_pairs={{0,4},{2,6},{4,0},{6,2},{8,12},{10,14},{12,8},{14,10},{1,5},{3,7},... | collective-permute-start | bytes 786440 | tf_op jit(solution)/shard_map/ppermute | solution.py:776
  494.4 13.5 %collective-permute-start.66 = (f32[1,256]{1,0:T(1,128)S(1)}, f32[1,256]{1,0:T(1,128)S(1)}, u32[]{:S(2)}, u32[]{:S(2)}) collective-permute-start(f32[1,256]{1,0:T(1,128)S(1)} %pad_maximum_fusion.10), channel_id=1, source_target_pairs={{0,1},{1,0},{2,3},{3,2},{4,5},{5,4},{6,7},{7,6},{8,9},{9,8},{10,11... | collective-permute-start | bytes 3080 | tf_op jit(solution)/shard_map/ppermute | solution.py:776
  (88 other events, 815.5 us)
Sparse Core Ops, SparseCore 0:
  10.9 69.4 all-gather.2
  90.9 68.7 all-gather.4
  235.5 121.3 reduce-scatter.1

commit v10 on v8

--- a/solution.py
+++ b/solution.py
@@ -1079,6 +1079,7 @@
     q_pieces = gather_far(q_near, kv_c)
 
     def queries(half, gain, pieces, whole=None):
+        scratch = []
         mine = lambda f: (half, 0)
         ins = [
             (normed, (rows, model), mine), (gain, (1, HEAD_SIZE), once),
@@ -1092,13 +1093,16 @@
             (shaped((rows, q_cols), BF), (rows, q_cols), once),
             (shaped((2 * rows, q_cols), F32), (rows, q_cols), mine),
         ]
-        if len(pieces) > 1:
+        if len(pieces) > 1 and whole is not None:
             outs.append((shaped((model, q_cols), BF), (model, q_cols), once))
-        return call(functools.partial(q_kernel, heads, len(pieces)), "queries", (1,), ins, outs, keep=keep)
-
-    q_c, q_lin, *w_q = queries(1, gain_q, q_pieces)
+        elif len(pieces) > 1:
+            scratch = [pltpu.VMEM((model, q_cols), BF)]
+        kernel = functools.partial(q_kernel, heads, len(pieces))
+        return call(kernel, "queries", (1,), ins, outs, scratch, keep=keep)
+
+    q_c, q_lin = queries(1, gain_q, q_pieces)
+    q_p, q_lin, *w_q = queries(0, after(gain_q, q_c), q_pieces, q_lin)
     (w_q,) = w_q or q_pieces
-    q_p, q_lin = queries(0, after(gain_q, q_c), [w_q], q_lin)
 
     def pick(source, wanted):
         return {s: source[s] for s in source if s in wanted}

time: 551 us -> 551 us (level)
    unnamed x133 -> x125, local copies, waits for them, and re-layouts: 11.6 us -> 11.5 us
  transfers between devices with their start and end apart: 79 -> 79, of which waited for: 21 -> 24; matrix products, arithmetic and copies ran while one was open for 6% -> 6% of each run, Pallas kernels for 59% -> 59%
where the time goes in v10:
time: 551 us; the launch traced here: 542 us
  Pallas kernels  321 us (58%)
  starting transfers between devices  82.5 us (15%)
  waiting for transfers between devices  76.5 us (14%)
  local copies, waits for them, and re-layouts  24 us (4%)
  other arithmetic  17.9 us (3%)
  between operations  15 us (3%)
    pallas_call x32, Pallas kernels, call(): pl.pallas_call(kernel, grid_spec=pltpu.PrefetchScalarGridSpec(num_scalar_...  321 us
    ppermute x69, starting transfers between devices, swap(): return lax.ppermute(value, axis, [(i, i ^ bit) for i in range(size)])  72 us
    ppermute x69, waiting for transfers between devices, swap(): return lax.ppermute(value, axis, [(i, i ^ bit) for i in range(size)])  61.2 us
    ppermute x2, waiting for transfers between devices, shift(): lax.ppermute(value, 'ctx', [(i, i + by) for i in range(size) if 0 <= i +...  15.2 us
    unnamed x125, local copies, waits for them, and re-layouts  11.5 us
  transfers between devices with their start and end apart: 79, of which 24 were waited for; matrix products, arithmetic and copies ran while one was open for 6% of the time, Pallas kernels for 59%

profile of v10, /device:TPU:0, one launch (start us, length us, event | category | flops | bytes accessed | tf_op | source)
XLA Modules:
  0.0 541.7 jit_solution(11554338046982522665)
XLA Ops:
  10.8 3.7 collective-permute-start
  21.6 2.6 collective-permute-start.2
  28.9 4.4 collective-permute-done.2.refs_3_
  37.3 3.7 fusion.5.x_ref
  47.5 5.0 collective-permute-done.7.refs_1_
  52.5 6.1 %collective-permute-done.10.refs_3_ = bf16[128,1024]{1,0:T(8,128)(2,1)S(1)} collective-permute-done((bf16[128,1024]{1,0:T(8,128)(2,1)S(1)}, bf16[128,1024]{1,0:T(8,128)(2,1)S(1)}, u32[]{:S(2)}, u32[]{:S(2)}) %collective-permute-start.10) | collective-permute-done | bytes 262176 | tf_op jit(solution)/shard_map/ppermute | solution.py:893
  59.5 5.6 %keys_values.2 = (bf16[1024,1024]{1,0:T(8,128)(2,1)}, bf16[2,512,512]{2,1,0:T(8,128)(2,1)}, f32[512,512]{1,0:T(8,128)}, bf16[1024,1024]{1,0:T(8,128)(2,1)}) custom-call(bf16[1024,1024]{1,0:T(8,128)(2,1)} %fusion.5.x_ref, f32[1,1024]{1,0:T(1,128)} %fusion.1.gain_ref, f32[1,128]{1,0:T(1,128)} %reshape.120.hgain_ref.gain_ref, ...), custom_call_target="tpu_custom_call" | custom-call | tf_op jit(solution)/shard_map/keys_values/pallas_call | solution.py:46
  68.6 5.7 %keys_values.3 = (bf16[1024,1024]{1,0:T(8,128)(2,1)}, bf16[2,512,512]{2,1,0:T(8,128)(2,1)}, f32[512,512]{1,0:T(8,128)}) custom-call(bf16[1024,1024]{1,0:T(8,128)(2,1)} %fusion.5.x_ref, f32[1,1024]{1,0:T(1,128)} %fusion.1.gain_ref, f32[1,128]{1,0:T(1,128)} %reshape.120.hgain_ref.gain_ref, ...), custom_call_target="tpu_custom_call", output_to_operand_aliasing={{0}: (6, {})} | custom-call | tf_op jit(solution)/shard_map/keys_values/pallas_call | solution.py:46
  75.0 16.5 %queries.2 = (bf16[512,1024]{1,0:T(8,128)(2,1)}, f32[1024,1024]{1,0:T(8,128)}) custom-call(bf16[1024,1024]{1,0:T(8,128)(2,1)} %get-tuple-element.199.normed_ref.left_ref, f32[1,128]{1,0:T(1,128)} %reshape.121.hgain_ref.gain_ref, f32[1024,128]{1,0:T(8,128)} %get-tuple-element.385.cos_ref, f32[1024,128]{1,0:T(8,128)} %get-tuple-element.386.sin_ref, ...), custom_call_target="tpu_custom_call" | custom-call | tf_op jit(solution)/shard_map/queries/pallas_call | solution.py:46
  91.4 6.5 %queries.3 = (bf16[512,1024]{1,0:T(8,128)(2,1)}, f32[1024,1024]{1,0:T(8,128)}, bf16[1024,1024]{1,0:T(8,128)(2,1)}) custom-call(bf16[1024,1024]{1,0:T(8,128)(2,1)} %get-tuple-element.199.normed_ref.left_ref, f32[1,128]{1,0:T(1,128)} %reshape.121.hgain_ref.gain_ref, f32[1024,128]{1,0:T(8,128)} %get-tuple-element.385.cos_ref, ...), custom_call_target="tpu_custom_call", output_to_operand_aliasing={{1}: (12, {})} | custom-call | tf_op jit(solution)/shard_map/queries/pallas_call | solution.py:46
  107.3 10.8 %attend.3 = (f32[512,1024]{1,0:T(8,128)}, f32[512,1024]{1,0:T(8,128)}) custom-call(s32[2]{0:T(128)} %pad_add_fusion.1.idx_ref, s32[512,128]{1,0:T(8,128)} %broadcast_in_dim.73.lo_ref, bf16[512,1024]{1,0:T(8,128)(2,1)} %get-tuple-element.205.refs_0_.q_ref, bf16[2,512,512]{2,1,0:T(8,128)(2,1)} %get-tuple-element.195.refs_1_.refs_0_, ...), custom_call_target="tpu_custom_call" | custom-call | tf_op jit(solution)/shard_map/attend/pallas_call | solution.py:46
  121.1 8.8 %attend.4 = (bf16[1024,1024]{1,0:T(8,128)(2,1)}, f32[4,8,512]{2,1,0:T(8,128)}) custom-call(s32[2]{0:T(128)} %pad_add_fusion.1.idx_ref, s32[512,128]{1,0:T(8,128)} %broadcast_in_dim.73.lo_ref, bf16[512,1024]{1,0:T(8,128)(2,1)} %get-tuple-element.239.refs_0_.qa_ref, bf16[2,512,512]{2,1,0:T(8,128)(2,1)} %get-tuple-element.195.refs_1_.refs_0_, ...), custom_call_target="tpu_custom_call" | custom-call | tf_op jit(solution)/shard_map/attend/pallas_call | solution.py:46
  130.0 3.9 out_projection.2.own_ref
  133.9 15.2 %collective-permute-done.29.refs_9_.refs_5_ = bf16[2,512,512]{2,1,0:T(8,128)(2,1)S(1)} collective-permute-done((bf16[2,512,512]{2,1,0:T(8,128)(2,1)}, bf16[2,512,512]{2,1,0:T(8,128)(2,1)S(1)}, u32[]{:S(2)}, u32[]{:S(2)}) %collective-permute-start.29) | collective-permute-done | bytes 1048608 | tf_op jit(solution)/shard_map/ppermute | solution.py:898
  154.5 19.6 %attend.5 = (bf16[1024,1024]{1,0:T(8,128)(2,1)}, f32[4,8,512]{2,1,0:T(8,128)}) custom-call(s32[2]{0:T(128)} %pad_add_fusion.1.idx_ref, s32[512,128]{1,0:T(8,128)} %broadcast_in_dim.73.lo_ref, bf16[512,1024]{1,0:T(8,128)(2,1)} %get-tuple-element.205.refs_0_.q_ref, bf16[2,512,512]{2,1,0:T(8,128)(2,1)} %copy-done.2, ...), custom_call_target="tpu_custom_call", output_to_operand_aliasing={{0}: (15, {})} | custom-call | tf_op jit(solution)/shard_map/attend/pallas_call | solution.py:46
  174.0 3.9 out_projection.3.own_ref
  179.2 7.9 %collective-permute-done.32.got_ref = bf16[512,1024]{1,0:T(8,128)(2,1)} collective-permute-done((bf16[512,1024]{1,0:T(8,128)(2,1)S(1)}, bf16[512,1024]{1,0:T(8,128)(2,1)}, u32[]{:S(2)}, u32[]{:S(2)}) %collective-permute-start.32) | collective-permute-done | bytes 1048608 | tf_op jit(solution)/shard_map/ppermute | solution.py:893
  187.1 18.3 %feed_forward.2 = (f32[512,1024]{1,0:T(8,128)}, bf16[1024,1024]{1,0:T(8,128)(2,1)}, bf16[1024,1536]{1,0:T(8,128)(2,1)}, bf16[1024,3072]{1,0:T(8,128)(2,1)}, bf16...) custom-call(bf16[1024,1024]{1,0:T(8,128)(2,1)} %x_ref.7, bf16[512,1024]{1,0:T(8,128)(2,1)} %out_projection.2.own_ref, ...), custom_call_target="tpu_custom_call" | custom-call | tf_op jit(solution)/shard_map/feed_forward/pallas_call | solution.py:46
  205.5 4.0 collective-permute-done.31.got_ref
  210.5 18.8 %feed_forward.3 = (f32[512,1024]{1,0:T(8,128)}, bf16[1024,1024]{1,0:T(8,128)(2,1)}, bf16[1024,1536]{1,0:T(8,128)(2,1)}, bf16[1024,3072]{1,0:T(8,128)(2,1)}, bf16...) custom-call(bf16[1024,1024]{1,0:T(8,128)(2,1)} %x_ref.7, ...), custom_call_target="tpu_custom_call", output_to_operand_aliasing={{1}: (7, {}), {2}: (8, {}), {3}: (9, {})} | custom-call | tf_op jit(solution)/shard_map/feed_forward/pallas_call | solution.py:46
  232.8 10.8 %weight_grad.2.refs_0_ = bf16[1024,4608]{1,0:T(8,128)(2,1)} custom-call(bf16[1024,1024]{1,0:T(8,128)(2,1)} %get-tuple-element.237.left_ref, bf16[1024,3072]{1,0:T(8,128)(2,1)} %get-tuple-element.238.right_ref), custom_call_target="tpu_custom_call" | custom-call | tf_op jit(solution)/shard_map/weight_grad/pallas_call | solution.py:46
  243.6 7.1 %weight_grad.3 = bf16[1024,4608]{1,0:T(8,128)(2,1)} custom-call(bf16[1024,1024]{1,0:T(8,128)(2,1)} %dy_ref.7, bf16[1024,1536]{1,0:T(8,128)(2,1)} %get-tuple-element.236.right_ref, bf16[1024,4608]{1,0:T(8,128)(2,1)} %weight_grad.2.refs_0_), custom_call_target="tpu_custom_call", output_to_operand_aliasing={{}: (2, {})} | custom-call | tf_op jit(solution)/shard_map/weight_grad/pallas_call | solution.py:46
  251.9 7.2 %mixed_back.2 = (f32[512,1024]{1,0:T(8,128)}, bf16[1024,1024]{1,0:T(8,128)(2,1)}, bf16[512,1024]{1,0:T(8,128)(2,1)}, f32[4,8,512]{2,1,0:T(8,128)}, f32[1,1024]{1,0:T(1,128)}) custom-call(bf16[512,1024]{1,0:T(8,128)(2,1)} %get-tuple-element.227.own_ref, bf16[512,1024]{1,0:T(8,128)(2,1)} %copy-done.18, f32[512,1024]{1,0:T(8,128)} %get-tuple-element.328.resid_ref, ...), custom_call_target="tpu_custom_call" | custom-call | tf_op jit(solution)/shard_map/mixed_back/pallas_call | solution.py:46
  262.0 7.5 %mixed_back.3 = (f32[512,1024]{1,0:T(8,128)}, bf16[1024,1024]{1,0:T(8,128)(2,1)}, bf16[512,1024]{1,0:T(8,128)(2,1)}, f32[4,8,512]{2,1,0:T(8,128)}, f32[1,1024]{1,0:T(1,128)}) custom-call(bf16[512,1024]{1,0:T(8,128)(2,1)} %get-tuple-element.234.own_ref, bf16[512,1024]{1,0:T(8,128)(2,1)} %copy-done.19, ...), custom_call_target="tpu_custom_call", output_to_operand_aliasing={{1}: (7, {})} | custom-call | tf_op jit(solution)/shard_map/mixed_back/pallas_call | solution.py:46
  269.5 6.5 %slot_weight_grad.1 = (bf16[512,1024]{1,0:T(8,128)(2,1)}, bf16[512,1024]{1,0:T(8,128)(2,1)}) custom-call(s32[1]{0:T(128)} %bitcast.10.part_ref, bf16[1024,1024]{1,0:T(8,128)(2,1)} %get-tuple-element.246.left_ref, bf16[1024,1024]{1,0:T(8,128)(2,1)} %get-tuple-element.222.att_ref.right_ref), custom_call_target="tpu_custom_call" | custom-call | tf_op jit(solution)/shard_map/slot_weight_grad/pallas_call | solution.py:46
  281.3 21.5 %attend_back.3 = (f32[512,1024]{1,0:T(8,128)}, bf16[2,512,512]{2,1,0:T(8,128)(2,1)}, bf16[2,512,512]{2,1,0:T(8,128)(2,1)}, bf16[2,512,512]{2,1,0:T(8,128)(2,1)},...) custom-call(s32[2]{0:T(128)} %pad_add_fusion.1.idx_ref, bf16[512,1024]{1,0:T(8,128)(2,1)} %get-tuple-element.205.refs_0_.q_ref, ...), custom_call_target="tpu_custom_call" | custom-call | flops 102000001024 | tf_op jit(solution)/shard_map/attend_back/pallas_call | solution.py:46
  302.8 6.4 %collective-permute-start.42 = (bf16[2,512,512]{2,1,0:T(8,128)(2,1)}, bf16[2,512,512]{2,1,0:T(8,128)(2,1)S(1)}, u32[]{:S(2)}, u32[]{:S(2)}) collective-permute-start(bf16[2,512,512]{2,1,0:T(8,128)(2,1)} %get-tuple-element.266), channel_id=1, source_target_pairs={{0,2},{2,0},{4,6},{6,4},{8,10},{10,8},{12,14},{14,12},{1,3},{3,1},... | collective-permute-start | bytes 3145736 | tf_op jit(solution)/shard_map/ppermute | solution.py:893
  309.9 4.7 collective-permute-done.37.got_ref
  315.2 37.2 %prompt_back.1 = (f32[256,1024]{1,0:T(8,128)}, bf16[256,1024]{1,0:T(8,128)(2,1)}, bf16[2,512,512]{2,1,0:T(8,128)(2,1)}, bf16[2,512,512]{2,1,0:T(8,128)(2,1)}, bf...) custom-call(s32[2]{0:T(128)} %pad_add_fusion.1.idx_ref, ...), custom_call_target="tpu_custom_call" | custom-call | flops 48000000000 | tf_op jit(solution)/shard_map/prompt_back/pallas_call | solution.py:46
  355.6 4.6 collective-permute-start.44
  362.9 25.8 %attend_back.4 = (f32[512,1024]{1,0:T(8,128)}, bf16[2,512,512]{2,1,0:T(8,128)(2,1)}, bf16[2,512,512]{2,1,0:T(8,128)(2,1)}, bf16[2,512,512]{2,1,0:T(8,128)(2,1)}, bf16[2,512,512]{2,1,0:T(8,128)(2,1)}) custom-call(s32[2]{0:T(128)} %pad_add_fusion.1.idx_ref, bf16[512,1024]{1,0:T(8,128)(2,1)} %get-tuple-element.205.refs_0_.q_ref, ...), custom_call_target="tpu_custom_call" | custom-call | flops 83999997952 | tf_op jit(solution)/shard_map/attend_back/pallas_call | solution.py:46
  388.6 2.6 collective-permute-done.44
  396.4 5.0 collective-permute-start.52
  401.6 15.1 %attend_back.5 = (f32[512,1024]{1,0:T(8,128)}, bf16[2,512,512]{2,1,0:T(8,128)(2,1)}, bf16[2,512,512]{2,1,0:T(8,128)(2,1)}) custom-call(s32[2]{0:T(128)} %pad_add_fusion.1.idx_ref, bf16[512,1024]{1,0:T(8,128)(2,1)} %get-tuple-element.205.refs_0_.q_ref, bf16[512,1024]{1,0:T(8,128)(2,1)} %get-tuple-element.249.do_ref, f32[4,8,512]{2,1,0:T(8,128)} %get-tuple-element.250.lse_ref, ...), custom_call_target="tpu_custom_call" | custom-call | flops 48000000000 | tf_op jit(solution)/shard_map/attend_back/pallas_call | solution.py:46
  420.5 3.8 merge.1
  428.6 12.0 %q_back.1 = (bf16[1024,1024]{1,0:T(8,128)(2,1)}, f32[1024,1024]{1,0:T(8,128)}, f32[1,128]{1,0:T(1,128)}) custom-call(f32[256,1024]{1,0:T(8,128)} %get-tuple-element.261.dqa_ref, bf16[256,1024]{1,0:T(8,128)(2,1)} %copy-done.33, f32[512,1024]{1,0:T(8,128)} %get-tuple-element.284.dqc_ref, f32[1024,1024]{1,0:T(8,128)} %get-tuple-element.285.lin_ref, ...), custom_call_target="tpu_custom_call" | custom-call | tf_op jit(solution)/shard_map/q_back/pallas_call | solution.py:46
  440.6 8.6 %kv_back.2 = (bf16[1024,1024]{1,0:T(8,128)(2,1)}, bf16[512,1024]{1,0:T(8,128)(2,1)}, f32[1,128]{1,0:T(1,128)}) custom-call(f32[512,512]{1,0:T(8,128)} %get-tuple-element.298.lin_ref, f32[1,128]{1,0:T(1,128)} %reshape.120.hgain_ref.gain_ref, f32[1024,128]{1,0:T(8,128)} %get-tuple-element.385.cos_ref, f32[1024,128]{1,0:T(8,128)} %get-tuple-element.386.sin_ref, ...), custom_call_target="tpu_custom_call" | custom-call | tf_op jit(solution)/shard_map/kv_back/pallas_call | solution.py:46
  449.3 5.8 %weight_halves.2 = (bf16[512,1024]{1,0:T(8,128)(2,1)}, bf16[512,1024]{1,0:T(8,128)(2,1)}) custom-call(bf16[1024,1024]{1,0:T(8,128)(2,1)} %get-tuple-element.199.normed_ref.left_ref, bf16[1024,1024]{1,0:T(8,128)(2,1)} %get-tuple-element.303.right_ref), custom_call_target="tpu_custom_call" | custom-call | tf_op jit(solution)/shard_map/weight_halves/pallas_call | solution.py:46
  458.2 8.9 %kv_back.3 = (bf16[1024,1024]{1,0:T(8,128)(2,1)}, bf16[512,1024]{1,0:T(8,128)(2,1)}, f32[1,128]{1,0:T(1,128)}) custom-call(f32[512,512]{1,0:T(8,128)} %get-tuple-element.233.lin_ref, f32[1,128]{1,0:T(1,128)} %reshape.120.hgain_ref.gain_ref, f32[1024,128]{1,0:T(8,128)} %get-tuple-element.385.cos_ref, ...), custom_call_target="tpu_custom_call", output_to_operand_aliasing={{0}: (15, {})} | custom-call | flops 8999999488 | tf_op jit(solution)/shard_map/kv_back/pallas_call | solution.py:46
  473.5 5.8 %weight_halves.3 = (bf16[512,1024]{1,0:T(8,128)(2,1)}, bf16[512,1024]{1,0:T(8,128)(2,1)}) custom-call(bf16[1024,1024]{1,0:T(8,128)(2,1)} %get-tuple-element.199.normed_ref.left_ref, bf16[1024,1024]{1,0:T(8,128)(2,1)} %get-tuple-element.314.right_ref), custom_call_target="tpu_custom_call" | custom-call | tf_op jit(solution)/shard_map/weight_halves/pallas_call | solution.py:46
  481.1 3.1 collective-permute-done.58.got_ref
  485.6 4.1 tokens_back.2
  495.7 3.1 add_layer.2.refs_0_
  504.8 3.1 add_layer.3
  509.1 4.0 tokens_back.3
  513.9 3.3 collective-permute-start.73
  518.7 5.5 %collective-permute-done.73 = bf16[64,1024]{1,0:T(8,128)(2,1)S(1)} collective-permute-done((bf16[64,1024]{1,0:T(8,128)(2,1)S(1)}, bf16[64,1024]{1,0:T(8,128)(2,1)S(1)}, u32[]{:S(2)}, u32[]{:S(2)}) %collective-permute-start.73) | collective-permute-done | bytes 131104 | tf_op jit(solution)/shard_map/ppermute | solution.py:893
  528.7 3.8 collective-permute-done.75
  (364 shorter events, 119.0 us)
Async XLA Ops:
  7.2 90.8 %all-gather.3.cloned.1.call-start = ((), (), s32[]{:S(2)}) async-start(), calls=%async_computation.1 | async-start | bytes 5570560 | tf_op jit(solution)/shard_map/all_gather | solution.py:1022
  9.4 177.7 %all-gather.5.cloned.1.call-start = ((), (), s32[]{:S(2)}) async-start(), calls=%async_computation.2 | async-start | bytes 6684672 | tf_op jit(solution)/shard_map/all_gather | solution.py:1130
  21.6 11.7 %collective-permute-start.2 = (bf16[128,1024]{1,0:T(8,128)(2,1)S(1)}, bf16[128,1024]{1,0:T(8,128)(2,1)S(1)}, u32[]{:S(2)}, u32[]{:S(2)}) collective-permute-start(bf16[128,1024]{1,0:T(8,128)(2,1)S(1)} %pad_maximum_fusion.2.refs_0_), channel_id=1, source_target_pairs={{0,12},{2,14},{4,8},{6,10},{8,4},{10,6},{12,0},{14,2},{1,13},{3,15... | collective-permute-start | bytes 786440 | tf_op jit(solution)/shard_map/ppermute | solution.py:893
  26.8 14.2 %collective-permute-start.11 = (bf16[128,1024]{1,0:T(8,128)(2,1)S(1)}, bf16[128,1024]{1,0:T(8,128)(2,1)}, u32[]{:S(2)}, u32[]{:S(2)}) collective-permute-start(bf16[128,1024]{1,0:T(8,128)(2,1)S(1)} %pad_maximum_fusion.2.refs_0_), channel_id=1, source_target_pairs={{0,4},{2,6},{4,0},{6,2},{8,12},{10,14},{12,8},{14,10},{1,5},{3,7},... | collective-permute-start | bytes 786440 | tf_op jit(solution)/shard_map/ppermute | solution.py:893
  28.0 14.6 %collective-permute-start.12 = (bf16[128,1024]{1,0:T(8,128)(2,1)S(1)}, bf16[128,1024]{1,0:T(8,128)(2,1)}, u32[]{:S(2)}, u32[]{:S(2)}) collective-permute-start(bf16[128,1024]{1,0:T(8,128)(2,1)S(1)} %pad_maximum_fusion.2.refs_0_), channel_id=1, source_target_pairs={{0,8},{2,10},{4,12},{6,14},{8,0},{10,2},{12,4},{14,6},{1,9},{3,11}... | collective-permute-start | bytes 786440 | tf_op jit(solution)/shard_map/ppermute | solution.py:893
  43.1 15.5 %collective-permute-start.10 = (bf16[128,1024]{1,0:T(8,128)(2,1)S(1)}, bf16[128,1024]{1,0:T(8,128)(2,1)S(1)}, u32[]{:S(2)}, u32[]{:S(2)}) collective-permute-start(bf16[128,1024]{1,0:T(8,128)(2,1)S(1)} %constant_dynamic-update-slice_fusion.refs_0_), channel_id=1, source_target_pairs={{0,12},{2,14},{4,8},{6,10},{8,4},{10,6},{12,0},{14,2},{1,13},{3,15... | collective-permute-start | bytes 786440 | tf_op jit(solution)/shard_map/ppermute | solution.py:893
  44.6 14.1 %collective-permute-start.14 = (bf16[128,1024]{1,0:T(8,128)(2,1)}, bf16[128,1024]{1,0:T(8,128)(2,1)S(1)}, u32[]{:S(2)}, u32[]{:S(2)}) collective-permute-start(bf16[128,1024]{1,0:T(8,128)(2,1)} %collective-permute-done.11.refs_1_), channel_id=1, source_target_pairs={{0,2},{2,0},{4,6},{6,4},{8,10},{10,8},{12,14},{14,12},{1,3},{3,1},... | collective-permute-start | bytes 786440 | tf_op jit(solution)/shard_map/ppermute | solution.py:893
  44.6 14.0 %collective-permute-start.15 = (bf16[128,1024]{1,0:T(8,128)(2,1)}, bf16[128,1024]{1,0:T(8,128)(2,1)S(1)}, u32[]{:S(2)}, u32[]{:S(2)}) collective-permute-start(bf16[128,1024]{1,0:T(8,128)(2,1)} %collective-permute-done.12.refs_2_), channel_id=1, source_target_pairs={{0,2},{2,0},{4,6},{6,4},{8,10},{10,8},{12,14},{14,12},{1,3},{3,1},... | collective-permute-start | bytes 786440 | tf_op jit(solution)/shard_map/ppermute | solution.py:893
  65.2 32.8 %collective-permute-start.21 = (bf16[2,512,512]{2,1,0:T(8,128)(2,1)}, bf16[2,512,512]{2,1,0:T(8,128)(2,1)S(1)}, u32[]{:S(2)}, u32[]{:S(2)}) collective-permute-start(bf16[2,512,512]{2,1,0:T(8,128)(2,1)} %get-tuple-element.195.refs_1_.refs_0_), channel_id=1, source_target_pairs={{0,8},{2,10},{4,12},{6,14},{8,0},{10,2},{12,4},{14,6},{1,9},{3,11}... | collective-permute-start | bytes 3145736 | tf_op jit(solution)/shard_map/ppermute | solution.py:893
  65.7 32.3 %collective-permute-start.16 = (bf16[2,512,512]{2,1,0:T(8,128)(2,1)}, bf16[2,512,512]{2,1,0:T(8,128)(2,1)S(1)}, u32[]{:S(2)}, u32[]{:S(2)}) collective-permute-start(bf16[2,512,512]{2,1,0:T(8,128)(2,1)} %get-tuple-element.195.refs_1_.refs_0_), channel_id=1, source_target_pairs={{0,4},{2,6},{4,0},{6,2},{8,12},{10,14},{12,8},{14,10},{1,5},{3,7},... | collective-permute-start | bytes 3145736 | tf_op jit(solution)/shard_map/ppermute | solution.py:893
  98.0 320.0 %reduce-scatter.2.cloned.1.call-start = ((), (), s32[]{:S(2)}) async-start(), calls=%async_computation.3 | async-start | bytes 10027008 | tf_op jit(solution)/shard_map/reduce_scatter | solution.py:1162
  98.6 19.5 %collective-permute-start.26 = (bf16[512,512]{1,0:T(8,128)(2,1)S(1)}, bf16[512,512]{1,0:T(8,128)(2,1)}, u32[]{:S(2)}, u32[]{:S(2)}) collective-permute-start(bf16[512,512]{1,0:T(8,128)(2,1)S(1)} %slice_bitcast_fusion.2), channel_id=1, source_target_pairs={{0,8},{2,10},{4,12},{6,14},{8,0},{10,2},{12,4},{14,6},{1,9},{3,11}... | collective-permute-start | bytes 1572872 | tf_op jit(solution)/shard_map/ppermute | solution.py:893
  100.1 18.0 %collective-permute-start.25 = (bf16[512,512]{1,0:T(8,128)(2,1)S(1)}, bf16[512,512]{1,0:T(8,128)(2,1)}, u32[]{:S(2)}, u32[]{:S(2)}) collective-permute-start(bf16[512,512]{1,0:T(8,128)(2,1)S(1)} %slice_bitcast_fusion.3), channel_id=1, source_target_pairs={{0,4},{2,6},{4,0},{6,2},{8,12},{10,14},{12,8},{14,10},{1,5},{3,7},... | collective-permute-start | bytes 1572872 | tf_op jit(solution)/shard_map/ppermute | solution.py:893
  101.6 19.5 %collective-permute-start.24 = (bf16[2,512,512]{2,1,0:T(8,128)(2,1)S(1)}, bf16[2,512,512]{2,1,0:T(8,128)(2,1)}, u32[]{:S(2)}, u32[]{:S(2)}) collective-permute-start(bf16[2,512,512]{2,1,0:T(8,128)(2,1)S(1)} %collective-permute-done.21.refs_4_.refs_2_.refs_3_.refs_1_), channel_id=1, source_target_pairs={{0,2},{2,0},{4,6},{6,4},{8,10},{10,8},{12,14},{14,12},{1,3},{3,1},... | collective-permute-start | bytes 3145736 | tf_op jit(solution)/shard_map/ppermute | solution.py:893
  101.6 19.5 %collective-permute-start.23 = (bf16[2,512,512]{2,1,0:T(8,128)(2,1)S(1)}, bf16[2,512,512]{2,1,0:T(8,128)(2,1)}, u32[]{:S(2)}, u32[]{:S(2)}) collective-permute-start(bf16[2,512,512]{2,1,0:T(8,128)(2,1)S(1)} %collective-permute-done.16.refs_3_.refs_1_.refs_2_.refs_0_), channel_id=1, source_target_pairs={{0,2},{2,0},{4,6},{6,4},{8,10},{10,8},{12,14},{14,12},{1,3},{3,1},... | collective-permute-start | bytes 3145736 | tf_op jit(solution)/shard_map/ppermute | solution.py:893
  102.1 46.9 %collective-permute-start.29 = (bf16[2,512,512]{2,1,0:T(8,128)(2,1)}, bf16[2,512,512]{2,1,0:T(8,128)(2,1)S(1)}, u32[]{:S(2)}, u32[]{:S(2)}) collective-permute-start(bf16[2,512,512]{2,1,0:T(8,128)(2,1)} %get-tuple-element.219.refs_3_.refs_4_), channel_id=1, source_target_pairs={{0,4},{2,6},{4,8},{6,10},{8,12},{10,14},{1,5},{3,7},{5,9},{7,11},{... | collective-permute-start | bytes 3145736 | tf_op jit(solution)/shard_map/ppermute | solution.py:898
  150.9 36.2 %collective-permute-start.32 = (bf16[512,1024]{1,0:T(8,128)(2,1)S(1)}, bf16[512,1024]{1,0:T(8,128)(2,1)}, u32[]{:S(2)}, u32[]{:S(2)}) collective-permute-start(bf16[512,1024]{1,0:T(8,128)(2,1)S(1)} %copy-done.9), channel_id=1, source_target_pairs={{0,1},{1,0},{2,3},{3,2},{4,5},{5,4},{6,7},{7,6},{8,9},{9,8},{10,11... | collective-permute-start | bytes 3145736 | tf_op jit(solution)/shard_map/ppermute | solution.py:893
  177.9 31.5 %collective-permute-start.31 = (bf16[512,1024]{1,0:T(8,128)(2,1)}, bf16[512,1024]{1,0:T(8,128)(2,1)S(1)}, u32[]{:S(2)}, u32[]{:S(2)}) collective-permute-start(bf16[512,1024]{1,0:T(8,128)(2,1)} %out_projection.3.own_ref), channel_id=1, source_target_pairs={{0,1},{1,0},{2,3},{3,2},{4,5},{5,4},{6,7},{7,6},{8,9},{9,8},{10,11... | collective-permute-start | bytes 3145736 | tf_op jit(solution)/shard_map/ppermute | solution.py:893
  205.4 45.4 %collective-permute-start.34 = (bf16[512,1024]{1,0:T(8,128)(2,1)}, bf16[512,1024]{1,0:T(8,128)(2,1)S(1)}, u32[]{:S(2)}, u32[]{:S(2)}) collective-permute-start(bf16[512,1024]{1,0:T(8,128)(2,1)} %get-tuple-element.227.own_ref), channel_id=1, source_target_pairs={{0,1},{1,0},{2,3},{3,2},{4,5},{5,4},{6,7},{7,6},{8,9},{9,8},{10,11... | collective-permute-start | bytes 3145736 | tf_op jit(solution)/shard_map/ppermute | solution.py:893
  229.2 31.8 %collective-permute-start.33 = (bf16[512,1024]{1,0:T(8,128)(2,1)}, bf16[512,1024]{1,0:T(8,128)(2,1)S(1)}, u32[]{:S(2)}, u32[]{:S(2)}) collective-permute-start(bf16[512,1024]{1,0:T(8,128)(2,1)} %get-tuple-element.234.own_ref), channel_id=1, source_target_pairs={{0,1},{1,0},{2,3},{3,2},{4,5},{5,4},{6,7},{7,6},{8,9},{9,8},{10,11... | collective-permute-start | bytes 3145736 | tf_op jit(solution)/shard_map/ppermute | solution.py:893
  230.2 20.7 %collective-permute-start.35 = (bf16[256,1024]{1,0:T(8,128)(2,1)}, bf16[256,1024]{1,0:T(8,128)(2,1)S(1)}, u32[]{:S(2)}, u32[]{:S(2)}) collective-permute-start(bf16[256,1024]{1,0:T(8,128)(2,1)} %slice.154), channel_id=1, source_target_pairs={{0,14},{2,12},{4,10},{6,8},{8,6},{10,4},{12,2},{14,0},{1,15},{3,13... | collective-permute-start | bytes 1572872 | tf_op jit(solution)/shard_map/ppermute | solution.py:1164
  232.1 18.7 %collective-permute-start.36 = (f32[4,8,256]{2,1,0:T(8,128)S(1)}, f32[4,8,256]{2,1,0:T(8,128)S(1)}, u32[]{:S(2)}, u32[]{:S(2)}) collective-permute-start(f32[4,8,256]{2,1,0:T(8,128)S(1)} %slice.155), channel_id=1, source_target_pairs={{0,14},{2,12},{4,10},{6,8},{8,6},{10,4},{12,2},{14,0},{1,15},{3,13... | collective-permute-start | bytes 98312 | tf_op jit(solution)/shard_map/ppermute | solution.py:1164
  276.0 33.2 %collective-permute-start.38 = (bf16[512,1024]{1,0:T(8,128)(2,1)}, bf16[512,1024]{1,0:T(8,128)(2,1)S(1)}, u32[]{:S(2)}, u32[]{:S(2)}) collective-permute-start(bf16[512,1024]{1,0:T(8,128)(2,1)} %get-tuple-element.255), channel_id=1, source_target_pairs={{0,2},{2,0},{4,6},{6,4},{8,10},{10,8},{12,14},{14,12},{1,3},{3,1},... | collective-permute-start | bytes 3145736 | tf_op jit(solution)/shard_map/ppermute | solution.py:893
  276.0 38.6 %collective-permute-start.37 = (bf16[512,1024]{1,0:T(8,128)(2,1)S(1)}, bf16[512,1024]{1,0:T(8,128)(2,1)S(1)}, u32[]{:S(2)}, u32[]{:S(2)}) collective-permute-start(bf16[512,1024]{1,0:T(8,128)(2,1)S(1)} %copy-done.25), channel_id=1, source_target_pairs={{0,1},{1,0},{2,3},{3,2},{4,5},{5,4},{6,7},{7,6},{8,9},{9,8},{10,11... | collective-permute-start | bytes 3145736 | tf_op jit(solution)/shard_map/ppermute | solution.py:893
  278.0 36.5 %collective-permute-start.39 = (bf16[256,1024]{1,0:T(8,128)(2,1)}, bf16[256,1024]{1,0:T(8,128)(2,1)}, u32[]{:S(2)}, u32[]{:S(2)}) collective-permute-start(bf16[256,1024]{1,0:T(8,128)(2,1)} %slice.156), channel_id=1, source_target_pairs={{0,14},{2,12},{4,10},{6,8},{8,6},{10,4},{12,2},{14,0},{1,15},{3,13... | collective-permute-start | bytes 1572872 | tf_op jit(solution)/shard_map/ppermute | solution.py:1164
  279.4 35.2 %collective-permute-start.40 = (f32[4,8,256]{2,1,0:T(8,128)S(1)}, f32[4,8,256]{2,1,0:T(8,128)S(1)}, u32[]{:S(2)}, u32[]{:S(2)}) collective-permute-start(f32[4,8,256]{2,1,0:T(8,128)S(1)} %slice.157), channel_id=1, source_target_pairs={{0,14},{2,12},{4,10},{6,8},{8,6},{10,4},{12,2},{14,0},{1,15},{3,13... | collective-permute-start | bytes 98312 | tf_op jit(solution)/shard_map/ppermute | solution.py:1164
  302.8 49.6 %collective-permute-start.42 = (bf16[2,512,512]{2,1,0:T(8,128)(2,1)}, bf16[2,512,512]{2,1,0:T(8,128)(2,1)S(1)}, u32[]{:S(2)}, u32[]{:S(2)}) collective-permute-start(bf16[2,512,512]{2,1,0:T(8,128)(2,1)} %get-tuple-element.266), channel_id=1, source_target_pairs={{0,2},{2,0},{4,6},{6,4},{8,10},{10,8},{12,14},{14,12},{1,3},{3,1},... | collective-permute-start | bytes 3145736 | tf_op jit(solution)/shard_map/ppermute | solution.py:893
  309.2 46.4 %collective-permute-start.41 = (bf16[512,1024]{1,0:T(8,128)(2,1)S(1)}, bf16[512,1024]{1,0:T(8,128)(2,1)}, u32[]{:S(2)}, u32[]{:S(2)}) collective-permute-start(bf16[512,1024]{1,0:T(8,128)(2,1)S(1)} %copy-done.27), channel_id=1, source_target_pairs={{0,1},{1,0},{2,3},{3,2},{4,5},{5,4},{6,7},{7,6},{8,9},{9,8},{10,11... | collective-permute-start | bytes 3145736 | tf_op jit(solution)/shard_map/ppermute | solution.py:893
  352.7 42.7 %collective-permute-start.48 = (bf16[2,512,512]{2,1,0:T(8,128)(2,1)S(1)}, bf16[2,512,512]{2,1,0:T(8,128)(2,1)S(1)}, u32[]{:S(2)}, u32[]{:S(2)}) collective-permute-start(bf16[2,512,512]{2,1,0:T(8,128)(2,1)S(1)} %add_convert_fusion.3), channel_id=1, source_target_pairs={{4,0},{6,2},{8,4},{10,6},{12,8},{14,10},{5,1},{7,3},{9,5},{11,7},{... | collective-permute-start | bytes 3145736 | tf_op jit(solution)/shard_map/ppermute | solution.py:898
  355.6 39.6 %collective-permute-start.47 = (bf16[2,512,512]{2,1,0:T(8,128)(2,1)}, bf16[2,512,512]{2,1,0:T(8,128)(2,1)S(1)}, u32[]{:S(2)}, u32[]{:S(2)}) collective-permute-start(bf16[2,512,512]{2,1,0:T(8,128)(2,1)} %get-tuple-element.279), channel_id=1, source_target_pairs={{0,2},{2,0},{4,6},{6,4},{8,10},{10,8},{12,14},{14,12},{1,3},{3,1},... | collective-permute-start | bytes 3145736 | tf_op jit(solution)/shard_map/ppermute | solution.py:893
  355.6 35.6 %collective-permute-start.44 = (bf16[128,1024]{1,0:T(8,128)(2,1)S(1)}, bf16[128,1024]{1,0:T(8,128)(2,1)}, u32[]{:S(2)}, u32[]{:S(2)}) collective-permute-start(bf16[128,1024]{1,0:T(8,128)(2,1)S(1)} %get-tuple-element.371), channel_id=1, source_target_pairs={{0,4},{2,6},{4,0},{6,2},{8,12},{10,14},{12,8},{14,10},{1,5},{3,7},... | collective-permute-start | bytes 786440 | tf_op jit(solution)/shard_map/ppermute | solution.py:893
  360.2 31.8 %collective-permute-start.45 = (bf16[128,1024]{1,0:T(8,128)(2,1)S(1)}, bf16[128,1024]{1,0:T(8,128)(2,1)S(1)}, u32[]{:S(2)}, u32[]{:S(2)}) collective-permute-start(bf16[128,1024]{1,0:T(8,128)(2,1)S(1)} %get-tuple-element.373), channel_id=1, source_target_pairs={{0,8},{2,10},{4,12},{6,14},{8,0},{10,2},{12,4},{14,6},{1,9},{3,11}... | collective-permute-start | bytes 786440 | tf_op jit(solution)/shard_map/ppermute | solution.py:893
  361.5 31.6 %collective-permute-start.46 = (bf16[128,1024]{1,0:T(8,128)(2,1)S(1)}, bf16[128,1024]{1,0:T(8,128)(2,1)S(1)}, u32[]{:S(2)}, u32[]{:S(2)}) collective-permute-start(bf16[128,1024]{1,0:T(8,128)(2,1)S(1)} %get-tuple-element.372), channel_id=1, source_target_pairs={{0,12},{2,14},{4,8},{6,10},{8,4},{10,6},{12,0},{14,2},{1,13},{3,15... | collective-permute-start | bytes 786440 | tf_op jit(solution)/shard_map/ppermute | solution.py:893
  391.2 25.5 %collective-permute-start.43 = (bf16[256,1024]{1,0:T(8,128)(2,1)}, bf16[256,1024]{1,0:T(8,128)(2,1)S(1)}, u32[]{:S(2)}, u32[]{:S(2)}) collective-permute-start(bf16[256,1024]{1,0:T(8,128)(2,1)} %get-tuple-element.274), channel_id=1, source_target_pairs={{0,14},{2,12},{4,10},{6,8},{8,6},{10,4},{12,2},{14,0},{1,15},{3,13... | collective-permute-start | bytes 1572872 | tf_op jit(solution)/shard_map/ppermute | solution.py:1164
  392.0 27.2 %collective-permute-start.50 = (bf16[2,512,512]{2,1,0:T(8,128)(2,1)}, bf16[2,512,512]{2,1,0:T(8,128)(2,1)S(1)}, u32[]{:S(2)}, u32[]{:S(2)}) collective-permute-start(bf16[2,512,512]{2,1,0:T(8,128)(2,1)} %get-tuple-element.290), channel_id=1, source_target_pairs={{0,2},{2,0},{4,6},{6,4},{8,10},{10,8},{12,14},{14,12},{1,3},{3,1},... | collective-permute-start | bytes 3145736 | tf_op jit(solution)/shard_map/ppermute | solution.py:893
  393.8 25.4 %collective-permute-start.49 = (bf16[2,512,512]{2,1,0:T(8,128)(2,1)}, bf16[2,512,512]{2,1,0:T(8,128)(2,1)S(1)}, u32[]{:S(2)}, u32[]{:S(2)}) collective-permute-start(bf16[2,512,512]{2,1,0:T(8,128)(2,1)} %get-tuple-element.287), channel_id=1, source_target_pairs={{0,2},{2,0},{4,6},{6,4},{8,10},{10,8},{12,14},{14,12},{1,3},{3,1},... | collective-permute-start | bytes 3145736 | tf_op jit(solution)/shard_map/ppermute | solution.py:893
  396.4 21.6 %collective-permute-start.52 = (bf16[512,512]{1,0:T(8,128)(2,1)S(1)}, bf16[512,512]{1,0:T(8,128)(2,1)}, u32[]{:S(2)}, u32[]{:S(2)}) collective-permute-start(bf16[512,512]{1,0:T(8,128)(2,1)S(1)} %get-tuple-element.369), channel_id=1, source_target_pairs={{0,8},{2,10},{4,12},{6,14},{8,0},{10,2},{12,4},{14,6},{1,9},{3,11}... | collective-permute-start | bytes 1572872 | tf_op jit(solution)/shard_map/ppermute | solution.py:893
  401.5 17.7 %collective-permute-start.51 = (bf16[512,512]{1,0:T(8,128)(2,1)}, bf16[512,512]{1,0:T(8,128)(2,1)}, u32[]{:S(2)}, u32[]{:S(2)}) collective-permute-start(bf16[512,512]{1,0:T(8,128)(2,1)} %get-tuple-element.370), channel_id=1, source_target_pairs={{0,4},{2,6},{4,0},{6,2},{8,12},{10,14},{12,8},{14,10},{1,5},{3,7},... | collective-permute-start | bytes 1572872 | tf_op jit(solution)/shard_map/ppermute | solution.py:893
  417.5 39.0 %collective-permute-start.53 = (bf16[2,512,512]{2,1,0:T(8,128)(2,1)}, bf16[2,512,512]{2,1,0:T(8,128)(2,1)S(1)}, u32[]{:S(2)}, u32[]{:S(2)}) collective-permute-start(bf16[2,512,512]{2,1,0:T(8,128)(2,1)} %get-tuple-element.307), channel_id=1, source_target_pairs={{0,2},{2,0},{4,6},{6,4},{8,10},{10,8},{12,14},{14,12},{1,3},{3,1},... | collective-permute-start | bytes 3145736 | tf_op jit(solution)/shard_map/ppermute | solution.py:893
  424.4 32.2 %collective-permute-start.54 = (bf16[2,512,512]{2,1,0:T(8,128)(2,1)}, bf16[2,512,512]{2,1,0:T(8,128)(2,1)S(1)}, u32[]{:S(2)}, u32[]{:S(2)}) collective-permute-start(bf16[2,512,512]{2,1,0:T(8,128)(2,1)} %get-tuple-element.294), channel_id=1, source_target_pairs={{0,4},{2,6},{4,0},{6,2},{8,12},{10,14},{12,8},{14,10},{1,5},{3,7},... | collective-permute-start | bytes 3145736 | tf_op jit(solution)/shard_map/ppermute | solution.py:893
  425.8 30.8 %collective-permute-start.55 = (bf16[2,512,512]{2,1,0:T(8,128)(2,1)}, bf16[2,512,512]{2,1,0:T(8,128)(2,1)S(1)}, u32[]{:S(2)}, u32[]{:S(2)}) collective-permute-start(bf16[2,512,512]{2,1,0:T(8,128)(2,1)} %get-tuple-element.308), channel_id=1, source_target_pairs={{0,8},{2,10},{4,12},{6,14},{8,0},{10,2},{12,4},{14,6},{1,9},{3,11}... | collective-permute-start | bytes 3145736 | tf_op jit(solution)/shard_map/ppermute | solution.py:893
  455.1 12.0 %collective-permute-start.56 = (bf16[512,1024]{1,0:T(8,128)(2,1)}, bf16[512,1024]{1,0:T(8,128)(2,1)S(1)}, u32[]{:S(2)}, u32[]{:S(2)}) collective-permute-start(bf16[512,1024]{1,0:T(8,128)(2,1)} %get-tuple-element.311), channel_id=1, source_target_pairs={{0,2},{2,0},{4,6},{6,4},{8,10},{10,8},{12,14},{14,12},{1,3},{3,1},... | collective-permute-start | bytes 3145736 | tf_op jit(solution)/shard_map/ppermute | solution.py:893
  455.1 29.1 %collective-permute-start.58 = (bf16[512,1024]{1,0:T(8,128)(2,1)}, bf16[512,1024]{1,0:T(8,128)(2,1)}, u32[]{:S(2)}, u32[]{:S(2)}) collective-permute-start(bf16[512,1024]{1,0:T(8,128)(2,1)} %get-tuple-element.302.own_ref), channel_id=1, source_target_pairs={{0,1},{1,0},{2,3},{3,2},{4,5},{5,4},{6,7},{7,6},{8,9},{9,8},{10,11... | collective-permute-start | bytes 3145736 | tf_op jit(solution)/shard_map/ppermute | solution.py:893
  470.5 19.2 %collective-permute-start.61 = (bf16[64,1024]{1,0:T(8,128)(2,1)S(1)}, bf16[64,1024]{1,0:T(8,128)(2,1)S(1)}, u32[]{:S(2)}, u32[]{:S(2)}) collective-permute-start(bf16[64,1024]{1,0:T(8,128)(2,1)S(1)} %slice.207), channel_id=1, source_target_pairs={{0,16},{16,0},{1,17},{17,1},{2,18},{18,2},{3,19},{19,3},{4,20},{20... | collective-permute-start | bytes 393224 | tf_op jit(solution)/shard_map/ppermute | solution.py:893
  472.4 36.7 %collective-permute-start.66 = (bf16[512,1024]{1,0:T(8,128)(2,1)S(1)}, bf16[512,1024]{1,0:T(8,128)(2,1)}, u32[]{:S(2)}, u32[]{:S(2)}) collective-permute-start(bf16[512,1024]{1,0:T(8,128)(2,1)S(1)} %copy-done.53), channel_id=1, source_target_pairs={{0,1},{1,0},{2,3},{3,2},{4,5},{5,4},{6,7},{7,6},{8,9},{9,8},{10,11... | collective-permute-start | bytes 3145736 | tf_op jit(solution)/shard_map/ppermute | solution.py:893
  479.3 13.3 %collective-permute-start.57 = (bf16[512,1024]{1,0:T(8,128)(2,1)}, bf16[512,1024]{1,0:T(8,128)(2,1)S(1)}, u32[]{:S(2)}, u32[]{:S(2)}) collective-permute-start(bf16[512,1024]{1,0:T(8,128)(2,1)} %get-tuple-element.316), channel_id=1, source_target_pairs={{0,2},{2,0},{4,6},{6,4},{8,10},{10,8},{12,14},{14,12},{1,3},{3,1},... | collective-permute-start | bytes 3145736 | tf_op jit(solution)/shard_map/ppermute | solution.py:893
  479.5 13.1 %collective-permute-start.63 = (bf16[128,1024]{1,0:T(8,128)(2,1)S(1)}, bf16[128,1024]{1,0:T(8,128)(2,1)S(1)}, u32[]{:S(2)}, u32[]{:S(2)}) collective-permute-start(bf16[128,1024]{1,0:T(8,128)(2,1)S(1)} %pad_maximum_fusion.3), channel_id=1, source_target_pairs={{0,4},{2,6},{4,0},{6,2},{8,12},{10,14},{12,8},{14,10},{1,5},{3,7},... | collective-permute-start | bytes 786440 | tf_op jit(solution)/shard_map/ppermute | solution.py:893
  495.3 12.6 %collective-permute-start.69 = (bf16[64,1024]{1,0:T(8,128)(2,1)S(1)}, bf16[64,1024]{1,0:T(8,128)(2,1)S(1)}, u32[]{:S(2)}, u32[]{:S(2)}) collective-permute-start(bf16[64,1024]{1,0:T(8,128)(2,1)S(1)} %slice.216), channel_id=1, source_target_pairs={{0,16},{16,0},{1,17},{17,1},{2,18},{18,2},{3,19},{19,3},{4,20},{20... | collective-permute-start | bytes 393224 | tf_op jit(solution)/shard_map/ppermute | solution.py:893
  (95 other events, 897.5 us)
Sparse Core Ops, SparseCore 0:
  10.9 69.4 all-gather.2
  98.2 68.8 all-gather.4
  250.9 118.2 reduce-scatter.1
